TPU v7x, 32 devices: a whole 2x2x4 slice. The times are simulated.
32 devices in a mesh: ctx: 4 (over y, x), exp: 8 (over z, core).
Axes of the slice: x: 2, y: 2, z: 4, core: 2. Of those that a mesh axis runs over, the one named last changes fastest.
Arguments:
- queries: bfloat16 [64, 2, 4096], P('exp'), may hold values from -36 to 36
- cache_keys: bfloat16 [64, 256, 256], P('exp', 'ctx'), may hold values from -6 to 6
- cache_values: bfloat16 [64, 256, 256], P('exp', 'ctx'), may hold values from -6 to 6
- new_keys: bfloat16 [64, 2, 256], P('exp'), may hold values from -6 to 6
- new_values: bfloat16 [64, 2, 256], P('exp'), may hold values from -6 to 6
- lengths: int32 [64], P('exp'), may hold values from 2 to 256, as said below
- residual: bfloat16 [64, 2, 2048], P('exp'), may hold values from -12 to 12
- out_weight: bfloat16 [4096, 2048], P('ctx'), may hold values from -0.25 to 0.25
- norm_gain: bfloat16 [2048], replicated, may hold values from 0.099609375 to 1.8984375
- expert_ids: int32 [64, 2, 8], P('exp'), may hold values from 0 to 31, all different within a row; in each aligned block of 16 rows (0 to 15, 16 to 31, ..., all dimensions but the last counted through in order) at most 4 rows name the same one
- expert_weights: float32 [64, 2, 8], P('exp'), may hold values from 0.05 to 0.5
- gate_proj: bfloat16 [8, 2048, 4096], P('exp', None, 'ctx'), may hold values from -0.125 to 0.125
- up_proj: bfloat16 [8, 2048, 4096], P('exp', None, 'ctx'), may hold values from -0.125 to 0.125
- down_proj: bfloat16 [8, 4096, 2048], P('exp', 'ctx'), may hold values from -0.1875 to 0.1875
Outputs:
- layer_output: bfloat16 [64, 2, 2048], P('exp')
Inputs may be any that keep to these rules, and one draw needn't show every extreme that they name: `expert_ids`: in the 8 rows of one index of exp (both steps together) no expert is named more than 4 times; each row names 8 different experts at each step. `lengths`: some row has all 256 positions live.
All inputs are finite; a program needn't handle non-finite values.
Results may differ from a plain program's by a relative error of at most 0.0055.
Values may be sent and summed in bfloat16 or wider, within the bound.
No kernel may reach another device: no remote copies, remote signals or barrier semaphores. Data moves between devices by JAX's collectives and lax.ppermute only.
A program may use at most 64 MiB of HBM per device.

v0:
```python
import math

import jax
import jax.numpy as jnp
from jax import lax
from jax.sharding import PartitionSpec as P

D = 2048
HEADS = 32
KV_HEADS = 2
HEAD_DIM = 128
EXP_DEV = 4
TOPK = 8


NORM_EPSILON = 1e-06
MASKED_SCORE = -1e30


def per_device(
    queries,
    cache_keys,
    cache_values,
    new_keys,
    new_values,
    lengths,
    residual,
    out_weight,
    norm_gain,
    expert_ids,
    expert_weights,
    gate_proj,
    up_proj,
    down_proj,
):
    row_count, step_count, query_width = queries.shape
    window_len = cache_keys.shape[1]
    group_size = HEADS // KV_HEADS
    ctx_count = lax.axis_size("ctx")
    exp_count = lax.axis_size("exp")
    ctx_index = lax.axis_index("ctx")
    score_scale = 1.0 / math.sqrt(HEAD_DIM)
    query_heads = queries.reshape(row_count, step_count, KV_HEADS, group_size, HEAD_DIM)
    cache_heads = cache_keys.reshape(row_count, window_len, KV_HEADS, HEAD_DIM)
    fresh_heads = new_keys.reshape(row_count, step_count, KV_HEADS, HEAD_DIM)
    cache_scores = (
        jnp.einsum(
            "rskgd,rckd->rskgc", query_heads, cache_heads, preferred_element_type=jnp.float32
        )
        * score_scale
    )
    fresh_scores = (
        jnp.einsum(
            "rskgd,rtkd->rskgt", query_heads, fresh_heads, preferred_element_type=jnp.float32
        )
        * score_scale
    )
    positions = ctx_index * window_len + jnp.arange(window_len)
    live_cache = positions[None, :] < lengths[:, None]
    live_fresh = (jnp.arange(step_count)[None, :] <= jnp.arange(step_count)[:, None]) & (
        ctx_index == 0
    )
    live_cache = jnp.broadcast_to(live_cache[:, None, None, None, :], cache_scores.shape)
    live_fresh = jnp.broadcast_to(live_fresh[None, :, None, None, :], fresh_scores.shape)
    scores = jnp.concatenate([cache_scores, fresh_scores], -1)
    live = jnp.concatenate([live_cache, live_fresh], -1)
    masked_scores = jnp.where(live, scores, MASKED_SCORE)
    local_max = jnp.max(masked_scores, -1)
    softmax_terms = jnp.where(live, jnp.exp(masked_scores - local_max[..., None]), 0.0)
    local_sum = jnp.sum(softmax_terms, -1)
    value_heads = jnp.concatenate(
        [
            cache_values.reshape(row_count, window_len, KV_HEADS, HEAD_DIM),
            new_values.reshape(row_count, step_count, KV_HEADS, HEAD_DIM),
        ],
        1,
    ).astype(jnp.float32)
    weighted = jnp.einsum(
        "rskgc,rckd->rskgd", softmax_terms, value_heads, precision=lax.Precision.HIGHEST
    )
    local_max = local_max.reshape(row_count, step_count, HEADS)
    local_sum = local_sum.reshape(row_count, step_count, HEADS)
    weighted = weighted.reshape(row_count, step_count, HEADS, HEAD_DIM)
    block_heads = HEADS // ctx_count
    part_max, part_sum, part_values = (
        lax.all_to_all(local_max, "ctx", split_axis=2, concat_axis=0, tiled=True),
        lax.all_to_all(local_sum, "ctx", split_axis=2, concat_axis=0, tiled=True),
        lax.all_to_all(weighted, "ctx", split_axis=2, concat_axis=0, tiled=True),
    )
    part_max = part_max.reshape(ctx_count, row_count, step_count, block_heads)
    part_sum = part_sum.reshape(ctx_count, row_count, step_count, block_heads)
    part_values = part_values.reshape(ctx_count, row_count, step_count, block_heads, HEAD_DIM)
    best_max = jnp.max(part_max, 0)
    factors = jnp.exp(part_max - best_max[None])
    block_sum = jnp.sum(part_sum * factors, 0)
    block_values = jnp.sum(part_values * factors[..., None], 0)
    attended = block_values / block_sum[..., None]
    row_steps = row_count * step_count
    attended = attended.astype(jnp.bfloat16).reshape(row_steps, block_heads * HEAD_DIM)
    projected_part = jnp.dot(attended, out_weight, preferred_element_type=jnp.float32)
    projected = lax.psum(projected_part, "ctx")
    state = residual.reshape(row_steps, D).astype(jnp.float32) + projected
    normed = (
        state
        * lax.rsqrt(jnp.mean(state * state, -1, keepdims=True) + NORM_EPSILON)
        * norm_gain.astype(jnp.float32)
    ).astype(jnp.bfloat16)
    experts_all = exp_count * EXP_DEV
    capacity = max(2, (row_steps * TOPK + experts_all - 1) // experts_all)
    shard_count = ctx_count // EXP_DEV
    member = ctx_index // shard_count
    route_ids = expert_ids.reshape(row_steps, TOPK)
    route_weights = expert_weights.reshape(row_steps, TOPK)
    targets = jnp.arange(exp_count) * EXP_DEV + member
    matches = route_ids[:, :, None] == targets[None, None, :]
    routed_here = jnp.any(matches, 1)
    routed_count = routed_here.astype(jnp.int32)
    slot_rank = jnp.cumsum(routed_count, 0) - routed_count
    selector = routed_here[:, :, None] & (
        slot_rank[:, :, None] == jnp.arange(capacity)[None, None, :]
    )
    outgoing = jnp.einsum(
        "ndc,nm->dcm", selector.astype(jnp.bfloat16), normed, preferred_element_type=jnp.float32
    ).astype(jnp.bfloat16)
    gate_local = gate_proj[0]
    up_local = up_proj[0]
    down_local = down_proj[0]
    arrived = lax.all_to_all(outgoing, "exp", split_axis=0, concat_axis=0, tiled=True)
    gate_terms = jnp.einsum("sim,mu->siu", arrived, gate_local, preferred_element_type=jnp.float32)
    up_terms = jnp.einsum("sim,mu->siu", arrived, up_local, preferred_element_type=jnp.float32)
    activation = (jax.nn.silu(gate_terms) * up_terms).astype(jnp.bfloat16)
    returned_terms = lax.all_to_all(
        jnp.einsum(
            "siu,um->sim", activation, down_local, preferred_element_type=jnp.float32
        ).astype(jnp.bfloat16),
        "exp",
        split_axis=0,
        concat_axis=0,
        tiled=True,
    ).astype(jnp.float32)
    weight_to = jnp.sum(jnp.where(matches, route_weights[:, :, None], 0.0), 1)
    selector_wide = selector.astype(jnp.float32)
    slot_weight = jnp.einsum(
        "ndc,nd->dc", selector_wide, weight_to, precision=lax.Precision.HIGHEST
    )
    scaled_terms = returned_terms * slot_weight[..., None]
    mixture_part = jnp.einsum(
        "ndc,dcm->nm", selector_wide, scaled_terms, precision=lax.Precision.HIGHEST
    )
    mixture = lax.psum(mixture_part.astype(jnp.bfloat16), "ctx").astype(jnp.float32)
    layer_rows = (state + mixture).astype(jnp.bfloat16)
    return layer_rows.reshape(row_count, step_count, D)


def solution(mesh):
    return jax.shard_map(
        per_device,
        mesh=mesh,
        in_specs=(
            P("exp", None, None),
            P("exp", "ctx", None),
            P("exp", "ctx", None),
            P("exp", None, None),
            P("exp", None, None),
            P("exp"),
            P("exp", None, None),
            P("ctx", None),
            P(),
            P("exp", None, None),
            P("exp", None, None),
            P("exp", None, "ctx"),
            P("exp", None, "ctx"),
            P("exp", "ctx", None),
        ),
        out_specs=P("exp", None, None),
        check_vma=False,
    )
```

profile of v0, /device:TPU:0, one launch (start us, length us, event | category | flops | bytes accessed | tf_op | source)
XLA Modules:
  0.0 166.4 jit_solution(13172639657657782064)
XLA Ops:
  6.6 1.1 reshape.118
  7.6 1.0 reshape.117
  8.9 1.1 fusion.34
  10.3 0.7 broadcast_compare_fusion
  11.9 0.7 reshape.137
  12.6 5.2 %all-to-all-start.2 = ((f32[4,1,128]{2,1,0:T(1,128)}), f32[4,1,128]{2,1,0:T(1,128)S(1)}, u32[]{:S(2)}, u32[]{:S(2)}) async-start(f32[4,1,128]{2,1,0:T(1,128)} %reshape.137), calls=%async_computation.2 | async-start | bytes 4096 | tf_op jit(solution)/shard_map/all_to_all | solution.py:87
  17.9 0.8 copy.168
  18.6 1.3 convolution_bitcast_fusion.1
  20.1 0.7 reshape.135
  20.9 1.5 all-to-all-done.2
  22.4 3.2 %all-to-all-start.1 = ((f32[4,1,128]{2,1,0:T(1,128)}), f32[4,1,128]{2,1,0:T(1,128)S(1)}, u32[]{:S(2)}, u32[]{:S(2)}) async-start(f32[4,1,128]{2,1,0:T(1,128)} %reshape.135), calls=%async_computation.1 | async-start | bytes 4096 | tf_op jit(solution)/shard_map/all_to_all | solution.py:86
  25.7 0.9 copy.158
  27.2 0.7 reduce
  28.0 2.0 %all-to-all-done.1 = f32[4,1,128]{2,1,0:T(1,128)S(1)} async-done(((f32[4,1,128]{2,1,0:T(1,128)}), f32[4,1,128]{2,1,0:T(1,128)S(1)}, u32[]{:S(2)}, u32[]{:S(2)}) %all-to-all-start.1) | async-done | bytes 2080 | tf_op jit(solution)/shard_map/all_to_all | solution.py:86
  30.1 3.4 %all-to-all-start = ((f32[8,2,32,128]{3,1,0,2:T(2,128)}), f32[8,2,32,128]{3,1,0,2:T(2,128)S(1)}, u32[]{:S(2)}, u32[]{:S(2)}) async-start(f32[8,2,32,128]{3,1,0,2:T(2,128)} %copy.158), calls=%async_computation | async-start | bytes 524288 | tf_op jit(solution)/shard_map/all_to_all | solution.py:88
  33.5 0.7 reduce.1
  34.7 4.1 %all-to-all-done = f32[8,2,32,128]{3,1,0,2:T(2,128)S(1)} async-done(((f32[8,2,32,128]{3,1,0,2:T(2,128)}), f32[8,2,32,128]{3,1,0,2:T(2,128)S(1)}, u32[]{:S(2)}, u32[]{:S(2)}) %all-to-all-start) | async-done | bytes 262176 | tf_op jit(solution)/shard_map/all_to_all | solution.py:88
  39.4 3.5 %fusion.44 = f32[16,2048]{1,0:T(8,128)} fusion(bf16[1024,2048]{1,0:T(8,128)(2,1)} %param.21, bf16[2,8,8,128]{3,2,1,0:T(8,128)(2,1)S(1)} %bitcast.97), kind=kOutput, calls=%fused_computation.51 | convolution fusion | flops 67108864 | bytes 4358144 | tf_op jit(solution)/shard_map/dot_general | solution.py:100
  42.9 42.2 %all-reduce.3.cloned.1.call-done = f32[16,2048]{1,0:T(8,128)} async-done(((f32[16,2048]{1,0:T(8,128)}), f32[16,2048]{1,0:T(8,128)}) %all-reduce.3.cloned.1.call-update) | async-done | bytes 131088 | tf_op jit(solution)/shard_map/psum | solution.py:101
  85.1 1.0 multiply_reduce_fusion.1
  86.4 0.7 copy.171
  87.1 4.6 %all-to-all-start.3 = ((bf16[8,4,2048]{2,1,0:T(4,128)(2,1)}), bf16[8,4,2048]{2,1,0:T(4,128)(2,1)S(1)}, u32[]{:S(2)}, u32[]{:S(2)}) async-start(bf16[8,4,2048]{2,1,0:T(4,128)(2,1)} %copy.171), calls=%async_computation.3 | async-start | bytes 262144 | tf_op jit(solution)/shard_map/all_to_all | solution.py:128
  91.8 6.7 %all-to-all-done.3 = bf16[8,4,2048]{2,1,0:T(4,128)(2,1)S(1)} async-done(((bf16[8,4,2048]{2,1,0:T(4,128)(2,1)}), bf16[8,4,2048]{2,1,0:T(4,128)(2,1)S(1)}, u32[]{:S(2)}, u32[]{:S(2)}) %all-to-all-start.3) | async-done | bytes 131104 | tf_op jit(solution)/shard_map/all_to_all | solution.py:128
  98.5 2.9 %fusion.4 = f32[8,4,1024]{2,0,1:T(8,128)S(1)} fusion(bf16[1,2048,1024]{2,1,0:T(8,128)(2,1)} %param.25, bf16[8,4,2048]{2,1,0:T(4,128)(2,1)S(1)} %all-to-all-done.3), kind=kOutput, calls=%fused_computation.4 | convolution fusion | flops 134217728 | bytes 4456448 | tf_op jit(solution)/shard_map/sim,mu->siu/dot_general | solution.py:129
  101.5 4.9 %fusion.6 = bf16[8,4,2048]{2,0,1:T(8,128)(2,1)S(1)} fusion(bf16[1,1024,2048]{2,1,0:T(8,128)(2,1)} %param.27, bf16[1,2048,1024]{2,1,0:T(8,128)(2,1)} %param.26, f32[8,4,1024]{2,0,1:T(8,128)S(1)} %fusion.4, bf16[8,4,2048]{2,1,0:T(4,128)(2,1)S(1)} %all-to-all-done.3), kind=kOutput, calls=%fused_computation.6 | convolution fusion | flops 268697600 | bytes 8781824 | tf_op jit(solution)/shard_map/siu,um->sim/dot_general | solution.py:133
  106.4 0.7 copy.174
  107.1 3.4 %all-to-all-start.4 = ((bf16[8,4,2048]{2,1,0:T(4,128)(2,1)}), bf16[8,4,2048]{2,1,0:T(4,128)(2,1)S(1)}, u32[]{:S(2)}, u32[]{:S(2)}) async-start(bf16[8,4,2048]{2,1,0:T(4,128)(2,1)} %copy.174), calls=%async_computation.4 | async-start | bytes 262144 | tf_op jit(solution)/shard_map/all_to_all | solution.py:132
  110.8 6.4 %all-to-all-done.4 = bf16[8,4,2048]{2,1,0:T(4,128)(2,1)S(1)} async-done(((bf16[8,4,2048]{2,1,0:T(4,128)(2,1)}), bf16[8,4,2048]{2,1,0:T(4,128)(2,1)S(1)}, u32[]{:S(2)}, u32[]{:S(2)}) %all-to-all-start.4) | async-done | bytes 131104 | tf_op jit(solution)/shard_map/all_to_all | solution.py:132
  117.3 1.0 fusion.9
  118.3 39.7 %all-reduce.5.cloned.1.call-done = bf16[16,2048]{1,0:T(8,128)(2,1)} async-done(((bf16[16,2048]{1,0:T(8,128)(2,1)}), bf16[16,2048]{1,0:T(8,128)(2,1)}) %all-reduce.5.cloned.1.call-update) | async-done | bytes 65552 | tf_op jit(solution)/shard_map/psum | solution.py:150
  158.0 0.9 add_convert_fusion
  158.9 0.7 reshape.123
  (51 shorter events, 4.5 us)
Async XLA Ops:
  6.5 11.3 %copy-start = (bf16[8,64,256]{2,1,0:T(8,128)(2,1)S(1)}, bf16[8,64,256]{2,1,0:T(8,128)(2,1)}, u32[]{:S(2)}) copy-start(bf16[8,64,256]{2,1,0:T(8,128)(2,1)} %param.16) | copy-start | bytes 786436
  6.5 20.0 %copy-start.1 = (bf16[8,2,2048]{2,1,0:T(2,128)(2,1)S(1)}, bf16[8,2,2048]{2,1,0:T(2,128)(2,1)}, u32[]{:S(2)}) copy-start(bf16[8,2,2048]{2,1,0:T(2,128)(2,1)} %param.20) | copy-start | bytes 196612
  6.5 20.1 %copy-start.3 = (bf16[2048]{0:T(1024)(128)(2,1)S(1)}, bf16[2048]{0:T(1024)(128)(2,1)}, u32[]{:S(2)}) copy-start(bf16[2048]{0:T(1024)(128)(2,1)} %param.22) | copy-start | bytes 12292
  12.6 9.7 %all-to-all-start.2 = ((f32[4,1,128]{2,1,0:T(1,128)}), f32[4,1,128]{2,1,0:T(1,128)S(1)}, u32[]{:S(2)}, u32[]{:S(2)}) async-start(f32[4,1,128]{2,1,0:T(1,128)} %reshape.137), calls=%async_computation.2 | async-start | bytes 4096 | tf_op jit(solution)/shard_map/all_to_all | solution.py:87
  22.4 7.7 %all-to-all-start.1 = ((f32[4,1,128]{2,1,0:T(1,128)}), f32[4,1,128]{2,1,0:T(1,128)S(1)}, u32[]{:S(2)}, u32[]{:S(2)}) async-start(f32[4,1,128]{2,1,0:T(1,128)} %reshape.135), calls=%async_computation.1 | async-start | bytes 4096 | tf_op jit(solution)/shard_map/all_to_all | solution.py:86
  25.6 66.1 %copy-start.2 = (f32[8,2,8]{2,1,0:T(2,128)S(1)}, f32[8,2,8]{2,1,0:T(2,128)}, u32[]{:S(2)}) copy-start(f32[8,2,8]{2,1,0:T(2,128)} %param.24) | copy-start | bytes 1540
  30.1 8.8 %all-to-all-start = ((f32[8,2,32,128]{3,1,0,2:T(2,128)}), f32[8,2,32,128]{3,1,0,2:T(2,128)S(1)}, u32[]{:S(2)}, u32[]{:S(2)}) async-start(f32[8,2,32,128]{3,1,0,2:T(2,128)} %copy.158), calls=%async_computation | async-start | bytes 524288 | tf_op jit(solution)/shard_map/all_to_all | solution.py:88
  33.5 51.6 %all-reduce.3.cloned.1.call-start = ((), (), s32[]{:S(2)}) async-start(), calls=%async_computation.5 | async-start | bytes 262144 | tf_op jit(solution)/shard_map/psum | solution.py:101
  87.1 11.4 %all-to-all-start.3 = ((bf16[8,4,2048]{2,1,0:T(4,128)(2,1)}), bf16[8,4,2048]{2,1,0:T(4,128)(2,1)S(1)}, u32[]{:S(2)}, u32[]{:S(2)}) async-start(bf16[8,4,2048]{2,1,0:T(4,128)(2,1)} %copy.171), calls=%async_computation.3 | async-start | bytes 262144 | tf_op jit(solution)/shard_map/all_to_all | solution.py:128
  107.1 10.1 %all-to-all-start.4 = ((bf16[8,4,2048]{2,1,0:T(4,128)(2,1)}), bf16[8,4,2048]{2,1,0:T(4,128)(2,1)S(1)}, u32[]{:S(2)}, u32[]{:S(2)}) async-start(bf16[8,4,2048]{2,1,0:T(4,128)(2,1)} %copy.174), calls=%async_computation.4 | async-start | bytes 262144 | tf_op jit(solution)/shard_map/all_to_all | solution.py:132
  110.5 47.5 %all-reduce.5.cloned.1.call-start = ((), (), s32[]{:S(2)}) async-start(), calls=%async_computation.6 | async-start | bytes 131072 | tf_op jit(solution)/shard_map/psum | solution.py:150
Sparse Core Ops, SparseCore 0:
  43.0 42.0 all-reduce.2
  118.5 39.5 all-reduce.4
where the time goes:
time: 167 us; the launch traced here: 166 us
  waiting for transfers between devices  103 us (62%)
  starting transfers between devices  19.9 us (12%)
  matrix products  15.3 us (9%)
  between operations  13.6 us (8%)
  local copies, waits for them, and re-layouts  9.28 us (6%)
  other arithmetic  5.67 us (3%)
    psum x1, waiting for transfers between devices, per_device(): projected = lax.psum(projected_part, 'ctx')  42.2 us
    psum x1, waiting for transfers between devices, per_device(): lax.psum(mixture_part.astype(jnp.bfloat16), 'ctx').astype(jnp.float32)  39.7 us
    all_to_all x1, waiting for transfers between devices, per_device(): lax.all_to_all(outgoing, 'exp', split_axis=0, concat_axis=0, tiled=True)  6.71 us
    all_to_all x1, waiting for transfers between devices, per_device(): lax.all_to_all(jnp.einsum('siu,um->sim', activation, down_local, preferre...  6.42 us
    all_to_all x1, starting transfers between devices, per_device(): lax.all_to_all(local_sum, 'ctx', split_axis=2, concat_axis=0, tiled=True)  5.16 us
    dot_general x1, matrix products, per_device(): jnp.einsum('siu,um->sim', activation, down_local, preferred_element_type=...  4.92 us
    all_to_all x1, starting transfers between devices, per_device(): lax.all_to_all(outgoing, 'exp', split_axis=0, concat_axis=0, tiled=True)  4.61 us
    all_to_all x1, waiting for transfers between devices, per_device(): lax.all_to_all(weighted, 'ctx', split_axis=2, concat_axis=0, tiled=True)  4.08 us
  transfers between devices with their start and end apart: 7, of which 7 were waited for; matrix products, arithmetic and copies ran while one was open for 4% of the time, Pallas kernels for 0%

commit v1 on v0

v1 whole, which is shorter than its diff:
```python
import functools
import math

import jax
import jax.numpy as jnp
from jax import lax
from jax.experimental import pallas as pl
from jax.experimental.pallas import tpu as pltpu
from jax.sharding import PartitionSpec as P

D = 2048
HEADS = 32
KV_HEADS = 2
HEAD_DIM = 128
EXP_DEV = 4
TOPK = 8
LANES = 128


NORM_EPSILON = 1e-06
MASKED_SCORE = -1e30


def iota(shape, dim):
    return lax.broadcasted_iota(jnp.int32, shape, dim)


def to_column(row, count):
    return jnp.transpose(jnp.broadcast_to(row, (LANES, LANES)))[:count]


def split_three(values):
    high = values.astype(jnp.bfloat16)
    rest = values - high.astype(jnp.float32)
    middle = rest.astype(jnp.bfloat16)
    low = (rest - middle.astype(jnp.float32)).astype(jnp.bfloat16)
    return high, middle, low


def attend_kernel(
    ctx_count, me_ref, len_ref, q_ref, k_ref, v_ref, nk_ref, nv_ref, *rest
):
    outs, blocks = rest[:ctx_count], rest[ctx_count]
    rows, steps, _ = q_ref.shape
    window = k_ref.shape[1]
    row_steps = rows * steps
    group = HEADS // KV_HEADS
    block_heads = HEADS // ctx_count
    high = group * row_steps
    wide = rows * window
    scale = 1.0 / math.sqrt(HEAD_DIM)
    me = me_ref[0]
    queries = jnp.concatenate([q_ref[r] for r in range(rows)], 0)
    keys = k_ref[...].reshape(wide, KV_HEADS * HEAD_DIM)
    values = v_ref[...].reshape(wide, KV_HEADS * HEAD_DIM)
    fresh_keys = jnp.concatenate([nk_ref[r] for r in range(rows)], 0)
    fresh_values = jnp.concatenate([nv_ref[r] for r in range(rows)], 0)
    column = iota((1, wide), 1)
    column_row = column // window
    position = me * window + column % window
    limit = jnp.zeros((1, wide), jnp.int32)
    for r in range(rows):
        limit = jnp.where(column_row == r, len_ref[r], limit)
    column_code = jnp.where(position < limit, column_row, -1)
    row_index = iota((high, 1), 0) % row_steps
    row_code = row_index // steps
    row_step = row_index % steps
    fresh_column = iota((1, row_steps), 1)
    fresh_row = jnp.where(me == 0, fresh_column // steps, -1)
    fresh_step = fresh_column % steps
    live = row_code == column_code
    fresh_live = (row_code == fresh_row) & (fresh_step <= row_step)
    contract_last = (((1,), (1,)), ((), ()))
    for kv in range(KV_HEADS):
        lanes = slice(kv * HEAD_DIM, (kv + 1) * HEAD_DIM)
        heads = jnp.concatenate(
            [
                queries[:, h * HEAD_DIM : (h + 1) * HEAD_DIM]
                for h in range(kv * group, (kv + 1) * group)
            ],
            0,
        )
        scores = lax.dot_general(
            heads, keys[:, lanes], contract_last, preferred_element_type=jnp.float32
        )
        fresh = lax.dot_general(
            heads, fresh_keys[:, lanes], contract_last, preferred_element_type=jnp.float32
        )
        scores = jnp.where(live, scores * scale, MASKED_SCORE)
        fresh = jnp.where(fresh_live, fresh * scale, MASKED_SCORE)
        top = jnp.maximum(
            jnp.max(scores, 1, keepdims=True), jnp.max(fresh, 1, keepdims=True)
        )
        terms = jnp.exp(scores - top)
        fresh_terms = jnp.exp(fresh - top)
        total = jnp.sum(terms, 1, keepdims=True) + jnp.sum(fresh_terms, 1, keepdims=True)
        weighted = jnp.dot(
            terms.astype(jnp.bfloat16), values[:, lanes], preferred_element_type=jnp.float32
        ) + jnp.dot(
            fresh_terms.astype(jnp.bfloat16),
            fresh_values[:, lanes],
            preferred_element_type=jnp.float32,
        )
        mean = (weighted / total).astype(jnp.bfloat16)
        level = jnp.broadcast_to(top + jnp.log(total), (high, LANES))
        span = block_heads * row_steps
        for part in range(high // LANES):
            level_row = jnp.transpose(level[part * LANES : (part + 1) * LANES])[:8]
            pieces = split_three(level_row)
            for sub in range(LANES // span):
                dest = (kv * high + part * LANES) // span + sub
                start = part * LANES + sub * span
                blocks[dest, :span, :] = mean[start : start + span]
                for i, piece in enumerate(pieces):
                    if sub > 0:
                        piece = jnp.concatenate(
                            [piece[:, sub * span :], piece[:, : sub * span]], 1
                        )
                    blocks[dest, span + 16 * i : span + 16 * (i + 1), :] = jnp.concatenate(
                        [piece, piece], 0
                    )
    for k in range(ctx_count):
        outs[k][...] = blocks[me ^ k]


def project_kernel(ctx_count, me_ref, w_ref, *rest):
    parts, own, outs, blocks = (
        rest[:ctx_count],
        rest[ctx_count],
        rest[ctx_count + 1 : 2 * ctx_count],
        rest[2 * ctx_count],
    )
    block_heads = HEADS // ctx_count
    span = parts[0].shape[0] - 48
    row_steps = span // block_heads
    width = D // ctx_count
    levels = [
        sum(
            part[span + 16 * i : span + 16 * (i + 1), :].astype(jnp.float32)[:1]
            for i in range(3)
        )
        for part in parts
    ]
    top = functools.reduce(jnp.maximum, levels)
    factors = [jnp.exp(level - top) for level in levels]
    total = functools.reduce(jnp.add, factors)
    mixed = None
    for part, factor in zip(parts, factors):
        term = part[:span, :].astype(jnp.float32) * to_column(factor / total, span)
        mixed = term if mixed is None else mixed + term
    mixed = mixed.astype(jnp.bfloat16)
    attended = jnp.concatenate(
        [mixed[h * row_steps : (h + 1) * row_steps] for h in range(block_heads)], 1
    )
    for dest in range(ctx_count):
        projected = jnp.dot(
            attended,
            w_ref[:, dest * width : (dest + 1) * width],
            preferred_element_type=jnp.float32,
        )
        for q in range(width // LANES):
            blocks[dest, q * row_steps : (q + 1) * row_steps, :] = projected[
                :, q * LANES : (q + 1) * LANES
            ]
    me = me_ref[0]
    own[...] = blocks[me]
    for k in range(1, ctx_count):
        outs[k - 1][...] = blocks[me ^ k].astype(jnp.bfloat16)


def route_kernel(
    ctx_count, exp_count, capacity, me_ref, ids_ref, weights_ref, residual_ref,
    selector_ref, high_ref, low_ref, slice_ref
):
    rows, steps, _ = residual_ref.shape
    row_steps = rows * steps
    chunks = D // ctx_count // LANES
    shard_count = ctx_count // EXP_DEV
    high, wide = chunks * row_steps, ctx_count * exp_count * chunks * capacity
    ids = jnp.concatenate([ids_ref[...]] * chunks, 0)
    weights = jnp.concatenate([weights_ref[...]] * chunks, 0)
    column = iota((1, wide), 1)
    slot = column % capacity
    chunk = column // capacity % chunks
    dest = column // (capacity * chunks)
    expert = dest % exp_count * EXP_DEV + dest // exp_count // shard_count
    matched = jnp.zeros((high, wide), jnp.float32)
    weight = jnp.zeros((high, wide), jnp.float32)
    for k in range(TOPK):
        hit = ids[:, k : k + 1] == expert
        matched = jnp.where(hit, 1.0, matched)
        weight = jnp.where(hit, weights[:, k : k + 1], weight)
    earlier_row, earlier_column = iota((high, high), 0), iota((high, high), 1)
    earlier = (earlier_column < earlier_row) & (
        earlier_column // row_steps == earlier_row // row_steps
    )
    rank = jnp.dot(
        jnp.where(earlier, 1.0, 0.0).astype(jnp.bfloat16),
        matched.astype(jnp.bfloat16),
        preferred_element_type=jnp.float32,
    )
    row_chunk = iota((high, 1), 0) // row_steps
    chosen = (
        (matched > 0.0) & (rank == slot.astype(jnp.float32)) & (row_chunk == chunk)
    )
    selector_ref[...] = jnp.where(chosen, 1.0, 0.0).astype(jnp.bfloat16)
    weight = jnp.where(chosen, weight, 0.0)
    weight_high = weight.astype(jnp.bfloat16)
    high_ref[...] = weight_high
    low_ref[...] = (weight - weight_high.astype(jnp.float32)).astype(jnp.bfloat16)
    me = me_ref[0]
    for q in range(chunks):
        start = pl.multiple_of((me * chunks + q) * LANES, LANES)
        piece = jnp.concatenate(
            [residual_ref[r, :, pl.ds(start, LANES)] for r in range(rows)], 0
        )
        slice_ref[q * row_steps : (q + 1) * row_steps, :] = piece.astype(jnp.float32)


def dispatch_kernel(ctx_count, residual_ref, selector_ref, *rest):
    parts, state_ref, out_ref = rest[:ctx_count], rest[ctx_count], rest[ctx_count + 1]
    state = residual_ref[...]
    for part in parts:
        state = state + part[...].astype(jnp.float32)
    state_ref[...] = state
    out_ref[...] = lax.dot_general(
        selector_ref[...],
        state.astype(jnp.bfloat16),
        (((0,), (0,)), ((), ())),
        preferred_element_type=jnp.float32,
    ).astype(jnp.bfloat16)


def expert_kernel(
    ctx_count, exp_count, capacity, in_ref, gain_ref, gate_ref, up_ref, down_ref, out_ref
):
    chunks = D // ctx_count // LANES
    block = exp_count * chunks * capacity
    named = exp_count * capacity
    wanted, given = iota((block, block), 0), iota((block, block), 1)
    source = (
        wanted // capacity % exp_count * (chunks * capacity)
        + wanted // named * capacity
        + wanted % capacity
    )
    order = jnp.where(source == given, 1.0, 0.0).astype(jnp.bfloat16)
    pieces = []
    for c in range(ctx_count):
        part = jnp.dot(
            order, in_ref[c * block : (c + 1) * block, :], preferred_element_type=jnp.float32
        )
        pieces += [part[q * named : (q + 1) * named] for q in range(chunks)]
    state = jnp.concatenate(pieces, 1)
    normed = (
        state
        * lax.rsqrt(jnp.mean(state * state, -1, keepdims=True) + NORM_EPSILON)
        * gain_ref[...].astype(jnp.float32)
    ).astype(jnp.bfloat16)
    gate = jnp.dot(normed, gate_ref[0], preferred_element_type=jnp.float32)
    up = jnp.dot(normed, up_ref[0], preferred_element_type=jnp.float32)
    activation = (gate / (1.0 + jnp.exp(-gate)) * up).astype(jnp.bfloat16)
    result = jnp.dot(activation, down_ref[0], preferred_element_type=jnp.float32).astype(
        jnp.bfloat16
    )
    for c in range(ctx_count):
        part = jnp.concatenate(
            [
                result[:, (c * chunks + q) * LANES : (c * chunks + q + 1) * LANES]
                for q in range(chunks)
            ],
            0,
        )
        out_ref[c * block : (c + 1) * block, :] = lax.dot_general(
            order, part, (((0,), (0,)), ((), ())), preferred_element_type=jnp.float32
        ).astype(jnp.bfloat16)


def combine_kernel(state_ref, high_ref, low_ref, in_ref, out_ref):
    returned = in_ref[...]
    mixture = jnp.dot(high_ref[...], returned, preferred_element_type=jnp.float32) + jnp.dot(
        low_ref[...], returned, preferred_element_type=jnp.float32
    )
    out_ref[...] = (state_ref[...] + mixture).astype(jnp.bfloat16)


def assemble_kernel(ctx_count, me_ref, *rest):
    parts, out_ref = rest[:ctx_count], rest[ctx_count]
    rows, steps, _ = out_ref.shape
    row_steps = rows * steps
    chunks = D // ctx_count // LANES
    me = me_ref[0]
    for k, part in enumerate(parts):
        for q in range(chunks):
            start = pl.multiple_of(((me ^ k) * chunks + q) * LANES, LANES)
            for r in range(rows):
                first = q * row_steps + r * steps
                out_ref[r, :, pl.ds(start, LANES)] = part[first : first + steps, :]


VMEM = pl.BlockSpec(memory_space=pltpu.VMEM)
SMEM = pl.BlockSpec(memory_space=pltpu.SMEM)


def call(kernel, name, in_specs, out_shapes, operands, scratch=(), vmem=None):
    return pl.pallas_call(
        kernel,
        name=name,
        in_specs=in_specs,
        out_specs=[VMEM] * len(out_shapes),
        out_shape=[jax.ShapeDtypeStruct(shape, dtype) for shape, dtype in out_shapes],
        scratch_shapes=list(scratch),
        compiler_params=pltpu.CompilerParams(vmem_limit_bytes=vmem),
    )(*operands)


def swap(blocks):
    count = lax.axis_size("ctx")
    return [
        lax.ppermute(block, "ctx", [(i, i ^ k) for i in range(count)])
        for k, block in enumerate(blocks, 1)
    ]


def per_device(
    queries,
    cache_keys,
    cache_values,
    new_keys,
    new_values,
    lengths,
    residual,
    out_weight,
    norm_gain,
    expert_ids,
    expert_weights,
    gate_proj,
    up_proj,
    down_proj,
):
    row_count, step_count, _ = queries.shape
    row_steps = row_count * step_count
    n = lax.axis_size("ctx")
    exp_count = lax.axis_size("exp")
    me = lax.axis_index("ctx").astype(jnp.int32).reshape(1)
    experts_all = exp_count * EXP_DEV
    capacity = max(2, (row_steps * TOPK + experts_all - 1) // experts_all)
    chunks = D // n // LANES
    device_rows = chunks * capacity
    all_rows = n * exp_count * device_rows
    span = HEADS // n * row_steps
    bf16, f32 = jnp.bfloat16, jnp.float32

    message = (span + 48, LANES)
    sent = call(
        functools.partial(attend_kernel, n),
        "attend",
        [SMEM, SMEM] + [VMEM] * 5,
        [(message, bf16)] * n,
        (me, lengths, queries, cache_keys, cache_values, new_keys, new_values),
        [pltpu.VMEM((n,) + message, bf16)],
    )
    got = swap(sent[1:])
    selector, weight_high, weight_low, residual_part = call(
        functools.partial(route_kernel, n, exp_count, capacity),
        "route",
        [SMEM] + [VMEM] * 3,
        [((chunks * row_steps, all_rows), bf16)] * 3 + [((chunks * row_steps, LANES), f32)],
        (
            me,
            expert_ids.reshape(row_steps, TOPK),
            expert_weights.reshape(row_steps, TOPK),
            residual,
        ),
    )
    part = (chunks * row_steps, LANES)
    sent = call(
        functools.partial(project_kernel, n),
        "project",
        [SMEM] + [VMEM] * (n + 1),
        [(part, f32)] + [(part, bf16)] * (n - 1),
        (me, out_weight, sent[0], *got),
        [pltpu.VMEM((n,) + part, f32)],
        32 * 1024 * 1024,
    )
    got = swap(sent[1:])
    state, outgoing = call(
        functools.partial(dispatch_kernel, n),
        "dispatch",
        [VMEM] * (n + 2),
        [(part, f32), ((all_rows, LANES), bf16)],
        (residual_part, selector, sent[0], *got),
    )

    def exchange(rows):
        rows = rows.reshape(n * exp_count, device_rows, LANES)
        rows = lax.all_to_all(rows, ("ctx", "exp"), split_axis=0, concat_axis=0, tiled=True)
        return rows.reshape(all_rows, LANES)

    arrived = exchange(outgoing)
    (results,) = call(
        functools.partial(expert_kernel, n, exp_count, capacity),
        "experts",
        [VMEM] * 5,
        [((all_rows, LANES), bf16)],
        (arrived, norm_gain.reshape(1, D), gate_proj, up_proj, down_proj),
        (),
        48 * 1024 * 1024,
    )
    returned = exchange(results)
    (layer_part,) = call(
        combine_kernel,
        "combine",
        [VMEM] * 4,
        [(part, bf16)],
        (state, weight_high, weight_low, returned),
    )
    got = swap([layer_part] * (n - 1))
    (layer_rows,) = call(
        functools.partial(assemble_kernel, n),
        "assemble",
        [SMEM] + [VMEM] * n,
        [((row_count, step_count, D), bf16)],
        (me, layer_part, *got),
    )
    return layer_rows


def solution(mesh):
    return jax.shard_map(
        per_device,
        mesh=mesh,
        in_specs=(
            P("exp", None, None),
            P("exp", "ctx", None),
            P("exp", "ctx", None),
            P("exp", None, None),
            P("exp", None, None),
            P("exp"),
            P("exp", None, None),
            P("ctx", None),
            P(),
            P("exp", None, None),
            P("exp", None, None),
            P("exp", None, "ctx"),
            P("exp", None, "ctx"),
            P("exp", "ctx", None),
        ),
        out_specs=P("exp", None, None),
        check_vma=False,
    )
```

time: 167 us -> 68.5 us (0.41)
  waiting for transfers between devices: 103 us -> 16.2 us
  Pallas kernels: 0 us -> 16.6 us
  matrix products: 15.3 us -> 0 us
  between operations: 13.6 us -> 0.1 us
  blocking collectives: 0 us -> 10.6 us
  other arithmetic: 5.67 us -> 0 us
  local copies, waits for them, and re-layouts: 9.28 us -> 6.97 us
  starting transfers between devices: 19.9 us -> 17.6 us
    psum x2 -> x0, waiting for transfers between devices: 81.9 us -> none  [the longest x1 42.2 us: per_device(): projected = lax.psum(projected_part, 'ctx')]
    pallas_call x0 -> x7, Pallas kernels: none -> 16.6 us  [call(): pl.pallas_call(kernel, name=name, in_specs=in_specs, out_specs=[VMEM] * l...]
    dot_general x9 -> x0, matrix products: 15.3 us -> none  [the longest x1 4.92 us: per_device(): jnp.einsum('siu,um->sim', activation, down_local, preferred_element_type=...]
    all_to_all x5 -> x1, starting transfers between devices: 19.8 us -> 6.2 us  [exchange(): lax.all_to_all(rows, ('ctx', 'exp'), split_axis=0, concat_axis=0, tiled=T...]
    all_to_all x5 -> x1, waiting for transfers between devices: 20.7 us -> 8.15 us  [exchange(): lax.all_to_all(rows, ('ctx', 'exp'), split_axis=0, concat_axis=0, tiled=T...]
    ppermute x0 -> x9, starting transfers between devices: none -> 11.4 us  [swap(): lax.ppermute(block, 'ctx', [(i, i ^ k) for i in range(count)])]
    all_to_all x0 -> x1, blocking collectives: none -> 10.6 us  [exchange(): lax.all_to_all(rows, ('ctx', 'exp'), split_axis=0, concat_axis=0, tiled=T...]
    ppermute x0 -> x9, waiting for transfers between devices: none -> 8.05 us  [swap(): lax.ppermute(block, 'ctx', [(i, i ^ k) for i in range(count)])]
  transfers between devices with their start and end apart: 7 -> 10, of which waited for: 7 -> 7; matrix products, arithmetic and copies ran while one was open for 4% -> 0% of each run, Pallas kernels for 0% -> 3%
where the time goes in v1:
time: 68.5 us; the launch traced here: 68 us
  starting transfers between devices  17.6 us (26%)
  Pallas kernels  16.6 us (24%)
  waiting for transfers between devices  16.2 us (24%)
  blocking collectives  10.6 us (15%)
  local copies, waits for them, and re-layouts  6.97 us (10%)
    pallas_call x7, Pallas kernels, call(): pl.pallas_call(kernel, name=name, in_specs=in_specs, out_specs=[VMEM] * l...  16.6 us
    ppermute x9, starting transfers between devices, swap(): lax.ppermute(block, 'ctx', [(i, i ^ k) for i in range(count)])  11.4 us
    all_to_all x1, blocking collectives, exchange(): lax.all_to_all(rows, ('ctx', 'exp'), split_axis=0, concat_axis=0, tiled=T...  10.6 us
    all_to_all x1, waiting for transfers between devices, exchange(): lax.all_to_all(rows, ('ctx', 'exp'), split_axis=0, concat_axis=0, tiled=T...  8.15 us
    ppermute x9, waiting for transfers between devices, swap(): lax.ppermute(block, 'ctx', [(i, i ^ k) for i in range(count)])  8.05 us
    unnamed x22, local copies, waits for them, and re-layouts  6.96 us
    all_to_all x1, starting transfers between devices, exchange(): lax.all_to_all(rows, ('ctx', 'exp'), split_axis=0, concat_axis=0, tiled=T...  6.2 us
  transfers between devices with their start and end apart: 10, of which 7 were waited for; matrix products, arithmetic and copies ran while one was open for 0% of the time, Pallas kernels for 3%

profile of v1, /device:TPU:0, one launch (start us, length us, event | category | flops | bytes accessed | tf_op | source)
XLA Modules:
  0.0 68.0 jit_solution(13933142470942924709)
XLA Ops:
  0.0 2.9 %attend.1 = (bf16[176,128]{1,0:T(8,128)(2,1)}, bf16[176,128]{1,0:T(8,128)(2,1)}, bf16[176,128]{1,0:T(8,128)(2,1)}, bf16[176,128]{1,0:T(8,128)(2,1)}) custom-call(s32[1]{0:T(128)} %bitcast.me_ref, s32[8]{0:T(128)} %len_ref.1, bf16[8,2,4096]{2,1,0:T(2,128)(2,1)} %q_ref.1, bf16[8,64,256]{2,1,0:T(8,128)(2,1)} %k_ref.1, bf16[8,64,256]{2,1,0:T(8,128)(2,1)} %v_ref.1, ...), custom_call_target="tpu_custom_call" | custom-call | tf_op jit(solution)/shard_map/attend/pallas_call | solution.py:305
  2.9 2.9 %collective-permute-start = (bf16[176,128]{1,0:T(8,128)(2,1)}, bf16[176,128]{1,0:T(8,128)(2,1)S(1)}, u32[]{:S(2)}, u32[]{:S(2)}) collective-permute-start(bf16[176,128]{1,0:T(8,128)(2,1)} %get-tuple-element.22), channel_id=1, source_target_pairs={{0,8},{8,0},{16,24},{24,16},{1,9},{9,1},{17,25},{25,17},{2,10},{10... | collective-permute-start | bytes 135176 | tf_op jit(solution)/shard_map/ppermute | solution.py:319
  5.8 1.5 %collective-permute-start.1 = (bf16[176,128]{1,0:T(8,128)(2,1)}, bf16[176,128]{1,0:T(8,128)(2,1)S(1)}, u32[]{:S(2)}, u32[]{:S(2)}) collective-permute-start(bf16[176,128]{1,0:T(8,128)(2,1)} %get-tuple-element.23), channel_id=1, source_target_pairs={{0,16},{8,24},{16,0},{24,8},{1,17},{9,25},{17,1},{25,9},{2,18},{10... | collective-permute-start | bytes 135176 | tf_op jit(solution)/shard_map/ppermute | solution.py:319
  7.4 0.7 %collective-permute-done.rest_1_ = bf16[176,128]{1,0:T(8,128)(2,1)S(1)} collective-permute-done((bf16[176,128]{1,0:T(8,128)(2,1)}, bf16[176,128]{1,0:T(8,128)(2,1)S(1)}, u32[]{:S(2)}, u32[]{:S(2)}) %collective-permute-start) | collective-permute-done | bytes 45088 | tf_op jit(solution)/shard_map/ppermute | solution.py:319
  8.1 2.0 %collective-permute-done.1.rest_2_ = bf16[176,128]{1,0:T(8,128)(2,1)S(1)} collective-permute-done((bf16[176,128]{1,0:T(8,128)(2,1)}, bf16[176,128]{1,0:T(8,128)(2,1)S(1)}, u32[]{:S(2)}, u32[]{:S(2)}) %collective-permute-start.1) | collective-permute-done | bytes 45088 | tf_op jit(solution)/shard_map/ppermute | solution.py:319
  10.1 2.4 %collective-permute-done.2.rest_3_ = bf16[176,128]{1,0:T(8,128)(2,1)S(1)} collective-permute-done((bf16[176,128]{1,0:T(8,128)(2,1)}, bf16[176,128]{1,0:T(8,128)(2,1)S(1)}, u32[]{:S(2)}, u32[]{:S(2)}) %collective-permute-start.2) | collective-permute-done | bytes 45088 | tf_op jit(solution)/shard_map/ppermute | solution.py:319
  12.5 2.2 %copy-done = bf16[1024,2048]{1,0:T(8,128)(2,1)S(1)} copy-done((bf16[1024,2048]{1,0:T(8,128)(2,1)S(1)}, bf16[1024,2048]{1,0:T(8,128)(2,1)}, u32[]{:S(2)}) %copy-start) | copy-done | bytes 4194328
  14.7 0.8 %copy-done.2 = bf16[176,128]{1,0:T(8,128)(2,1)S(1)} copy-done((bf16[176,128]{1,0:T(8,128)(2,1)S(1)}, bf16[176,128]{1,0:T(8,128)(2,1)}, u32[]{:S(2)}) %copy-start.2) | copy-done | bytes 45080
  15.5 0.8 %project.1 = (f32[64,128]{1,0:T(8,128)S(1)}, bf16[64,128]{1,0:T(8,128)(2,1)S(1)}, bf16[64,128]{1,0:T(8,128)(2,1)S(1)}, bf16[64,128]{1,0:T(8,128)(2,1)S(1)}) custom-call(s32[1]{0:T(128)} %bitcast.me_ref, bf16[1024,2048]{1,0:T(8,128)(2,1)S(1)} %copy-done, bf16[176,128]{1,0:T(8,128)(2,1)S(1)} %copy-done.2, bf16[176,128]{1,0:T(8,128)(2,1)S(1)} %collective-permute-done.rest_1_, ...), custom_call_target="tpu_custom_call" | custom-call | tf_op jit(solution)/shard_map/project/pallas_call | solution.py:305
  16.3 0.6 copy-done.3
  16.9 0.5 collective-permute-start.3
  17.4 0.0 collective-permute-start.4
  17.4 2.9 %collective-permute-start.5 = (bf16[64,128]{1,0:T(8,128)(2,1)S(1)}, bf16[64,128]{1,0:T(8,128)(2,1)S(1)}, u32[]{:S(2)}, u32[]{:S(2)}) collective-permute-start(bf16[64,128]{1,0:T(8,128)(2,1)S(1)} %get-tuple-element.28), channel_id=1, source_target_pairs={{0,24},{8,16},{16,8},{24,0},{1,25},{9,17},{17,9},{25,1},{2,26},{10... | collective-permute-start | bytes 49160 | tf_op jit(solution)/shard_map/ppermute | solution.py:319
  20.4 1.8 %route.1 = (bf16[64,512]{1,0:T(8,128)(2,1)}, bf16[64,512]{1,0:T(8,128)(2,1)}, bf16[64,512]{1,0:T(8,128)(2,1)}, f32[64,128]{1,0:T(8,128)}) custom-call(s32[1]{0:T(128)} %bitcast.me_ref, s32[16,8]{1,0:T(8,128)} %bitcast.11, f32[16,8]{1,0:T(8,128)} %bitcast.12, bf16[8,2,2048]{2,1,0:T(2,128)(2,1)} %residual_ref.1), custom_call_target="tpu_custom_call" | custom-call | tf_op jit(solution)/shard_map/route/pallas_call | solution.py:305
  22.2 0.6 copy-done.4
  22.8 0.0 copy-done.5
  22.8 0.0 copy-done.6
  22.8 1.7 %dispatch.1 = (f32[64,128]{1,0:T(8,128)}, bf16[512,128]{1,0:T(8,128)(2,1)}) custom-call(f32[64,128]{1,0:T(8,128)} %get-tuple-element.19.residual_ref, bf16[64,512]{1,0:T(8,128)(2,1)} %get-tuple-element.20.selector_ref, f32[64,128]{1,0:T(8,128)} %copy-done.3, bf16[64,128]{1,0:T(8,128)(2,1)} %copy-done.4, bf16[64,128]{1,0:T(8,128)(2,1)} %copy-done.5, ...), custom_call_target="tpu_custom_call" | custom-call | tf_op jit(solution)/shard_map/dispatch/pallas_call | solution.py:305
  24.5 6.2 %all-to-all-start = ((bf16[32,16,128]{2,1,0:T(8,128)(2,1)}), bf16[32,16,128]{2,1,0:T(8,128)(2,1)S(1)}, u32[]{:S(2)}, u32[]{:S(2)}) async-start(bf16[32,16,128]{2,1,0:T(8,128)(2,1)} %bitcast.10), calls=%async_computation | async-start | bytes 262144 | tf_op jit(solution)/shard_map/all_to_all | solution.py:396
  30.7 8.1 %all-to-all-done = bf16[32,16,128]{2,1,0:T(8,128)(2,1)S(1)} async-done(((bf16[32,16,128]{2,1,0:T(8,128)(2,1)}), bf16[32,16,128]{2,1,0:T(8,128)(2,1)S(1)}, u32[]{:S(2)}, u32[]{:S(2)}) %all-to-all-start) | async-done | bytes 131104 | tf_op jit(solution)/shard_map/all_to_all | solution.py:396
  38.9 2.2 %copy-done.1 = bf16[1,2048,1024]{2,1,0:T(8,128)(2,1)S(1)} copy-done((bf16[1,2048,1024]{2,1,0:T(8,128)(2,1)S(1)}, bf16[1,2048,1024]{2,1,0:T(8,128)(2,1)}, u32[]{:S(2)}) %copy-start.1) | copy-done | bytes 4194328
  41.1 6.1 %experts.1 = bf16[512,128]{1,0:T(8,128)(2,1)S(1)} custom-call(bf16[512,128]{1,0:T(8,128)(2,1)S(1)} %bitcast.7, bf16[1,2048]{1,0:T(2,128)(2,1)S(1)} %reshape.29.gain_ref, bf16[1,2048,1024]{2,1,0:T(8,128)(2,1)S(1)} %copy-done.1, bf16[1,2048,1024]{2,1,0:T(8,128)(2,1)} %up_ref.1, bf16[1,1024,2048]{2,1,0:T(8,128)(2,1)} %down_ref.1), custom_call_target="tpu_custom_call" | custom-call | tf_op jit(solution)/shard_map/experts/pallas_call | solution.py:305
  47.2 10.6 %all_to_all.10 = bf16[32,16,128]{2,1,0:T(8,128)(2,1)} all-to-all(bf16[32,16,128]{2,1,0:T(8,128)(2,1)S(1)} %bitcast.8), channel_id=1, replica_groups=mesh['ctx'=4,'exp'=8] {'ctx','exp'}, dimensions={0} | all-to-all | bytes 262144 | tf_op jit(solution)/shard_map/all_to_all | solution.py:396
  57.8 1.8 %combine.1.rest_0_ = bf16[64,128]{1,0:T(8,128)(2,1)} custom-call(f32[64,128]{1,0:T(8,128)} %get-tuple-element.29.state_ref, bf16[64,512]{1,0:T(8,128)(2,1)} %get-tuple-element.30.high_ref, bf16[64,512]{1,0:T(8,128)(2,1)} %get-tuple-element.31.low_ref, bf16[512,128]{1,0:T(8,128)(2,1)} %bitcast.9), custom_call_target="tpu_custom_call" | custom-call | tf_op jit(solution)/shard_map/combine/pallas_call | solution.py:305
  59.6 0.8 %collective-permute-start.6 = (bf16[64,128]{1,0:T(8,128)(2,1)}, bf16[64,128]{1,0:T(8,128)(2,1)S(1)}, u32[]{:S(2)}, u32[]{:S(2)}) collective-permute-start(bf16[64,128]{1,0:T(8,128)(2,1)} %combine.1.rest_0_), channel_id=1, source_target_pairs={{0,8},{8,0},{16,24},{24,16},{1,9},{9,1},{17,25},{25,17},{2,10},{10... | collective-permute-start | bytes 49160 | tf_op jit(solution)/shard_map/ppermute | solution.py:319
  60.4 0.7 %collective-permute-start.7 = (bf16[64,128]{1,0:T(8,128)(2,1)}, bf16[64,128]{1,0:T(8,128)(2,1)S(1)}, u32[]{:S(2)}, u32[]{:S(2)}) collective-permute-start(bf16[64,128]{1,0:T(8,128)(2,1)} %combine.1.rest_0_), channel_id=1, source_target_pairs={{0,16},{8,24},{16,0},{24,8},{1,17},{9,25},{17,1},{25,9},{2,18},{10... | collective-permute-start | bytes 49160 | tf_op jit(solution)/shard_map/ppermute | solution.py:319
  61.1 2.0 %collective-permute-start.8 = (bf16[64,128]{1,0:T(8,128)(2,1)}, bf16[64,128]{1,0:T(8,128)(2,1)S(1)}, u32[]{:S(2)}, u32[]{:S(2)}) collective-permute-start(bf16[64,128]{1,0:T(8,128)(2,1)} %combine.1.rest_0_), channel_id=1, source_target_pairs={{0,24},{8,16},{16,8},{24,0},{1,25},{9,17},{17,9},{25,1},{2,26},{10... | collective-permute-start | bytes 49160 | tf_op jit(solution)/shard_map/ppermute | solution.py:319
  63.1 0.5 collective-permute-done.6.rest_1_
  63.5 1.0 %collective-permute-done.7.rest_2_ = bf16[64,128]{1,0:T(8,128)(2,1)S(1)} collective-permute-done((bf16[64,128]{1,0:T(8,128)(2,1)}, bf16[64,128]{1,0:T(8,128)(2,1)S(1)}, u32[]{:S(2)}, u32[]{:S(2)}) %collective-permute-start.7) | collective-permute-done | bytes 16416 | tf_op jit(solution)/shard_map/ppermute | solution.py:319
  64.5 1.4 %collective-permute-done.8.rest_3_ = bf16[64,128]{1,0:T(8,128)(2,1)S(1)} collective-permute-done((bf16[64,128]{1,0:T(8,128)(2,1)}, bf16[64,128]{1,0:T(8,128)(2,1)S(1)}, u32[]{:S(2)}, u32[]{:S(2)}) %collective-permute-start.8) | collective-permute-done | bytes 16416 | tf_op jit(solution)/shard_map/ppermute | solution.py:319
  66.0 0.6 copy-done.9
  66.6 1.5 %assemble.1 = bf16[8,2,2048]{2,1,0:T(2,128)(2,1)} custom-call(s32[1]{0:T(128)} %bitcast.me_ref, bf16[64,128]{1,0:T(8,128)(2,1)} %combine.1.rest_0_, bf16[64,128]{1,0:T(8,128)(2,1)} %copy-done.7, bf16[64,128]{1,0:T(8,128)(2,1)} %copy-done.8, bf16[64,128]{1,0:T(8,128)(2,1)} %copy-done.9), custom_call_target="tpu_custom_call" | custom-call | tf_op jit(solution)/shard_map/assemble/pallas_call | solution.py:305
  (19 shorter events, 0.0 us)
Async XLA Ops:
  0.0 30.7 %copy-start.10 = (bf16[2048]{0:T(1024)(128)(2,1)S(1)}, bf16[2048]{0:T(1024)(128)(2,1)}, u32[]{:S(2)}) copy-start(bf16[2048]{0:T(1024)(128)(2,1)} %param.22) | copy-start | bytes 12292
  2.9 5.2 %collective-permute-start = (bf16[176,128]{1,0:T(8,128)(2,1)}, bf16[176,128]{1,0:T(8,128)(2,1)S(1)}, u32[]{:S(2)}, u32[]{:S(2)}) collective-permute-start(bf16[176,128]{1,0:T(8,128)(2,1)} %get-tuple-element.22), channel_id=1, source_target_pairs={{0,8},{8,0},{16,24},{24,16},{1,9},{9,1},{17,25},{25,17},{2,10},{10... | collective-permute-start | bytes 135176 | tf_op jit(solution)/shard_map/ppermute | solution.py:319
  5.8 4.3 %collective-permute-start.1 = (bf16[176,128]{1,0:T(8,128)(2,1)}, bf16[176,128]{1,0:T(8,128)(2,1)S(1)}, u32[]{:S(2)}, u32[]{:S(2)}) collective-permute-start(bf16[176,128]{1,0:T(8,128)(2,1)} %get-tuple-element.23), channel_id=1, source_target_pairs={{0,16},{8,24},{16,0},{24,8},{1,17},{9,25},{17,1},{25,9},{2,18},{10... | collective-permute-start | bytes 135176 | tf_op jit(solution)/shard_map/ppermute | solution.py:319
  7.4 5.2 %collective-permute-start.2 = (bf16[176,128]{1,0:T(8,128)(2,1)}, bf16[176,128]{1,0:T(8,128)(2,1)S(1)}, u32[]{:S(2)}, u32[]{:S(2)}) collective-permute-start(bf16[176,128]{1,0:T(8,128)(2,1)} %get-tuple-element.24), channel_id=1, source_target_pairs={{0,24},{8,16},{16,8},{24,0},{1,25},{9,17},{17,9},{25,1},{2,26},{10... | collective-permute-start | bytes 135176 | tf_op jit(solution)/shard_map/ppermute | solution.py:319
  12.5 2.2 %copy-start = (bf16[1024,2048]{1,0:T(8,128)(2,1)S(1)}, bf16[1024,2048]{1,0:T(8,128)(2,1)}, u32[]{:S(2)}) copy-start(bf16[1024,2048]{1,0:T(8,128)(2,1)} %w_ref.1) | copy-start | bytes 12582916
  14.7 0.8 %copy-start.2 = (bf16[176,128]{1,0:T(8,128)(2,1)S(1)}, bf16[176,128]{1,0:T(8,128)(2,1)}, u32[]{:S(2)}) copy-start(bf16[176,128]{1,0:T(8,128)(2,1)} %get-tuple-element.21.rest_0_) | copy-start | bytes 135172
  16.3 0.6 copy-start.3
  16.9 5.3 %collective-permute-start.3 = (bf16[64,128]{1,0:T(8,128)(2,1)S(1)}, bf16[64,128]{1,0:T(8,128)(2,1)S(1)}, u32[]{:S(2)}, u32[]{:S(2)}) collective-permute-start(bf16[64,128]{1,0:T(8,128)(2,1)S(1)} %get-tuple-element.26), channel_id=1, source_target_pairs={{0,8},{8,0},{16,24},{24,16},{1,9},{9,1},{17,25},{25,17},{2,10},{10... | collective-permute-start | bytes 49160 | tf_op jit(solution)/shard_map/ppermute | solution.py:319
  17.4 4.8 %collective-permute-start.4 = (bf16[64,128]{1,0:T(8,128)(2,1)S(1)}, bf16[64,128]{1,0:T(8,128)(2,1)S(1)}, u32[]{:S(2)}, u32[]{:S(2)}) collective-permute-start(bf16[64,128]{1,0:T(8,128)(2,1)S(1)} %get-tuple-element.27), channel_id=1, source_target_pairs={{0,16},{8,24},{16,0},{24,8},{1,17},{9,25},{17,1},{25,9},{2,18},{10... | collective-permute-start | bytes 49160 | tf_op jit(solution)/shard_map/ppermute | solution.py:319
  17.4 4.8 %collective-permute-start.5 = (bf16[64,128]{1,0:T(8,128)(2,1)S(1)}, bf16[64,128]{1,0:T(8,128)(2,1)S(1)}, u32[]{:S(2)}, u32[]{:S(2)}) collective-permute-start(bf16[64,128]{1,0:T(8,128)(2,1)S(1)} %get-tuple-element.28), channel_id=1, source_target_pairs={{0,24},{8,16},{16,8},{24,0},{1,25},{9,17},{17,9},{25,1},{2,26},{10... | collective-permute-start | bytes 49160 | tf_op jit(solution)/shard_map/ppermute | solution.py:319
  22.2 0.6 copy-start.4
  22.2 0.6 copy-start.5
  22.2 0.6 copy-start.6
  24.5 14.4 %all-to-all-start = ((bf16[32,16,128]{2,1,0:T(8,128)(2,1)}), bf16[32,16,128]{2,1,0:T(8,128)(2,1)S(1)}, u32[]{:S(2)}, u32[]{:S(2)}) async-start(bf16[32,16,128]{2,1,0:T(8,128)(2,1)} %bitcast.10), calls=%async_computation | async-start | bytes 262144 | tf_op jit(solution)/shard_map/all_to_all | solution.py:396
  38.9 2.2 %copy-start.1 = (bf16[1,2048,1024]{2,1,0:T(8,128)(2,1)S(1)}, bf16[1,2048,1024]{2,1,0:T(8,128)(2,1)}, u32[]{:S(2)}) copy-start(bf16[1,2048,1024]{2,1,0:T(8,128)(2,1)} %gate_ref.1) | copy-start | bytes 12582916
  59.6 3.9 %collective-permute-start.6 = (bf16[64,128]{1,0:T(8,128)(2,1)}, bf16[64,128]{1,0:T(8,128)(2,1)S(1)}, u32[]{:S(2)}, u32[]{:S(2)}) collective-permute-start(bf16[64,128]{1,0:T(8,128)(2,1)} %combine.1.rest_0_), channel_id=1, source_target_pairs={{0,8},{8,0},{16,24},{24,16},{1,9},{9,1},{17,25},{25,17},{2,10},{10... | collective-permute-start | bytes 49160 | tf_op jit(solution)/shard_map/ppermute | solution.py:319
  60.4 4.1 %collective-permute-start.7 = (bf16[64,128]{1,0:T(8,128)(2,1)}, bf16[64,128]{1,0:T(8,128)(2,1)S(1)}, u32[]{:S(2)}, u32[]{:S(2)}) collective-permute-start(bf16[64,128]{1,0:T(8,128)(2,1)} %combine.1.rest_0_), channel_id=1, source_target_pairs={{0,16},{8,24},{16,0},{24,8},{1,17},{9,25},{17,1},{25,9},{2,18},{10... | collective-permute-start | bytes 49160 | tf_op jit(solution)/shard_map/ppermute | solution.py:319
  61.1 4.8 %collective-permute-start.8 = (bf16[64,128]{1,0:T(8,128)(2,1)}, bf16[64,128]{1,0:T(8,128)(2,1)S(1)}, u32[]{:S(2)}, u32[]{:S(2)}) collective-permute-start(bf16[64,128]{1,0:T(8,128)(2,1)} %combine.1.rest_0_), channel_id=1, source_target_pairs={{0,24},{8,16},{16,8},{24,0},{1,25},{9,17},{17,9},{25,1},{2,26},{10... | collective-permute-start | bytes 49160 | tf_op jit(solution)/shard_map/ppermute | solution.py:319
  63.5 2.4 %copy-start.7 = (bf16[64,128]{1,0:T(8,128)(2,1)}, bf16[64,128]{1,0:T(8,128)(2,1)S(1)}, u32[]{:S(2)}) copy-start(bf16[64,128]{1,0:T(8,128)(2,1)S(1)} %collective-permute-done.6.rest_1_) | copy-start | bytes 49156
  64.5 1.4 %copy-start.8 = (bf16[64,128]{1,0:T(8,128)(2,1)}, bf16[64,128]{1,0:T(8,128)(2,1)S(1)}, u32[]{:S(2)}) copy-start(bf16[64,128]{1,0:T(8,128)(2,1)S(1)} %collective-permute-done.7.rest_2_) | copy-start | bytes 49156
  65.9 0.6 copy-start.9

commit v2 on v1

--- a/solution.py
+++ b/solution.py
@@ -38,9 +38,24 @@
 
 
 def attend_kernel(
-    ctx_count, me_ref, len_ref, q_ref, k_ref, v_ref, nk_ref, nv_ref, *rest
+    ctx_count, me_ref, len_ref, q_hbm, k_hbm, v_hbm, nk_hbm, nv_hbm, *rest
 ):
     outs, blocks = rest[:ctx_count], rest[ctx_count]
+    q_ref, k_ref, v_ref, nk_ref, nv_ref, sems = rest[ctx_count + 1 :]
+    copies = [
+        pltpu.make_async_copy(source, target, sems.at[i])
+        for i, (source, target) in enumerate(
+            (
+                (k_hbm, k_ref),
+                (q_hbm, q_ref),
+                (nk_hbm, nk_ref),
+                (v_hbm, v_ref),
+                (nv_hbm, nv_ref),
+            )
+        )
+    ]
+    for copy in copies:
+        copy.start()
     rows, steps, _ = q_ref.shape
     window = k_ref.shape[1]
     row_steps = rows * steps
@@ -50,6 +65,8 @@
     wide = rows * window
     scale = 1.0 / math.sqrt(HEAD_DIM)
     me = me_ref[0]
+    for copy in copies:
+        copy.wait()
     queries = jnp.concatenate([q_ref[r] for r in range(rows)], 0)
     keys = k_ref[...].reshape(wide, KV_HEADS * HEAD_DIM)
     values = v_ref[...].reshape(wide, KV_HEADS * HEAD_DIM)
@@ -251,10 +268,12 @@
         )
         pieces += [part[q * named : (q + 1) * named] for q in range(chunks)]
     state = jnp.concatenate(pieces, 1)
+    gains = gain_ref[...].astype(jnp.float32)
+    gain = jnp.concatenate([gains[i : i + 1] for i in range(D // LANES)], 1)
     normed = (
         state
         * lax.rsqrt(jnp.mean(state * state, -1, keepdims=True) + NORM_EPSILON)
-        * gain_ref[...].astype(jnp.float32)
+        * gain
     ).astype(jnp.bfloat16)
     gate = jnp.dot(normed, gate_ref[0], preferred_element_type=jnp.float32)
     up = jnp.dot(normed, up_ref[0], preferred_element_type=jnp.float32)
@@ -298,10 +317,11 @@
 
 
 VMEM = pl.BlockSpec(memory_space=pltpu.VMEM)
+HBM = pl.BlockSpec(memory_space=pltpu.HBM)
 SMEM = pl.BlockSpec(memory_space=pltpu.SMEM)
 
 
-def call(kernel, name, in_specs, out_shapes, operands, scratch=(), vmem=None):
+def call(kernel, name, in_specs, out_shapes, operands, scratch=(), vmem=4 * 1024 * 1024, cost=None):
     return pl.pallas_call(
         kernel,
         name=name,
@@ -310,7 +330,12 @@
         out_shape=[jax.ShapeDtypeStruct(shape, dtype) for shape, dtype in out_shapes],
         scratch_shapes=list(scratch),
         compiler_params=pltpu.CompilerParams(vmem_limit_bytes=vmem),
+        cost_estimate=cost,
     )(*operands)
+
+
+def cost(micros):
+    return pl.CostEstimate(flops=micros * 1_000_000_000, bytes_accessed=1 << 20, transcendentals=0)
 
 
 def swap(blocks):
@@ -351,13 +376,17 @@
     bf16, f32 = jnp.bfloat16, jnp.float32
 
     message = (span + 48, LANES)
+    inputs = (queries, cache_keys, cache_values, new_keys, new_values)
     sent = call(
         functools.partial(attend_kernel, n),
         "attend",
-        [SMEM, SMEM] + [VMEM] * 5,
+        [SMEM, SMEM] + [HBM] * 5,
         [(message, bf16)] * n,
-        (me, lengths, queries, cache_keys, cache_values, new_keys, new_values),
-        [pltpu.VMEM((n,) + message, bf16)],
+        (me, lengths) + tuple(pltpu.with_memory_space_constraint(x, pltpu.HBM) for x in inputs),
+        [pltpu.VMEM((n,) + message, bf16)]
+        + [pltpu.VMEM(x.shape, x.dtype) for x in inputs]
+        + [pltpu.SemaphoreType.DMA((len(inputs),))],
+        cost=cost(10),
     )
     got = swap(sent[1:])
     selector, weight_high, weight_low, residual_part = call(
@@ -380,7 +409,8 @@
         [(part, f32)] + [(part, bf16)] * (n - 1),
         (me, out_weight, sent[0], *got),
         [pltpu.VMEM((n,) + part, f32)],
-        32 * 1024 * 1024,
+        8 * 1024 * 1024,
+        cost(10),
     )
     got = swap(sent[1:])
     state, outgoing = call(
@@ -389,6 +419,7 @@
         [VMEM] * (n + 2),
         [(part, f32), ((all_rows, LANES), bf16)],
         (residual_part, selector, sent[0], *got),
+        cost=cost(10),
     )
 
     def exchange(rows):
@@ -402,9 +433,10 @@
         "experts",
         [VMEM] * 5,
         [((all_rows, LANES), bf16)],
-        (arrived, norm_gain.reshape(1, D), gate_proj, up_proj, down_proj),
+        (arrived, norm_gain.reshape(D // LANES, LANES), gate_proj, up_proj, down_proj),
         (),
-        48 * 1024 * 1024,
+        20 * 1024 * 1024,
+        cost(10),
     )
     returned = exchange(results)
     (layer_part,) = call(

time: 68.5 us -> 53.6 us (0.78)
  blocking collectives: 10.6 us -> 24.2 us
  Pallas kernels: 16.6 us -> 7.91 us
  waiting for transfers between devices: 16.2 us -> 8.9 us
  local copies, waits for them, and re-layouts: 6.97 us -> 0.68 us
  starting transfers between devices: 17.6 us -> 11.6 us
    all_to_all x1 -> x2, blocking collectives: 10.6 us -> 24.2 us  [exchange(): lax.all_to_all(rows, ('ctx', 'exp'), split_axis=0, concat_axis=0, tiled=T...]
    pallas_call x7, Pallas kernels: 16.6 us -> 7.91 us  [call(): pl.pallas_call(kernel, name=name, in_specs=in_specs, out_specs=[VMEM] * l...]
    all_to_all x1 -> x0, waiting for transfers between devices: 8.15 us -> none  [exchange(): lax.all_to_all(rows, ('ctx', 'exp'), split_axis=0, concat_axis=0, tiled=T...]
    unnamed x22 -> x18, local copies, waits for them, and re-layouts: 6.96 us -> 0.68 us
    all_to_all x1 -> x0, starting transfers between devices: 6.2 us -> none  [exchange(): lax.all_to_all(rows, ('ctx', 'exp'), split_axis=0, concat_axis=0, tiled=T...]
    ppermute x9, waiting for transfers between devices: 8.05 us -> 8.9 us  [swap(): lax.ppermute(block, 'ctx', [(i, i ^ k) for i in range(count)])]
  transfers between devices with their start and end apart: 10 -> 9, of which waited for: 7 -> 7; matrix products, arithmetic and copies ran while one was open for 0% -> 0% of each run, Pallas kernels for 3% -> 1%
where the time goes in v2:
time: 53.6 us; the launch traced here: 53.4 us
  blocking collectives  24.2 us (45%)
  starting transfers between devices  11.6 us (22%)
  waiting for transfers between devices  8.9 us (17%)
  Pallas kernels  7.91 us (15%)
  local copies, waits for them, and re-layouts  0.68 us (1%)
    all_to_all x2, blocking collectives, exchange(): lax.all_to_all(rows, ('ctx', 'exp'), split_axis=0, concat_axis=0, tiled=T...  24.2 us
    ppermute x9, starting transfers between devices, swap(): lax.ppermute(block, 'ctx', [(i, i ^ k) for i in range(count)])  11.6 us
    ppermute x9, waiting for transfers between devices, swap(): lax.ppermute(block, 'ctx', [(i, i ^ k) for i in range(count)])  8.9 us
    pallas_call x7, Pallas kernels, call(): pl.pallas_call(kernel, name=name, in_specs=in_specs, out_specs=[VMEM] * l...  7.91 us
  transfers between devices with their start and end apart: 9, of which 7 were waited for; matrix products, arithmetic and copies ran while one was open for 0% of the time, Pallas kernels for 1%

profile of v2, /device:TPU:0, one launch (start us, length us, event | category | flops | bytes accessed | tf_op | source)
XLA Modules:
  0.0 53.4 jit_solution(12857212016009016760)
XLA Ops:
  0.0 0.7 %copy-done.8 = s32[8]{0:T(128)S(1)} copy-done((s32[8]{0:T(128)S(1)}, s32[8]{0:T(128)}, u32[]{:S(2)}) %copy-start.8) | copy-done | bytes 56
  0.7 3.1 %attend.1 = (bf16[176,128]{1,0:T(8,128)(2,1)S(1)}, bf16[176,128]{1,0:T(8,128)(2,1)S(1)}, bf16[176,128]{1,0:T(8,128)(2,1)S(1)}, bf16[176,128]{1,0:T(8,128)(2,1)S(1)}) custom-call(s32[1]{0:T(128)} %bitcast.me_ref, s32[8]{0:T(128)S(1)} %copy-done.8, bf16[8,2,4096]{2,1,0:T(2,128)(2,1)} %q_hbm.1, bf16[8,64,256]{2,1,0:T(8,128)(2,1)} %k_hbm.1, ...), custom_call_target="tpu_custom_call" | custom-call | flops 10000000000 | bytes 1048576 | tf_op jit(solution)/shard_map/attend/pallas_call | solution.py:325
  3.7 3.0 %collective-permute-start = (bf16[176,128]{1,0:T(8,128)(2,1)S(1)}, bf16[176,128]{1,0:T(8,128)(2,1)S(1)}, u32[]{:S(2)}, u32[]{:S(2)}) collective-permute-start(bf16[176,128]{1,0:T(8,128)(2,1)S(1)} %get-tuple-element.22), channel_id=1, source_target_pairs={{0,8},{8,0},{16,24},{24,16},{1,9},{9,1},{17,25},{25,17},{2,10},{10... | collective-permute-start | bytes 135176 | tf_op jit(solution)/shard_map/ppermute | solution.py:344
  6.7 1.5 %collective-permute-start.1 = (bf16[176,128]{1,0:T(8,128)(2,1)S(1)}, bf16[176,128]{1,0:T(8,128)(2,1)S(1)}, u32[]{:S(2)}, u32[]{:S(2)}) collective-permute-start(bf16[176,128]{1,0:T(8,128)(2,1)S(1)} %get-tuple-element.23), channel_id=1, source_target_pairs={{0,16},{8,24},{16,0},{24,8},{1,17},{9,25},{17,1},{25,9},{2,18},{10... | collective-permute-start | bytes 135176 | tf_op jit(solution)/shard_map/ppermute | solution.py:344
  8.3 0.0 collective-permute-start.2
  8.3 0.5 collective-permute-done.rest_1_
  8.8 2.0 %collective-permute-done.1.rest_2_ = bf16[176,128]{1,0:T(8,128)(2,1)S(1)} collective-permute-done((bf16[176,128]{1,0:T(8,128)(2,1)S(1)}, bf16[176,128]{1,0:T(8,128)(2,1)S(1)}, u32[]{:S(2)}, u32[]{:S(2)}) %collective-permute-start.1) | collective-permute-done | bytes 45088 | tf_op jit(solution)/shard_map/ppermute | solution.py:344
  10.8 2.4 %collective-permute-done.2.rest_3_ = bf16[176,128]{1,0:T(8,128)(2,1)S(1)} collective-permute-done((bf16[176,128]{1,0:T(8,128)(2,1)S(1)}, bf16[176,128]{1,0:T(8,128)(2,1)S(1)}, u32[]{:S(2)}, u32[]{:S(2)}) %collective-permute-start.2) | collective-permute-done | bytes 45088 | tf_op jit(solution)/shard_map/ppermute | solution.py:344
  13.2 0.0 copy-done.3
  13.2 0.8 %project.1 = (f32[64,128]{1,0:T(8,128)S(1)}, bf16[64,128]{1,0:T(8,128)(2,1)S(1)}, bf16[64,128]{1,0:T(8,128)(2,1)S(1)}, bf16[64,128]{1,0:T(8,128)(2,1)S(1)}) custom-call(s32[1]{0:T(128)} %bitcast.me_ref, bf16[1024,2048]{1,0:T(8,128)(2,1)S(1)} %copy-done.3, bf16[176,128]{1,0:T(8,128)(2,1)S(1)} %get-tuple-element.21.rest_0_, ...), custom_call_target="tpu_custom_call" | custom-call | flops 10000000000 | bytes 1048576 | tf_op jit(solution)/shard_map/project/pallas_call | solution.py:325
  14.0 0.6 %collective-permute-start.3 = (bf16[64,128]{1,0:T(8,128)(2,1)S(1)}, bf16[64,128]{1,0:T(8,128)(2,1)S(1)}, u32[]{:S(2)}, u32[]{:S(2)}) collective-permute-start(bf16[64,128]{1,0:T(8,128)(2,1)S(1)} %get-tuple-element.26), channel_id=1, source_target_pairs={{0,8},{8,0},{16,24},{24,16},{1,9},{9,1},{17,25},{25,17},{2,10},{10... | collective-permute-start | bytes 49160 | tf_op jit(solution)/shard_map/ppermute | solution.py:344
  14.6 0.0 collective-permute-start.4
  14.7 2.9 %collective-permute-start.5 = (bf16[64,128]{1,0:T(8,128)(2,1)S(1)}, bf16[64,128]{1,0:T(8,128)(2,1)S(1)}, u32[]{:S(2)}, u32[]{:S(2)}) collective-permute-start(bf16[64,128]{1,0:T(8,128)(2,1)S(1)} %get-tuple-element.28), channel_id=1, source_target_pairs={{0,24},{8,16},{16,8},{24,0},{1,25},{9,17},{17,9},{25,1},{2,26},{10... | collective-permute-start | bytes 49160 | tf_op jit(solution)/shard_map/ppermute | solution.py:344
  17.6 0.0 copy-done
  17.6 0.0 copy-done.1
  17.6 0.3 route.1
  17.9 0.0 collective-permute-done.3.rest_1_
  17.9 0.5 collective-permute-done.4.rest_2_
  18.4 0.9 %collective-permute-done.5.rest_3_ = bf16[64,128]{1,0:T(8,128)(2,1)S(1)} collective-permute-done((bf16[64,128]{1,0:T(8,128)(2,1)S(1)}, bf16[64,128]{1,0:T(8,128)(2,1)S(1)}, u32[]{:S(2)}, u32[]{:S(2)}) %collective-permute-start.5) | collective-permute-done | bytes 16416 | tf_op jit(solution)/shard_map/ppermute | solution.py:344
  19.3 0.2 dispatch.1
  19.5 14.3 %all_to_all.10 = bf16[32,16,128]{2,1,0:T(8,128)(2,1)S(1)} all-to-all(bf16[32,16,128]{2,1,0:T(8,128)(2,1)S(1)} %bitcast.9), channel_id=1, replica_groups=mesh['ctx'=4,'exp'=8] {'ctx','exp'}, dimensions={0} | all-to-all | bytes 262144 | tf_op jit(solution)/shard_map/all_to_all | solution.py:427
  33.8 0.0 copy-done.5
  33.8 2.7 %experts.1 = bf16[512,128]{1,0:T(8,128)(2,1)S(1)} custom-call(bf16[512,128]{1,0:T(8,128)(2,1)S(1)} %bitcast.10, bf16[16,128]{1,0:T(8,128)(2,1)S(1)} %bitcast.14, bf16[1,2048,1024]{2,1,0:T(8,128)(2,1)S(1)} %copy-done.4, bf16[1,2048,1024]{2,1,0:T(8,128)(2,1)S(1)} %copy-done.5, bf16[1,1024,2048]{2,1,0:T(8,128)(2,1)S(1)} %copy-done.6), custom_call_target="tpu_custom_call" | custom-call | flops 10000000000 | bytes 1048576 | tf_op jit(solution)/shard_map/experts/pallas_call | solution.py:325
  36.5 9.9 %all_to_all.11 = bf16[32,16,128]{2,1,0:T(8,128)(2,1)S(1)} all-to-all(bf16[32,16,128]{2,1,0:T(8,128)(2,1)S(1)} %bitcast.11), channel_id=1, replica_groups=mesh['ctx'=4,'exp'=8] {'ctx','exp'}, dimensions={0} | all-to-all | bytes 262144 | tf_op jit(solution)/shard_map/all_to_all | solution.py:427
  46.4 0.2 combine.1.rest_0_
  46.6 1.0 %collective-permute-start.8 = (bf16[64,128]{1,0:T(8,128)(2,1)S(1)}, bf16[64,128]{1,0:T(8,128)(2,1)S(1)}, u32[]{:S(2)}, u32[]{:S(2)}) collective-permute-start(bf16[64,128]{1,0:T(8,128)(2,1)S(1)} %combine.1.rest_0_), channel_id=1, source_target_pairs={{0,24},{8,16},{16,8},{24,0},{1,25},{9,17},{17,9},{25,1},{2,26},{10... | collective-permute-start | bytes 49160 | tf_op jit(solution)/shard_map/ppermute | solution.py:344
  47.6 1.3 %collective-permute-start.7 = (bf16[64,128]{1,0:T(8,128)(2,1)S(1)}, bf16[64,128]{1,0:T(8,128)(2,1)S(1)}, u32[]{:S(2)}, u32[]{:S(2)}) collective-permute-start(bf16[64,128]{1,0:T(8,128)(2,1)S(1)} %combine.1.rest_0_), channel_id=1, source_target_pairs={{0,16},{8,24},{16,0},{24,8},{1,17},{9,25},{17,1},{25,9},{2,18},{10... | collective-permute-start | bytes 49160 | tf_op jit(solution)/shard_map/ppermute | solution.py:344
  49.0 1.2 %collective-permute-start.6 = (bf16[64,128]{1,0:T(8,128)(2,1)S(1)}, bf16[64,128]{1,0:T(8,128)(2,1)S(1)}, u32[]{:S(2)}, u32[]{:S(2)}) collective-permute-start(bf16[64,128]{1,0:T(8,128)(2,1)S(1)} %combine.1.rest_0_), channel_id=1, source_target_pairs={{0,8},{8,0},{16,24},{24,16},{1,9},{9,1},{17,25},{25,17},{2,10},{10... | collective-permute-start | bytes 49160 | tf_op jit(solution)/shard_map/ppermute | solution.py:344
  50.2 1.4 %collective-permute-done.8.rest_3_ = bf16[64,128]{1,0:T(8,128)(2,1)S(1)} collective-permute-done((bf16[64,128]{1,0:T(8,128)(2,1)S(1)}, bf16[64,128]{1,0:T(8,128)(2,1)S(1)}, u32[]{:S(2)}, u32[]{:S(2)}) %collective-permute-start.8) | collective-permute-done | bytes 16416 | tf_op jit(solution)/shard_map/ppermute | solution.py:344
  51.5 0.0 collective-permute-done.7.rest_2_
  51.5 1.2 %collective-permute-done.6.rest_1_ = bf16[64,128]{1,0:T(8,128)(2,1)S(1)} collective-permute-done((bf16[64,128]{1,0:T(8,128)(2,1)S(1)}, bf16[64,128]{1,0:T(8,128)(2,1)S(1)}, u32[]{:S(2)}, u32[]{:S(2)}) %collective-permute-start.6) | collective-permute-done | bytes 16416 | tf_op jit(solution)/shard_map/ppermute | solution.py:344
  52.7 0.7 %assemble.1 = bf16[8,2,2048]{2,1,0:T(2,128)(2,1)} custom-call(s32[1]{0:T(128)} %bitcast.me_ref, bf16[64,128]{1,0:T(8,128)(2,1)S(1)} %combine.1.rest_0_, bf16[64,128]{1,0:T(8,128)(2,1)S(1)} %collective-permute-done.6.rest_1_, bf16[64,128]{1,0:T(8,128)(2,1)S(1)} %collective-permute-done.7.rest_2_, bf16[64,128]{1,0:T(8,128)(2,1)S(1)} %collective-permute-done.8.rest_3_), custom_call_target="tpu_custom_call" | custom-call | tf_op jit(solution)/shard_map/assemble/pallas_call | solution.py:325
  (13 shorter events, 0.0 us)
Async XLA Ops:
  0.0 0.7 %copy-start.8 = (s32[8]{0:T(128)S(1)}, s32[8]{0:T(128)}, u32[]{:S(2)}) copy-start(s32[8]{0:T(128)} %len_ref.1) | copy-start | bytes 100
  0.7 12.6 %copy-start.3 = (bf16[1024,2048]{1,0:T(8,128)(2,1)S(1)}, bf16[1024,2048]{1,0:T(8,128)(2,1)}, u32[]{:S(2)}) copy-start(bf16[1024,2048]{1,0:T(8,128)(2,1)} %w_ref.1) | copy-start | bytes 12582916
  3.7 5.0 %collective-permute-start = (bf16[176,128]{1,0:T(8,128)(2,1)S(1)}, bf16[176,128]{1,0:T(8,128)(2,1)S(1)}, u32[]{:S(2)}, u32[]{:S(2)}) collective-permute-start(bf16[176,128]{1,0:T(8,128)(2,1)S(1)} %get-tuple-element.22), channel_id=1, source_target_pairs={{0,8},{8,0},{16,24},{24,16},{1,9},{9,1},{17,25},{25,17},{2,10},{10... | collective-permute-start | bytes 135176 | tf_op jit(solution)/shard_map/ppermute | solution.py:344
  6.7 4.0 %collective-permute-start.1 = (bf16[176,128]{1,0:T(8,128)(2,1)S(1)}, bf16[176,128]{1,0:T(8,128)(2,1)S(1)}, u32[]{:S(2)}, u32[]{:S(2)}) collective-permute-start(bf16[176,128]{1,0:T(8,128)(2,1)S(1)} %get-tuple-element.23), channel_id=1, source_target_pairs={{0,16},{8,24},{16,0},{24,8},{1,17},{9,25},{17,1},{25,9},{2,18},{10... | collective-permute-start | bytes 135176 | tf_op jit(solution)/shard_map/ppermute | solution.py:344
  8.3 4.9 %collective-permute-start.2 = (bf16[176,128]{1,0:T(8,128)(2,1)S(1)}, bf16[176,128]{1,0:T(8,128)(2,1)S(1)}, u32[]{:S(2)}, u32[]{:S(2)}) collective-permute-start(bf16[176,128]{1,0:T(8,128)(2,1)S(1)} %get-tuple-element.24), channel_id=1, source_target_pairs={{0,24},{8,16},{16,8},{24,0},{1,25},{9,17},{17,9},{25,1},{2,26},{10... | collective-permute-start | bytes 135176 | tf_op jit(solution)/shard_map/ppermute | solution.py:344
  13.2 4.4 %copy-start = (bf16[8,2,2048]{2,1,0:T(2,128)(2,1)S(1)}, bf16[8,2,2048]{2,1,0:T(2,128)(2,1)}, u32[]{:S(2)}) copy-start(bf16[8,2,2048]{2,1,0:T(2,128)(2,1)} %residual_ref.1) | copy-start | bytes 196612
  13.2 4.4 %copy-start.1 = (s32[8,2,8]{2,1,0:T(2,128)S(1)}, s32[8,2,8]{2,1,0:T(2,128)}, u32[]{:S(2)}) copy-start(s32[8,2,8]{2,1,0:T(2,128)} %param.23) | copy-start | bytes 1540
  13.2 4.4 %copy-start.2 = (f32[8,2,8]{2,1,0:T(2,128)S(1)}, f32[8,2,8]{2,1,0:T(2,128)}, u32[]{:S(2)}) copy-start(f32[8,2,8]{2,1,0:T(2,128)} %param.24) | copy-start | bytes 1540
  14.0 3.8 %collective-permute-start.3 = (bf16[64,128]{1,0:T(8,128)(2,1)S(1)}, bf16[64,128]{1,0:T(8,128)(2,1)S(1)}, u32[]{:S(2)}, u32[]{:S(2)}) collective-permute-start(bf16[64,128]{1,0:T(8,128)(2,1)S(1)} %get-tuple-element.26), channel_id=1, source_target_pairs={{0,8},{8,0},{16,24},{24,16},{1,9},{9,1},{17,25},{25,17},{2,10},{10... | collective-permute-start | bytes 49160 | tf_op jit(solution)/shard_map/ppermute | solution.py:344
  14.6 3.7 %collective-permute-start.4 = (bf16[64,128]{1,0:T(8,128)(2,1)S(1)}, bf16[64,128]{1,0:T(8,128)(2,1)S(1)}, u32[]{:S(2)}, u32[]{:S(2)}) collective-permute-start(bf16[64,128]{1,0:T(8,128)(2,1)S(1)} %get-tuple-element.27), channel_id=1, source_target_pairs={{0,16},{8,24},{16,0},{24,8},{1,17},{9,25},{17,1},{25,9},{2,18},{10... | collective-permute-start | bytes 49160 | tf_op jit(solution)/shard_map/ppermute | solution.py:344
  14.7 4.6 %collective-permute-start.5 = (bf16[64,128]{1,0:T(8,128)(2,1)S(1)}, bf16[64,128]{1,0:T(8,128)(2,1)S(1)}, u32[]{:S(2)}, u32[]{:S(2)}) collective-permute-start(bf16[64,128]{1,0:T(8,128)(2,1)S(1)} %get-tuple-element.28), channel_id=1, source_target_pairs={{0,24},{8,16},{16,8},{24,0},{1,25},{9,17},{17,9},{25,1},{2,26},{10... | collective-permute-start | bytes 49160 | tf_op jit(solution)/shard_map/ppermute | solution.py:344
  19.3 14.5 %copy-start.4 = (bf16[1,2048,1024]{2,1,0:T(8,128)(2,1)S(1)}, bf16[1,2048,1024]{2,1,0:T(8,128)(2,1)}, u32[]{:S(2)}) copy-start(bf16[1,2048,1024]{2,1,0:T(8,128)(2,1)} %gate_ref.1) | copy-start | bytes 12582916
  19.3 14.5 %copy-start.5 = (bf16[1,2048,1024]{2,1,0:T(8,128)(2,1)S(1)}, bf16[1,2048,1024]{2,1,0:T(8,128)(2,1)}, u32[]{:S(2)}) copy-start(bf16[1,2048,1024]{2,1,0:T(8,128)(2,1)} %up_ref.1) | copy-start | bytes 12582916
  19.3 14.5 %copy-start.6 = (bf16[1,1024,2048]{2,1,0:T(8,128)(2,1)S(1)}, bf16[1,1024,2048]{2,1,0:T(8,128)(2,1)}, u32[]{:S(2)}) copy-start(bf16[1,1024,2048]{2,1,0:T(8,128)(2,1)} %down_ref.1) | copy-start | bytes 12582916
  19.3 14.5 %copy-start.7 = (bf16[2048]{0:T(1024)(128)(2,1)S(1)}, bf16[2048]{0:T(1024)(128)(2,1)}, u32[]{:S(2)}) copy-start(bf16[2048]{0:T(1024)(128)(2,1)} %param.22) | copy-start | bytes 12292
  46.6 4.9 %collective-permute-start.8 = (bf16[64,128]{1,0:T(8,128)(2,1)S(1)}, bf16[64,128]{1,0:T(8,128)(2,1)S(1)}, u32[]{:S(2)}, u32[]{:S(2)}) collective-permute-start(bf16[64,128]{1,0:T(8,128)(2,1)S(1)} %combine.1.rest_0_), channel_id=1, source_target_pairs={{0,24},{8,16},{16,8},{24,0},{1,25},{9,17},{17,9},{25,1},{2,26},{10... | collective-permute-start | bytes 49160 | tf_op jit(solution)/shard_map/ppermute | solution.py:344
  47.6 3.9 %collective-permute-start.7 = (bf16[64,128]{1,0:T(8,128)(2,1)S(1)}, bf16[64,128]{1,0:T(8,128)(2,1)S(1)}, u32[]{:S(2)}, u32[]{:S(2)}) collective-permute-start(bf16[64,128]{1,0:T(8,128)(2,1)S(1)} %combine.1.rest_0_), channel_id=1, source_target_pairs={{0,16},{8,24},{16,0},{24,8},{1,17},{9,25},{17,1},{25,9},{2,18},{10... | collective-permute-start | bytes 49160 | tf_op jit(solution)/shard_map/ppermute | solution.py:344
  49.0 3.7 %collective-permute-start.6 = (bf16[64,128]{1,0:T(8,128)(2,1)S(1)}, bf16[64,128]{1,0:T(8,128)(2,1)S(1)}, u32[]{:S(2)}, u32[]{:S(2)}) collective-permute-start(bf16[64,128]{1,0:T(8,128)(2,1)S(1)} %combine.1.rest_0_), channel_id=1, source_target_pairs={{0,8},{8,0},{16,24},{24,16},{1,9},{9,1},{17,25},{25,17},{2,10},{10... | collective-permute-start | bytes 49160 | tf_op jit(solution)/shard_map/ppermute | solution.py:344

commit v3 on v2

v3 whole, which is shorter than its diff:
```python
import functools
import math

import jax
import jax.numpy as jnp
from jax import lax
from jax.experimental import pallas as pl
from jax.experimental.pallas import tpu as pltpu
from jax.sharding import PartitionSpec as P

D = 2048
HEADS = 32
KV_HEADS = 2
HEAD_DIM = 128
EXP_DEV = 4
TOPK = 8
LANES = 128
SUBLANES = 8


NORM_EPSILON = 1e-06
MASKED_SCORE = -1e30


def iota(shape, dim):
    return lax.broadcasted_iota(jnp.int32, shape, dim)


def to_column(row, count):
    return jnp.transpose(jnp.broadcast_to(row, (LANES, LANES)))[:count]


def split_three(values):
    high = values.astype(jnp.bfloat16)
    rest = values - high.astype(jnp.float32)
    middle = rest.astype(jnp.bfloat16)
    low = (rest - middle.astype(jnp.float32)).astype(jnp.bfloat16)
    return high, middle, low


def every(values, first, step):
    count = values.shape[0] // SUBLANES
    return jnp.concatenate(
        [values[i * SUBLANES : (i + 1) * SUBLANES] for i in range(first, count, step)], 0
    )


def interleave(parts):
    count = parts[0].shape[0] // SUBLANES
    return jnp.concatenate(
        [part[i * SUBLANES : (i + 1) * SUBLANES] for i in range(count) for part in parts], 0
    )


def attend_kernel(
    ctx_count, me_ref, len_hbm, q_hbm, k_hbm, v_hbm, nk_hbm, nv_hbm, *rest
):
    outs, blocks = rest[:ctx_count], rest[ctx_count]
    len_ref, q_ref, k_ref, v_ref, nk_ref, nv_ref, sems = rest[ctx_count + 1 :]
    early, late = [
        [pltpu.make_async_copy(source, target, sems.at[i]) for i, source, target in group]
        for group in (
            (
                (0, k_hbm, k_ref),
                (1, q_hbm, q_ref),
                (2, len_hbm, len_ref),
                (3, nk_hbm, nk_ref),
            ),
            ((4, v_hbm, v_ref), (5, nv_hbm, nv_ref)),
        )
    ]
    for copy in early + late:
        copy.start()
    rows, steps, _ = q_ref.shape
    window = k_ref.shape[1]
    row_steps = rows * steps
    group = HEADS // KV_HEADS
    block_heads = HEADS // ctx_count
    high = group * row_steps
    wide = rows * window
    pieces = row_steps // SUBLANES
    piece_rows = rows // pieces
    piece_high = group * SUBLANES
    piece_wide = piece_rows * window
    scale = 1.0 / math.sqrt(HEAD_DIM)
    me = me_ref[0]
    for copy in early + late:
        copy.wait()
    values = v_ref[...].reshape(wide, KV_HEADS * HEAD_DIM)
    fresh_values = jnp.concatenate([nv_ref[r] for r in range(rows)], 0)
    queries = jnp.concatenate([q_ref[r] for r in range(rows)], 0)
    keys = k_ref[...].reshape(wide, KV_HEADS * HEAD_DIM)
    fresh_keys = jnp.concatenate([nk_ref[r] for r in range(rows)], 0)
    column = iota((1, piece_wide), 1)
    column_row = column // window
    position = me * window + column % window
    row_index = iota((piece_high, 1), 0) % SUBLANES
    fresh_column = iota((1, row_steps), 1)
    live, fresh_live = [], []
    for p in range(pieces):
        limit = jnp.zeros((1, piece_wide), jnp.int32)
        for r in range(piece_rows):
            limit = jnp.where(column_row == r, len_ref[p * piece_rows + r], limit)
        live.append(row_index // steps == jnp.where(position < limit, column_row, -1))
        fresh_row = jnp.where(me == 0, fresh_column // steps - p * piece_rows, -1)
        fresh_live.append(
            (row_index // steps == fresh_row) & (fresh_column % steps <= row_index % steps)
        )
    contract_last = (((1,), (1,)), ((), ()))
    for kv in range(KV_HEADS):
        lanes = slice(kv * HEAD_DIM, (kv + 1) * HEAD_DIM)
        heads = jnp.concatenate(
            [
                queries[:, h * HEAD_DIM : (h + 1) * HEAD_DIM]
                for h in range(kv * group, (kv + 1) * group)
            ],
            0,
        )
        scores = lax.dot_general(
            heads, keys[:, lanes], contract_last, preferred_element_type=jnp.float32
        )
        fresh = lax.dot_general(
            heads, fresh_keys[:, lanes], contract_last, preferred_element_type=jnp.float32
        )
        means, levels = [], []
        for p in range(pieces):
            span = slice(p * piece_wide, (p + 1) * piece_wide)
            part = every(scores[:, span], p, pieces)
            part = jnp.where(live[p], part * scale, MASKED_SCORE)
            last = every(fresh, p, pieces)
            last = jnp.where(fresh_live[p], last * scale, MASKED_SCORE)
            top = jnp.maximum(
                jnp.max(part, 1, keepdims=True), jnp.max(last, 1, keepdims=True)
            )
            terms = jnp.exp(part - top)
            last_terms = jnp.exp(last - top)
            total = jnp.sum(terms, 1, keepdims=True) + jnp.sum(last_terms, 1, keepdims=True)
            weighted = jnp.dot(
                terms.astype(jnp.bfloat16),
                values[span, lanes],
                preferred_element_type=jnp.float32,
            ) + jnp.dot(
                last_terms.astype(jnp.bfloat16),
                fresh_values[:, lanes],
                preferred_element_type=jnp.float32,
            )
            means.append(weighted / total)
            levels.append(jnp.broadcast_to(top + jnp.log(total), (piece_high, LANES)))
        mean = interleave(means).astype(jnp.bfloat16)
        level = interleave(levels)
        span = block_heads * row_steps
        for part in range(high // LANES):
            level_row = jnp.transpose(level[part * LANES : (part + 1) * LANES])[:SUBLANES]
            splits = split_three(level_row)
            for sub in range(LANES // span):
                dest = (kv * high + part * LANES) // span + sub
                start = part * LANES + sub * span
                blocks[dest, :span, :] = mean[start : start + span]
                for i, piece in enumerate(splits):
                    if sub > 0:
                        piece = jnp.concatenate(
                            [piece[:, sub * span :], piece[:, : sub * span]], 1
                        )
                    blocks[dest, span + 16 * i : span + 16 * (i + 1), :] = jnp.concatenate(
                        [piece, piece], 0
                    )
    for k in range(ctx_count):
        outs[k][...] = blocks[me ^ k]


def project_kernel(ctx_count, w_ref, *rest):
    parts, out_ref = rest[:ctx_count], rest[ctx_count]
    block_heads = HEADS // ctx_count
    span = parts[0].shape[0] - 48
    row_steps = span // block_heads
    levels = [
        sum(
            part[span + 16 * i : span + 16 * (i + 1), :].astype(jnp.float32)[:1]
            for i in range(3)
        )
        for part in parts
    ]
    top = functools.reduce(jnp.maximum, levels)
    factors = [jnp.exp(level - top) for level in levels]
    total = functools.reduce(jnp.add, factors)
    mixed = None
    for part, factor in zip(parts, factors):
        term = part[:span, :].astype(jnp.float32) * to_column(factor / total, span)
        mixed = term if mixed is None else mixed + term
    mixed = mixed.astype(jnp.bfloat16)
    attended = jnp.concatenate(
        [mixed[h * row_steps : (h + 1) * row_steps] for h in range(block_heads)], 1
    )
    out_ref[...] = jnp.dot(
        attended, w_ref[...], preferred_element_type=jnp.float32
    ).astype(jnp.bfloat16)


def route_kernel(
    ctx_count, exp_count, capacity, me_ref, home_ref, ids_ref, weights_ref, residual_ref,
    selector_ref, high_ref, low_ref, rows_ref
):
    rows, steps, _ = residual_ref.shape
    row_steps = rows * steps
    wide = exp_count * capacity
    me, home = me_ref[0], home_ref[0]
    column = iota((1, wide), 1)
    slot = column % capacity
    other = column // capacity % 2
    hop = column // (2 * capacity)
    crossed = jnp.where(hop == 0, 0, 1)
    device = home ^ (2 * hop) ^ crossed ^ other
    expert = device * EXP_DEV + me // (ctx_count // EXP_DEV)
    matched = jnp.zeros((row_steps, wide), jnp.float32)
    weight = jnp.zeros((row_steps, wide), jnp.float32)
    for k in range(TOPK):
        hit = ids_ref[:, k : k + 1] == expert
        matched = jnp.where(hit, 1.0, matched)
        weight = jnp.where(hit, weights_ref[:, k : k + 1], weight)
    earlier = iota((row_steps, row_steps), 1) < iota((row_steps, row_steps), 0)
    rank = jnp.dot(
        jnp.where(earlier, 1.0, 0.0).astype(jnp.bfloat16),
        matched.astype(jnp.bfloat16),
        preferred_element_type=jnp.float32,
    )
    chosen = (matched > 0.0) & (rank == slot.astype(jnp.float32))
    selector_ref[...] = jnp.where(chosen, 1.0, 0.0).astype(jnp.bfloat16)
    weight = jnp.where(chosen, weight, 0.0)
    weight_high = weight.astype(jnp.bfloat16)
    high_ref[...] = weight_high
    low_ref[...] = (weight - weight_high.astype(jnp.float32)).astype(jnp.bfloat16)
    rows_ref[...] = jnp.concatenate(
        [residual_ref[r].astype(jnp.float32) for r in range(rows)], 0
    )


def tree_sum(parts):
    values = [part[...].astype(jnp.float32) for part in parts]
    while len(values) > 1:
        values = [values[i] + values[i + 1] for i in range(0, len(values), 2)]
    return values[0]


def dispatch_kernel(ctx_count, residual_ref, selector_ref, *rest):
    parts, state_ref, outs = rest[:ctx_count], rest[ctx_count], rest[ctx_count + 1 :]
    state = residual_ref[...] + tree_sum(parts)
    state_ref[...] = state
    picked = lax.dot_general(
        selector_ref[...],
        state.astype(jnp.bfloat16),
        (((0,), (0,)), ((), ())),
        preferred_element_type=jnp.float32,
    )
    block = outs[0].shape[0]
    for j, out in enumerate(outs):
        out[...] = picked[j * block : (j + 1) * block].astype(jnp.bfloat16)


def gather_kernel(*refs):
    blocks, keep_ref, send_ref = refs[:-2], refs[-2], refs[-1]
    half = blocks[0].shape[0] // 2
    values = [block[...].astype(jnp.float32) for block in blocks]
    keep_ref[...] = jnp.concatenate([value[:half] for value in values], 0).astype(jnp.bfloat16)
    send_ref[...] = jnp.concatenate([value[half:] for value in values], 0).astype(jnp.bfloat16)


def expert_kernel(kept_ref, got_ref, gain_ref, gate_ref, up_ref, down_ref, keep_ref, send_ref):
    half = kept_ref.shape[0]
    state = jnp.concatenate(
        [kept_ref[...].astype(jnp.float32), got_ref[...].astype(jnp.float32)], 0
    )
    gains = gain_ref[...].astype(jnp.float32)
    gain = jnp.concatenate([gains[i : i + 1] for i in range(D // LANES)], 1)
    normed = (
        state
        * lax.rsqrt(jnp.mean(state * state, -1, keepdims=True) + NORM_EPSILON)
        * gain
    ).astype(jnp.bfloat16)
    spare = max(0, LANES - 2 * half)
    if spare:
        normed = jnp.concatenate([normed, jnp.zeros((spare, D), jnp.bfloat16)], 0)
    gate = jnp.dot(normed, gate_ref[0], preferred_element_type=jnp.float32)
    up = jnp.dot(normed, up_ref[0], preferred_element_type=jnp.float32)
    activation = (gate / (1.0 + jnp.exp(-gate)) * up).astype(jnp.bfloat16)
    result = jnp.dot(activation, down_ref[0], preferred_element_type=jnp.float32)
    keep_ref[...] = result[:half].astype(jnp.bfloat16)
    send_ref[...] = result[half : 2 * half].astype(jnp.bfloat16)


def scatter_kernel(kept_ref, got_ref, *outs):
    half = outs[0].shape[0] // 2
    kept, got = kept_ref[...].astype(jnp.float32), got_ref[...].astype(jnp.float32)
    for j, out in enumerate(outs):
        span = slice(j * half, (j + 1) * half)
        out[...] = jnp.concatenate([kept[span], got[span]], 0).astype(jnp.bfloat16)


def combine_kernel(high_ref, low_ref, *refs):
    blocks, out_ref = refs[:-1], refs[-1]
    returned = jnp.concatenate([block[...].astype(jnp.float32) for block in blocks], 0).astype(
        jnp.bfloat16
    )
    mixture = jnp.dot(high_ref[...], returned, preferred_element_type=jnp.float32) + jnp.dot(
        low_ref[...], returned, preferred_element_type=jnp.float32
    )
    out_ref[...] = mixture.astype(jnp.bfloat16)


def finish_kernel(state_ref, *refs):
    parts, out_ref = refs[:-1], refs[-1]
    rows, steps, _ = out_ref.shape
    layer = (state_ref[...] + tree_sum(parts)).astype(jnp.bfloat16)
    for r in range(rows):
        out_ref[r] = layer[r * steps : (r + 1) * steps]


VMEM = pl.BlockSpec(memory_space=pltpu.VMEM)
HBM = pl.BlockSpec(memory_space=pltpu.HBM)
SMEM = pl.BlockSpec(memory_space=pltpu.SMEM)


def call(kernel, name, in_specs, out_shapes, operands, scratch=(), out_spec=None, vmem=4 * 1024 * 1024, cost=None):
    return pl.pallas_call(
        kernel,
        name=name,
        in_specs=in_specs,
        out_specs=[out_spec or VMEM] * len(out_shapes),
        out_shape=[jax.ShapeDtypeStruct(shape, dtype) for shape, dtype in out_shapes],
        scratch_shapes=list(scratch),
        compiler_params=pltpu.CompilerParams(vmem_limit_bytes=vmem),
        cost_estimate=cost,
    )(*operands)


def cost(micros):
    return pl.CostEstimate(flops=micros * 1_000_000_000, bytes_accessed=1 << 20, transcendentals=0)


def move(block, ctx_hop, exp_hop):
    n, exp_count = lax.axis_size("ctx"), lax.axis_size("exp")
    pairs = [
        (c * exp_count + e, (c ^ ctx_hop) * exp_count + (e ^ exp_hop))
        for c in range(n)
        for e in range(exp_count)
    ]
    return lax.ppermute(block, ("ctx", "exp"), pairs)


def per_device(
    queries,
    cache_keys,
    cache_values,
    new_keys,
    new_values,
    lengths,
    residual,
    out_weight,
    norm_gain,
    expert_ids,
    expert_weights,
    gate_proj,
    up_proj,
    down_proj,
):
    row_count, step_count, _ = queries.shape
    row_steps = row_count * step_count
    n = lax.axis_size("ctx")
    exp_count = lax.axis_size("exp")
    me = lax.axis_index("ctx").astype(jnp.int32).reshape(1)
    home = lax.axis_index("exp").astype(jnp.int32).reshape(1)
    experts_all = exp_count * EXP_DEV
    capacity = max(2, (row_steps * TOPK + experts_all - 1) // experts_all)
    chips = exp_count // 2
    span = HEADS // n * row_steps
    bf16, f32 = jnp.bfloat16, jnp.float32
    hidden = (row_steps, D)
    block = (2 * capacity, D)
    half = (chips * capacity, D)

    message = (span + 48, LANES)
    inputs = (lengths, queries, cache_keys, cache_values, new_keys, new_values)
    sent = call(
        functools.partial(attend_kernel, n),
        "attend",
        [SMEM] + [HBM] * 6,
        [(message, bf16)] * n,
        (me,) + tuple(pltpu.with_memory_space_constraint(x, pltpu.HBM) for x in inputs),
        [pltpu.VMEM((n,) + message, bf16)]
        + [pltpu.SMEM(lengths.shape, lengths.dtype)]
        + [pltpu.VMEM(x.shape, x.dtype) for x in inputs[1:]]
        + [pltpu.SemaphoreType.DMA((len(inputs),))],
        cost=cost(10),
    )
    got = [move(x, j, 1) for j, x in enumerate(sent)]
    selector, weight_high, weight_low, residual_rows = call(
        functools.partial(route_kernel, n, exp_count, capacity),
        "route",
        [SMEM] * 2 + [VMEM] * 3,
        [((row_steps, exp_count * capacity), bf16)] * 3 + [(hidden, f32)],
        (
            me,
            home,
            expert_ids.reshape(row_steps, TOPK),
            expert_weights.reshape(row_steps, TOPK),
            residual,
        ),
    )
    (projected,) = call(
        functools.partial(project_kernel, n),
        "project",
        [VMEM] * (n + 1),
        [(hidden, bf16)],
        (out_weight, *got),
        vmem=8 * 1024 * 1024,
        cost=cost(10),
    )
    got = [move(projected, j, 1) for j in range(n)]
    state, *outgoing = call(
        functools.partial(dispatch_kernel, n),
        "dispatch",
        [VMEM] * (n + 2),
        [(hidden, f32)] + [(block, bf16)] * chips,
        (residual_rows, selector, *got),
        cost=cost(10),
    )

    def spread(blocks):
        return [blocks[0]] + [move(blocks[j], 0, 2 * j + 1) for j in range(1, chips)]

    kept, sent = call(
        gather_kernel,
        "gather",
        [VMEM] * chips,
        [(half, bf16)] * 2,
        spread(outgoing),
    )
    kept, sent = call(
        expert_kernel,
        "experts",
        [VMEM] * 6,
        [(half, bf16)] * 2,
        (
            kept,
            move(sent, 0, 1),
            norm_gain.reshape(D // LANES, LANES),
            gate_proj,
            up_proj,
            down_proj,
        ),
        vmem=20 * 1024 * 1024,
        cost=cost(10),
    )
    results = call(
        scatter_kernel,
        "scatter",
        [VMEM] * 2,
        [(block, bf16)] * chips,
        (kept, move(sent, 0, 1)),
    )
    (mixture,) = call(
        combine_kernel,
        "combine",
        [VMEM] * (chips + 2),
        [(hidden, bf16)],
        (weight_high, weight_low, *spread(results)),
    )
    got = [mixture] + [move(mixture, j, 0) for j in range(1, n)]
    (layer_rows,) = call(
        finish_kernel,
        "finish",
        [VMEM] * (n + 1),
        [((row_count, step_count, D), bf16)],
        (state, *got),
    )
    return layer_rows


def solution(mesh):
    return jax.shard_map(
        per_device,
        mesh=mesh,
        in_specs=(
            P("exp", None, None),
            P("exp", "ctx", None),
            P("exp", "ctx", None),
            P("exp", None, None),
            P("exp", None, None),
            P("exp"),
            P("exp", None, None),
            P("ctx", None),
            P(),
            P("exp", None, None),
            P("exp", None, None),
            P("exp", None, "ctx"),
            P("exp", None, "ctx"),
            P("exp", "ctx", None),
        ),
        out_specs=P("exp", None, None),
        check_vma=False,
    )
```

time: 53.6 us -> 46.3 us (0.86)
  blocking collectives: 24.2 us -> 0 us
  waiting for transfers between devices: 8.9 us -> 19.6 us
  starting transfers between devices: 11.6 us -> 20.1 us
  Pallas kernels: 7.91 us -> 6.31 us
  local copies, waits for them, and re-layouts: 0.68 us -> 0.03 us
    all_to_all x2 -> x0, blocking collectives: 24.2 us -> none  [exchange(): lax.all_to_all(rows, ('ctx', 'exp'), split_axis=0, concat_axis=0, tiled=T...]
    ppermute x9 -> x19, waiting for transfers between devices: 8.9 us -> 19.6 us  [move(): return lax.ppermute(block, ('ctx', 'exp'), pairs)]
    ppermute x9 -> x19, starting transfers between devices: 11.6 us -> 20.1 us  [move(): return lax.ppermute(block, ('ctx', 'exp'), pairs)]
    pallas_call x7 -> x9, Pallas kernels: 7.91 us -> 6.31 us  [call(): pl.pallas_call(kernel, name=name, in_specs=in_specs, out_specs=[out_spec...]
    unnamed x18 -> x16, local copies, waits for them, and re-layouts: 0.68 us -> 0.03 us
  transfers between devices with their start and end apart: 9 -> 19, of which waited for: 7 -> 15; matrix products, arithmetic and copies ran while one was open for 0% -> 0% of each run, Pallas kernels for 1% -> 0%
where the time goes in v3:
time: 46.3 us; the launch traced here: 46.2 us
  starting transfers between devices  20.1 us (43%)
  waiting for transfers between devices  19.6 us (42%)
  Pallas kernels  6.31 us (14%)
    ppermute x19, starting transfers between devices, move(): return lax.ppermute(block, ('ctx', 'exp'), pairs)  20.1 us
    ppermute x19, waiting for transfers between devices, move(): return lax.ppermute(block, ('ctx', 'exp'), pairs)  19.6 us
    pallas_call x9, Pallas kernels, call(): pl.pallas_call(kernel, name=name, in_specs=in_specs, out_specs=[out_spec...  6.31 us
  transfers between devices with their start and end apart: 19, of which 15 were waited for; matrix products, arithmetic and copies ran while one was open for 0% of the time, Pallas kernels for 0%

profile of v3, /device:TPU:0, one launch (start us, length us, event | category | flops | bytes accessed | tf_op | source)
XLA Modules:
  0.0 46.2 jit_solution(2799681822854176232)
XLA Ops:
  0.0 2.3 %attend.1 = (bf16[176,128]{1,0:T(8,128)(2,1)S(1)}, bf16[176,128]{1,0:T(8,128)(2,1)S(1)}, bf16[176,128]{1,0:T(8,128)(2,1)S(1)}, bf16[176,128]{1,0:T(8,128)(2,1)S(1)}) custom-call(s32[1]{0:T(128)} %bitcast.me_ref, s32[8]{0:T(128)} %len_hbm.1, bf16[8,2,4096]{2,1,0:T(2,128)(2,1)} %q_hbm.1, bf16[8,64,256]{2,1,0:T(8,128)(2,1)} %k_hbm.1, ...), custom_call_target="tpu_custom_call" | custom-call | flops 10000000000 | bytes 1048576 | tf_op jit(solution)/shard_map/attend/pallas_call | solution.py:323
  2.3 0.5 %collective-permute-start = (bf16[176,128]{1,0:T(8,128)(2,1)S(1)}, bf16[176,128]{1,0:T(8,128)(2,1)S(1)}, u32[]{:S(2)}, u32[]{:S(2)}) collective-permute-start(bf16[176,128]{1,0:T(8,128)(2,1)S(1)} %get-tuple-element.28), channel_id=1, source_target_pairs={{0,1},{1,0},{2,3},{3,2},{4,5},{5,4},{6,7},{7,6},{8,9},{9,8},{10,11... | collective-permute-start | bytes 135176 | tf_op jit(solution)/shard_map/ppermute | solution.py:346
  2.8 2.6 %collective-permute-start.1 = (bf16[176,128]{1,0:T(8,128)(2,1)S(1)}, bf16[176,128]{1,0:T(8,128)(2,1)S(1)}, u32[]{:S(2)}, u32[]{:S(2)}) collective-permute-start(bf16[176,128]{1,0:T(8,128)(2,1)S(1)} %get-tuple-element.29), channel_id=1, source_target_pairs={{0,9},{1,8},{2,11},{3,10},{4,13},{5,12},{6,15},{7,14},{8,1},{9,0},... | collective-permute-start | bytes 135176 | tf_op jit(solution)/shard_map/ppermute | solution.py:346
  5.4 1.2 %collective-permute-start.2 = (bf16[176,128]{1,0:T(8,128)(2,1)S(1)}, bf16[176,128]{1,0:T(8,128)(2,1)S(1)}, u32[]{:S(2)}, u32[]{:S(2)}) collective-permute-start(bf16[176,128]{1,0:T(8,128)(2,1)S(1)} %get-tuple-element.30), channel_id=1, source_target_pairs={{0,17},{1,16},{2,19},{3,18},{4,21},{5,20},{6,23},{7,22},{8,25},{9,... | collective-permute-start | bytes 135176 | tf_op jit(solution)/shard_map/ppermute | solution.py:346
  6.7 0.7 %collective-permute-done.1.rest_1_ = bf16[176,128]{1,0:T(8,128)(2,1)S(1)} collective-permute-done((bf16[176,128]{1,0:T(8,128)(2,1)S(1)}, bf16[176,128]{1,0:T(8,128)(2,1)S(1)}, u32[]{:S(2)}, u32[]{:S(2)}) %collective-permute-start.1) | collective-permute-done | bytes 45088 | tf_op jit(solution)/shard_map/ppermute | solution.py:346
  7.3 1.8 %collective-permute-done.2.rest_2_ = bf16[176,128]{1,0:T(8,128)(2,1)S(1)} collective-permute-done((bf16[176,128]{1,0:T(8,128)(2,1)S(1)}, bf16[176,128]{1,0:T(8,128)(2,1)S(1)}, u32[]{:S(2)}, u32[]{:S(2)}) %collective-permute-start.2) | collective-permute-done | bytes 45088 | tf_op jit(solution)/shard_map/ppermute | solution.py:346
  9.1 1.9 %collective-permute-done.3.rest_3_ = bf16[176,128]{1,0:T(8,128)(2,1)S(1)} collective-permute-done((bf16[176,128]{1,0:T(8,128)(2,1)S(1)}, bf16[176,128]{1,0:T(8,128)(2,1)S(1)}, u32[]{:S(2)}, u32[]{:S(2)}) %collective-permute-start.3) | collective-permute-done | bytes 45088 | tf_op jit(solution)/shard_map/ppermute | solution.py:346
  11.0 0.8 %project.1 = bf16[16,2048]{1,0:T(8,128)(2,1)S(1)} custom-call(bf16[1024,2048]{1,0:T(8,128)(2,1)S(1)} %copy-done.3, bf16[176,128]{1,0:T(8,128)(2,1)S(1)} %collective-permute-done.rest_0_, bf16[176,128]{1,0:T(8,128)(2,1)S(1)} %collective-permute-done.1.rest_1_, bf16[176,128]{1,0:T(8,128)(2,1)S(1)} %collective-permute-done.2.rest_2_, ...), custom_call_target="tpu_custom_call" | custom-call | flops 10000000000 | bytes 1048576 | tf_op jit(solution)/shard_map/project/pallas_call | solution.py:323
  11.7 0.3 collective-permute-start.7
  12.1 1.4 %collective-permute-start.6 = (bf16[16,2048]{1,0:T(8,128)(2,1)S(1)}, bf16[16,2048]{1,0:T(8,128)(2,1)S(1)}, u32[]{:S(2)}, u32[]{:S(2)}) collective-permute-start(bf16[16,2048]{1,0:T(8,128)(2,1)S(1)} %project.1), channel_id=1, source_target_pairs={{0,17},{1,16},{2,19},{3,18},{4,21},{5,20},{6,23},{7,22},{8,25},{9,... | collective-permute-start | bytes 196616 | tf_op jit(solution)/shard_map/ppermute | solution.py:346
  13.5 1.5 %collective-permute-start.5 = (bf16[16,2048]{1,0:T(8,128)(2,1)S(1)}, bf16[16,2048]{1,0:T(8,128)(2,1)S(1)}, u32[]{:S(2)}, u32[]{:S(2)}) collective-permute-start(bf16[16,2048]{1,0:T(8,128)(2,1)S(1)} %project.1), channel_id=1, source_target_pairs={{0,9},{1,8},{2,11},{3,10},{4,13},{5,12},{6,15},{7,14},{8,1},{9,0},... | collective-permute-start | bytes 196616 | tf_op jit(solution)/shard_map/ppermute | solution.py:346
  15.3 1.3 %collective-permute-done.7.rest_3_ = bf16[16,2048]{1,0:T(8,128)(2,1)S(1)} collective-permute-done((bf16[16,2048]{1,0:T(8,128)(2,1)S(1)}, bf16[16,2048]{1,0:T(8,128)(2,1)S(1)}, u32[]{:S(2)}, u32[]{:S(2)}) %collective-permute-start.7) | collective-permute-done | bytes 65568 | tf_op jit(solution)/shard_map/ppermute | solution.py:346
  16.6 0.5 %collective-permute-done.6.rest_2_ = bf16[16,2048]{1,0:T(8,128)(2,1)S(1)} collective-permute-done((bf16[16,2048]{1,0:T(8,128)(2,1)S(1)}, bf16[16,2048]{1,0:T(8,128)(2,1)S(1)}, u32[]{:S(2)}, u32[]{:S(2)}) %collective-permute-start.6) | collective-permute-done | bytes 65568 | tf_op jit(solution)/shard_map/ppermute | solution.py:346
  17.5 1.9 %collective-permute-start.8 = (bf16[8,2048]{1,0:T(8,128)(2,1)S(1)}, bf16[8,2048]{1,0:T(8,128)(2,1)S(1)}, u32[]{:S(2)}, u32[]{:S(2)}) collective-permute-start(bf16[8,2048]{1,0:T(8,128)(2,1)S(1)} %get-tuple-element.36), channel_id=1, source_target_pairs={{0,3},{1,2},{2,1},{3,0},{4,7},{5,6},{6,5},{7,4},{8,11},{9,10},{10,... | collective-permute-start | bytes 98312 | tf_op jit(solution)/shard_map/ppermute | solution.py:346
  19.5 2.6 %collective-permute-start.9 = (bf16[8,2048]{1,0:T(8,128)(2,1)S(1)}, bf16[8,2048]{1,0:T(8,128)(2,1)S(1)}, u32[]{:S(2)}, u32[]{:S(2)}) collective-permute-start(bf16[8,2048]{1,0:T(8,128)(2,1)S(1)} %get-tuple-element.37), channel_id=1, source_target_pairs={{0,5},{1,4},{2,7},{3,6},{4,1},{5,0},{6,3},{7,2},{8,13},{9,12},{10,... | collective-permute-start | bytes 98312 | tf_op jit(solution)/shard_map/ppermute | solution.py:346
  22.1 1.7 %collective-permute-done.9.refs_2_ = bf16[8,2048]{1,0:T(8,128)(2,1)S(1)} collective-permute-done((bf16[8,2048]{1,0:T(8,128)(2,1)S(1)}, bf16[8,2048]{1,0:T(8,128)(2,1)S(1)}, u32[]{:S(2)}, u32[]{:S(2)}) %collective-permute-start.9) | collective-permute-done | bytes 32800 | tf_op jit(solution)/shard_map/ppermute | solution.py:346
  23.8 3.5 %collective-permute-done.10.refs_3_ = bf16[8,2048]{1,0:T(8,128)(2,1)S(1)} collective-permute-done((bf16[8,2048]{1,0:T(8,128)(2,1)S(1)}, bf16[8,2048]{1,0:T(8,128)(2,1)S(1)}, u32[]{:S(2)}, u32[]{:S(2)}) %collective-permute-start.10) | collective-permute-done | bytes 32800 | tf_op jit(solution)/shard_map/ppermute | solution.py:346
  27.5 1.1 %collective-permute-done.11.got_ref = bf16[16,2048]{1,0:T(8,128)(2,1)S(1)} collective-permute-done((bf16[16,2048]{1,0:T(8,128)(2,1)S(1)}, bf16[16,2048]{1,0:T(8,128)(2,1)S(1)}, u32[]{:S(2)}, u32[]{:S(2)}) %collective-permute-start.11) | collective-permute-done | bytes 65568 | tf_op jit(solution)/shard_map/ppermute | solution.py:346
  28.7 2.0 %experts.1 = (bf16[16,2048]{1,0:T(8,128)(2,1)S(1)}, bf16[16,2048]{1,0:T(8,128)(2,1)S(1)}) custom-call(bf16[16,2048]{1,0:T(8,128)(2,1)S(1)} %get-tuple-element.39.kept_ref, bf16[16,2048]{1,0:T(8,128)(2,1)S(1)} %collective-permute-done.11.got_ref, bf16[16,128]{1,0:T(8,128)(2,1)S(1)} %bitcast.7, bf16[1,2048,1024]{2,1,0:T(8,128)(2,1)S(1)} %copy-done.4, ...), custom_call_target="tpu_custom_call" | custom-call | flops 10000000000 | bytes 1048576 | tf_op jit(solution)/shard_map/experts/pallas_call | solution.py:323
  30.6 0.2 collective-permute-start.12
  30.9 1.1 %collective-permute-done.12.got_ref = bf16[16,2048]{1,0:T(8,128)(2,1)S(1)} collective-permute-done((bf16[16,2048]{1,0:T(8,128)(2,1)S(1)}, bf16[16,2048]{1,0:T(8,128)(2,1)S(1)}, u32[]{:S(2)}, u32[]{:S(2)}) %collective-permute-start.12) | collective-permute-done | bytes 65568 | tf_op jit(solution)/shard_map/ppermute | solution.py:346
  32.1 0.8 %collective-permute-start.14 = (bf16[8,2048]{1,0:T(8,128)(2,1)S(1)}, bf16[8,2048]{1,0:T(8,128)(2,1)S(1)}, u32[]{:S(2)}, u32[]{:S(2)}) collective-permute-start(bf16[8,2048]{1,0:T(8,128)(2,1)S(1)} %get-tuple-element.45), channel_id=1, source_target_pairs={{0,5},{1,4},{2,7},{3,6},{4,1},{5,0},{6,3},{7,2},{8,13},{9,12},{10,... | collective-permute-start | bytes 98312 | tf_op jit(solution)/shard_map/ppermute | solution.py:346
  32.9 3.0 %collective-permute-start.15 = (bf16[8,2048]{1,0:T(8,128)(2,1)S(1)}, bf16[8,2048]{1,0:T(8,128)(2,1)S(1)}, u32[]{:S(2)}, u32[]{:S(2)}) collective-permute-start(bf16[8,2048]{1,0:T(8,128)(2,1)S(1)} %get-tuple-element.46), channel_id=1, source_target_pairs={{0,7},{1,6},{2,5},{3,4},{4,3},{5,2},{6,1},{7,0},{8,15},{9,14},{10,... | collective-permute-start | bytes 98312 | tf_op jit(solution)/shard_map/ppermute | solution.py:346
  35.9 0.5 collective-permute-done.14.refs_2_
  36.4 2.1 %collective-permute-done.15.refs_3_ = bf16[8,2048]{1,0:T(8,128)(2,1)S(1)} collective-permute-done((bf16[8,2048]{1,0:T(8,128)(2,1)S(1)}, bf16[8,2048]{1,0:T(8,128)(2,1)S(1)}, u32[]{:S(2)}, u32[]{:S(2)}) %collective-permute-start.15) | collective-permute-done | bytes 32800 | tf_op jit(solution)/shard_map/ppermute | solution.py:346
  38.6 1.0 %collective-permute-start.18 = (bf16[16,2048]{1,0:T(8,128)(2,1)S(1)}, bf16[16,2048]{1,0:T(8,128)(2,1)S(1)}, u32[]{:S(2)}, u32[]{:S(2)}) collective-permute-start(bf16[16,2048]{1,0:T(8,128)(2,1)S(1)} %combine.1.refs_0_), channel_id=1, source_target_pairs={{0,24},{1,25},{2,26},{3,27},{4,28},{5,29},{6,30},{7,31},{8,16},{9,... | collective-permute-start | bytes 196616 | tf_op jit(solution)/shard_map/ppermute | solution.py:346
  39.7 1.6 %collective-permute-start.17 = (bf16[16,2048]{1,0:T(8,128)(2,1)S(1)}, bf16[16,2048]{1,0:T(8,128)(2,1)S(1)}, u32[]{:S(2)}, u32[]{:S(2)}) collective-permute-start(bf16[16,2048]{1,0:T(8,128)(2,1)S(1)} %combine.1.refs_0_), channel_id=1, source_target_pairs={{0,16},{1,17},{2,18},{3,19},{4,20},{5,21},{6,22},{7,23},{8,24},{9,... | collective-permute-start | bytes 196616 | tf_op jit(solution)/shard_map/ppermute | solution.py:346
  41.2 1.0 %collective-permute-start.16 = (bf16[16,2048]{1,0:T(8,128)(2,1)S(1)}, bf16[16,2048]{1,0:T(8,128)(2,1)S(1)}, u32[]{:S(2)}, u32[]{:S(2)}) collective-permute-start(bf16[16,2048]{1,0:T(8,128)(2,1)S(1)} %combine.1.refs_0_), channel_id=1, source_target_pairs={{0,8},{1,9},{2,10},{3,11},{4,12},{5,13},{6,14},{7,15},{8,0},{9,1},... | collective-permute-start | bytes 196616 | tf_op jit(solution)/shard_map/ppermute | solution.py:346
  42.2 2.2 %collective-permute-done.18.refs_3_ = bf16[16,2048]{1,0:T(8,128)(2,1)S(1)} collective-permute-done((bf16[16,2048]{1,0:T(8,128)(2,1)S(1)}, bf16[16,2048]{1,0:T(8,128)(2,1)S(1)}, u32[]{:S(2)}, u32[]{:S(2)}) %collective-permute-start.18) | collective-permute-done | bytes 65568 | tf_op jit(solution)/shard_map/ppermute | solution.py:346
  44.4 0.5 %collective-permute-done.17.refs_2_ = bf16[16,2048]{1,0:T(8,128)(2,1)S(1)} collective-permute-done((bf16[16,2048]{1,0:T(8,128)(2,1)S(1)}, bf16[16,2048]{1,0:T(8,128)(2,1)S(1)}, u32[]{:S(2)}, u32[]{:S(2)}) %collective-permute-start.17) | collective-permute-done | bytes 65568 | tf_op jit(solution)/shard_map/ppermute | solution.py:346
  44.9 0.5 %collective-permute-done.16.refs_1_ = bf16[16,2048]{1,0:T(8,128)(2,1)S(1)} collective-permute-done((bf16[16,2048]{1,0:T(8,128)(2,1)S(1)}, bf16[16,2048]{1,0:T(8,128)(2,1)S(1)}, u32[]{:S(2)}, u32[]{:S(2)}) %collective-permute-start.16) | collective-permute-done | bytes 65568 | tf_op jit(solution)/shard_map/ppermute | solution.py:346
  45.5 0.7 %finish.1 = bf16[8,2,2048]{2,1,0:T(2,128)(2,1)} custom-call(f32[16,2048]{1,0:T(8,128)S(1)} %get-tuple-element.32.state_ref, bf16[16,2048]{1,0:T(8,128)(2,1)S(1)} %combine.1.refs_0_, bf16[16,2048]{1,0:T(8,128)(2,1)S(1)} %collective-permute-done.16.refs_1_, bf16[16,2048]{1,0:T(8,128)(2,1)S(1)} %collective-permute-done.17.refs_2_, ...), custom_call_target="tpu_custom_call" | custom-call | tf_op jit(solution)/shard_map/finish/pallas_call | solution.py:323
  (31 shorter events, 1.2 us)
Async XLA Ops:
  0.0 11.0 %copy-start.3 = (bf16[1024,2048]{1,0:T(8,128)(2,1)S(1)}, bf16[1024,2048]{1,0:T(8,128)(2,1)}, u32[]{:S(2)}) copy-start(bf16[1024,2048]{1,0:T(8,128)(2,1)} %w_ref.1) | copy-start | bytes 12582916
  2.3 4.4 %collective-permute-start = (bf16[176,128]{1,0:T(8,128)(2,1)S(1)}, bf16[176,128]{1,0:T(8,128)(2,1)S(1)}, u32[]{:S(2)}, u32[]{:S(2)}) collective-permute-start(bf16[176,128]{1,0:T(8,128)(2,1)S(1)} %get-tuple-element.28), channel_id=1, source_target_pairs={{0,1},{1,0},{2,3},{3,2},{4,5},{5,4},{6,7},{7,6},{8,9},{9,8},{10,11... | collective-permute-start | bytes 135176 | tf_op jit(solution)/shard_map/ppermute | solution.py:346
  2.8 4.5 %collective-permute-start.1 = (bf16[176,128]{1,0:T(8,128)(2,1)S(1)}, bf16[176,128]{1,0:T(8,128)(2,1)S(1)}, u32[]{:S(2)}, u32[]{:S(2)}) collective-permute-start(bf16[176,128]{1,0:T(8,128)(2,1)S(1)} %get-tuple-element.29), channel_id=1, source_target_pairs={{0,9},{1,8},{2,11},{3,10},{4,13},{5,12},{6,15},{7,14},{8,1},{9,0},... | collective-permute-start | bytes 135176 | tf_op jit(solution)/shard_map/ppermute | solution.py:346
  5.4 3.7 %collective-permute-start.2 = (bf16[176,128]{1,0:T(8,128)(2,1)S(1)}, bf16[176,128]{1,0:T(8,128)(2,1)S(1)}, u32[]{:S(2)}, u32[]{:S(2)}) collective-permute-start(bf16[176,128]{1,0:T(8,128)(2,1)S(1)} %get-tuple-element.30), channel_id=1, source_target_pairs={{0,17},{1,16},{2,19},{3,18},{4,21},{5,20},{6,23},{7,22},{8,25},{9,... | collective-permute-start | bytes 135176 | tf_op jit(solution)/shard_map/ppermute | solution.py:346
  6.6 8.5 %copy-start = (bf16[8,2,2048]{2,1,0:T(2,128)(2,1)S(1)}, bf16[8,2,2048]{2,1,0:T(2,128)(2,1)}, u32[]{:S(2)}) copy-start(bf16[8,2,2048]{2,1,0:T(2,128)(2,1)} %residual_ref.1) | copy-start | bytes 196612
  6.6 8.5 %copy-start.1 = (s32[8,2,8]{2,1,0:T(2,128)S(1)}, s32[8,2,8]{2,1,0:T(2,128)}, u32[]{:S(2)}) copy-start(s32[8,2,8]{2,1,0:T(2,128)} %param.23) | copy-start | bytes 1540
  6.6 8.5 %copy-start.2 = (f32[8,2,8]{2,1,0:T(2,128)S(1)}, f32[8,2,8]{2,1,0:T(2,128)}, u32[]{:S(2)}) copy-start(f32[8,2,8]{2,1,0:T(2,128)} %param.24) | copy-start | bytes 1540
  6.6 4.4 %collective-permute-start.3 = (bf16[176,128]{1,0:T(8,128)(2,1)S(1)}, bf16[176,128]{1,0:T(8,128)(2,1)S(1)}, u32[]{:S(2)}, u32[]{:S(2)}) collective-permute-start(bf16[176,128]{1,0:T(8,128)(2,1)S(1)} %get-tuple-element.31), channel_id=1, source_target_pairs={{0,25},{1,24},{2,27},{3,26},{4,29},{5,28},{6,31},{7,30},{8,17},{9,... | collective-permute-start | bytes 135176 | tf_op jit(solution)/shard_map/ppermute | solution.py:346
  11.7 4.8 %collective-permute-start.7 = (bf16[16,2048]{1,0:T(8,128)(2,1)S(1)}, bf16[16,2048]{1,0:T(8,128)(2,1)S(1)}, u32[]{:S(2)}, u32[]{:S(2)}) collective-permute-start(bf16[16,2048]{1,0:T(8,128)(2,1)S(1)} %project.1), channel_id=1, source_target_pairs={{0,25},{1,24},{2,27},{3,26},{4,29},{5,28},{6,31},{7,30},{8,17},{9,... | collective-permute-start | bytes 196616 | tf_op jit(solution)/shard_map/ppermute | solution.py:346
  12.1 5.0 %collective-permute-start.6 = (bf16[16,2048]{1,0:T(8,128)(2,1)S(1)}, bf16[16,2048]{1,0:T(8,128)(2,1)S(1)}, u32[]{:S(2)}, u32[]{:S(2)}) collective-permute-start(bf16[16,2048]{1,0:T(8,128)(2,1)S(1)} %project.1), channel_id=1, source_target_pairs={{0,17},{1,16},{2,19},{3,18},{4,21},{5,20},{6,23},{7,22},{8,25},{9,... | collective-permute-start | bytes 196616 | tf_op jit(solution)/shard_map/ppermute | solution.py:346
  13.5 3.8 %collective-permute-start.5 = (bf16[16,2048]{1,0:T(8,128)(2,1)S(1)}, bf16[16,2048]{1,0:T(8,128)(2,1)S(1)}, u32[]{:S(2)}, u32[]{:S(2)}) collective-permute-start(bf16[16,2048]{1,0:T(8,128)(2,1)S(1)} %project.1), channel_id=1, source_target_pairs={{0,9},{1,8},{2,11},{3,10},{4,13},{5,12},{6,15},{7,14},{8,1},{9,0},... | collective-permute-start | bytes 196616 | tf_op jit(solution)/shard_map/ppermute | solution.py:346
  15.0 2.3 %collective-permute-start.4 = (bf16[16,2048]{1,0:T(8,128)(2,1)S(1)}, bf16[16,2048]{1,0:T(8,128)(2,1)S(1)}, u32[]{:S(2)}, u32[]{:S(2)}) collective-permute-start(bf16[16,2048]{1,0:T(8,128)(2,1)S(1)} %project.1), channel_id=1, source_target_pairs={{0,1},{1,0},{2,3},{3,2},{4,5},{5,4},{6,7},{7,6},{8,9},{9,8},{10,11... | collective-permute-start | bytes 196616 | tf_op jit(solution)/shard_map/ppermute | solution.py:346
  17.3 11.4 %copy-start.4 = (bf16[1,2048,1024]{2,1,0:T(8,128)(2,1)S(1)}, bf16[1,2048,1024]{2,1,0:T(8,128)(2,1)}, u32[]{:S(2)}) copy-start(bf16[1,2048,1024]{2,1,0:T(8,128)(2,1)} %gate_ref.1) | copy-start | bytes 12582916
  17.3 11.4 %copy-start.5 = (bf16[1,2048,1024]{2,1,0:T(8,128)(2,1)S(1)}, bf16[1,2048,1024]{2,1,0:T(8,128)(2,1)}, u32[]{:S(2)}) copy-start(bf16[1,2048,1024]{2,1,0:T(8,128)(2,1)} %up_ref.1) | copy-start | bytes 12582916
  17.3 11.4 %copy-start.6 = (bf16[1,1024,2048]{2,1,0:T(8,128)(2,1)S(1)}, bf16[1,1024,2048]{2,1,0:T(8,128)(2,1)}, u32[]{:S(2)}) copy-start(bf16[1,1024,2048]{2,1,0:T(8,128)(2,1)} %down_ref.1) | copy-start | bytes 12582916
  17.3 11.4 %copy-start.7 = (bf16[2048]{0:T(1024)(128)(2,1)S(1)}, bf16[2048]{0:T(1024)(128)(2,1)}, u32[]{:S(2)}) copy-start(bf16[2048]{0:T(1024)(128)(2,1)} %param.22) | copy-start | bytes 12292
  17.5 4.6 %collective-permute-start.8 = (bf16[8,2048]{1,0:T(8,128)(2,1)S(1)}, bf16[8,2048]{1,0:T(8,128)(2,1)S(1)}, u32[]{:S(2)}, u32[]{:S(2)}) collective-permute-start(bf16[8,2048]{1,0:T(8,128)(2,1)S(1)} %get-tuple-element.36), channel_id=1, source_target_pairs={{0,3},{1,2},{2,1},{3,0},{4,7},{5,6},{6,5},{7,4},{8,11},{9,10},{10,... | collective-permute-start | bytes 98312 | tf_op jit(solution)/shard_map/ppermute | solution.py:346
  19.5 4.3 %collective-permute-start.9 = (bf16[8,2048]{1,0:T(8,128)(2,1)S(1)}, bf16[8,2048]{1,0:T(8,128)(2,1)S(1)}, u32[]{:S(2)}, u32[]{:S(2)}) collective-permute-start(bf16[8,2048]{1,0:T(8,128)(2,1)S(1)} %get-tuple-element.37), channel_id=1, source_target_pairs={{0,5},{1,4},{2,7},{3,6},{4,1},{5,0},{6,3},{7,2},{8,13},{9,12},{10,... | collective-permute-start | bytes 98312 | tf_op jit(solution)/shard_map/ppermute | solution.py:346
  22.1 5.2 %collective-permute-start.10 = (bf16[8,2048]{1,0:T(8,128)(2,1)S(1)}, bf16[8,2048]{1,0:T(8,128)(2,1)S(1)}, u32[]{:S(2)}, u32[]{:S(2)}) collective-permute-start(bf16[8,2048]{1,0:T(8,128)(2,1)S(1)} %get-tuple-element.38), channel_id=1, source_target_pairs={{0,7},{1,6},{2,5},{3,4},{4,3},{5,2},{6,1},{7,0},{8,15},{9,14},{10,... | collective-permute-start | bytes 98312 | tf_op jit(solution)/shard_map/ppermute | solution.py:346
  27.3 1.3 %collective-permute-start.11 = (bf16[16,2048]{1,0:T(8,128)(2,1)S(1)}, bf16[16,2048]{1,0:T(8,128)(2,1)S(1)}, u32[]{:S(2)}, u32[]{:S(2)}) collective-permute-start(bf16[16,2048]{1,0:T(8,128)(2,1)S(1)} %get-tuple-element.40), channel_id=1, source_target_pairs={{0,1},{1,0},{2,3},{3,2},{4,5},{5,4},{6,7},{7,6},{8,9},{9,8},{10,11... | collective-permute-start | bytes 196616 | tf_op jit(solution)/shard_map/ppermute | solution.py:346
  30.6 1.3 %collective-permute-start.12 = (bf16[16,2048]{1,0:T(8,128)(2,1)S(1)}, bf16[16,2048]{1,0:T(8,128)(2,1)S(1)}, u32[]{:S(2)}, u32[]{:S(2)}) collective-permute-start(bf16[16,2048]{1,0:T(8,128)(2,1)S(1)} %get-tuple-element.42), channel_id=1, source_target_pairs={{0,1},{1,0},{2,3},{3,2},{4,5},{5,4},{6,7},{7,6},{8,9},{9,8},{10,11... | collective-permute-start | bytes 196616 | tf_op jit(solution)/shard_map/ppermute | solution.py:346
  32.0 3.9 %collective-permute-start.13 = (bf16[8,2048]{1,0:T(8,128)(2,1)S(1)}, bf16[8,2048]{1,0:T(8,128)(2,1)S(1)}, u32[]{:S(2)}, u32[]{:S(2)}) collective-permute-start(bf16[8,2048]{1,0:T(8,128)(2,1)S(1)} %get-tuple-element.44), channel_id=1, source_target_pairs={{0,3},{1,2},{2,1},{3,0},{4,7},{5,6},{6,5},{7,4},{8,11},{9,10},{10,... | collective-permute-start | bytes 98312 | tf_op jit(solution)/shard_map/ppermute | solution.py:346
  32.1 4.3 %collective-permute-start.14 = (bf16[8,2048]{1,0:T(8,128)(2,1)S(1)}, bf16[8,2048]{1,0:T(8,128)(2,1)S(1)}, u32[]{:S(2)}, u32[]{:S(2)}) collective-permute-start(bf16[8,2048]{1,0:T(8,128)(2,1)S(1)} %get-tuple-element.45), channel_id=1, source_target_pairs={{0,5},{1,4},{2,7},{3,6},{4,1},{5,0},{6,3},{7,2},{8,13},{9,12},{10,... | collective-permute-start | bytes 98312 | tf_op jit(solution)/shard_map/ppermute | solution.py:346
  32.9 5.5 %collective-permute-start.15 = (bf16[8,2048]{1,0:T(8,128)(2,1)S(1)}, bf16[8,2048]{1,0:T(8,128)(2,1)S(1)}, u32[]{:S(2)}, u32[]{:S(2)}) collective-permute-start(bf16[8,2048]{1,0:T(8,128)(2,1)S(1)} %get-tuple-element.46), channel_id=1, source_target_pairs={{0,7},{1,6},{2,5},{3,4},{4,3},{5,2},{6,1},{7,0},{8,15},{9,14},{10,... | collective-permute-start | bytes 98312 | tf_op jit(solution)/shard_map/ppermute | solution.py:346
  38.6 5.8 %collective-permute-start.18 = (bf16[16,2048]{1,0:T(8,128)(2,1)S(1)}, bf16[16,2048]{1,0:T(8,128)(2,1)S(1)}, u32[]{:S(2)}, u32[]{:S(2)}) collective-permute-start(bf16[16,2048]{1,0:T(8,128)(2,1)S(1)} %combine.1.refs_0_), channel_id=1, source_target_pairs={{0,24},{1,25},{2,26},{3,27},{4,28},{5,29},{6,30},{7,31},{8,16},{9,... | collective-permute-start | bytes 196616 | tf_op jit(solution)/shard_map/ppermute | solution.py:346
  39.7 5.3 %collective-permute-start.17 = (bf16[16,2048]{1,0:T(8,128)(2,1)S(1)}, bf16[16,2048]{1,0:T(8,128)(2,1)S(1)}, u32[]{:S(2)}, u32[]{:S(2)}) collective-permute-start(bf16[16,2048]{1,0:T(8,128)(2,1)S(1)} %combine.1.refs_0_), channel_id=1, source_target_pairs={{0,16},{1,17},{2,18},{3,19},{4,20},{5,21},{6,22},{7,23},{8,24},{9,... | collective-permute-start | bytes 196616 | tf_op jit(solution)/shard_map/ppermute | solution.py:346
  41.2 4.3 %collective-permute-start.16 = (bf16[16,2048]{1,0:T(8,128)(2,1)S(1)}, bf16[16,2048]{1,0:T(8,128)(2,1)S(1)}, u32[]{:S(2)}, u32[]{:S(2)}) collective-permute-start(bf16[16,2048]{1,0:T(8,128)(2,1)S(1)} %combine.1.refs_0_), channel_id=1, source_target_pairs={{0,8},{1,9},{2,10},{3,11},{4,12},{5,13},{6,14},{7,15},{8,0},{9,1},... | collective-permute-start | bytes 196616 | tf_op jit(solution)/shard_map/ppermute | solution.py:346

commit v4 on v3

--- a/solution.py
+++ b/solution.py
@@ -16,6 +16,7 @@
 TOPK = 8
 LANES = 128
 SUBLANES = 8
+STAT_ROWS = 16
 
 
 NORM_EPSILON = 1e-06
@@ -31,11 +32,9 @@
 
 
 def split_three(values):
-    high = values.astype(jnp.bfloat16)
-    rest = values - high.astype(jnp.float32)
-    middle = rest.astype(jnp.bfloat16)
-    low = (rest - middle.astype(jnp.float32)).astype(jnp.bfloat16)
-    return high, middle, low
+    high = values.astype(jnp.bfloat16).astype(jnp.float32)
+    middle = (values - high).astype(jnp.bfloat16).astype(jnp.float32)
+    return high, middle, values - high - middle
 
 
 def every(values, first, step):
@@ -151,35 +150,29 @@
         span = block_heads * row_steps
         for part in range(high // LANES):
             level_row = jnp.transpose(level[part * LANES : (part + 1) * LANES])[:SUBLANES]
-            splits = split_three(level_row)
+            high_part, middle_part, low_part = split_three(level_row)
+            row = iota((SUBLANES, LANES), 0)
+            stats = jnp.where(row == 0, high_part, jnp.where(row == 1, middle_part, low_part))
+            stats = jnp.concatenate([stats, stats], 0).astype(jnp.bfloat16)
             for sub in range(LANES // span):
                 dest = (kv * high + part * LANES) // span + sub
                 start = part * LANES + sub * span
                 blocks[dest, :span, :] = mean[start : start + span]
-                for i, piece in enumerate(splits):
-                    if sub > 0:
-                        piece = jnp.concatenate(
-                            [piece[:, sub * span :], piece[:, : sub * span]], 1
-                        )
-                    blocks[dest, span + 16 * i : span + 16 * (i + 1), :] = jnp.concatenate(
-                        [piece, piece], 0
-                    )
-    for k in range(ctx_count):
-        outs[k][...] = blocks[me ^ k]
+                piece = stats
+                if sub > 0:
+                    piece = jnp.concatenate([stats[:, sub * span :], stats[:, : sub * span]], 1)
+                blocks[dest, span:, :] = piece
+    for k, out in zip(reversed(range(ctx_count)), outs):
+        out[...] = blocks[me ^ k]
 
 
 def project_kernel(ctx_count, w_ref, *rest):
     parts, out_ref = rest[:ctx_count], rest[ctx_count]
     block_heads = HEADS // ctx_count
-    span = parts[0].shape[0] - 48
+    span = parts[0].shape[0] - STAT_ROWS
     row_steps = span // block_heads
-    levels = [
-        sum(
-            part[span + 16 * i : span + 16 * (i + 1), :].astype(jnp.float32)[:1]
-            for i in range(3)
-        )
-        for part in parts
-    ]
+    stats = [part[span:, :].astype(jnp.float32) for part in parts]
+    levels = [stat[0:1] + stat[1:2] + stat[2:3] for stat in stats]
     top = functools.reduce(jnp.maximum, levels)
     factors = [jnp.exp(level - top) for level in levels]
     total = functools.reduce(jnp.add, factors)
@@ -241,7 +234,7 @@
     return values[0]
 
 
-def dispatch_kernel(ctx_count, residual_ref, selector_ref, *rest):
+def dispatch_kernel(ctx_count, hops, residual_ref, selector_ref, *rest):
     parts, state_ref, outs = rest[:ctx_count], rest[ctx_count], rest[ctx_count + 1 :]
     state = residual_ref[...] + tree_sum(parts)
     state_ref[...] = state
@@ -252,7 +245,7 @@
         preferred_element_type=jnp.float32,
     )
     block = outs[0].shape[0]
-    for j, out in enumerate(outs):
+    for j, out in zip(hops, outs):
         out[...] = picked[j * block : (j + 1) * block].astype(jnp.bfloat16)
 
 
@@ -295,8 +288,8 @@
         out[...] = jnp.concatenate([kept[span], got[span]], 0).astype(jnp.bfloat16)
 
 
-def combine_kernel(high_ref, low_ref, *refs):
-    blocks, out_ref = refs[:-1], refs[-1]
+def combine_kernel(hops, high_ref, low_ref, *refs):
+    blocks, out_ref = [refs[hops.index(j)] for j in range(len(hops))], refs[-1]
     returned = jnp.concatenate([block[...].astype(jnp.float32) for block in blocks], 0).astype(
         jnp.bfloat16
     )
@@ -371,13 +364,14 @@
     experts_all = exp_count * EXP_DEV
     capacity = max(2, (row_steps * TOPK + experts_all - 1) // experts_all)
     chips = exp_count // 2
+    hops = (chips - 1, *range(1, chips - 1), 0)
     span = HEADS // n * row_steps
     bf16, f32 = jnp.bfloat16, jnp.float32
     hidden = (row_steps, D)
     block = (2 * capacity, D)
     half = (chips * capacity, D)
 
-    message = (span + 48, LANES)
+    message = (span + STAT_ROWS, LANES)
     inputs = (lengths, queries, cache_keys, cache_values, new_keys, new_values)
     sent = call(
         functools.partial(attend_kernel, n),
@@ -391,7 +385,7 @@
         + [pltpu.SemaphoreType.DMA((len(inputs),))],
         cost=cost(10),
     )
-    got = [move(x, j, 1) for j, x in enumerate(sent)]
+    got = [move(x, j, 1) for j, x in zip(reversed(range(n)), sent)]
     selector, weight_high, weight_low, residual_rows = call(
         functools.partial(route_kernel, n, exp_count, capacity),
         "route",
@@ -416,7 +410,7 @@
     )
     got = [move(projected, j, 1) for j in range(n)]
     state, *outgoing = call(
-        functools.partial(dispatch_kernel, n),
+        functools.partial(dispatch_kernel, n, hops),
         "dispatch",
         [VMEM] * (n + 2),
         [(hidden, f32)] + [(block, bf16)] * chips,
@@ -425,7 +419,7 @@
     )
 
     def spread(blocks):
-        return [blocks[0]] + [move(blocks[j], 0, 2 * j + 1) for j in range(1, chips)]
+        return [x if j == 0 else move(x, 0, 2 * j + 1) for j, x in zip(hops, blocks)]
 
     kept, sent = call(
         gather_kernel,
@@ -458,13 +452,13 @@
         (kept, move(sent, 0, 1)),
     )
     (mixture,) = call(
-        combine_kernel,
+        functools.partial(combine_kernel, hops),
         "combine",
         [VMEM] * (chips + 2),
         [(hidden, bf16)],
         (weight_high, weight_low, *spread(results)),
     )
-    got = [mixture] + [move(mixture, j, 0) for j in range(1, n)]
+    got = [move(mixture, j, 0) if j else mixture for j in range(n)]
     (layer_rows,) = call(
         finish_kernel,
         "finish",

time: 46.3 us -> 44.6 us (0.963)
  waiting for transfers between devices: 19.6 us -> 17.8 us
    ppermute x19, waiting for transfers between devices: 19.6 us -> 17.8 us  [move(): return lax.ppermute(block, ('ctx', 'exp'), pairs)]
  transfers between devices with their start and end apart: 19 -> 19, of which waited for: 15 -> 14; matrix products, arithmetic and copies ran while one was open for 0% -> 0% of each run, Pallas kernels for 0% -> 0%
where the time goes in v4:
time: 44.6 us; the launch traced here: 44.5 us
  starting transfers between devices  20.3 us (46%)
  waiting for transfers between devices  17.8 us (40%)
  Pallas kernels  6.31 us (14%)
    ppermute x19, starting transfers between devices, move(): return lax.ppermute(block, ('ctx', 'exp'), pairs)  20.3 us
    ppermute x19, waiting for transfers between devices, move(): return lax.ppermute(block, ('ctx', 'exp'), pairs)  17.8 us
    pallas_call x9, Pallas kernels, call(): pl.pallas_call(kernel, name=name, in_specs=in_specs, out_specs=[out_spec...  6.31 us
  transfers between devices with their start and end apart: 19, of which 14 were waited for; matrix products, arithmetic and copies ran while one was open for 0% of the time, Pallas kernels for 0%

profile of v4, /device:TPU:0, one launch (start us, length us, event | category | flops | bytes accessed | tf_op | source)
XLA Modules:
  0.0 44.5 jit_solution(880130000389330827)
XLA Ops:
  0.0 2.3 %attend.1 = (bf16[144,128]{1,0:T(8,128)(2,1)S(1)}, bf16[144,128]{1,0:T(8,128)(2,1)S(1)}, bf16[144,128]{1,0:T(8,128)(2,1)S(1)}, bf16[144,128]{1,0:T(8,128)(2,1)S(1)}) custom-call(s32[1]{0:T(128)} %bitcast.me_ref, s32[8]{0:T(128)} %len_hbm.1, bf16[8,2,4096]{2,1,0:T(2,128)(2,1)} %q_hbm.1, bf16[8,64,256]{2,1,0:T(8,128)(2,1)} %k_hbm.1, ...), custom_call_target="tpu_custom_call" | custom-call | flops 10000000000 | bytes 1048576 | tf_op jit(solution)/shard_map/attend/pallas_call | solution.py:316
  2.3 3.4 %collective-permute-start = (bf16[144,128]{1,0:T(8,128)(2,1)S(1)}, bf16[144,128]{1,0:T(8,128)(2,1)S(1)}, u32[]{:S(2)}, u32[]{:S(2)}) collective-permute-start(bf16[144,128]{1,0:T(8,128)(2,1)S(1)} %get-tuple-element.28), channel_id=1, source_target_pairs={{0,25},{1,24},{2,27},{3,26},{4,29},{5,28},{6,31},{7,30},{8,17},{9,... | collective-permute-start | bytes 110600 | tf_op jit(solution)/shard_map/ppermute | solution.py:339
  5.7 0.8 %collective-permute-start.1 = (bf16[144,128]{1,0:T(8,128)(2,1)S(1)}, bf16[144,128]{1,0:T(8,128)(2,1)S(1)}, u32[]{:S(2)}, u32[]{:S(2)}) collective-permute-start(bf16[144,128]{1,0:T(8,128)(2,1)S(1)} %get-tuple-element.29), channel_id=1, source_target_pairs={{0,17},{1,16},{2,19},{3,18},{4,21},{5,20},{6,23},{7,22},{8,25},{9,... | collective-permute-start | bytes 110600 | tf_op jit(solution)/shard_map/ppermute | solution.py:339
  6.6 0.9 %collective-permute-done.rest_0_ = bf16[144,128]{1,0:T(8,128)(2,1)S(1)} collective-permute-done((bf16[144,128]{1,0:T(8,128)(2,1)S(1)}, bf16[144,128]{1,0:T(8,128)(2,1)S(1)}, u32[]{:S(2)}, u32[]{:S(2)}) %collective-permute-start) | collective-permute-done | bytes 36896 | tf_op jit(solution)/shard_map/ppermute | solution.py:339
  7.5 1.5 %collective-permute-done.1.rest_1_ = bf16[144,128]{1,0:T(8,128)(2,1)S(1)} collective-permute-done((bf16[144,128]{1,0:T(8,128)(2,1)S(1)}, bf16[144,128]{1,0:T(8,128)(2,1)S(1)}, u32[]{:S(2)}, u32[]{:S(2)}) %collective-permute-start.1) | collective-permute-done | bytes 36896 | tf_op jit(solution)/shard_map/ppermute | solution.py:339
  9.1 1.1 %collective-permute-done.2.rest_2_ = bf16[144,128]{1,0:T(8,128)(2,1)S(1)} collective-permute-done((bf16[144,128]{1,0:T(8,128)(2,1)S(1)}, bf16[144,128]{1,0:T(8,128)(2,1)S(1)}, u32[]{:S(2)}, u32[]{:S(2)}) %collective-permute-start.2) | collective-permute-done | bytes 36896 | tf_op jit(solution)/shard_map/ppermute | solution.py:339
  10.2 0.8 %project.1 = bf16[16,2048]{1,0:T(8,128)(2,1)S(1)} custom-call(bf16[1024,2048]{1,0:T(8,128)(2,1)S(1)} %copy-done.3, bf16[144,128]{1,0:T(8,128)(2,1)S(1)} %collective-permute-done.rest_0_, bf16[144,128]{1,0:T(8,128)(2,1)S(1)} %collective-permute-done.1.rest_1_, bf16[144,128]{1,0:T(8,128)(2,1)S(1)} %collective-permute-done.2.rest_2_, ...), custom_call_target="tpu_custom_call" | custom-call | flops 10000000000 | bytes 1048576 | tf_op jit(solution)/shard_map/project/pallas_call | solution.py:316
  10.9 1.2 %collective-permute-start.7 = (bf16[16,2048]{1,0:T(8,128)(2,1)S(1)}, bf16[16,2048]{1,0:T(8,128)(2,1)S(1)}, u32[]{:S(2)}, u32[]{:S(2)}) collective-permute-start(bf16[16,2048]{1,0:T(8,128)(2,1)S(1)} %project.1), channel_id=1, source_target_pairs={{0,25},{1,24},{2,27},{3,26},{4,29},{5,28},{6,31},{7,30},{8,17},{9,... | collective-permute-start | bytes 196616 | tf_op jit(solution)/shard_map/ppermute | solution.py:339
  12.2 0.4 collective-permute-start.6
  12.6 1.3 %collective-permute-start.5 = (bf16[16,2048]{1,0:T(8,128)(2,1)S(1)}, bf16[16,2048]{1,0:T(8,128)(2,1)S(1)}, u32[]{:S(2)}, u32[]{:S(2)}) collective-permute-start(bf16[16,2048]{1,0:T(8,128)(2,1)S(1)} %project.1), channel_id=1, source_target_pairs={{0,9},{1,8},{2,11},{3,10},{4,13},{5,12},{6,15},{7,14},{8,1},{9,0},... | collective-permute-start | bytes 196616 | tf_op jit(solution)/shard_map/ppermute | solution.py:339
  13.9 0.4 collective-permute-start.4
  14.5 1.5 %collective-permute-done.7.rest_3_ = bf16[16,2048]{1,0:T(8,128)(2,1)S(1)} collective-permute-done((bf16[16,2048]{1,0:T(8,128)(2,1)S(1)}, bf16[16,2048]{1,0:T(8,128)(2,1)S(1)}, u32[]{:S(2)}, u32[]{:S(2)}) %collective-permute-start.7) | collective-permute-done | bytes 65568 | tf_op jit(solution)/shard_map/ppermute | solution.py:339
  16.0 1.6 %collective-permute-done.6.rest_2_ = bf16[16,2048]{1,0:T(8,128)(2,1)S(1)} collective-permute-done((bf16[16,2048]{1,0:T(8,128)(2,1)S(1)}, bf16[16,2048]{1,0:T(8,128)(2,1)S(1)}, u32[]{:S(2)}, u32[]{:S(2)}) %collective-permute-start.6) | collective-permute-done | bytes 65568 | tf_op jit(solution)/shard_map/ppermute | solution.py:339
  17.8 3.4 %collective-permute-start.8 = (bf16[8,2048]{1,0:T(8,128)(2,1)S(1)}, bf16[8,2048]{1,0:T(8,128)(2,1)S(1)}, u32[]{:S(2)}, u32[]{:S(2)}) collective-permute-start(bf16[8,2048]{1,0:T(8,128)(2,1)S(1)} %get-tuple-element.35), channel_id=1, source_target_pairs={{0,7},{1,6},{2,5},{3,4},{4,3},{5,2},{6,1},{7,0},{8,15},{9,14},{10,... | collective-permute-start | bytes 98312 | tf_op jit(solution)/shard_map/ppermute | solution.py:339
  21.2 0.6 %collective-permute-start.10 = (bf16[8,2048]{1,0:T(8,128)(2,1)S(1)}, bf16[8,2048]{1,0:T(8,128)(2,1)S(1)}, u32[]{:S(2)}, u32[]{:S(2)}) collective-permute-start(bf16[8,2048]{1,0:T(8,128)(2,1)S(1)} %get-tuple-element.37), channel_id=1, source_target_pairs={{0,5},{1,4},{2,7},{3,6},{4,1},{5,0},{6,3},{7,2},{8,13},{9,12},{10,... | collective-permute-start | bytes 98312 | tf_op jit(solution)/shard_map/ppermute | solution.py:339
  21.9 1.2 %collective-permute-done.8.refs_0_ = bf16[8,2048]{1,0:T(8,128)(2,1)S(1)} collective-permute-done((bf16[8,2048]{1,0:T(8,128)(2,1)S(1)}, bf16[8,2048]{1,0:T(8,128)(2,1)S(1)}, u32[]{:S(2)}, u32[]{:S(2)}) %collective-permute-start.8) | collective-permute-done | bytes 32800 | tf_op jit(solution)/shard_map/ppermute | solution.py:339
  23.1 1.5 %collective-permute-done.9.refs_1_ = bf16[8,2048]{1,0:T(8,128)(2,1)S(1)} collective-permute-done((bf16[8,2048]{1,0:T(8,128)(2,1)S(1)}, bf16[8,2048]{1,0:T(8,128)(2,1)S(1)}, u32[]{:S(2)}, u32[]{:S(2)}) %collective-permute-start.9) | collective-permute-done | bytes 32800 | tf_op jit(solution)/shard_map/ppermute | solution.py:339
  24.6 1.0 %collective-permute-done.10.refs_2_ = bf16[8,2048]{1,0:T(8,128)(2,1)S(1)} collective-permute-done((bf16[8,2048]{1,0:T(8,128)(2,1)S(1)}, bf16[8,2048]{1,0:T(8,128)(2,1)S(1)}, u32[]{:S(2)}, u32[]{:S(2)}) %collective-permute-start.10) | collective-permute-done | bytes 32800 | tf_op jit(solution)/shard_map/ppermute | solution.py:339
  25.6 0.4 collective-permute-start.11
  26.0 0.9 %collective-permute-done.11.got_ref = bf16[16,2048]{1,0:T(8,128)(2,1)S(1)} collective-permute-done((bf16[16,2048]{1,0:T(8,128)(2,1)S(1)}, bf16[16,2048]{1,0:T(8,128)(2,1)S(1)}, u32[]{:S(2)}, u32[]{:S(2)}) %collective-permute-start.11) | collective-permute-done | bytes 65568 | tf_op jit(solution)/shard_map/ppermute | solution.py:339
  26.9 1.9 %experts.1 = (bf16[16,2048]{1,0:T(8,128)(2,1)S(1)}, bf16[16,2048]{1,0:T(8,128)(2,1)S(1)}) custom-call(bf16[16,2048]{1,0:T(8,128)(2,1)S(1)} %get-tuple-element.39.kept_ref, bf16[16,2048]{1,0:T(8,128)(2,1)S(1)} %collective-permute-done.11.got_ref, bf16[16,128]{1,0:T(8,128)(2,1)S(1)} %bitcast.7, bf16[1,2048,1024]{2,1,0:T(8,128)(2,1)S(1)} %copy-done.4, ...), custom_call_target="tpu_custom_call" | custom-call | flops 10000000000 | bytes 1048576 | tf_op jit(solution)/shard_map/experts/pallas_call | solution.py:316
  28.9 0.4 collective-permute-start.12
  29.3 0.9 %collective-permute-done.12.got_ref = bf16[16,2048]{1,0:T(8,128)(2,1)S(1)} collective-permute-done((bf16[16,2048]{1,0:T(8,128)(2,1)S(1)}, bf16[16,2048]{1,0:T(8,128)(2,1)S(1)}, u32[]{:S(2)}, u32[]{:S(2)}) %collective-permute-start.12) | collective-permute-done | bytes 65568 | tf_op jit(solution)/shard_map/ppermute | solution.py:339
  30.3 1.9 %collective-permute-start.13 = (bf16[8,2048]{1,0:T(8,128)(2,1)S(1)}, bf16[8,2048]{1,0:T(8,128)(2,1)S(1)}, u32[]{:S(2)}, u32[]{:S(2)}) collective-permute-start(bf16[8,2048]{1,0:T(8,128)(2,1)S(1)} %get-tuple-element.43), channel_id=1, source_target_pairs={{0,7},{1,6},{2,5},{3,4},{4,3},{5,2},{6,1},{7,0},{8,15},{9,14},{10,... | collective-permute-start | bytes 98312 | tf_op jit(solution)/shard_map/ppermute | solution.py:339
  32.3 2.1 %collective-permute-start.15 = (bf16[8,2048]{1,0:T(8,128)(2,1)S(1)}, bf16[8,2048]{1,0:T(8,128)(2,1)S(1)}, u32[]{:S(2)}, u32[]{:S(2)}) collective-permute-start(bf16[8,2048]{1,0:T(8,128)(2,1)S(1)} %get-tuple-element.45), channel_id=1, source_target_pairs={{0,5},{1,4},{2,7},{3,6},{4,1},{5,0},{6,3},{7,2},{8,13},{9,12},{10,... | collective-permute-start | bytes 98312 | tf_op jit(solution)/shard_map/ppermute | solution.py:339
  34.4 1.3 %collective-permute-done.13.refs_0_ = bf16[8,2048]{1,0:T(8,128)(2,1)S(1)} collective-permute-done((bf16[8,2048]{1,0:T(8,128)(2,1)S(1)}, bf16[8,2048]{1,0:T(8,128)(2,1)S(1)}, u32[]{:S(2)}, u32[]{:S(2)}) %collective-permute-start.13) | collective-permute-done | bytes 32800 | tf_op jit(solution)/shard_map/ppermute | solution.py:339
  35.7 1.4 %collective-permute-done.14.refs_1_ = bf16[8,2048]{1,0:T(8,128)(2,1)S(1)} collective-permute-done((bf16[8,2048]{1,0:T(8,128)(2,1)S(1)}, bf16[8,2048]{1,0:T(8,128)(2,1)S(1)}, u32[]{:S(2)}, u32[]{:S(2)}) %collective-permute-start.14) | collective-permute-done | bytes 32800 | tf_op jit(solution)/shard_map/ppermute | solution.py:339
  37.3 1.8 %collective-permute-start.18 = (bf16[16,2048]{1,0:T(8,128)(2,1)S(1)}, bf16[16,2048]{1,0:T(8,128)(2,1)S(1)}, u32[]{:S(2)}, u32[]{:S(2)}) collective-permute-start(bf16[16,2048]{1,0:T(8,128)(2,1)S(1)} %combine.1.refs_0_), channel_id=1, source_target_pairs={{0,24},{1,25},{2,26},{3,27},{4,28},{5,29},{6,30},{7,31},{8,16},{9,... | collective-permute-start | bytes 196616 | tf_op jit(solution)/shard_map/ppermute | solution.py:339
  39.6 1.3 %collective-permute-start.16 = (bf16[16,2048]{1,0:T(8,128)(2,1)S(1)}, bf16[16,2048]{1,0:T(8,128)(2,1)S(1)}, u32[]{:S(2)}, u32[]{:S(2)}) collective-permute-start(bf16[16,2048]{1,0:T(8,128)(2,1)S(1)} %combine.1.refs_0_), channel_id=1, source_target_pairs={{0,8},{1,9},{2,10},{3,11},{4,12},{5,13},{6,14},{7,15},{8,0},{9,1},... | collective-permute-start | bytes 196616 | tf_op jit(solution)/shard_map/ppermute | solution.py:339
  40.8 1.7 %collective-permute-done.18.refs_3_ = bf16[16,2048]{1,0:T(8,128)(2,1)S(1)} collective-permute-done((bf16[16,2048]{1,0:T(8,128)(2,1)S(1)}, bf16[16,2048]{1,0:T(8,128)(2,1)S(1)}, u32[]{:S(2)}, u32[]{:S(2)}) %collective-permute-start.18) | collective-permute-done | bytes 65568 | tf_op jit(solution)/shard_map/ppermute | solution.py:339
  42.6 1.2 %collective-permute-done.17.refs_2_ = bf16[16,2048]{1,0:T(8,128)(2,1)S(1)} collective-permute-done((bf16[16,2048]{1,0:T(8,128)(2,1)S(1)}, bf16[16,2048]{1,0:T(8,128)(2,1)S(1)}, u32[]{:S(2)}, u32[]{:S(2)}) %collective-permute-start.17) | collective-permute-done | bytes 65568 | tf_op jit(solution)/shard_map/ppermute | solution.py:339
  43.8 0.7 %finish.1 = bf16[8,2,2048]{2,1,0:T(2,128)(2,1)} custom-call(f32[16,2048]{1,0:T(8,128)S(1)} %get-tuple-element.32.state_ref, bf16[16,2048]{1,0:T(8,128)(2,1)S(1)} %combine.1.refs_0_, bf16[16,2048]{1,0:T(8,128)(2,1)S(1)} %collective-permute-done.16.refs_1_, bf16[16,2048]{1,0:T(8,128)(2,1)S(1)} %collective-permute-done.17.refs_2_, ...), custom_call_target="tpu_custom_call" | custom-call | tf_op jit(solution)/shard_map/finish/pallas_call | solution.py:316
  (31 shorter events, 1.4 us)
Async XLA Ops:
  0.0 10.2 %copy-start.3 = (bf16[1024,2048]{1,0:T(8,128)(2,1)S(1)}, bf16[1024,2048]{1,0:T(8,128)(2,1)}, u32[]{:S(2)}) copy-start(bf16[1024,2048]{1,0:T(8,128)(2,1)} %w_ref.1) | copy-start | bytes 12582916
  2.3 5.3 %collective-permute-start = (bf16[144,128]{1,0:T(8,128)(2,1)S(1)}, bf16[144,128]{1,0:T(8,128)(2,1)S(1)}, u32[]{:S(2)}, u32[]{:S(2)}) collective-permute-start(bf16[144,128]{1,0:T(8,128)(2,1)S(1)} %get-tuple-element.28), channel_id=1, source_target_pairs={{0,25},{1,24},{2,27},{3,26},{4,29},{5,28},{6,31},{7,30},{8,17},{9,... | collective-permute-start | bytes 110600 | tf_op jit(solution)/shard_map/ppermute | solution.py:339
  5.7 3.4 %collective-permute-start.1 = (bf16[144,128]{1,0:T(8,128)(2,1)S(1)}, bf16[144,128]{1,0:T(8,128)(2,1)S(1)}, u32[]{:S(2)}, u32[]{:S(2)}) collective-permute-start(bf16[144,128]{1,0:T(8,128)(2,1)S(1)} %get-tuple-element.29), channel_id=1, source_target_pairs={{0,17},{1,16},{2,19},{3,18},{4,21},{5,20},{6,23},{7,22},{8,25},{9,... | collective-permute-start | bytes 110600 | tf_op jit(solution)/shard_map/ppermute | solution.py:339
  6.5 3.7 %collective-permute-start.2 = (bf16[144,128]{1,0:T(8,128)(2,1)S(1)}, bf16[144,128]{1,0:T(8,128)(2,1)S(1)}, u32[]{:S(2)}, u32[]{:S(2)}) collective-permute-start(bf16[144,128]{1,0:T(8,128)(2,1)S(1)} %get-tuple-element.30), channel_id=1, source_target_pairs={{0,9},{1,8},{2,11},{3,10},{4,13},{5,12},{6,15},{7,14},{8,1},{9,0},... | collective-permute-start | bytes 110600 | tf_op jit(solution)/shard_map/ppermute | solution.py:339
  6.6 7.7 %copy-start = (bf16[8,2,2048]{2,1,0:T(2,128)(2,1)S(1)}, bf16[8,2,2048]{2,1,0:T(2,128)(2,1)}, u32[]{:S(2)}) copy-start(bf16[8,2,2048]{2,1,0:T(2,128)(2,1)} %residual_ref.1) | copy-start | bytes 196612
  6.6 7.7 %copy-start.1 = (s32[8,2,8]{2,1,0:T(2,128)S(1)}, s32[8,2,8]{2,1,0:T(2,128)}, u32[]{:S(2)}) copy-start(s32[8,2,8]{2,1,0:T(2,128)} %param.23) | copy-start | bytes 1540
  6.6 7.7 %copy-start.2 = (f32[8,2,8]{2,1,0:T(2,128)S(1)}, f32[8,2,8]{2,1,0:T(2,128)}, u32[]{:S(2)}) copy-start(f32[8,2,8]{2,1,0:T(2,128)} %param.24) | copy-start | bytes 1540
  6.6 3.6 %collective-permute-start.3 = (bf16[144,128]{1,0:T(8,128)(2,1)S(1)}, bf16[144,128]{1,0:T(8,128)(2,1)S(1)}, u32[]{:S(2)}, u32[]{:S(2)}) collective-permute-start(bf16[144,128]{1,0:T(8,128)(2,1)S(1)} %get-tuple-element.31), channel_id=1, source_target_pairs={{0,1},{1,0},{2,3},{3,2},{4,5},{5,4},{6,7},{7,6},{8,9},{9,8},{10,11... | collective-permute-start | bytes 110600 | tf_op jit(solution)/shard_map/ppermute | solution.py:339
  10.9 5.1 %collective-permute-start.7 = (bf16[16,2048]{1,0:T(8,128)(2,1)S(1)}, bf16[16,2048]{1,0:T(8,128)(2,1)S(1)}, u32[]{:S(2)}, u32[]{:S(2)}) collective-permute-start(bf16[16,2048]{1,0:T(8,128)(2,1)S(1)} %project.1), channel_id=1, source_target_pairs={{0,25},{1,24},{2,27},{3,26},{4,29},{5,28},{6,31},{7,30},{8,17},{9,... | collective-permute-start | bytes 196616 | tf_op jit(solution)/shard_map/ppermute | solution.py:339
  12.2 5.4 %collective-permute-start.6 = (bf16[16,2048]{1,0:T(8,128)(2,1)S(1)}, bf16[16,2048]{1,0:T(8,128)(2,1)S(1)}, u32[]{:S(2)}, u32[]{:S(2)}) collective-permute-start(bf16[16,2048]{1,0:T(8,128)(2,1)S(1)} %project.1), channel_id=1, source_target_pairs={{0,17},{1,16},{2,19},{3,18},{4,21},{5,20},{6,23},{7,22},{8,25},{9,... | collective-permute-start | bytes 196616 | tf_op jit(solution)/shard_map/ppermute | solution.py:339
  12.6 5.0 %collective-permute-start.5 = (bf16[16,2048]{1,0:T(8,128)(2,1)S(1)}, bf16[16,2048]{1,0:T(8,128)(2,1)S(1)}, u32[]{:S(2)}, u32[]{:S(2)}) collective-permute-start(bf16[16,2048]{1,0:T(8,128)(2,1)S(1)} %project.1), channel_id=1, source_target_pairs={{0,9},{1,8},{2,11},{3,10},{4,13},{5,12},{6,15},{7,14},{8,1},{9,0},... | collective-permute-start | bytes 196616 | tf_op jit(solution)/shard_map/ppermute | solution.py:339
  13.9 3.7 %collective-permute-start.4 = (bf16[16,2048]{1,0:T(8,128)(2,1)S(1)}, bf16[16,2048]{1,0:T(8,128)(2,1)S(1)}, u32[]{:S(2)}, u32[]{:S(2)}) collective-permute-start(bf16[16,2048]{1,0:T(8,128)(2,1)S(1)} %project.1), channel_id=1, source_target_pairs={{0,1},{1,0},{2,3},{3,2},{4,5},{5,4},{6,7},{7,6},{8,9},{9,8},{10,11... | collective-permute-start | bytes 196616 | tf_op jit(solution)/shard_map/ppermute | solution.py:339
  17.6 9.3 %copy-start.4 = (bf16[1,2048,1024]{2,1,0:T(8,128)(2,1)S(1)}, bf16[1,2048,1024]{2,1,0:T(8,128)(2,1)}, u32[]{:S(2)}) copy-start(bf16[1,2048,1024]{2,1,0:T(8,128)(2,1)} %gate_ref.1) | copy-start | bytes 12582916
  17.6 9.3 %copy-start.5 = (bf16[1,2048,1024]{2,1,0:T(8,128)(2,1)S(1)}, bf16[1,2048,1024]{2,1,0:T(8,128)(2,1)}, u32[]{:S(2)}) copy-start(bf16[1,2048,1024]{2,1,0:T(8,128)(2,1)} %up_ref.1) | copy-start | bytes 12582916
  17.6 9.3 %copy-start.6 = (bf16[1,1024,2048]{2,1,0:T(8,128)(2,1)S(1)}, bf16[1,1024,2048]{2,1,0:T(8,128)(2,1)}, u32[]{:S(2)}) copy-start(bf16[1,1024,2048]{2,1,0:T(8,128)(2,1)} %down_ref.1) | copy-start | bytes 12582916
  17.6 9.3 %copy-start.7 = (bf16[2048]{0:T(1024)(128)(2,1)S(1)}, bf16[2048]{0:T(1024)(128)(2,1)}, u32[]{:S(2)}) copy-start(bf16[2048]{0:T(1024)(128)(2,1)} %param.22) | copy-start | bytes 12292
  17.8 5.2 %collective-permute-start.8 = (bf16[8,2048]{1,0:T(8,128)(2,1)S(1)}, bf16[8,2048]{1,0:T(8,128)(2,1)S(1)}, u32[]{:S(2)}, u32[]{:S(2)}) collective-permute-start(bf16[8,2048]{1,0:T(8,128)(2,1)S(1)} %get-tuple-element.35), channel_id=1, source_target_pairs={{0,7},{1,6},{2,5},{3,4},{4,3},{5,2},{6,1},{7,0},{8,15},{9,14},{10,... | collective-permute-start | bytes 98312 | tf_op jit(solution)/shard_map/ppermute | solution.py:339
  21.2 3.3 %collective-permute-start.9 = (bf16[8,2048]{1,0:T(8,128)(2,1)S(1)}, bf16[8,2048]{1,0:T(8,128)(2,1)S(1)}, u32[]{:S(2)}, u32[]{:S(2)}) collective-permute-start(bf16[8,2048]{1,0:T(8,128)(2,1)S(1)} %get-tuple-element.36), channel_id=1, source_target_pairs={{0,3},{1,2},{2,1},{3,0},{4,7},{5,6},{6,5},{7,4},{8,11},{9,10},{10,... | collective-permute-start | bytes 98312 | tf_op jit(solution)/shard_map/ppermute | solution.py:339
  21.2 4.3 %collective-permute-start.10 = (bf16[8,2048]{1,0:T(8,128)(2,1)S(1)}, bf16[8,2048]{1,0:T(8,128)(2,1)S(1)}, u32[]{:S(2)}, u32[]{:S(2)}) collective-permute-start(bf16[8,2048]{1,0:T(8,128)(2,1)S(1)} %get-tuple-element.37), channel_id=1, source_target_pairs={{0,5},{1,4},{2,7},{3,6},{4,1},{5,0},{6,3},{7,2},{8,13},{9,12},{10,... | collective-permute-start | bytes 98312 | tf_op jit(solution)/shard_map/ppermute | solution.py:339
  25.6 1.3 %collective-permute-start.11 = (bf16[16,2048]{1,0:T(8,128)(2,1)S(1)}, bf16[16,2048]{1,0:T(8,128)(2,1)S(1)}, u32[]{:S(2)}, u32[]{:S(2)}) collective-permute-start(bf16[16,2048]{1,0:T(8,128)(2,1)S(1)} %get-tuple-element.40), channel_id=1, source_target_pairs={{0,1},{1,0},{2,3},{3,2},{4,5},{5,4},{6,7},{7,6},{8,9},{9,8},{10,11... | collective-permute-start | bytes 196616 | tf_op jit(solution)/shard_map/ppermute | solution.py:339
  28.9 1.3 %collective-permute-start.12 = (bf16[16,2048]{1,0:T(8,128)(2,1)S(1)}, bf16[16,2048]{1,0:T(8,128)(2,1)S(1)}, u32[]{:S(2)}, u32[]{:S(2)}) collective-permute-start(bf16[16,2048]{1,0:T(8,128)(2,1)S(1)} %get-tuple-element.42), channel_id=1, source_target_pairs={{0,1},{1,0},{2,3},{3,2},{4,5},{5,4},{6,7},{7,6},{8,9},{9,8},{10,11... | collective-permute-start | bytes 196616 | tf_op jit(solution)/shard_map/ppermute | solution.py:339
  30.3 5.4 %collective-permute-start.13 = (bf16[8,2048]{1,0:T(8,128)(2,1)S(1)}, bf16[8,2048]{1,0:T(8,128)(2,1)S(1)}, u32[]{:S(2)}, u32[]{:S(2)}) collective-permute-start(bf16[8,2048]{1,0:T(8,128)(2,1)S(1)} %get-tuple-element.43), channel_id=1, source_target_pairs={{0,7},{1,6},{2,5},{3,4},{4,3},{5,2},{6,1},{7,0},{8,15},{9,14},{10,... | collective-permute-start | bytes 98312 | tf_op jit(solution)/shard_map/ppermute | solution.py:339
  32.2 4.9 %collective-permute-start.14 = (bf16[8,2048]{1,0:T(8,128)(2,1)S(1)}, bf16[8,2048]{1,0:T(8,128)(2,1)S(1)}, u32[]{:S(2)}, u32[]{:S(2)}) collective-permute-start(bf16[8,2048]{1,0:T(8,128)(2,1)S(1)} %get-tuple-element.44), channel_id=1, source_target_pairs={{0,3},{1,2},{2,1},{3,0},{4,7},{5,6},{6,5},{7,4},{8,11},{9,10},{10,... | collective-permute-start | bytes 98312 | tf_op jit(solution)/shard_map/ppermute | solution.py:339
  32.3 4.8 %collective-permute-start.15 = (bf16[8,2048]{1,0:T(8,128)(2,1)S(1)}, bf16[8,2048]{1,0:T(8,128)(2,1)S(1)}, u32[]{:S(2)}, u32[]{:S(2)}) collective-permute-start(bf16[8,2048]{1,0:T(8,128)(2,1)S(1)} %get-tuple-element.45), channel_id=1, source_target_pairs={{0,5},{1,4},{2,7},{3,6},{4,1},{5,0},{6,3},{7,2},{8,13},{9,12},{10,... | collective-permute-start | bytes 98312 | tf_op jit(solution)/shard_map/ppermute | solution.py:339
  37.3 5.3 %collective-permute-start.18 = (bf16[16,2048]{1,0:T(8,128)(2,1)S(1)}, bf16[16,2048]{1,0:T(8,128)(2,1)S(1)}, u32[]{:S(2)}, u32[]{:S(2)}) collective-permute-start(bf16[16,2048]{1,0:T(8,128)(2,1)S(1)} %combine.1.refs_0_), channel_id=1, source_target_pairs={{0,24},{1,25},{2,26},{3,27},{4,28},{5,29},{6,30},{7,31},{8,16},{9,... | collective-permute-start | bytes 196616 | tf_op jit(solution)/shard_map/ppermute | solution.py:339
  39.1 4.6 %collective-permute-start.17 = (bf16[16,2048]{1,0:T(8,128)(2,1)S(1)}, bf16[16,2048]{1,0:T(8,128)(2,1)S(1)}, u32[]{:S(2)}, u32[]{:S(2)}) collective-permute-start(bf16[16,2048]{1,0:T(8,128)(2,1)S(1)} %combine.1.refs_0_), channel_id=1, source_target_pairs={{0,16},{1,17},{2,18},{3,19},{4,20},{5,21},{6,22},{7,23},{8,24},{9,... | collective-permute-start | bytes 196616 | tf_op jit(solution)/shard_map/ppermute | solution.py:339
  39.6 4.3 %collective-permute-start.16 = (bf16[16,2048]{1,0:T(8,128)(2,1)S(1)}, bf16[16,2048]{1,0:T(8,128)(2,1)S(1)}, u32[]{:S(2)}, u32[]{:S(2)}) collective-permute-start(bf16[16,2048]{1,0:T(8,128)(2,1)S(1)} %combine.1.refs_0_), channel_id=1, source_target_pairs={{0,8},{1,9},{2,10},{3,11},{4,12},{5,13},{6,14},{7,15},{8,0},{9,1},... | collective-permute-start | bytes 196616 | tf_op jit(solution)/shard_map/ppermute | solution.py:339

commit v5 on v4

--- a/solution.py
+++ b/solution.py
@@ -35,13 +35,6 @@
     high = values.astype(jnp.bfloat16).astype(jnp.float32)
     middle = (values - high).astype(jnp.bfloat16).astype(jnp.float32)
     return high, middle, values - high - middle
-
-
-def every(values, first, step):
-    count = values.shape[0] // SUBLANES
-    return jnp.concatenate(
-        [values[i * SUBLANES : (i + 1) * SUBLANES] for i in range(first, count, step)], 0
-    )
 
 
 def interleave(parts):
@@ -87,7 +80,10 @@
         copy.wait()
     values = v_ref[...].reshape(wide, KV_HEADS * HEAD_DIM)
     fresh_values = jnp.concatenate([nv_ref[r] for r in range(rows)], 0)
-    queries = jnp.concatenate([q_ref[r] for r in range(rows)], 0)
+    queries = [
+        jnp.concatenate([q_ref[p * piece_rows + r] for r in range(piece_rows)], 0)
+        for p in range(pieces)
+    ]
     keys = k_ref[...].reshape(wide, KV_HEADS * HEAD_DIM)
     fresh_keys = jnp.concatenate([nk_ref[r] for r in range(rows)], 0)
     column = iota((1, piece_wide), 1)
@@ -106,52 +102,58 @@
             (row_index // steps == fresh_row) & (fresh_column % steps <= row_index % steps)
         )
     contract_last = (((1,), (1,)), ((), ()))
+    kv_lanes = [slice(kv * HEAD_DIM, (kv + 1) * HEAD_DIM) for kv in range(KV_HEADS)]
+    spans = [slice(p * piece_wide, (p + 1) * piece_wide) for p in range(pieces)]
+    scores, fresh = {}, {}
+    for kv, lanes in enumerate(kv_lanes):
+        for p, span in enumerate(spans):
+            heads = jnp.concatenate(
+                [
+                    queries[p][:, h * HEAD_DIM : (h + 1) * HEAD_DIM]
+                    for h in range(kv * group, (kv + 1) * group)
+                ],
+                0,
+            )
+            scores[kv, p] = lax.dot_general(
+                heads, keys[span, lanes], contract_last, preferred_element_type=jnp.float32
+            )
+            fresh[kv, p] = lax.dot_general(
+                heads, fresh_keys[:, lanes], contract_last, preferred_element_type=jnp.float32
+            )
+    terms, last_terms, tops, totals = {}, {}, {}, {}
     for kv in range(KV_HEADS):
-        lanes = slice(kv * HEAD_DIM, (kv + 1) * HEAD_DIM)
-        heads = jnp.concatenate(
-            [
-                queries[:, h * HEAD_DIM : (h + 1) * HEAD_DIM]
-                for h in range(kv * group, (kv + 1) * group)
-            ],
-            0,
-        )
-        scores = lax.dot_general(
-            heads, keys[:, lanes], contract_last, preferred_element_type=jnp.float32
-        )
-        fresh = lax.dot_general(
-            heads, fresh_keys[:, lanes], contract_last, preferred_element_type=jnp.float32
-        )
-        means, levels = [], []
         for p in range(pieces):
-            span = slice(p * piece_wide, (p + 1) * piece_wide)
-            part = every(scores[:, span], p, pieces)
-            part = jnp.where(live[p], part * scale, MASKED_SCORE)
-            last = every(fresh, p, pieces)
-            last = jnp.where(fresh_live[p], last * scale, MASKED_SCORE)
+            part = jnp.where(live[p], scores[kv, p] * scale, MASKED_SCORE)
+            last = jnp.where(fresh_live[p], fresh[kv, p] * scale, MASKED_SCORE)
             top = jnp.maximum(
                 jnp.max(part, 1, keepdims=True), jnp.max(last, 1, keepdims=True)
             )
-            terms = jnp.exp(part - top)
-            last_terms = jnp.exp(last - top)
-            total = jnp.sum(terms, 1, keepdims=True) + jnp.sum(last_terms, 1, keepdims=True)
-            weighted = jnp.dot(
-                terms.astype(jnp.bfloat16),
-                values[span, lanes],
-                preferred_element_type=jnp.float32,
+            part, last = jnp.exp(part - top), jnp.exp(last - top)
+            terms[kv, p], last_terms[kv, p] = part.astype(jnp.bfloat16), last.astype(jnp.bfloat16)
+            tops[kv, p] = top
+            totals[kv, p] = jnp.sum(part, 1, keepdims=True) + jnp.sum(last, 1, keepdims=True)
+    weighted = {}
+    for kv, lanes in enumerate(kv_lanes):
+        for p, span in enumerate(spans):
+            weighted[kv, p] = jnp.dot(
+                terms[kv, p], values[span, lanes], preferred_element_type=jnp.float32
             ) + jnp.dot(
-                last_terms.astype(jnp.bfloat16),
-                fresh_values[:, lanes],
-                preferred_element_type=jnp.float32,
+                last_terms[kv, p], fresh_values[:, lanes], preferred_element_type=jnp.float32
             )
-            means.append(weighted / total)
-            levels.append(jnp.broadcast_to(top + jnp.log(total), (piece_high, LANES)))
-        mean = interleave(means).astype(jnp.bfloat16)
-        level = interleave(levels)
-        span = block_heads * row_steps
+    span = block_heads * row_steps
+    row = iota((SUBLANES, LANES), 0)
+    for kv in range(KV_HEADS):
+        level = interleave(
+            [
+                jnp.broadcast_to(tops[kv, p] + jnp.log(totals[kv, p]), (piece_high, LANES))
+                for p in range(pieces)
+            ]
+        )
+        mean = interleave([weighted[kv, p] / totals[kv, p] for p in range(pieces)])
+        mean = mean.astype(jnp.bfloat16)
         for part in range(high // LANES):
             level_row = jnp.transpose(level[part * LANES : (part + 1) * LANES])[:SUBLANES]
             high_part, middle_part, low_part = split_three(level_row)
-            row = iota((SUBLANES, LANES), 0)
             stats = jnp.where(row == 0, high_part, jnp.where(row == 1, middle_part, low_part))
             stats = jnp.concatenate([stats, stats], 0).astype(jnp.bfloat16)
             for sub in range(LANES // span):

time: 44.6 us -> 44.3 us (level)
  transfers between devices with their start and end apart: 19 -> 19, of which waited for: 14 -> 15; matrix products, arithmetic and copies ran while one was open for 0% -> 0% of each run, Pallas kernels for 0% -> 0%
where the time goes in v5:
time: 44.3 us; the launch traced here: 44.2 us
  starting transfers between devices  20.3 us (46%)
  waiting for transfers between devices  17.8 us (40%)
  Pallas kernels  5.97 us (13%)
    ppermute x19, starting transfers between devices, move(): return lax.ppermute(block, ('ctx', 'exp'), pairs)  20.3 us
    ppermute x19, waiting for transfers between devices, move(): return lax.ppermute(block, ('ctx', 'exp'), pairs)  17.8 us
    pallas_call x9, Pallas kernels, call(): pl.pallas_call(kernel, name=name, in_specs=in_specs, out_specs=[out_spec...  5.97 us
  transfers between devices with their start and end apart: 19, of which 15 were waited for; matrix products, arithmetic and copies ran while one was open for 0% of the time, Pallas kernels for 0%

profile of v5, /device:TPU:0, one launch (start us, length us, event | category | flops | bytes accessed | tf_op | source)
XLA Modules:
  0.0 44.2 jit_solution(14229583280037861864)
XLA Ops:
  0.0 1.9 %attend.1 = (bf16[144,128]{1,0:T(8,128)(2,1)S(1)}, bf16[144,128]{1,0:T(8,128)(2,1)S(1)}, bf16[144,128]{1,0:T(8,128)(2,1)S(1)}, bf16[144,128]{1,0:T(8,128)(2,1)S(1)}) custom-call(s32[1]{0:T(128)} %bitcast.me_ref, s32[8]{0:T(128)} %len_hbm.1, bf16[8,2,4096]{2,1,0:T(2,128)(2,1)} %q_hbm.1, bf16[8,64,256]{2,1,0:T(8,128)(2,1)} %k_hbm.1, ...), custom_call_target="tpu_custom_call" | custom-call | flops 10000000000 | bytes 1048576 | tf_op jit(solution)/shard_map/attend/pallas_call | solution.py:318
  1.9 3.4 %collective-permute-start = (bf16[144,128]{1,0:T(8,128)(2,1)S(1)}, bf16[144,128]{1,0:T(8,128)(2,1)S(1)}, u32[]{:S(2)}, u32[]{:S(2)}) collective-permute-start(bf16[144,128]{1,0:T(8,128)(2,1)S(1)} %get-tuple-element.28), channel_id=1, source_target_pairs={{0,25},{1,24},{2,27},{3,26},{4,29},{5,28},{6,31},{7,30},{8,17},{9,... | collective-permute-start | bytes 110600 | tf_op jit(solution)/shard_map/ppermute | solution.py:341
  5.3 0.8 %collective-permute-start.1 = (bf16[144,128]{1,0:T(8,128)(2,1)S(1)}, bf16[144,128]{1,0:T(8,128)(2,1)S(1)}, u32[]{:S(2)}, u32[]{:S(2)}) collective-permute-start(bf16[144,128]{1,0:T(8,128)(2,1)S(1)} %get-tuple-element.29), channel_id=1, source_target_pairs={{0,17},{1,16},{2,19},{3,18},{4,21},{5,20},{6,23},{7,22},{8,25},{9,... | collective-permute-start | bytes 110600 | tf_op jit(solution)/shard_map/ppermute | solution.py:341
  6.3 0.9 %collective-permute-done.rest_0_ = bf16[144,128]{1,0:T(8,128)(2,1)S(1)} collective-permute-done((bf16[144,128]{1,0:T(8,128)(2,1)S(1)}, bf16[144,128]{1,0:T(8,128)(2,1)S(1)}, u32[]{:S(2)}, u32[]{:S(2)}) %collective-permute-start) | collective-permute-done | bytes 36896 | tf_op jit(solution)/shard_map/ppermute | solution.py:341
  7.2 1.5 %collective-permute-done.1.rest_1_ = bf16[144,128]{1,0:T(8,128)(2,1)S(1)} collective-permute-done((bf16[144,128]{1,0:T(8,128)(2,1)S(1)}, bf16[144,128]{1,0:T(8,128)(2,1)S(1)}, u32[]{:S(2)}, u32[]{:S(2)}) %collective-permute-start.1) | collective-permute-done | bytes 36896 | tf_op jit(solution)/shard_map/ppermute | solution.py:341
  8.7 1.1 %collective-permute-done.2.rest_2_ = bf16[144,128]{1,0:T(8,128)(2,1)S(1)} collective-permute-done((bf16[144,128]{1,0:T(8,128)(2,1)S(1)}, bf16[144,128]{1,0:T(8,128)(2,1)S(1)}, u32[]{:S(2)}, u32[]{:S(2)}) %collective-permute-start.2) | collective-permute-done | bytes 36896 | tf_op jit(solution)/shard_map/ppermute | solution.py:341
  9.8 0.8 %project.1 = bf16[16,2048]{1,0:T(8,128)(2,1)S(1)} custom-call(bf16[1024,2048]{1,0:T(8,128)(2,1)S(1)} %copy-done.3, bf16[144,128]{1,0:T(8,128)(2,1)S(1)} %collective-permute-done.rest_0_, bf16[144,128]{1,0:T(8,128)(2,1)S(1)} %collective-permute-done.1.rest_1_, bf16[144,128]{1,0:T(8,128)(2,1)S(1)} %collective-permute-done.2.rest_2_, ...), custom_call_target="tpu_custom_call" | custom-call | flops 10000000000 | bytes 1048576 | tf_op jit(solution)/shard_map/project/pallas_call | solution.py:318
  10.6 1.2 %collective-permute-start.7 = (bf16[16,2048]{1,0:T(8,128)(2,1)S(1)}, bf16[16,2048]{1,0:T(8,128)(2,1)S(1)}, u32[]{:S(2)}, u32[]{:S(2)}) collective-permute-start(bf16[16,2048]{1,0:T(8,128)(2,1)S(1)} %project.1), channel_id=1, source_target_pairs={{0,25},{1,24},{2,27},{3,26},{4,29},{5,28},{6,31},{7,30},{8,17},{9,... | collective-permute-start | bytes 196616 | tf_op jit(solution)/shard_map/ppermute | solution.py:341
  11.8 0.4 collective-permute-start.6
  12.3 1.2 %collective-permute-start.5 = (bf16[16,2048]{1,0:T(8,128)(2,1)S(1)}, bf16[16,2048]{1,0:T(8,128)(2,1)S(1)}, u32[]{:S(2)}, u32[]{:S(2)}) collective-permute-start(bf16[16,2048]{1,0:T(8,128)(2,1)S(1)} %project.1), channel_id=1, source_target_pairs={{0,9},{1,8},{2,11},{3,10},{4,13},{5,12},{6,15},{7,14},{8,1},{9,0},... | collective-permute-start | bytes 196616 | tf_op jit(solution)/shard_map/ppermute | solution.py:341
  13.5 0.4 collective-permute-start.4
  14.2 1.5 %collective-permute-done.7.rest_3_ = bf16[16,2048]{1,0:T(8,128)(2,1)S(1)} collective-permute-done((bf16[16,2048]{1,0:T(8,128)(2,1)S(1)}, bf16[16,2048]{1,0:T(8,128)(2,1)S(1)}, u32[]{:S(2)}, u32[]{:S(2)}) %collective-permute-start.7) | collective-permute-done | bytes 65568 | tf_op jit(solution)/shard_map/ppermute | solution.py:341
  15.7 1.6 %collective-permute-done.6.rest_2_ = bf16[16,2048]{1,0:T(8,128)(2,1)S(1)} collective-permute-done((bf16[16,2048]{1,0:T(8,128)(2,1)S(1)}, bf16[16,2048]{1,0:T(8,128)(2,1)S(1)}, u32[]{:S(2)}, u32[]{:S(2)}) %collective-permute-start.6) | collective-permute-done | bytes 65568 | tf_op jit(solution)/shard_map/ppermute | solution.py:341
  17.5 3.4 %collective-permute-start.8 = (bf16[8,2048]{1,0:T(8,128)(2,1)S(1)}, bf16[8,2048]{1,0:T(8,128)(2,1)S(1)}, u32[]{:S(2)}, u32[]{:S(2)}) collective-permute-start(bf16[8,2048]{1,0:T(8,128)(2,1)S(1)} %get-tuple-element.35), channel_id=1, source_target_pairs={{0,7},{1,6},{2,5},{3,4},{4,3},{5,2},{6,1},{7,0},{8,15},{9,14},{10,... | collective-permute-start | bytes 98312 | tf_op jit(solution)/shard_map/ppermute | solution.py:341
  20.9 0.6 %collective-permute-start.10 = (bf16[8,2048]{1,0:T(8,128)(2,1)S(1)}, bf16[8,2048]{1,0:T(8,128)(2,1)S(1)}, u32[]{:S(2)}, u32[]{:S(2)}) collective-permute-start(bf16[8,2048]{1,0:T(8,128)(2,1)S(1)} %get-tuple-element.37), channel_id=1, source_target_pairs={{0,5},{1,4},{2,7},{3,6},{4,1},{5,0},{6,3},{7,2},{8,13},{9,12},{10,... | collective-permute-start | bytes 98312 | tf_op jit(solution)/shard_map/ppermute | solution.py:341
  21.5 1.2 %collective-permute-done.8.refs_0_ = bf16[8,2048]{1,0:T(8,128)(2,1)S(1)} collective-permute-done((bf16[8,2048]{1,0:T(8,128)(2,1)S(1)}, bf16[8,2048]{1,0:T(8,128)(2,1)S(1)}, u32[]{:S(2)}, u32[]{:S(2)}) %collective-permute-start.8) | collective-permute-done | bytes 32800 | tf_op jit(solution)/shard_map/ppermute | solution.py:341
  22.7 1.5 %collective-permute-done.9.refs_1_ = bf16[8,2048]{1,0:T(8,128)(2,1)S(1)} collective-permute-done((bf16[8,2048]{1,0:T(8,128)(2,1)S(1)}, bf16[8,2048]{1,0:T(8,128)(2,1)S(1)}, u32[]{:S(2)}, u32[]{:S(2)}) %collective-permute-start.9) | collective-permute-done | bytes 32800 | tf_op jit(solution)/shard_map/ppermute | solution.py:341
  24.2 1.0 %collective-permute-done.10.refs_2_ = bf16[8,2048]{1,0:T(8,128)(2,1)S(1)} collective-permute-done((bf16[8,2048]{1,0:T(8,128)(2,1)S(1)}, bf16[8,2048]{1,0:T(8,128)(2,1)S(1)}, u32[]{:S(2)}, u32[]{:S(2)}) %collective-permute-start.10) | collective-permute-done | bytes 32800 | tf_op jit(solution)/shard_map/ppermute | solution.py:341
  25.2 0.4 collective-permute-start.11
  25.7 0.9 %collective-permute-done.11.got_ref = bf16[16,2048]{1,0:T(8,128)(2,1)S(1)} collective-permute-done((bf16[16,2048]{1,0:T(8,128)(2,1)S(1)}, bf16[16,2048]{1,0:T(8,128)(2,1)S(1)}, u32[]{:S(2)}, u32[]{:S(2)}) %collective-permute-start.11) | collective-permute-done | bytes 65568 | tf_op jit(solution)/shard_map/ppermute | solution.py:341
  26.6 2.0 %experts.1 = (bf16[16,2048]{1,0:T(8,128)(2,1)S(1)}, bf16[16,2048]{1,0:T(8,128)(2,1)S(1)}) custom-call(bf16[16,2048]{1,0:T(8,128)(2,1)S(1)} %get-tuple-element.39.kept_ref, bf16[16,2048]{1,0:T(8,128)(2,1)S(1)} %collective-permute-done.11.got_ref, bf16[16,128]{1,0:T(8,128)(2,1)S(1)} %bitcast.7, bf16[1,2048,1024]{2,1,0:T(8,128)(2,1)S(1)} %copy-done.4, ...), custom_call_target="tpu_custom_call" | custom-call | flops 10000000000 | bytes 1048576 | tf_op jit(solution)/shard_map/experts/pallas_call | solution.py:318
  29.0 0.9 %collective-permute-done.12.got_ref = bf16[16,2048]{1,0:T(8,128)(2,1)S(1)} collective-permute-done((bf16[16,2048]{1,0:T(8,128)(2,1)S(1)}, bf16[16,2048]{1,0:T(8,128)(2,1)S(1)}, u32[]{:S(2)}, u32[]{:S(2)}) %collective-permute-start.12) | collective-permute-done | bytes 65568 | tf_op jit(solution)/shard_map/ppermute | solution.py:341
  29.9 1.9 %collective-permute-start.13 = (bf16[8,2048]{1,0:T(8,128)(2,1)S(1)}, bf16[8,2048]{1,0:T(8,128)(2,1)S(1)}, u32[]{:S(2)}, u32[]{:S(2)}) collective-permute-start(bf16[8,2048]{1,0:T(8,128)(2,1)S(1)} %get-tuple-element.43), channel_id=1, source_target_pairs={{0,7},{1,6},{2,5},{3,4},{4,3},{5,2},{6,1},{7,0},{8,15},{9,14},{10,... | collective-permute-start | bytes 98312 | tf_op jit(solution)/shard_map/ppermute | solution.py:341
  31.9 2.1 %collective-permute-start.15 = (bf16[8,2048]{1,0:T(8,128)(2,1)S(1)}, bf16[8,2048]{1,0:T(8,128)(2,1)S(1)}, u32[]{:S(2)}, u32[]{:S(2)}) collective-permute-start(bf16[8,2048]{1,0:T(8,128)(2,1)S(1)} %get-tuple-element.45), channel_id=1, source_target_pairs={{0,5},{1,4},{2,7},{3,6},{4,1},{5,0},{6,3},{7,2},{8,13},{9,12},{10,... | collective-permute-start | bytes 98312 | tf_op jit(solution)/shard_map/ppermute | solution.py:341
  34.0 1.3 %collective-permute-done.13.refs_0_ = bf16[8,2048]{1,0:T(8,128)(2,1)S(1)} collective-permute-done((bf16[8,2048]{1,0:T(8,128)(2,1)S(1)}, bf16[8,2048]{1,0:T(8,128)(2,1)S(1)}, u32[]{:S(2)}, u32[]{:S(2)}) %collective-permute-start.13) | collective-permute-done | bytes 32800 | tf_op jit(solution)/shard_map/ppermute | solution.py:341
  35.3 1.5 %collective-permute-done.14.refs_1_ = bf16[8,2048]{1,0:T(8,128)(2,1)S(1)} collective-permute-done((bf16[8,2048]{1,0:T(8,128)(2,1)S(1)}, bf16[8,2048]{1,0:T(8,128)(2,1)S(1)}, u32[]{:S(2)}, u32[]{:S(2)}) %collective-permute-start.14) | collective-permute-done | bytes 32800 | tf_op jit(solution)/shard_map/ppermute | solution.py:341
  36.9 1.8 %collective-permute-start.18 = (bf16[16,2048]{1,0:T(8,128)(2,1)S(1)}, bf16[16,2048]{1,0:T(8,128)(2,1)S(1)}, u32[]{:S(2)}, u32[]{:S(2)}) collective-permute-start(bf16[16,2048]{1,0:T(8,128)(2,1)S(1)} %combine.1.refs_0_), channel_id=1, source_target_pairs={{0,24},{1,25},{2,26},{3,27},{4,28},{5,29},{6,30},{7,31},{8,16},{9,... | collective-permute-start | bytes 196616 | tf_op jit(solution)/shard_map/ppermute | solution.py:341
  38.8 0.5 %collective-permute-start.17 = (bf16[16,2048]{1,0:T(8,128)(2,1)S(1)}, bf16[16,2048]{1,0:T(8,128)(2,1)S(1)}, u32[]{:S(2)}, u32[]{:S(2)}) collective-permute-start(bf16[16,2048]{1,0:T(8,128)(2,1)S(1)} %combine.1.refs_0_), channel_id=1, source_target_pairs={{0,16},{1,17},{2,18},{3,19},{4,20},{5,21},{6,22},{7,23},{8,24},{9,... | collective-permute-start | bytes 196616 | tf_op jit(solution)/shard_map/ppermute | solution.py:341
  39.2 1.3 %collective-permute-start.16 = (bf16[16,2048]{1,0:T(8,128)(2,1)S(1)}, bf16[16,2048]{1,0:T(8,128)(2,1)S(1)}, u32[]{:S(2)}, u32[]{:S(2)}) collective-permute-start(bf16[16,2048]{1,0:T(8,128)(2,1)S(1)} %combine.1.refs_0_), channel_id=1, source_target_pairs={{0,8},{1,9},{2,10},{3,11},{4,12},{5,13},{6,14},{7,15},{8,0},{9,1},... | collective-permute-start | bytes 196616 | tf_op jit(solution)/shard_map/ppermute | solution.py:341
  40.5 1.7 %collective-permute-done.18.refs_3_ = bf16[16,2048]{1,0:T(8,128)(2,1)S(1)} collective-permute-done((bf16[16,2048]{1,0:T(8,128)(2,1)S(1)}, bf16[16,2048]{1,0:T(8,128)(2,1)S(1)}, u32[]{:S(2)}, u32[]{:S(2)}) %collective-permute-start.18) | collective-permute-done | bytes 65568 | tf_op jit(solution)/shard_map/ppermute | solution.py:341
  42.2 1.2 %collective-permute-done.17.refs_2_ = bf16[16,2048]{1,0:T(8,128)(2,1)S(1)} collective-permute-done((bf16[16,2048]{1,0:T(8,128)(2,1)S(1)}, bf16[16,2048]{1,0:T(8,128)(2,1)S(1)}, u32[]{:S(2)}, u32[]{:S(2)}) %collective-permute-start.17) | collective-permute-done | bytes 65568 | tf_op jit(solution)/shard_map/ppermute | solution.py:341
  43.5 0.7 %finish.1 = bf16[8,2,2048]{2,1,0:T(2,128)(2,1)} custom-call(f32[16,2048]{1,0:T(8,128)S(1)} %get-tuple-element.32.state_ref, bf16[16,2048]{1,0:T(8,128)(2,1)S(1)} %combine.1.refs_0_, bf16[16,2048]{1,0:T(8,128)(2,1)S(1)} %collective-permute-done.16.refs_1_, bf16[16,2048]{1,0:T(8,128)(2,1)S(1)} %collective-permute-done.17.refs_2_, ...), custom_call_target="tpu_custom_call" | custom-call | tf_op jit(solution)/shard_map/finish/pallas_call | solution.py:318
  (31 shorter events, 1.4 us)
Async XLA Ops:
  0.0 9.8 %copy-start.3 = (bf16[1024,2048]{1,0:T(8,128)(2,1)S(1)}, bf16[1024,2048]{1,0:T(8,128)(2,1)}, u32[]{:S(2)}) copy-start(bf16[1024,2048]{1,0:T(8,128)(2,1)} %w_ref.1) | copy-start | bytes 12582916
  1.9 5.3 %collective-permute-start = (bf16[144,128]{1,0:T(8,128)(2,1)S(1)}, bf16[144,128]{1,0:T(8,128)(2,1)S(1)}, u32[]{:S(2)}, u32[]{:S(2)}) collective-permute-start(bf16[144,128]{1,0:T(8,128)(2,1)S(1)} %get-tuple-element.28), channel_id=1, source_target_pairs={{0,25},{1,24},{2,27},{3,26},{4,29},{5,28},{6,31},{7,30},{8,17},{9,... | collective-permute-start | bytes 110600 | tf_op jit(solution)/shard_map/ppermute | solution.py:341
  5.3 3.4 %collective-permute-start.1 = (bf16[144,128]{1,0:T(8,128)(2,1)S(1)}, bf16[144,128]{1,0:T(8,128)(2,1)S(1)}, u32[]{:S(2)}, u32[]{:S(2)}) collective-permute-start(bf16[144,128]{1,0:T(8,128)(2,1)S(1)} %get-tuple-element.29), channel_id=1, source_target_pairs={{0,17},{1,16},{2,19},{3,18},{4,21},{5,20},{6,23},{7,22},{8,25},{9,... | collective-permute-start | bytes 110600 | tf_op jit(solution)/shard_map/ppermute | solution.py:341
  6.1 3.7 %collective-permute-start.2 = (bf16[144,128]{1,0:T(8,128)(2,1)S(1)}, bf16[144,128]{1,0:T(8,128)(2,1)S(1)}, u32[]{:S(2)}, u32[]{:S(2)}) collective-permute-start(bf16[144,128]{1,0:T(8,128)(2,1)S(1)} %get-tuple-element.30), channel_id=1, source_target_pairs={{0,9},{1,8},{2,11},{3,10},{4,13},{5,12},{6,15},{7,14},{8,1},{9,0},... | collective-permute-start | bytes 110600 | tf_op jit(solution)/shard_map/ppermute | solution.py:341
  6.2 7.7 %copy-start = (bf16[8,2,2048]{2,1,0:T(2,128)(2,1)S(1)}, bf16[8,2,2048]{2,1,0:T(2,128)(2,1)}, u32[]{:S(2)}) copy-start(bf16[8,2,2048]{2,1,0:T(2,128)(2,1)} %residual_ref.1) | copy-start | bytes 196612
  6.2 7.7 %copy-start.1 = (s32[8,2,8]{2,1,0:T(2,128)S(1)}, s32[8,2,8]{2,1,0:T(2,128)}, u32[]{:S(2)}) copy-start(s32[8,2,8]{2,1,0:T(2,128)} %param.23) | copy-start | bytes 1540
  6.3 7.7 %copy-start.2 = (f32[8,2,8]{2,1,0:T(2,128)S(1)}, f32[8,2,8]{2,1,0:T(2,128)}, u32[]{:S(2)}) copy-start(f32[8,2,8]{2,1,0:T(2,128)} %param.24) | copy-start | bytes 1540
  6.3 3.6 %collective-permute-start.3 = (bf16[144,128]{1,0:T(8,128)(2,1)S(1)}, bf16[144,128]{1,0:T(8,128)(2,1)S(1)}, u32[]{:S(2)}, u32[]{:S(2)}) collective-permute-start(bf16[144,128]{1,0:T(8,128)(2,1)S(1)} %get-tuple-element.31), channel_id=1, source_target_pairs={{0,1},{1,0},{2,3},{3,2},{4,5},{5,4},{6,7},{7,6},{8,9},{9,8},{10,11... | collective-permute-start | bytes 110600 | tf_op jit(solution)/shard_map/ppermute | solution.py:341
  10.6 5.1 %collective-permute-start.7 = (bf16[16,2048]{1,0:T(8,128)(2,1)S(1)}, bf16[16,2048]{1,0:T(8,128)(2,1)S(1)}, u32[]{:S(2)}, u32[]{:S(2)}) collective-permute-start(bf16[16,2048]{1,0:T(8,128)(2,1)S(1)} %project.1), channel_id=1, source_target_pairs={{0,25},{1,24},{2,27},{3,26},{4,29},{5,28},{6,31},{7,30},{8,17},{9,... | collective-permute-start | bytes 196616 | tf_op jit(solution)/shard_map/ppermute | solution.py:341
  11.8 5.4 %collective-permute-start.6 = (bf16[16,2048]{1,0:T(8,128)(2,1)S(1)}, bf16[16,2048]{1,0:T(8,128)(2,1)S(1)}, u32[]{:S(2)}, u32[]{:S(2)}) collective-permute-start(bf16[16,2048]{1,0:T(8,128)(2,1)S(1)} %project.1), channel_id=1, source_target_pairs={{0,17},{1,16},{2,19},{3,18},{4,21},{5,20},{6,23},{7,22},{8,25},{9,... | collective-permute-start | bytes 196616 | tf_op jit(solution)/shard_map/ppermute | solution.py:341
  12.3 5.0 %collective-permute-start.5 = (bf16[16,2048]{1,0:T(8,128)(2,1)S(1)}, bf16[16,2048]{1,0:T(8,128)(2,1)S(1)}, u32[]{:S(2)}, u32[]{:S(2)}) collective-permute-start(bf16[16,2048]{1,0:T(8,128)(2,1)S(1)} %project.1), channel_id=1, source_target_pairs={{0,9},{1,8},{2,11},{3,10},{4,13},{5,12},{6,15},{7,14},{8,1},{9,0},... | collective-permute-start | bytes 196616 | tf_op jit(solution)/shard_map/ppermute | solution.py:341
  13.5 3.7 %collective-permute-start.4 = (bf16[16,2048]{1,0:T(8,128)(2,1)S(1)}, bf16[16,2048]{1,0:T(8,128)(2,1)S(1)}, u32[]{:S(2)}, u32[]{:S(2)}) collective-permute-start(bf16[16,2048]{1,0:T(8,128)(2,1)S(1)} %project.1), channel_id=1, source_target_pairs={{0,1},{1,0},{2,3},{3,2},{4,5},{5,4},{6,7},{7,6},{8,9},{9,8},{10,11... | collective-permute-start | bytes 196616 | tf_op jit(solution)/shard_map/ppermute | solution.py:341
  17.2 9.3 %copy-start.4 = (bf16[1,2048,1024]{2,1,0:T(8,128)(2,1)S(1)}, bf16[1,2048,1024]{2,1,0:T(8,128)(2,1)}, u32[]{:S(2)}) copy-start(bf16[1,2048,1024]{2,1,0:T(8,128)(2,1)} %gate_ref.1) | copy-start | bytes 12582916
  17.2 9.3 %copy-start.5 = (bf16[1,2048,1024]{2,1,0:T(8,128)(2,1)S(1)}, bf16[1,2048,1024]{2,1,0:T(8,128)(2,1)}, u32[]{:S(2)}) copy-start(bf16[1,2048,1024]{2,1,0:T(8,128)(2,1)} %up_ref.1) | copy-start | bytes 12582916
  17.3 9.3 %copy-start.6 = (bf16[1,1024,2048]{2,1,0:T(8,128)(2,1)S(1)}, bf16[1,1024,2048]{2,1,0:T(8,128)(2,1)}, u32[]{:S(2)}) copy-start(bf16[1,1024,2048]{2,1,0:T(8,128)(2,1)} %down_ref.1) | copy-start | bytes 12582916
  17.3 9.3 %copy-start.7 = (bf16[2048]{0:T(1024)(128)(2,1)S(1)}, bf16[2048]{0:T(1024)(128)(2,1)}, u32[]{:S(2)}) copy-start(bf16[2048]{0:T(1024)(128)(2,1)} %param.22) | copy-start | bytes 12292
  17.5 5.2 %collective-permute-start.8 = (bf16[8,2048]{1,0:T(8,128)(2,1)S(1)}, bf16[8,2048]{1,0:T(8,128)(2,1)S(1)}, u32[]{:S(2)}, u32[]{:S(2)}) collective-permute-start(bf16[8,2048]{1,0:T(8,128)(2,1)S(1)} %get-tuple-element.35), channel_id=1, source_target_pairs={{0,7},{1,6},{2,5},{3,4},{4,3},{5,2},{6,1},{7,0},{8,15},{9,14},{10,... | collective-permute-start | bytes 98312 | tf_op jit(solution)/shard_map/ppermute | solution.py:341
  20.9 3.3 %collective-permute-start.9 = (bf16[8,2048]{1,0:T(8,128)(2,1)S(1)}, bf16[8,2048]{1,0:T(8,128)(2,1)S(1)}, u32[]{:S(2)}, u32[]{:S(2)}) collective-permute-start(bf16[8,2048]{1,0:T(8,128)(2,1)S(1)} %get-tuple-element.36), channel_id=1, source_target_pairs={{0,3},{1,2},{2,1},{3,0},{4,7},{5,6},{6,5},{7,4},{8,11},{9,10},{10,... | collective-permute-start | bytes 98312 | tf_op jit(solution)/shard_map/ppermute | solution.py:341
  20.9 4.3 %collective-permute-start.10 = (bf16[8,2048]{1,0:T(8,128)(2,1)S(1)}, bf16[8,2048]{1,0:T(8,128)(2,1)S(1)}, u32[]{:S(2)}, u32[]{:S(2)}) collective-permute-start(bf16[8,2048]{1,0:T(8,128)(2,1)S(1)} %get-tuple-element.37), channel_id=1, source_target_pairs={{0,5},{1,4},{2,7},{3,6},{4,1},{5,0},{6,3},{7,2},{8,13},{9,12},{10,... | collective-permute-start | bytes 98312 | tf_op jit(solution)/shard_map/ppermute | solution.py:341
  25.2 1.3 %collective-permute-start.11 = (bf16[16,2048]{1,0:T(8,128)(2,1)S(1)}, bf16[16,2048]{1,0:T(8,128)(2,1)S(1)}, u32[]{:S(2)}, u32[]{:S(2)}) collective-permute-start(bf16[16,2048]{1,0:T(8,128)(2,1)S(1)} %get-tuple-element.40), channel_id=1, source_target_pairs={{0,1},{1,0},{2,3},{3,2},{4,5},{5,4},{6,7},{7,6},{8,9},{9,8},{10,11... | collective-permute-start | bytes 196616 | tf_op jit(solution)/shard_map/ppermute | solution.py:341
  28.5 1.3 %collective-permute-start.12 = (bf16[16,2048]{1,0:T(8,128)(2,1)S(1)}, bf16[16,2048]{1,0:T(8,128)(2,1)S(1)}, u32[]{:S(2)}, u32[]{:S(2)}) collective-permute-start(bf16[16,2048]{1,0:T(8,128)(2,1)S(1)} %get-tuple-element.42), channel_id=1, source_target_pairs={{0,1},{1,0},{2,3},{3,2},{4,5},{5,4},{6,7},{7,6},{8,9},{9,8},{10,11... | collective-permute-start | bytes 196616 | tf_op jit(solution)/shard_map/ppermute | solution.py:341
  29.9 5.4 %collective-permute-start.13 = (bf16[8,2048]{1,0:T(8,128)(2,1)S(1)}, bf16[8,2048]{1,0:T(8,128)(2,1)S(1)}, u32[]{:S(2)}, u32[]{:S(2)}) collective-permute-start(bf16[8,2048]{1,0:T(8,128)(2,1)S(1)} %get-tuple-element.43), channel_id=1, source_target_pairs={{0,7},{1,6},{2,5},{3,4},{4,3},{5,2},{6,1},{7,0},{8,15},{9,14},{10,... | collective-permute-start | bytes 98312 | tf_op jit(solution)/shard_map/ppermute | solution.py:341
  31.8 4.9 %collective-permute-start.14 = (bf16[8,2048]{1,0:T(8,128)(2,1)S(1)}, bf16[8,2048]{1,0:T(8,128)(2,1)S(1)}, u32[]{:S(2)}, u32[]{:S(2)}) collective-permute-start(bf16[8,2048]{1,0:T(8,128)(2,1)S(1)} %get-tuple-element.44), channel_id=1, source_target_pairs={{0,3},{1,2},{2,1},{3,0},{4,7},{5,6},{6,5},{7,4},{8,11},{9,10},{10,... | collective-permute-start | bytes 98312 | tf_op jit(solution)/shard_map/ppermute | solution.py:341
  31.9 4.9 %collective-permute-start.15 = (bf16[8,2048]{1,0:T(8,128)(2,1)S(1)}, bf16[8,2048]{1,0:T(8,128)(2,1)S(1)}, u32[]{:S(2)}, u32[]{:S(2)}) collective-permute-start(bf16[8,2048]{1,0:T(8,128)(2,1)S(1)} %get-tuple-element.45), channel_id=1, source_target_pairs={{0,5},{1,4},{2,7},{3,6},{4,1},{5,0},{6,3},{7,2},{8,13},{9,12},{10,... | collective-permute-start | bytes 98312 | tf_op jit(solution)/shard_map/ppermute | solution.py:341
  36.9 5.3 %collective-permute-start.18 = (bf16[16,2048]{1,0:T(8,128)(2,1)S(1)}, bf16[16,2048]{1,0:T(8,128)(2,1)S(1)}, u32[]{:S(2)}, u32[]{:S(2)}) collective-permute-start(bf16[16,2048]{1,0:T(8,128)(2,1)S(1)} %combine.1.refs_0_), channel_id=1, source_target_pairs={{0,24},{1,25},{2,26},{3,27},{4,28},{5,29},{6,30},{7,31},{8,16},{9,... | collective-permute-start | bytes 196616 | tf_op jit(solution)/shard_map/ppermute | solution.py:341
  38.8 4.7 %collective-permute-start.17 = (bf16[16,2048]{1,0:T(8,128)(2,1)S(1)}, bf16[16,2048]{1,0:T(8,128)(2,1)S(1)}, u32[]{:S(2)}, u32[]{:S(2)}) collective-permute-start(bf16[16,2048]{1,0:T(8,128)(2,1)S(1)} %combine.1.refs_0_), channel_id=1, source_target_pairs={{0,16},{1,17},{2,18},{3,19},{4,20},{5,21},{6,22},{7,23},{8,24},{9,... | collective-permute-start | bytes 196616 | tf_op jit(solution)/shard_map/ppermute | solution.py:341
  39.2 4.3 %collective-permute-start.16 = (bf16[16,2048]{1,0:T(8,128)(2,1)S(1)}, bf16[16,2048]{1,0:T(8,128)(2,1)S(1)}, u32[]{:S(2)}, u32[]{:S(2)}) collective-permute-start(bf16[16,2048]{1,0:T(8,128)(2,1)S(1)} %combine.1.refs_0_), channel_id=1, source_target_pairs={{0,8},{1,9},{2,10},{3,11},{4,12},{5,13},{6,14},{7,15},{8,0},{9,1},... | collective-permute-start | bytes 196616 | tf_op jit(solution)/shard_map/ppermute | solution.py:341

commit v6 on v5

--- a/solution.py
+++ b/solution.py
@@ -17,6 +17,7 @@
 LANES = 128
 SUBLANES = 8
 STAT_ROWS = 16
+MEAN_SCALE = 2.0**26
 
 
 NORM_EPSILON = 1e-06
@@ -29,6 +30,32 @@
 
 def to_column(row, count):
     return jnp.transpose(jnp.broadcast_to(row, (LANES, LANES)))[:count]
+
+
+def encode(values):
+    square = values * values
+    return jnp.where(values < 0.0, -square * square, square * square).astype(jnp.bfloat16)
+
+
+def decode(codes):
+    codes = codes.astype(jnp.float32)
+    root = lax.rsqrt(lax.rsqrt(jnp.abs(codes)))
+    return jnp.where(codes < 0.0, -root, root)
+
+
+def encode_mean(values):
+    return encode(values * jnp.abs(values) * MEAN_SCALE)
+
+
+def decode_mean(codes):
+    root = decode(codes)
+    size = jnp.abs(root)
+    return jnp.where(size > 0.0, root * lax.rsqrt(size) * MEAN_SCALE**-0.5, 0.0)
+
+
+def split_two(values):
+    high = values.astype(jnp.bfloat16)
+    return high, (values - high.astype(jnp.float32)).astype(jnp.bfloat16)
 
 
 def split_three(values):
@@ -129,16 +156,16 @@
                 jnp.max(part, 1, keepdims=True), jnp.max(last, 1, keepdims=True)
             )
             part, last = jnp.exp(part - top), jnp.exp(last - top)
-            terms[kv, p], last_terms[kv, p] = part.astype(jnp.bfloat16), last.astype(jnp.bfloat16)
+            terms[kv, p], last_terms[kv, p] = split_two(part), split_two(last)
             tops[kv, p] = top
             totals[kv, p] = jnp.sum(part, 1, keepdims=True) + jnp.sum(last, 1, keepdims=True)
     weighted = {}
     for kv, lanes in enumerate(kv_lanes):
         for p, span in enumerate(spans):
-            weighted[kv, p] = jnp.dot(
-                terms[kv, p], values[span, lanes], preferred_element_type=jnp.float32
-            ) + jnp.dot(
-                last_terms[kv, p], fresh_values[:, lanes], preferred_element_type=jnp.float32
+            weighted[kv, p] = sum(
+                jnp.dot(term, values[span, lanes], preferred_element_type=jnp.float32)
+                + jnp.dot(last, fresh_values[:, lanes], preferred_element_type=jnp.float32)
+                for term, last in zip(terms[kv, p], last_terms[kv, p])
             )
     span = block_heads * row_steps
     row = iota((SUBLANES, LANES), 0)
@@ -150,7 +177,7 @@
             ]
         )
         mean = interleave([weighted[kv, p] / totals[kv, p] for p in range(pieces)])
-        mean = mean.astype(jnp.bfloat16)
+        mean = encode_mean(mean)
         for part in range(high // LANES):
             level_row = jnp.transpose(level[part * LANES : (part + 1) * LANES])[:SUBLANES]
             high_part, middle_part, low_part = split_three(level_row)
@@ -180,15 +207,15 @@
     total = functools.reduce(jnp.add, factors)
     mixed = None
     for part, factor in zip(parts, factors):
-        term = part[:span, :].astype(jnp.float32) * to_column(factor / total, span)
+        term = decode_mean(part[:span, :]) * to_column(factor / total, span)
         mixed = term if mixed is None else mixed + term
     mixed = mixed.astype(jnp.bfloat16)
     attended = jnp.concatenate(
         [mixed[h * row_steps : (h + 1) * row_steps] for h in range(block_heads)], 1
     )
-    out_ref[...] = jnp.dot(
-        attended, w_ref[...], preferred_element_type=jnp.float32
-    ).astype(jnp.bfloat16)
+    out_ref[...] = encode(
+        jnp.dot(attended, w_ref[...], preferred_element_type=jnp.float32)
+    )
 
 
 def route_kernel(
@@ -230,19 +257,26 @@
 
 
 def tree_sum(parts):
-    values = [part[...].astype(jnp.float32) for part in parts]
+    values = list(parts)
     while len(values) > 1:
         values = [values[i] + values[i + 1] for i in range(0, len(values), 2)]
     return values[0]
 
 
-def dispatch_kernel(ctx_count, hops, residual_ref, selector_ref, *rest):
+def dispatch_kernel(ctx_count, hops, residual_ref, gain_ref, selector_ref, *rest):
     parts, state_ref, outs = rest[:ctx_count], rest[ctx_count], rest[ctx_count + 1 :]
-    state = residual_ref[...] + tree_sum(parts)
+    state = residual_ref[...] + tree_sum([decode(part[...]) for part in parts])
     state_ref[...] = state
+    gains = gain_ref[...].astype(jnp.float32)
+    gain = jnp.concatenate([gains[i : i + 1] for i in range(D // LANES)], 1)
+    normed = (
+        state
+        * lax.rsqrt(jnp.mean(state * state, -1, keepdims=True) + NORM_EPSILON)
+        * gain
+    ).astype(jnp.bfloat16)
     picked = lax.dot_general(
         selector_ref[...],
-        state.astype(jnp.bfloat16),
+        normed,
         (((0,), (0,)), ((), ())),
         preferred_element_type=jnp.float32,
     )
@@ -259,17 +293,10 @@
     send_ref[...] = jnp.concatenate([value[half:] for value in values], 0).astype(jnp.bfloat16)
 
 
-def expert_kernel(kept_ref, got_ref, gain_ref, gate_ref, up_ref, down_ref, keep_ref, send_ref):
+def expert_kernel(kept_ref, got_ref, gate_ref, up_ref, down_ref, keep_ref, send_ref):
     half = kept_ref.shape[0]
-    state = jnp.concatenate(
+    normed = jnp.concatenate(
         [kept_ref[...].astype(jnp.float32), got_ref[...].astype(jnp.float32)], 0
-    )
-    gains = gain_ref[...].astype(jnp.float32)
-    gain = jnp.concatenate([gains[i : i + 1] for i in range(D // LANES)], 1)
-    normed = (
-        state
-        * lax.rsqrt(jnp.mean(state * state, -1, keepdims=True) + NORM_EPSILON)
-        * gain
     ).astype(jnp.bfloat16)
     spare = max(0, LANES - 2 * half)
     if spare:
@@ -278,8 +305,8 @@
     up = jnp.dot(normed, up_ref[0], preferred_element_type=jnp.float32)
     activation = (gate / (1.0 + jnp.exp(-gate)) * up).astype(jnp.bfloat16)
     result = jnp.dot(activation, down_ref[0], preferred_element_type=jnp.float32)
-    keep_ref[...] = result[:half].astype(jnp.bfloat16)
-    send_ref[...] = result[half : 2 * half].astype(jnp.bfloat16)
+    keep_ref[...] = encode(result[:half])
+    send_ref[...] = encode(result[half : 2 * half])
 
 
 def scatter_kernel(kept_ref, got_ref, *outs):
@@ -292,19 +319,25 @@
 
 def combine_kernel(hops, high_ref, low_ref, *refs):
     blocks, out_ref = [refs[hops.index(j)] for j in range(len(hops))], refs[-1]
-    returned = jnp.concatenate([block[...].astype(jnp.float32) for block in blocks], 0).astype(
-        jnp.bfloat16
-    )
-    mixture = jnp.dot(high_ref[...], returned, preferred_element_type=jnp.float32) + jnp.dot(
-        low_ref[...], returned, preferred_element_type=jnp.float32
-    )
-    out_ref[...] = mixture.astype(jnp.bfloat16)
+    returned = decode(
+        jnp.concatenate([block[...].astype(jnp.float32) for block in blocks], 0)
+    )
+    returned_high, returned_low = split_two(returned)
+    weight_high, weight_low = high_ref[...], low_ref[...]
+    mixture = (
+        jnp.dot(weight_high, returned_high, preferred_element_type=jnp.float32)
+        + jnp.dot(weight_high, returned_low, preferred_element_type=jnp.float32)
+        + jnp.dot(weight_low, returned_high, preferred_element_type=jnp.float32)
+    )
+    out_ref[...] = encode(mixture)
 
 
 def finish_kernel(state_ref, *refs):
     parts, out_ref = refs[:-1], refs[-1]
     rows, steps, _ = out_ref.shape
-    layer = (state_ref[...] + tree_sum(parts)).astype(jnp.bfloat16)
+    layer = (
+        state_ref[...] + tree_sum([decode(part[...]) for part in parts])
+    ).astype(jnp.bfloat16)
     for r in range(rows):
         out_ref[r] = layer[r * steps : (r + 1) * steps]
 
@@ -414,9 +447,9 @@
     state, *outgoing = call(
         functools.partial(dispatch_kernel, n, hops),
         "dispatch",
-        [VMEM] * (n + 2),
+        [VMEM] * (n + 3),
         [(hidden, f32)] + [(block, bf16)] * chips,
-        (residual_rows, selector, *got),
+        (residual_rows, norm_gain.reshape(D // LANES, LANES), selector, *got),
         cost=cost(10),
     )
 
@@ -433,12 +466,11 @@
     kept, sent = call(
         expert_kernel,
         "experts",
-        [VMEM] * 6,
+        [VMEM] * 5,
         [(half, bf16)] * 2,
         (
             kept,
             move(sent, 0, 1),
-            norm_gain.reshape(D // LANES, LANES),
             gate_proj,
             up_proj,
             down_proj,

time: 44.3 us -> 44.8 us (1.011)
  Pallas kernels: 5.97 us -> 6.45 us
    pallas_call x9, Pallas kernels: 5.97 us -> 6.45 us  [call(): pl.pallas_call(kernel, name=name, in_specs=in_specs, out_specs=[out_spec...]
  transfers between devices with their start and end apart: 19 -> 19, of which waited for: 15 -> 14; matrix products, arithmetic and copies ran while one was open for 0% -> 0% of each run, Pallas kernels for 0% -> 0%
where the time goes in v6:
time: 44.8 us; the launch traced here: 44.7 us
  starting transfers between devices  20.4 us (46%)
  waiting for transfers between devices  17.7 us (40%)
  Pallas kernels  6.45 us (14%)
    ppermute x19, starting transfers between devices, move(): return lax.ppermute(block, ('ctx', 'exp'), pairs)  20.4 us
    ppermute x19, waiting for transfers between devices, move(): return lax.ppermute(block, ('ctx', 'exp'), pairs)  17.7 us
    pallas_call x9, Pallas kernels, call(): pl.pallas_call(kernel, name=name, in_specs=in_specs, out_specs=[out_spec...  6.45 us
  transfers between devices with their start and end apart: 19, of which 14 were waited for; matrix products, arithmetic and copies ran while one was open for 0% of the time, Pallas kernels for 0%

profile of v6, /device:TPU:0, one launch (start us, length us, event | category | flops | bytes accessed | tf_op | source)
XLA Modules:
  0.0 44.7 jit_solution(14092137126071001506)
XLA Ops:
  0.0 2.0 %attend.1 = (bf16[144,128]{1,0:T(8,128)(2,1)S(1)}, bf16[144,128]{1,0:T(8,128)(2,1)S(1)}, bf16[144,128]{1,0:T(8,128)(2,1)S(1)}, bf16[144,128]{1,0:T(8,128)(2,1)S(1)}) custom-call(s32[1]{0:T(128)} %bitcast.me_ref, s32[8]{0:T(128)} %len_hbm.1, bf16[8,2,4096]{2,1,0:T(2,128)(2,1)} %q_hbm.1, bf16[8,64,256]{2,1,0:T(8,128)(2,1)} %k_hbm.1, ...), custom_call_target="tpu_custom_call" | custom-call | flops 10000000000 | bytes 1048576 | tf_op jit(solution)/shard_map/attend/pallas_call | solution.py:351
  2.0 3.4 %collective-permute-start = (bf16[144,128]{1,0:T(8,128)(2,1)S(1)}, bf16[144,128]{1,0:T(8,128)(2,1)S(1)}, u32[]{:S(2)}, u32[]{:S(2)}) collective-permute-start(bf16[144,128]{1,0:T(8,128)(2,1)S(1)} %get-tuple-element.28), channel_id=1, source_target_pairs={{0,25},{1,24},{2,27},{3,26},{4,29},{5,28},{6,31},{7,30},{8,17},{9,... | collective-permute-start | bytes 110600 | tf_op jit(solution)/shard_map/ppermute | solution.py:374
  5.4 0.8 %collective-permute-start.1 = (bf16[144,128]{1,0:T(8,128)(2,1)S(1)}, bf16[144,128]{1,0:T(8,128)(2,1)S(1)}, u32[]{:S(2)}, u32[]{:S(2)}) collective-permute-start(bf16[144,128]{1,0:T(8,128)(2,1)S(1)} %get-tuple-element.29), channel_id=1, source_target_pairs={{0,17},{1,16},{2,19},{3,18},{4,21},{5,20},{6,23},{7,22},{8,25},{9,... | collective-permute-start | bytes 110600 | tf_op jit(solution)/shard_map/ppermute | solution.py:374
  6.4 0.9 %collective-permute-done.rest_0_ = bf16[144,128]{1,0:T(8,128)(2,1)S(1)} collective-permute-done((bf16[144,128]{1,0:T(8,128)(2,1)S(1)}, bf16[144,128]{1,0:T(8,128)(2,1)S(1)}, u32[]{:S(2)}, u32[]{:S(2)}) %collective-permute-start) | collective-permute-done | bytes 36896 | tf_op jit(solution)/shard_map/ppermute | solution.py:374
  7.3 1.5 %collective-permute-done.1.rest_1_ = bf16[144,128]{1,0:T(8,128)(2,1)S(1)} collective-permute-done((bf16[144,128]{1,0:T(8,128)(2,1)S(1)}, bf16[144,128]{1,0:T(8,128)(2,1)S(1)}, u32[]{:S(2)}, u32[]{:S(2)}) %collective-permute-start.1) | collective-permute-done | bytes 36896 | tf_op jit(solution)/shard_map/ppermute | solution.py:374
  8.8 1.1 %collective-permute-done.2.rest_2_ = bf16[144,128]{1,0:T(8,128)(2,1)S(1)} collective-permute-done((bf16[144,128]{1,0:T(8,128)(2,1)S(1)}, bf16[144,128]{1,0:T(8,128)(2,1)S(1)}, u32[]{:S(2)}, u32[]{:S(2)}) %collective-permute-start.2) | collective-permute-done | bytes 36896 | tf_op jit(solution)/shard_map/ppermute | solution.py:374
  9.9 0.8 %project.1 = bf16[16,2048]{1,0:T(8,128)(2,1)S(1)} custom-call(bf16[1024,2048]{1,0:T(8,128)(2,1)S(1)} %copy-done.3, bf16[144,128]{1,0:T(8,128)(2,1)S(1)} %collective-permute-done.rest_0_, bf16[144,128]{1,0:T(8,128)(2,1)S(1)} %collective-permute-done.1.rest_1_, bf16[144,128]{1,0:T(8,128)(2,1)S(1)} %collective-permute-done.2.rest_2_, ...), custom_call_target="tpu_custom_call" | custom-call | flops 10000000000 | bytes 1048576 | tf_op jit(solution)/shard_map/project/pallas_call | solution.py:351
  10.7 1.3 %collective-permute-start.7 = (bf16[16,2048]{1,0:T(8,128)(2,1)S(1)}, bf16[16,2048]{1,0:T(8,128)(2,1)S(1)}, u32[]{:S(2)}, u32[]{:S(2)}) collective-permute-start(bf16[16,2048]{1,0:T(8,128)(2,1)S(1)} %project.1), channel_id=1, source_target_pairs={{0,25},{1,24},{2,27},{3,26},{4,29},{5,28},{6,31},{7,30},{8,17},{9,... | collective-permute-start | bytes 196616 | tf_op jit(solution)/shard_map/ppermute | solution.py:374
  12.0 0.4 collective-permute-start.6
  12.4 1.3 %collective-permute-start.5 = (bf16[16,2048]{1,0:T(8,128)(2,1)S(1)}, bf16[16,2048]{1,0:T(8,128)(2,1)S(1)}, u32[]{:S(2)}, u32[]{:S(2)}) collective-permute-start(bf16[16,2048]{1,0:T(8,128)(2,1)S(1)} %project.1), channel_id=1, source_target_pairs={{0,9},{1,8},{2,11},{3,10},{4,13},{5,12},{6,15},{7,14},{8,1},{9,0},... | collective-permute-start | bytes 196616 | tf_op jit(solution)/shard_map/ppermute | solution.py:374
  14.3 1.5 %collective-permute-done.7.rest_3_ = bf16[16,2048]{1,0:T(8,128)(2,1)S(1)} collective-permute-done((bf16[16,2048]{1,0:T(8,128)(2,1)S(1)}, bf16[16,2048]{1,0:T(8,128)(2,1)S(1)}, u32[]{:S(2)}, u32[]{:S(2)}) %collective-permute-start.7) | collective-permute-done | bytes 65568 | tf_op jit(solution)/shard_map/ppermute | solution.py:374
  15.8 1.6 %collective-permute-done.6.rest_2_ = bf16[16,2048]{1,0:T(8,128)(2,1)S(1)} collective-permute-done((bf16[16,2048]{1,0:T(8,128)(2,1)S(1)}, bf16[16,2048]{1,0:T(8,128)(2,1)S(1)}, u32[]{:S(2)}, u32[]{:S(2)}) %collective-permute-start.6) | collective-permute-done | bytes 65568 | tf_op jit(solution)/shard_map/ppermute | solution.py:374
  17.5 0.4 dispatch.1
  17.9 3.4 %collective-permute-start.8 = (bf16[8,2048]{1,0:T(8,128)(2,1)S(1)}, bf16[8,2048]{1,0:T(8,128)(2,1)S(1)}, u32[]{:S(2)}, u32[]{:S(2)}) collective-permute-start(bf16[8,2048]{1,0:T(8,128)(2,1)S(1)} %get-tuple-element.35), channel_id=1, source_target_pairs={{0,7},{1,6},{2,5},{3,4},{4,3},{5,2},{6,1},{7,0},{8,15},{9,14},{10,... | collective-permute-start | bytes 98312 | tf_op jit(solution)/shard_map/ppermute | solution.py:374
  21.3 0.6 %collective-permute-start.10 = (bf16[8,2048]{1,0:T(8,128)(2,1)S(1)}, bf16[8,2048]{1,0:T(8,128)(2,1)S(1)}, u32[]{:S(2)}, u32[]{:S(2)}) collective-permute-start(bf16[8,2048]{1,0:T(8,128)(2,1)S(1)} %get-tuple-element.37), channel_id=1, source_target_pairs={{0,5},{1,4},{2,7},{3,6},{4,1},{5,0},{6,3},{7,2},{8,13},{9,12},{10,... | collective-permute-start | bytes 98312 | tf_op jit(solution)/shard_map/ppermute | solution.py:374
  21.9 1.2 %collective-permute-done.8.refs_0_ = bf16[8,2048]{1,0:T(8,128)(2,1)S(1)} collective-permute-done((bf16[8,2048]{1,0:T(8,128)(2,1)S(1)}, bf16[8,2048]{1,0:T(8,128)(2,1)S(1)}, u32[]{:S(2)}, u32[]{:S(2)}) %collective-permute-start.8) | collective-permute-done | bytes 32800 | tf_op jit(solution)/shard_map/ppermute | solution.py:374
  23.1 1.5 %collective-permute-done.9.refs_1_ = bf16[8,2048]{1,0:T(8,128)(2,1)S(1)} collective-permute-done((bf16[8,2048]{1,0:T(8,128)(2,1)S(1)}, bf16[8,2048]{1,0:T(8,128)(2,1)S(1)}, u32[]{:S(2)}, u32[]{:S(2)}) %collective-permute-start.9) | collective-permute-done | bytes 32800 | tf_op jit(solution)/shard_map/ppermute | solution.py:374
  24.6 1.0 %collective-permute-done.10.refs_2_ = bf16[8,2048]{1,0:T(8,128)(2,1)S(1)} collective-permute-done((bf16[8,2048]{1,0:T(8,128)(2,1)S(1)}, bf16[8,2048]{1,0:T(8,128)(2,1)S(1)}, u32[]{:S(2)}, u32[]{:S(2)}) %collective-permute-start.10) | collective-permute-done | bytes 32800 | tf_op jit(solution)/shard_map/ppermute | solution.py:374
  25.6 0.4 collective-permute-start.11
  26.1 0.9 %collective-permute-done.11.got_ref = bf16[16,2048]{1,0:T(8,128)(2,1)S(1)} collective-permute-done((bf16[16,2048]{1,0:T(8,128)(2,1)S(1)}, bf16[16,2048]{1,0:T(8,128)(2,1)S(1)}, u32[]{:S(2)}, u32[]{:S(2)}) %collective-permute-start.11) | collective-permute-done | bytes 65568 | tf_op jit(solution)/shard_map/ppermute | solution.py:374
  27.0 1.9 %experts.1 = (bf16[16,2048]{1,0:T(8,128)(2,1)S(1)}, bf16[16,2048]{1,0:T(8,128)(2,1)S(1)}) custom-call(bf16[16,2048]{1,0:T(8,128)(2,1)S(1)} %get-tuple-element.39.kept_ref, bf16[16,2048]{1,0:T(8,128)(2,1)S(1)} %collective-permute-done.11.got_ref, bf16[1,2048,1024]{2,1,0:T(8,128)(2,1)S(1)} %copy-done.4, bf16[1,2048,1024]{2,1,0:T(8,128)(2,1)S(1)} %copy-done.5, ...), custom_call_target="tpu_custom_call" | custom-call | flops 10000000000 | bytes 1048576 | tf_op jit(solution)/shard_map/experts/pallas_call | solution.py:351
  29.3 0.9 %collective-permute-done.12.got_ref = bf16[16,2048]{1,0:T(8,128)(2,1)S(1)} collective-permute-done((bf16[16,2048]{1,0:T(8,128)(2,1)S(1)}, bf16[16,2048]{1,0:T(8,128)(2,1)S(1)}, u32[]{:S(2)}, u32[]{:S(2)}) %collective-permute-start.12) | collective-permute-done | bytes 65568 | tf_op jit(solution)/shard_map/ppermute | solution.py:374
  30.2 1.9 %collective-permute-start.13 = (bf16[8,2048]{1,0:T(8,128)(2,1)S(1)}, bf16[8,2048]{1,0:T(8,128)(2,1)S(1)}, u32[]{:S(2)}, u32[]{:S(2)}) collective-permute-start(bf16[8,2048]{1,0:T(8,128)(2,1)S(1)} %get-tuple-element.43), channel_id=1, source_target_pairs={{0,7},{1,6},{2,5},{3,4},{4,3},{5,2},{6,1},{7,0},{8,15},{9,14},{10,... | collective-permute-start | bytes 98312 | tf_op jit(solution)/shard_map/ppermute | solution.py:374
  32.2 2.1 %collective-permute-start.15 = (bf16[8,2048]{1,0:T(8,128)(2,1)S(1)}, bf16[8,2048]{1,0:T(8,128)(2,1)S(1)}, u32[]{:S(2)}, u32[]{:S(2)}) collective-permute-start(bf16[8,2048]{1,0:T(8,128)(2,1)S(1)} %get-tuple-element.45), channel_id=1, source_target_pairs={{0,5},{1,4},{2,7},{3,6},{4,1},{5,0},{6,3},{7,2},{8,13},{9,12},{10,... | collective-permute-start | bytes 98312 | tf_op jit(solution)/shard_map/ppermute | solution.py:374
  34.3 1.3 %collective-permute-done.13.refs_0_ = bf16[8,2048]{1,0:T(8,128)(2,1)S(1)} collective-permute-done((bf16[8,2048]{1,0:T(8,128)(2,1)S(1)}, bf16[8,2048]{1,0:T(8,128)(2,1)S(1)}, u32[]{:S(2)}, u32[]{:S(2)}) %collective-permute-start.13) | collective-permute-done | bytes 32800 | tf_op jit(solution)/shard_map/ppermute | solution.py:374
  35.6 1.5 %collective-permute-done.14.refs_1_ = bf16[8,2048]{1,0:T(8,128)(2,1)S(1)} collective-permute-done((bf16[8,2048]{1,0:T(8,128)(2,1)S(1)}, bf16[8,2048]{1,0:T(8,128)(2,1)S(1)}, u32[]{:S(2)}, u32[]{:S(2)}) %collective-permute-start.14) | collective-permute-done | bytes 32800 | tf_op jit(solution)/shard_map/ppermute | solution.py:374
  37.4 1.8 %collective-permute-start.18 = (bf16[16,2048]{1,0:T(8,128)(2,1)S(1)}, bf16[16,2048]{1,0:T(8,128)(2,1)S(1)}, u32[]{:S(2)}, u32[]{:S(2)}) collective-permute-start(bf16[16,2048]{1,0:T(8,128)(2,1)S(1)} %combine.1.refs_0_), channel_id=1, source_target_pairs={{0,24},{1,25},{2,26},{3,27},{4,28},{5,29},{6,30},{7,31},{8,16},{9,... | collective-permute-start | bytes 196616 | tf_op jit(solution)/shard_map/ppermute | solution.py:374
  39.2 0.4 collective-permute-start.17
  39.6 1.3 %collective-permute-start.16 = (bf16[16,2048]{1,0:T(8,128)(2,1)S(1)}, bf16[16,2048]{1,0:T(8,128)(2,1)S(1)}, u32[]{:S(2)}, u32[]{:S(2)}) collective-permute-start(bf16[16,2048]{1,0:T(8,128)(2,1)S(1)} %combine.1.refs_0_), channel_id=1, source_target_pairs={{0,8},{1,9},{2,10},{3,11},{4,12},{5,13},{6,14},{7,15},{8,0},{9,1},... | collective-permute-start | bytes 196616 | tf_op jit(solution)/shard_map/ppermute | solution.py:374
  40.9 1.7 %collective-permute-done.18.refs_3_ = bf16[16,2048]{1,0:T(8,128)(2,1)S(1)} collective-permute-done((bf16[16,2048]{1,0:T(8,128)(2,1)S(1)}, bf16[16,2048]{1,0:T(8,128)(2,1)S(1)}, u32[]{:S(2)}, u32[]{:S(2)}) %collective-permute-start.18) | collective-permute-done | bytes 65568 | tf_op jit(solution)/shard_map/ppermute | solution.py:374
  42.6 1.2 %collective-permute-done.17.refs_2_ = bf16[16,2048]{1,0:T(8,128)(2,1)S(1)} collective-permute-done((bf16[16,2048]{1,0:T(8,128)(2,1)S(1)}, bf16[16,2048]{1,0:T(8,128)(2,1)S(1)}, u32[]{:S(2)}, u32[]{:S(2)}) %collective-permute-start.17) | collective-permute-done | bytes 65568 | tf_op jit(solution)/shard_map/ppermute | solution.py:374
  43.9 0.8 %finish.1 = bf16[8,2,2048]{2,1,0:T(2,128)(2,1)} custom-call(f32[16,2048]{1,0:T(8,128)S(1)} %get-tuple-element.32.state_ref, bf16[16,2048]{1,0:T(8,128)(2,1)S(1)} %combine.1.refs_0_, bf16[16,2048]{1,0:T(8,128)(2,1)S(1)} %collective-permute-done.16.refs_1_, bf16[16,2048]{1,0:T(8,128)(2,1)S(1)} %collective-permute-done.17.refs_2_, ...), custom_call_target="tpu_custom_call" | custom-call | tf_op jit(solution)/shard_map/finish/pallas_call | solution.py:351
  (31 shorter events, 1.8 us)
Async XLA Ops:
  0.0 9.9 %copy-start.3 = (bf16[1024,2048]{1,0:T(8,128)(2,1)S(1)}, bf16[1024,2048]{1,0:T(8,128)(2,1)}, u32[]{:S(2)}) copy-start(bf16[1024,2048]{1,0:T(8,128)(2,1)} %w_ref.1) | copy-start | bytes 12582916
  2.0 5.3 %collective-permute-start = (bf16[144,128]{1,0:T(8,128)(2,1)S(1)}, bf16[144,128]{1,0:T(8,128)(2,1)S(1)}, u32[]{:S(2)}, u32[]{:S(2)}) collective-permute-start(bf16[144,128]{1,0:T(8,128)(2,1)S(1)} %get-tuple-element.28), channel_id=1, source_target_pairs={{0,25},{1,24},{2,27},{3,26},{4,29},{5,28},{6,31},{7,30},{8,17},{9,... | collective-permute-start | bytes 110600 | tf_op jit(solution)/shard_map/ppermute | solution.py:374
  5.4 3.4 %collective-permute-start.1 = (bf16[144,128]{1,0:T(8,128)(2,1)S(1)}, bf16[144,128]{1,0:T(8,128)(2,1)S(1)}, u32[]{:S(2)}, u32[]{:S(2)}) collective-permute-start(bf16[144,128]{1,0:T(8,128)(2,1)S(1)} %get-tuple-element.29), channel_id=1, source_target_pairs={{0,17},{1,16},{2,19},{3,18},{4,21},{5,20},{6,23},{7,22},{8,25},{9,... | collective-permute-start | bytes 110600 | tf_op jit(solution)/shard_map/ppermute | solution.py:374
  6.2 3.7 %collective-permute-start.2 = (bf16[144,128]{1,0:T(8,128)(2,1)S(1)}, bf16[144,128]{1,0:T(8,128)(2,1)S(1)}, u32[]{:S(2)}, u32[]{:S(2)}) collective-permute-start(bf16[144,128]{1,0:T(8,128)(2,1)S(1)} %get-tuple-element.30), channel_id=1, source_target_pairs={{0,9},{1,8},{2,11},{3,10},{4,13},{5,12},{6,15},{7,14},{8,1},{9,0},... | collective-permute-start | bytes 110600 | tf_op jit(solution)/shard_map/ppermute | solution.py:374
  6.3 7.8 %copy-start = (bf16[8,2,2048]{2,1,0:T(2,128)(2,1)S(1)}, bf16[8,2,2048]{2,1,0:T(2,128)(2,1)}, u32[]{:S(2)}) copy-start(bf16[8,2,2048]{2,1,0:T(2,128)(2,1)} %residual_ref.1) | copy-start | bytes 196612
  6.3 7.8 %copy-start.1 = (s32[8,2,8]{2,1,0:T(2,128)S(1)}, s32[8,2,8]{2,1,0:T(2,128)}, u32[]{:S(2)}) copy-start(s32[8,2,8]{2,1,0:T(2,128)} %param.23) | copy-start | bytes 1540
  6.3 7.8 %copy-start.2 = (f32[8,2,8]{2,1,0:T(2,128)S(1)}, f32[8,2,8]{2,1,0:T(2,128)}, u32[]{:S(2)}) copy-start(f32[8,2,8]{2,1,0:T(2,128)} %param.24) | copy-start | bytes 1540
  6.3 11.1 %copy-start.7 = (bf16[2048]{0:T(1024)(128)(2,1)S(1)}, bf16[2048]{0:T(1024)(128)(2,1)}, u32[]{:S(2)}) copy-start(bf16[2048]{0:T(1024)(128)(2,1)} %param.22) | copy-start | bytes 12292
  6.3 3.6 %collective-permute-start.3 = (bf16[144,128]{1,0:T(8,128)(2,1)S(1)}, bf16[144,128]{1,0:T(8,128)(2,1)S(1)}, u32[]{:S(2)}, u32[]{:S(2)}) collective-permute-start(bf16[144,128]{1,0:T(8,128)(2,1)S(1)} %get-tuple-element.31), channel_id=1, source_target_pairs={{0,1},{1,0},{2,3},{3,2},{4,5},{5,4},{6,7},{7,6},{8,9},{9,8},{10,11... | collective-permute-start | bytes 110600 | tf_op jit(solution)/shard_map/ppermute | solution.py:374
  10.7 5.1 %collective-permute-start.7 = (bf16[16,2048]{1,0:T(8,128)(2,1)S(1)}, bf16[16,2048]{1,0:T(8,128)(2,1)S(1)}, u32[]{:S(2)}, u32[]{:S(2)}) collective-permute-start(bf16[16,2048]{1,0:T(8,128)(2,1)S(1)} %project.1), channel_id=1, source_target_pairs={{0,25},{1,24},{2,27},{3,26},{4,29},{5,28},{6,31},{7,30},{8,17},{9,... | collective-permute-start | bytes 196616 | tf_op jit(solution)/shard_map/ppermute | solution.py:374
  12.0 5.4 %collective-permute-start.6 = (bf16[16,2048]{1,0:T(8,128)(2,1)S(1)}, bf16[16,2048]{1,0:T(8,128)(2,1)S(1)}, u32[]{:S(2)}, u32[]{:S(2)}) collective-permute-start(bf16[16,2048]{1,0:T(8,128)(2,1)S(1)} %project.1), channel_id=1, source_target_pairs={{0,17},{1,16},{2,19},{3,18},{4,21},{5,20},{6,23},{7,22},{8,25},{9,... | collective-permute-start | bytes 196616 | tf_op jit(solution)/shard_map/ppermute | solution.py:374
  12.4 5.0 %collective-permute-start.5 = (bf16[16,2048]{1,0:T(8,128)(2,1)S(1)}, bf16[16,2048]{1,0:T(8,128)(2,1)S(1)}, u32[]{:S(2)}, u32[]{:S(2)}) collective-permute-start(bf16[16,2048]{1,0:T(8,128)(2,1)S(1)} %project.1), channel_id=1, source_target_pairs={{0,9},{1,8},{2,11},{3,10},{4,13},{5,12},{6,15},{7,14},{8,1},{9,0},... | collective-permute-start | bytes 196616 | tf_op jit(solution)/shard_map/ppermute | solution.py:374
  13.7 3.7 %collective-permute-start.4 = (bf16[16,2048]{1,0:T(8,128)(2,1)S(1)}, bf16[16,2048]{1,0:T(8,128)(2,1)S(1)}, u32[]{:S(2)}, u32[]{:S(2)}) collective-permute-start(bf16[16,2048]{1,0:T(8,128)(2,1)S(1)} %project.1), channel_id=1, source_target_pairs={{0,1},{1,0},{2,3},{3,2},{4,5},{5,4},{6,7},{7,6},{8,9},{9,8},{10,11... | collective-permute-start | bytes 196616 | tf_op jit(solution)/shard_map/ppermute | solution.py:374
  17.4 9.6 %copy-start.4 = (bf16[1,2048,1024]{2,1,0:T(8,128)(2,1)S(1)}, bf16[1,2048,1024]{2,1,0:T(8,128)(2,1)}, u32[]{:S(2)}) copy-start(bf16[1,2048,1024]{2,1,0:T(8,128)(2,1)} %gate_ref.1) | copy-start | bytes 12582916
  17.4 9.5 %copy-start.5 = (bf16[1,2048,1024]{2,1,0:T(8,128)(2,1)S(1)}, bf16[1,2048,1024]{2,1,0:T(8,128)(2,1)}, u32[]{:S(2)}) copy-start(bf16[1,2048,1024]{2,1,0:T(8,128)(2,1)} %up_ref.1) | copy-start | bytes 12582916
  17.4 9.5 %copy-start.6 = (bf16[1,1024,2048]{2,1,0:T(8,128)(2,1)S(1)}, bf16[1,1024,2048]{2,1,0:T(8,128)(2,1)}, u32[]{:S(2)}) copy-start(bf16[1,1024,2048]{2,1,0:T(8,128)(2,1)} %down_ref.1) | copy-start | bytes 12582916
  17.9 5.2 %collective-permute-start.8 = (bf16[8,2048]{1,0:T(8,128)(2,1)S(1)}, bf16[8,2048]{1,0:T(8,128)(2,1)S(1)}, u32[]{:S(2)}, u32[]{:S(2)}) collective-permute-start(bf16[8,2048]{1,0:T(8,128)(2,1)S(1)} %get-tuple-element.35), channel_id=1, source_target_pairs={{0,7},{1,6},{2,5},{3,4},{4,3},{5,2},{6,1},{7,0},{8,15},{9,14},{10,... | collective-permute-start | bytes 98312 | tf_op jit(solution)/shard_map/ppermute | solution.py:374
  21.3 3.3 %collective-permute-start.9 = (bf16[8,2048]{1,0:T(8,128)(2,1)S(1)}, bf16[8,2048]{1,0:T(8,128)(2,1)S(1)}, u32[]{:S(2)}, u32[]{:S(2)}) collective-permute-start(bf16[8,2048]{1,0:T(8,128)(2,1)S(1)} %get-tuple-element.36), channel_id=1, source_target_pairs={{0,3},{1,2},{2,1},{3,0},{4,7},{5,6},{6,5},{7,4},{8,11},{9,10},{10,... | collective-permute-start | bytes 98312 | tf_op jit(solution)/shard_map/ppermute | solution.py:374
  21.3 4.3 %collective-permute-start.10 = (bf16[8,2048]{1,0:T(8,128)(2,1)S(1)}, bf16[8,2048]{1,0:T(8,128)(2,1)S(1)}, u32[]{:S(2)}, u32[]{:S(2)}) collective-permute-start(bf16[8,2048]{1,0:T(8,128)(2,1)S(1)} %get-tuple-element.37), channel_id=1, source_target_pairs={{0,5},{1,4},{2,7},{3,6},{4,1},{5,0},{6,3},{7,2},{8,13},{9,12},{10,... | collective-permute-start | bytes 98312 | tf_op jit(solution)/shard_map/ppermute | solution.py:374
  25.6 1.3 %collective-permute-start.11 = (bf16[16,2048]{1,0:T(8,128)(2,1)S(1)}, bf16[16,2048]{1,0:T(8,128)(2,1)S(1)}, u32[]{:S(2)}, u32[]{:S(2)}) collective-permute-start(bf16[16,2048]{1,0:T(8,128)(2,1)S(1)} %get-tuple-element.40), channel_id=1, source_target_pairs={{0,1},{1,0},{2,3},{3,2},{4,5},{5,4},{6,7},{7,6},{8,9},{9,8},{10,11... | collective-permute-start | bytes 196616 | tf_op jit(solution)/shard_map/ppermute | solution.py:374
  28.9 1.3 %collective-permute-start.12 = (bf16[16,2048]{1,0:T(8,128)(2,1)S(1)}, bf16[16,2048]{1,0:T(8,128)(2,1)S(1)}, u32[]{:S(2)}, u32[]{:S(2)}) collective-permute-start(bf16[16,2048]{1,0:T(8,128)(2,1)S(1)} %get-tuple-element.42), channel_id=1, source_target_pairs={{0,1},{1,0},{2,3},{3,2},{4,5},{5,4},{6,7},{7,6},{8,9},{9,8},{10,11... | collective-permute-start | bytes 196616 | tf_op jit(solution)/shard_map/ppermute | solution.py:374
  30.2 5.4 %collective-permute-start.13 = (bf16[8,2048]{1,0:T(8,128)(2,1)S(1)}, bf16[8,2048]{1,0:T(8,128)(2,1)S(1)}, u32[]{:S(2)}, u32[]{:S(2)}) collective-permute-start(bf16[8,2048]{1,0:T(8,128)(2,1)S(1)} %get-tuple-element.43), channel_id=1, source_target_pairs={{0,7},{1,6},{2,5},{3,4},{4,3},{5,2},{6,1},{7,0},{8,15},{9,14},{10,... | collective-permute-start | bytes 98312 | tf_op jit(solution)/shard_map/ppermute | solution.py:374
  32.1 4.9 %collective-permute-start.14 = (bf16[8,2048]{1,0:T(8,128)(2,1)S(1)}, bf16[8,2048]{1,0:T(8,128)(2,1)S(1)}, u32[]{:S(2)}, u32[]{:S(2)}) collective-permute-start(bf16[8,2048]{1,0:T(8,128)(2,1)S(1)} %get-tuple-element.44), channel_id=1, source_target_pairs={{0,3},{1,2},{2,1},{3,0},{4,7},{5,6},{6,5},{7,4},{8,11},{9,10},{10,... | collective-permute-start | bytes 98312 | tf_op jit(solution)/shard_map/ppermute | solution.py:374
  32.2 4.9 %collective-permute-start.15 = (bf16[8,2048]{1,0:T(8,128)(2,1)S(1)}, bf16[8,2048]{1,0:T(8,128)(2,1)S(1)}, u32[]{:S(2)}, u32[]{:S(2)}) collective-permute-start(bf16[8,2048]{1,0:T(8,128)(2,1)S(1)} %get-tuple-element.45), channel_id=1, source_target_pairs={{0,5},{1,4},{2,7},{3,6},{4,1},{5,0},{6,3},{7,2},{8,13},{9,12},{10,... | collective-permute-start | bytes 98312 | tf_op jit(solution)/shard_map/ppermute | solution.py:374
  37.4 5.3 %collective-permute-start.18 = (bf16[16,2048]{1,0:T(8,128)(2,1)S(1)}, bf16[16,2048]{1,0:T(8,128)(2,1)S(1)}, u32[]{:S(2)}, u32[]{:S(2)}) collective-permute-start(bf16[16,2048]{1,0:T(8,128)(2,1)S(1)} %combine.1.refs_0_), channel_id=1, source_target_pairs={{0,24},{1,25},{2,26},{3,27},{4,28},{5,29},{6,30},{7,31},{8,16},{9,... | collective-permute-start | bytes 196616 | tf_op jit(solution)/shard_map/ppermute | solution.py:374
  39.2 4.7 %collective-permute-start.17 = (bf16[16,2048]{1,0:T(8,128)(2,1)S(1)}, bf16[16,2048]{1,0:T(8,128)(2,1)S(1)}, u32[]{:S(2)}, u32[]{:S(2)}) collective-permute-start(bf16[16,2048]{1,0:T(8,128)(2,1)S(1)} %combine.1.refs_0_), channel_id=1, source_target_pairs={{0,16},{1,17},{2,18},{3,19},{4,20},{5,21},{6,22},{7,23},{8,24},{9,... | collective-permute-start | bytes 196616 | tf_op jit(solution)/shard_map/ppermute | solution.py:374
  39.6 4.3 %collective-permute-start.16 = (bf16[16,2048]{1,0:T(8,128)(2,1)S(1)}, bf16[16,2048]{1,0:T(8,128)(2,1)S(1)}, u32[]{:S(2)}, u32[]{:S(2)}) collective-permute-start(bf16[16,2048]{1,0:T(8,128)(2,1)S(1)} %combine.1.refs_0_), channel_id=1, source_target_pairs={{0,8},{1,9},{2,10},{3,11},{4,12},{5,13},{6,14},{7,15},{8,0},{9,1},... | collective-permute-start | bytes 196616 | tf_op jit(solution)/shard_map/ppermute | solution.py:374

commit v7 on v6

--- a/solution.py
+++ b/solution.py
@@ -18,6 +18,7 @@
 SUBLANES = 8
 STAT_ROWS = 16
 MEAN_SCALE = 2.0**26
+TERM_SCALE = 2.0**20
 
 
 NORM_EPSILON = 1e-06
@@ -209,7 +210,7 @@
     for part, factor in zip(parts, factors):
         term = decode_mean(part[:span, :]) * to_column(factor / total, span)
         mixed = term if mixed is None else mixed + term
-    mixed = mixed.astype(jnp.bfloat16)
+    mixed = (mixed * TERM_SCALE).astype(jnp.bfloat16)
     attended = jnp.concatenate(
         [mixed[h * row_steps : (h + 1) * row_steps] for h in range(block_heads)], 1
     )
@@ -265,7 +266,8 @@
 
 def dispatch_kernel(ctx_count, hops, residual_ref, gain_ref, selector_ref, *rest):
     parts, state_ref, outs = rest[:ctx_count], rest[ctx_count], rest[ctx_count + 1 :]
-    state = residual_ref[...] + tree_sum([decode(part[...]) for part in parts])
+    terms = tree_sum([decode(part[...]) for part in parts])
+    state = residual_ref[...] + terms * (1.0 / TERM_SCALE)
     state_ref[...] = state
     gains = gain_ref[...].astype(jnp.float32)
     gain = jnp.concatenate([gains[i : i + 1] for i in range(D // LANES)], 1)

time: 44.8 us -> 44.8 us (level)
  no operation moved by 1% of the time
where the time goes in v7:
time: 44.8 us; the launch traced here: 44.7 us
  starting transfers between devices  20.4 us (46%)
  waiting for transfers between devices  17.7 us (40%)
  Pallas kernels  6.44 us (14%)
    ppermute x19, starting transfers between devices, move(): return lax.ppermute(block, ('ctx', 'exp'), pairs)  20.4 us
    ppermute x19, waiting for transfers between devices, move(): return lax.ppermute(block, ('ctx', 'exp'), pairs)  17.7 us
    pallas_call x9, Pallas kernels, call(): pl.pallas_call(kernel, name=name, in_specs=in_specs, out_specs=[out_spec...  6.44 us
  transfers between devices with their start and end apart: 19, of which 14 were waited for; matrix products, arithmetic and copies ran while one was open for 0% of the time, Pallas kernels for 0%

profile of v7, /device:TPU:0, one launch (start us, length us, event | category | flops | bytes accessed | tf_op | source)
XLA Modules:
  0.0 44.7 jit_solution(13994113663294763768)
XLA Ops:
  0.0 2.0 %attend.1 = (bf16[144,128]{1,0:T(8,128)(2,1)S(1)}, bf16[144,128]{1,0:T(8,128)(2,1)S(1)}, bf16[144,128]{1,0:T(8,128)(2,1)S(1)}, bf16[144,128]{1,0:T(8,128)(2,1)S(1)}) custom-call(s32[1]{0:T(128)} %bitcast.me_ref, s32[8]{0:T(128)} %len_hbm.1, bf16[8,2,4096]{2,1,0:T(2,128)(2,1)} %q_hbm.1, bf16[8,64,256]{2,1,0:T(8,128)(2,1)} %k_hbm.1, ...), custom_call_target="tpu_custom_call" | custom-call | flops 10000000000 | bytes 1048576 | tf_op jit(solution)/shard_map/attend/pallas_call | solution.py:353
  2.0 3.4 %collective-permute-start = (bf16[144,128]{1,0:T(8,128)(2,1)S(1)}, bf16[144,128]{1,0:T(8,128)(2,1)S(1)}, u32[]{:S(2)}, u32[]{:S(2)}) collective-permute-start(bf16[144,128]{1,0:T(8,128)(2,1)S(1)} %get-tuple-element.28), channel_id=1, source_target_pairs={{0,25},{1,24},{2,27},{3,26},{4,29},{5,28},{6,31},{7,30},{8,17},{9,... | collective-permute-start | bytes 110600 | tf_op jit(solution)/shard_map/ppermute | solution.py:376
  5.4 0.8 %collective-permute-start.1 = (bf16[144,128]{1,0:T(8,128)(2,1)S(1)}, bf16[144,128]{1,0:T(8,128)(2,1)S(1)}, u32[]{:S(2)}, u32[]{:S(2)}) collective-permute-start(bf16[144,128]{1,0:T(8,128)(2,1)S(1)} %get-tuple-element.29), channel_id=1, source_target_pairs={{0,17},{1,16},{2,19},{3,18},{4,21},{5,20},{6,23},{7,22},{8,25},{9,... | collective-permute-start | bytes 110600 | tf_op jit(solution)/shard_map/ppermute | solution.py:376
  6.4 0.9 %collective-permute-done.rest_0_ = bf16[144,128]{1,0:T(8,128)(2,1)S(1)} collective-permute-done((bf16[144,128]{1,0:T(8,128)(2,1)S(1)}, bf16[144,128]{1,0:T(8,128)(2,1)S(1)}, u32[]{:S(2)}, u32[]{:S(2)}) %collective-permute-start) | collective-permute-done | bytes 36896 | tf_op jit(solution)/shard_map/ppermute | solution.py:376
  7.3 1.5 %collective-permute-done.1.rest_1_ = bf16[144,128]{1,0:T(8,128)(2,1)S(1)} collective-permute-done((bf16[144,128]{1,0:T(8,128)(2,1)S(1)}, bf16[144,128]{1,0:T(8,128)(2,1)S(1)}, u32[]{:S(2)}, u32[]{:S(2)}) %collective-permute-start.1) | collective-permute-done | bytes 36896 | tf_op jit(solution)/shard_map/ppermute | solution.py:376
  8.8 1.1 %collective-permute-done.2.rest_2_ = bf16[144,128]{1,0:T(8,128)(2,1)S(1)} collective-permute-done((bf16[144,128]{1,0:T(8,128)(2,1)S(1)}, bf16[144,128]{1,0:T(8,128)(2,1)S(1)}, u32[]{:S(2)}, u32[]{:S(2)}) %collective-permute-start.2) | collective-permute-done | bytes 36896 | tf_op jit(solution)/shard_map/ppermute | solution.py:376
  9.9 0.8 %project.1 = bf16[16,2048]{1,0:T(8,128)(2,1)S(1)} custom-call(bf16[1024,2048]{1,0:T(8,128)(2,1)S(1)} %copy-done.3, bf16[144,128]{1,0:T(8,128)(2,1)S(1)} %collective-permute-done.rest_0_, bf16[144,128]{1,0:T(8,128)(2,1)S(1)} %collective-permute-done.1.rest_1_, bf16[144,128]{1,0:T(8,128)(2,1)S(1)} %collective-permute-done.2.rest_2_, ...), custom_call_target="tpu_custom_call" | custom-call | flops 10000000000 | bytes 1048576 | tf_op jit(solution)/shard_map/project/pallas_call | solution.py:353
  10.7 1.3 %collective-permute-start.7 = (bf16[16,2048]{1,0:T(8,128)(2,1)S(1)}, bf16[16,2048]{1,0:T(8,128)(2,1)S(1)}, u32[]{:S(2)}, u32[]{:S(2)}) collective-permute-start(bf16[16,2048]{1,0:T(8,128)(2,1)S(1)} %project.1), channel_id=1, source_target_pairs={{0,25},{1,24},{2,27},{3,26},{4,29},{5,28},{6,31},{7,30},{8,17},{9,... | collective-permute-start | bytes 196616 | tf_op jit(solution)/shard_map/ppermute | solution.py:376
  12.0 0.4 collective-permute-start.6
  12.4 1.3 %collective-permute-start.5 = (bf16[16,2048]{1,0:T(8,128)(2,1)S(1)}, bf16[16,2048]{1,0:T(8,128)(2,1)S(1)}, u32[]{:S(2)}, u32[]{:S(2)}) collective-permute-start(bf16[16,2048]{1,0:T(8,128)(2,1)S(1)} %project.1), channel_id=1, source_target_pairs={{0,9},{1,8},{2,11},{3,10},{4,13},{5,12},{6,15},{7,14},{8,1},{9,0},... | collective-permute-start | bytes 196616 | tf_op jit(solution)/shard_map/ppermute | solution.py:376
  14.3 1.5 %collective-permute-done.7.rest_3_ = bf16[16,2048]{1,0:T(8,128)(2,1)S(1)} collective-permute-done((bf16[16,2048]{1,0:T(8,128)(2,1)S(1)}, bf16[16,2048]{1,0:T(8,128)(2,1)S(1)}, u32[]{:S(2)}, u32[]{:S(2)}) %collective-permute-start.7) | collective-permute-done | bytes 65568 | tf_op jit(solution)/shard_map/ppermute | solution.py:376
  15.8 1.6 %collective-permute-done.6.rest_2_ = bf16[16,2048]{1,0:T(8,128)(2,1)S(1)} collective-permute-done((bf16[16,2048]{1,0:T(8,128)(2,1)S(1)}, bf16[16,2048]{1,0:T(8,128)(2,1)S(1)}, u32[]{:S(2)}, u32[]{:S(2)}) %collective-permute-start.6) | collective-permute-done | bytes 65568 | tf_op jit(solution)/shard_map/ppermute | solution.py:376
  17.4 0.4 dispatch.1
  17.9 3.4 %collective-permute-start.8 = (bf16[8,2048]{1,0:T(8,128)(2,1)S(1)}, bf16[8,2048]{1,0:T(8,128)(2,1)S(1)}, u32[]{:S(2)}, u32[]{:S(2)}) collective-permute-start(bf16[8,2048]{1,0:T(8,128)(2,1)S(1)} %get-tuple-element.35), channel_id=1, source_target_pairs={{0,7},{1,6},{2,5},{3,4},{4,3},{5,2},{6,1},{7,0},{8,15},{9,14},{10,... | collective-permute-start | bytes 98312 | tf_op jit(solution)/shard_map/ppermute | solution.py:376
  21.3 0.6 %collective-permute-start.10 = (bf16[8,2048]{1,0:T(8,128)(2,1)S(1)}, bf16[8,2048]{1,0:T(8,128)(2,1)S(1)}, u32[]{:S(2)}, u32[]{:S(2)}) collective-permute-start(bf16[8,2048]{1,0:T(8,128)(2,1)S(1)} %get-tuple-element.37), channel_id=1, source_target_pairs={{0,5},{1,4},{2,7},{3,6},{4,1},{5,0},{6,3},{7,2},{8,13},{9,12},{10,... | collective-permute-start | bytes 98312 | tf_op jit(solution)/shard_map/ppermute | solution.py:376
  21.9 1.2 %collective-permute-done.8.refs_0_ = bf16[8,2048]{1,0:T(8,128)(2,1)S(1)} collective-permute-done((bf16[8,2048]{1,0:T(8,128)(2,1)S(1)}, bf16[8,2048]{1,0:T(8,128)(2,1)S(1)}, u32[]{:S(2)}, u32[]{:S(2)}) %collective-permute-start.8) | collective-permute-done | bytes 32800 | tf_op jit(solution)/shard_map/ppermute | solution.py:376
  23.1 1.5 %collective-permute-done.9.refs_1_ = bf16[8,2048]{1,0:T(8,128)(2,1)S(1)} collective-permute-done((bf16[8,2048]{1,0:T(8,128)(2,1)S(1)}, bf16[8,2048]{1,0:T(8,128)(2,1)S(1)}, u32[]{:S(2)}, u32[]{:S(2)}) %collective-permute-start.9) | collective-permute-done | bytes 32800 | tf_op jit(solution)/shard_map/ppermute | solution.py:376
  24.6 1.0 %collective-permute-done.10.refs_2_ = bf16[8,2048]{1,0:T(8,128)(2,1)S(1)} collective-permute-done((bf16[8,2048]{1,0:T(8,128)(2,1)S(1)}, bf16[8,2048]{1,0:T(8,128)(2,1)S(1)}, u32[]{:S(2)}, u32[]{:S(2)}) %collective-permute-start.10) | collective-permute-done | bytes 32800 | tf_op jit(solution)/shard_map/ppermute | solution.py:376
  25.6 0.4 collective-permute-start.11
  26.1 0.9 %collective-permute-done.11.got_ref = bf16[16,2048]{1,0:T(8,128)(2,1)S(1)} collective-permute-done((bf16[16,2048]{1,0:T(8,128)(2,1)S(1)}, bf16[16,2048]{1,0:T(8,128)(2,1)S(1)}, u32[]{:S(2)}, u32[]{:S(2)}) %collective-permute-start.11) | collective-permute-done | bytes 65568 | tf_op jit(solution)/shard_map/ppermute | solution.py:376
  27.0 1.9 %experts.1 = (bf16[16,2048]{1,0:T(8,128)(2,1)S(1)}, bf16[16,2048]{1,0:T(8,128)(2,1)S(1)}) custom-call(bf16[16,2048]{1,0:T(8,128)(2,1)S(1)} %get-tuple-element.39.kept_ref, bf16[16,2048]{1,0:T(8,128)(2,1)S(1)} %collective-permute-done.11.got_ref, bf16[1,2048,1024]{2,1,0:T(8,128)(2,1)S(1)} %copy-done.4, bf16[1,2048,1024]{2,1,0:T(8,128)(2,1)S(1)} %copy-done.5, ...), custom_call_target="tpu_custom_call" | custom-call | flops 10000000000 | bytes 1048576 | tf_op jit(solution)/shard_map/experts/pallas_call | solution.py:353
  29.3 0.9 %collective-permute-done.12.got_ref = bf16[16,2048]{1,0:T(8,128)(2,1)S(1)} collective-permute-done((bf16[16,2048]{1,0:T(8,128)(2,1)S(1)}, bf16[16,2048]{1,0:T(8,128)(2,1)S(1)}, u32[]{:S(2)}, u32[]{:S(2)}) %collective-permute-start.12) | collective-permute-done | bytes 65568 | tf_op jit(solution)/shard_map/ppermute | solution.py:376
  30.2 1.9 %collective-permute-start.13 = (bf16[8,2048]{1,0:T(8,128)(2,1)S(1)}, bf16[8,2048]{1,0:T(8,128)(2,1)S(1)}, u32[]{:S(2)}, u32[]{:S(2)}) collective-permute-start(bf16[8,2048]{1,0:T(8,128)(2,1)S(1)} %get-tuple-element.43), channel_id=1, source_target_pairs={{0,7},{1,6},{2,5},{3,4},{4,3},{5,2},{6,1},{7,0},{8,15},{9,14},{10,... | collective-permute-start | bytes 98312 | tf_op jit(solution)/shard_map/ppermute | solution.py:376
  32.2 2.1 %collective-permute-start.15 = (bf16[8,2048]{1,0:T(8,128)(2,1)S(1)}, bf16[8,2048]{1,0:T(8,128)(2,1)S(1)}, u32[]{:S(2)}, u32[]{:S(2)}) collective-permute-start(bf16[8,2048]{1,0:T(8,128)(2,1)S(1)} %get-tuple-element.45), channel_id=1, source_target_pairs={{0,5},{1,4},{2,7},{3,6},{4,1},{5,0},{6,3},{7,2},{8,13},{9,12},{10,... | collective-permute-start | bytes 98312 | tf_op jit(solution)/shard_map/ppermute | solution.py:376
  34.3 1.3 %collective-permute-done.13.refs_0_ = bf16[8,2048]{1,0:T(8,128)(2,1)S(1)} collective-permute-done((bf16[8,2048]{1,0:T(8,128)(2,1)S(1)}, bf16[8,2048]{1,0:T(8,128)(2,1)S(1)}, u32[]{:S(2)}, u32[]{:S(2)}) %collective-permute-start.13) | collective-permute-done | bytes 32800 | tf_op jit(solution)/shard_map/ppermute | solution.py:376
  35.6 1.5 %collective-permute-done.14.refs_1_ = bf16[8,2048]{1,0:T(8,128)(2,1)S(1)} collective-permute-done((bf16[8,2048]{1,0:T(8,128)(2,1)S(1)}, bf16[8,2048]{1,0:T(8,128)(2,1)S(1)}, u32[]{:S(2)}, u32[]{:S(2)}) %collective-permute-start.14) | collective-permute-done | bytes 32800 | tf_op jit(solution)/shard_map/ppermute | solution.py:376
  37.4 1.8 %collective-permute-start.18 = (bf16[16,2048]{1,0:T(8,128)(2,1)S(1)}, bf16[16,2048]{1,0:T(8,128)(2,1)S(1)}, u32[]{:S(2)}, u32[]{:S(2)}) collective-permute-start(bf16[16,2048]{1,0:T(8,128)(2,1)S(1)} %combine.1.refs_0_), channel_id=1, source_target_pairs={{0,24},{1,25},{2,26},{3,27},{4,28},{5,29},{6,30},{7,31},{8,16},{9,... | collective-permute-start | bytes 196616 | tf_op jit(solution)/shard_map/ppermute | solution.py:376
  39.2 0.4 collective-permute-start.17
  39.6 1.3 %collective-permute-start.16 = (bf16[16,2048]{1,0:T(8,128)(2,1)S(1)}, bf16[16,2048]{1,0:T(8,128)(2,1)S(1)}, u32[]{:S(2)}, u32[]{:S(2)}) collective-permute-start(bf16[16,2048]{1,0:T(8,128)(2,1)S(1)} %combine.1.refs_0_), channel_id=1, source_target_pairs={{0,8},{1,9},{2,10},{3,11},{4,12},{5,13},{6,14},{7,15},{8,0},{9,1},... | collective-permute-start | bytes 196616 | tf_op jit(solution)/shard_map/ppermute | solution.py:376
  40.9 1.7 %collective-permute-done.18.refs_3_ = bf16[16,2048]{1,0:T(8,128)(2,1)S(1)} collective-permute-done((bf16[16,2048]{1,0:T(8,128)(2,1)S(1)}, bf16[16,2048]{1,0:T(8,128)(2,1)S(1)}, u32[]{:S(2)}, u32[]{:S(2)}) %collective-permute-start.18) | collective-permute-done | bytes 65568 | tf_op jit(solution)/shard_map/ppermute | solution.py:376
  42.7 1.2 %collective-permute-done.17.refs_2_ = bf16[16,2048]{1,0:T(8,128)(2,1)S(1)} collective-permute-done((bf16[16,2048]{1,0:T(8,128)(2,1)S(1)}, bf16[16,2048]{1,0:T(8,128)(2,1)S(1)}, u32[]{:S(2)}, u32[]{:S(2)}) %collective-permute-start.17) | collective-permute-done | bytes 65568 | tf_op jit(solution)/shard_map/ppermute | solution.py:376
  43.9 0.8 %finish.1 = bf16[8,2,2048]{2,1,0:T(2,128)(2,1)} custom-call(f32[16,2048]{1,0:T(8,128)S(1)} %get-tuple-element.32.state_ref, bf16[16,2048]{1,0:T(8,128)(2,1)S(1)} %combine.1.refs_0_, bf16[16,2048]{1,0:T(8,128)(2,1)S(1)} %collective-permute-done.16.refs_1_, bf16[16,2048]{1,0:T(8,128)(2,1)S(1)} %collective-permute-done.17.refs_2_, ...), custom_call_target="tpu_custom_call" | custom-call | tf_op jit(solution)/shard_map/finish/pallas_call | solution.py:353
  (31 shorter events, 1.7 us)
Async XLA Ops:
  0.0 9.9 %copy-start.3 = (bf16[1024,2048]{1,0:T(8,128)(2,1)S(1)}, bf16[1024,2048]{1,0:T(8,128)(2,1)}, u32[]{:S(2)}) copy-start(bf16[1024,2048]{1,0:T(8,128)(2,1)} %w_ref.1) | copy-start | bytes 12582916
  2.0 5.3 %collective-permute-start = (bf16[144,128]{1,0:T(8,128)(2,1)S(1)}, bf16[144,128]{1,0:T(8,128)(2,1)S(1)}, u32[]{:S(2)}, u32[]{:S(2)}) collective-permute-start(bf16[144,128]{1,0:T(8,128)(2,1)S(1)} %get-tuple-element.28), channel_id=1, source_target_pairs={{0,25},{1,24},{2,27},{3,26},{4,29},{5,28},{6,31},{7,30},{8,17},{9,... | collective-permute-start | bytes 110600 | tf_op jit(solution)/shard_map/ppermute | solution.py:376
  5.4 3.4 %collective-permute-start.1 = (bf16[144,128]{1,0:T(8,128)(2,1)S(1)}, bf16[144,128]{1,0:T(8,128)(2,1)S(1)}, u32[]{:S(2)}, u32[]{:S(2)}) collective-permute-start(bf16[144,128]{1,0:T(8,128)(2,1)S(1)} %get-tuple-element.29), channel_id=1, source_target_pairs={{0,17},{1,16},{2,19},{3,18},{4,21},{5,20},{6,23},{7,22},{8,25},{9,... | collective-permute-start | bytes 110600 | tf_op jit(solution)/shard_map/ppermute | solution.py:376
  6.2 3.7 %collective-permute-start.2 = (bf16[144,128]{1,0:T(8,128)(2,1)S(1)}, bf16[144,128]{1,0:T(8,128)(2,1)S(1)}, u32[]{:S(2)}, u32[]{:S(2)}) collective-permute-start(bf16[144,128]{1,0:T(8,128)(2,1)S(1)} %get-tuple-element.30), channel_id=1, source_target_pairs={{0,9},{1,8},{2,11},{3,10},{4,13},{5,12},{6,15},{7,14},{8,1},{9,0},... | collective-permute-start | bytes 110600 | tf_op jit(solution)/shard_map/ppermute | solution.py:376
  6.3 7.8 %copy-start = (bf16[8,2,2048]{2,1,0:T(2,128)(2,1)S(1)}, bf16[8,2,2048]{2,1,0:T(2,128)(2,1)}, u32[]{:S(2)}) copy-start(bf16[8,2,2048]{2,1,0:T(2,128)(2,1)} %residual_ref.1) | copy-start | bytes 196612
  6.3 7.8 %copy-start.1 = (s32[8,2,8]{2,1,0:T(2,128)S(1)}, s32[8,2,8]{2,1,0:T(2,128)}, u32[]{:S(2)}) copy-start(s32[8,2,8]{2,1,0:T(2,128)} %param.23) | copy-start | bytes 1540
  6.3 7.8 %copy-start.2 = (f32[8,2,8]{2,1,0:T(2,128)S(1)}, f32[8,2,8]{2,1,0:T(2,128)}, u32[]{:S(2)}) copy-start(f32[8,2,8]{2,1,0:T(2,128)} %param.24) | copy-start | bytes 1540
  6.3 11.1 %copy-start.7 = (bf16[2048]{0:T(1024)(128)(2,1)S(1)}, bf16[2048]{0:T(1024)(128)(2,1)}, u32[]{:S(2)}) copy-start(bf16[2048]{0:T(1024)(128)(2,1)} %param.22) | copy-start | bytes 12292
  6.3 3.6 %collective-permute-start.3 = (bf16[144,128]{1,0:T(8,128)(2,1)S(1)}, bf16[144,128]{1,0:T(8,128)(2,1)S(1)}, u32[]{:S(2)}, u32[]{:S(2)}) collective-permute-start(bf16[144,128]{1,0:T(8,128)(2,1)S(1)} %get-tuple-element.31), channel_id=1, source_target_pairs={{0,1},{1,0},{2,3},{3,2},{4,5},{5,4},{6,7},{7,6},{8,9},{9,8},{10,11... | collective-permute-start | bytes 110600 | tf_op jit(solution)/shard_map/ppermute | solution.py:376
  10.7 5.1 %collective-permute-start.7 = (bf16[16,2048]{1,0:T(8,128)(2,1)S(1)}, bf16[16,2048]{1,0:T(8,128)(2,1)S(1)}, u32[]{:S(2)}, u32[]{:S(2)}) collective-permute-start(bf16[16,2048]{1,0:T(8,128)(2,1)S(1)} %project.1), channel_id=1, source_target_pairs={{0,25},{1,24},{2,27},{3,26},{4,29},{5,28},{6,31},{7,30},{8,17},{9,... | collective-permute-start | bytes 196616 | tf_op jit(solution)/shard_map/ppermute | solution.py:376
  12.0 5.4 %collective-permute-start.6 = (bf16[16,2048]{1,0:T(8,128)(2,1)S(1)}, bf16[16,2048]{1,0:T(8,128)(2,1)S(1)}, u32[]{:S(2)}, u32[]{:S(2)}) collective-permute-start(bf16[16,2048]{1,0:T(8,128)(2,1)S(1)} %project.1), channel_id=1, source_target_pairs={{0,17},{1,16},{2,19},{3,18},{4,21},{5,20},{6,23},{7,22},{8,25},{9,... | collective-permute-start | bytes 196616 | tf_op jit(solution)/shard_map/ppermute | solution.py:376
  12.4 5.0 %collective-permute-start.5 = (bf16[16,2048]{1,0:T(8,128)(2,1)S(1)}, bf16[16,2048]{1,0:T(8,128)(2,1)S(1)}, u32[]{:S(2)}, u32[]{:S(2)}) collective-permute-start(bf16[16,2048]{1,0:T(8,128)(2,1)S(1)} %project.1), channel_id=1, source_target_pairs={{0,9},{1,8},{2,11},{3,10},{4,13},{5,12},{6,15},{7,14},{8,1},{9,0},... | collective-permute-start | bytes 196616 | tf_op jit(solution)/shard_map/ppermute | solution.py:376
  13.7 3.7 %collective-permute-start.4 = (bf16[16,2048]{1,0:T(8,128)(2,1)S(1)}, bf16[16,2048]{1,0:T(8,128)(2,1)S(1)}, u32[]{:S(2)}, u32[]{:S(2)}) collective-permute-start(bf16[16,2048]{1,0:T(8,128)(2,1)S(1)} %project.1), channel_id=1, source_target_pairs={{0,1},{1,0},{2,3},{3,2},{4,5},{5,4},{6,7},{7,6},{8,9},{9,8},{10,11... | collective-permute-start | bytes 196616 | tf_op jit(solution)/shard_map/ppermute | solution.py:376
  17.4 9.6 %copy-start.4 = (bf16[1,2048,1024]{2,1,0:T(8,128)(2,1)S(1)}, bf16[1,2048,1024]{2,1,0:T(8,128)(2,1)}, u32[]{:S(2)}) copy-start(bf16[1,2048,1024]{2,1,0:T(8,128)(2,1)} %gate_ref.1) | copy-start | bytes 12582916
  17.4 9.6 %copy-start.5 = (bf16[1,2048,1024]{2,1,0:T(8,128)(2,1)S(1)}, bf16[1,2048,1024]{2,1,0:T(8,128)(2,1)}, u32[]{:S(2)}) copy-start(bf16[1,2048,1024]{2,1,0:T(8,128)(2,1)} %up_ref.1) | copy-start | bytes 12582916
  17.4 9.5 %copy-start.6 = (bf16[1,1024,2048]{2,1,0:T(8,128)(2,1)S(1)}, bf16[1,1024,2048]{2,1,0:T(8,128)(2,1)}, u32[]{:S(2)}) copy-start(bf16[1,1024,2048]{2,1,0:T(8,128)(2,1)} %down_ref.1) | copy-start | bytes 12582916
  17.9 5.2 %collective-permute-start.8 = (bf16[8,2048]{1,0:T(8,128)(2,1)S(1)}, bf16[8,2048]{1,0:T(8,128)(2,1)S(1)}, u32[]{:S(2)}, u32[]{:S(2)}) collective-permute-start(bf16[8,2048]{1,0:T(8,128)(2,1)S(1)} %get-tuple-element.35), channel_id=1, source_target_pairs={{0,7},{1,6},{2,5},{3,4},{4,3},{5,2},{6,1},{7,0},{8,15},{9,14},{10,... | collective-permute-start | bytes 98312 | tf_op jit(solution)/shard_map/ppermute | solution.py:376
  21.3 3.3 %collective-permute-start.9 = (bf16[8,2048]{1,0:T(8,128)(2,1)S(1)}, bf16[8,2048]{1,0:T(8,128)(2,1)S(1)}, u32[]{:S(2)}, u32[]{:S(2)}) collective-permute-start(bf16[8,2048]{1,0:T(8,128)(2,1)S(1)} %get-tuple-element.36), channel_id=1, source_target_pairs={{0,3},{1,2},{2,1},{3,0},{4,7},{5,6},{6,5},{7,4},{8,11},{9,10},{10,... | collective-permute-start | bytes 98312 | tf_op jit(solution)/shard_map/ppermute | solution.py:376
  21.3 4.3 %collective-permute-start.10 = (bf16[8,2048]{1,0:T(8,128)(2,1)S(1)}, bf16[8,2048]{1,0:T(8,128)(2,1)S(1)}, u32[]{:S(2)}, u32[]{:S(2)}) collective-permute-start(bf16[8,2048]{1,0:T(8,128)(2,1)S(1)} %get-tuple-element.37), channel_id=1, source_target_pairs={{0,5},{1,4},{2,7},{3,6},{4,1},{5,0},{6,3},{7,2},{8,13},{9,12},{10,... | collective-permute-start | bytes 98312 | tf_op jit(solution)/shard_map/ppermute | solution.py:376
  25.6 1.3 %collective-permute-start.11 = (bf16[16,2048]{1,0:T(8,128)(2,1)S(1)}, bf16[16,2048]{1,0:T(8,128)(2,1)S(1)}, u32[]{:S(2)}, u32[]{:S(2)}) collective-permute-start(bf16[16,2048]{1,0:T(8,128)(2,1)S(1)} %get-tuple-element.40), channel_id=1, source_target_pairs={{0,1},{1,0},{2,3},{3,2},{4,5},{5,4},{6,7},{7,6},{8,9},{9,8},{10,11... | collective-permute-start | bytes 196616 | tf_op jit(solution)/shard_map/ppermute | solution.py:376
  28.9 1.3 %collective-permute-start.12 = (bf16[16,2048]{1,0:T(8,128)(2,1)S(1)}, bf16[16,2048]{1,0:T(8,128)(2,1)S(1)}, u32[]{:S(2)}, u32[]{:S(2)}) collective-permute-start(bf16[16,2048]{1,0:T(8,128)(2,1)S(1)} %get-tuple-element.42), channel_id=1, source_target_pairs={{0,1},{1,0},{2,3},{3,2},{4,5},{5,4},{6,7},{7,6},{8,9},{9,8},{10,11... | collective-permute-start | bytes 196616 | tf_op jit(solution)/shard_map/ppermute | solution.py:376
  30.2 5.4 %collective-permute-start.13 = (bf16[8,2048]{1,0:T(8,128)(2,1)S(1)}, bf16[8,2048]{1,0:T(8,128)(2,1)S(1)}, u32[]{:S(2)}, u32[]{:S(2)}) collective-permute-start(bf16[8,2048]{1,0:T(8,128)(2,1)S(1)} %get-tuple-element.43), channel_id=1, source_target_pairs={{0,7},{1,6},{2,5},{3,4},{4,3},{5,2},{6,1},{7,0},{8,15},{9,14},{10,... | collective-permute-start | bytes 98312 | tf_op jit(solution)/shard_map/ppermute | solution.py:376
  32.2 4.9 %collective-permute-start.14 = (bf16[8,2048]{1,0:T(8,128)(2,1)S(1)}, bf16[8,2048]{1,0:T(8,128)(2,1)S(1)}, u32[]{:S(2)}, u32[]{:S(2)}) collective-permute-start(bf16[8,2048]{1,0:T(8,128)(2,1)S(1)} %get-tuple-element.44), channel_id=1, source_target_pairs={{0,3},{1,2},{2,1},{3,0},{4,7},{5,6},{6,5},{7,4},{8,11},{9,10},{10,... | collective-permute-start | bytes 98312 | tf_op jit(solution)/shard_map/ppermute | solution.py:376
  32.2 4.9 %collective-permute-start.15 = (bf16[8,2048]{1,0:T(8,128)(2,1)S(1)}, bf16[8,2048]{1,0:T(8,128)(2,1)S(1)}, u32[]{:S(2)}, u32[]{:S(2)}) collective-permute-start(bf16[8,2048]{1,0:T(8,128)(2,1)S(1)} %get-tuple-element.45), channel_id=1, source_target_pairs={{0,5},{1,4},{2,7},{3,6},{4,1},{5,0},{6,3},{7,2},{8,13},{9,12},{10,... | collective-permute-start | bytes 98312 | tf_op jit(solution)/shard_map/ppermute | solution.py:376
  37.4 5.3 %collective-permute-start.18 = (bf16[16,2048]{1,0:T(8,128)(2,1)S(1)}, bf16[16,2048]{1,0:T(8,128)(2,1)S(1)}, u32[]{:S(2)}, u32[]{:S(2)}) collective-permute-start(bf16[16,2048]{1,0:T(8,128)(2,1)S(1)} %combine.1.refs_0_), channel_id=1, source_target_pairs={{0,24},{1,25},{2,26},{3,27},{4,28},{5,29},{6,30},{7,31},{8,16},{9,... | collective-permute-start | bytes 196616 | tf_op jit(solution)/shard_map/ppermute | solution.py:376
  39.2 4.7 %collective-permute-start.17 = (bf16[16,2048]{1,0:T(8,128)(2,1)S(1)}, bf16[16,2048]{1,0:T(8,128)(2,1)S(1)}, u32[]{:S(2)}, u32[]{:S(2)}) collective-permute-start(bf16[16,2048]{1,0:T(8,128)(2,1)S(1)} %combine.1.refs_0_), channel_id=1, source_target_pairs={{0,16},{1,17},{2,18},{3,19},{4,20},{5,21},{6,22},{7,23},{8,24},{9,... | collective-permute-start | bytes 196616 | tf_op jit(solution)/shard_map/ppermute | solution.py:376
  39.6 4.3 %collective-permute-start.16 = (bf16[16,2048]{1,0:T(8,128)(2,1)S(1)}, bf16[16,2048]{1,0:T(8,128)(2,1)S(1)}, u32[]{:S(2)}, u32[]{:S(2)}) collective-permute-start(bf16[16,2048]{1,0:T(8,128)(2,1)S(1)} %combine.1.refs_0_), channel_id=1, source_target_pairs={{0,8},{1,9},{2,10},{3,11},{4,12},{5,13},{6,14},{7,15},{8,0},{9,1},... | collective-permute-start | bytes 196616 | tf_op jit(solution)/shard_map/ppermute | solution.py:376

commit v8 on v7

--- a/solution.py
+++ b/solution.py
@@ -42,6 +42,15 @@
     codes = codes.astype(jnp.float32)
     root = lax.rsqrt(lax.rsqrt(jnp.abs(codes)))
     return jnp.where(codes < 0.0, -root, root)
+
+
+def encode_square(values):
+    return (values * jnp.abs(values)).astype(jnp.bfloat16)
+
+
+def decode_square(codes):
+    codes = codes.astype(jnp.float32)
+    return codes * lax.rsqrt(jnp.maximum(jnp.abs(codes), 1e-37))
 
 
 def encode_mean(values):
@@ -307,8 +316,8 @@
     up = jnp.dot(normed, up_ref[0], preferred_element_type=jnp.float32)
     activation = (gate / (1.0 + jnp.exp(-gate)) * up).astype(jnp.bfloat16)
     result = jnp.dot(activation, down_ref[0], preferred_element_type=jnp.float32)
-    keep_ref[...] = encode(result[:half])
-    send_ref[...] = encode(result[half : 2 * half])
+    keep_ref[...] = encode_square(result[:half])
+    send_ref[...] = encode_square(result[half : 2 * half])
 
 
 def scatter_kernel(kept_ref, got_ref, *outs):
@@ -321,7 +330,7 @@
 
 def combine_kernel(hops, high_ref, low_ref, *refs):
     blocks, out_ref = [refs[hops.index(j)] for j in range(len(hops))], refs[-1]
-    returned = decode(
+    returned = decode_square(
         jnp.concatenate([block[...].astype(jnp.float32) for block in blocks], 0)
     )
     returned_high, returned_low = split_two(returned)
@@ -331,14 +340,14 @@
         + jnp.dot(weight_high, returned_low, preferred_element_type=jnp.float32)
         + jnp.dot(weight_low, returned_high, preferred_element_type=jnp.float32)
     )
-    out_ref[...] = encode(mixture)
+    out_ref[...] = encode_square(mixture)
 
 
 def finish_kernel(state_ref, *refs):
     parts, out_ref = refs[:-1], refs[-1]
     rows, steps, _ = out_ref.shape
     layer = (
-        state_ref[...] + tree_sum([decode(part[...]) for part in parts])
+        state_ref[...] + tree_sum([decode_square(part[...]) for part in parts])
     ).astype(jnp.bfloat16)
     for r in range(rows):
         out_ref[r] = layer[r * steps : (r + 1) * steps]

time: 44.8 us -> 44.7 us (level)
  no operation moved by 1% of the time
where the time goes in v8:
time: 44.7 us; the launch traced here: 44.6 us
  starting transfers between devices  20.4 us (46%)
  waiting for transfers between devices  17.7 us (40%)
  Pallas kernels  6.36 us (14%)
    ppermute x19, starting transfers between devices, move(): return lax.ppermute(block, ('ctx', 'exp'), pairs)  20.4 us
    ppermute x19, waiting for transfers between devices, move(): return lax.ppermute(block, ('ctx', 'exp'), pairs)  17.7 us
    pallas_call x9, Pallas kernels, call(): pl.pallas_call(kernel, name=name, in_specs=in_specs, out_specs=[out_spec...  6.36 us
  transfers between devices with their start and end apart: 19, of which 14 were waited for; matrix products, arithmetic and copies ran while one was open for 0% of the time, Pallas kernels for 0%

profile of v8, /device:TPU:0, one launch (start us, length us, event | category | flops | bytes accessed | tf_op | source)
XLA Modules:
  0.0 44.6 jit_solution(8391966207399653874)
XLA Ops:
  0.0 2.0 %attend.1 = (bf16[144,128]{1,0:T(8,128)(2,1)S(1)}, bf16[144,128]{1,0:T(8,128)(2,1)S(1)}, bf16[144,128]{1,0:T(8,128)(2,1)S(1)}, bf16[144,128]{1,0:T(8,128)(2,1)S(1)}) custom-call(s32[1]{0:T(128)} %bitcast.me_ref, s32[8]{0:T(128)} %len_hbm.1, bf16[8,2,4096]{2,1,0:T(2,128)(2,1)} %q_hbm.1, bf16[8,64,256]{2,1,0:T(8,128)(2,1)} %k_hbm.1, ...), custom_call_target="tpu_custom_call" | custom-call | flops 10000000000 | bytes 1048576 | tf_op jit(solution)/shard_map/attend/pallas_call | solution.py:362
  2.0 3.4 %collective-permute-start = (bf16[144,128]{1,0:T(8,128)(2,1)S(1)}, bf16[144,128]{1,0:T(8,128)(2,1)S(1)}, u32[]{:S(2)}, u32[]{:S(2)}) collective-permute-start(bf16[144,128]{1,0:T(8,128)(2,1)S(1)} %get-tuple-element.28), channel_id=1, source_target_pairs={{0,25},{1,24},{2,27},{3,26},{4,29},{5,28},{6,31},{7,30},{8,17},{9,... | collective-permute-start | bytes 110600 | tf_op jit(solution)/shard_map/ppermute | solution.py:385
  5.4 0.8 %collective-permute-start.1 = (bf16[144,128]{1,0:T(8,128)(2,1)S(1)}, bf16[144,128]{1,0:T(8,128)(2,1)S(1)}, u32[]{:S(2)}, u32[]{:S(2)}) collective-permute-start(bf16[144,128]{1,0:T(8,128)(2,1)S(1)} %get-tuple-element.29), channel_id=1, source_target_pairs={{0,17},{1,16},{2,19},{3,18},{4,21},{5,20},{6,23},{7,22},{8,25},{9,... | collective-permute-start | bytes 110600 | tf_op jit(solution)/shard_map/ppermute | solution.py:385
  6.4 0.9 %collective-permute-done.rest_0_ = bf16[144,128]{1,0:T(8,128)(2,1)S(1)} collective-permute-done((bf16[144,128]{1,0:T(8,128)(2,1)S(1)}, bf16[144,128]{1,0:T(8,128)(2,1)S(1)}, u32[]{:S(2)}, u32[]{:S(2)}) %collective-permute-start) | collective-permute-done | bytes 36896 | tf_op jit(solution)/shard_map/ppermute | solution.py:385
  7.3 1.5 %collective-permute-done.1.rest_1_ = bf16[144,128]{1,0:T(8,128)(2,1)S(1)} collective-permute-done((bf16[144,128]{1,0:T(8,128)(2,1)S(1)}, bf16[144,128]{1,0:T(8,128)(2,1)S(1)}, u32[]{:S(2)}, u32[]{:S(2)}) %collective-permute-start.1) | collective-permute-done | bytes 36896 | tf_op jit(solution)/shard_map/ppermute | solution.py:385
  8.8 1.1 %collective-permute-done.2.rest_2_ = bf16[144,128]{1,0:T(8,128)(2,1)S(1)} collective-permute-done((bf16[144,128]{1,0:T(8,128)(2,1)S(1)}, bf16[144,128]{1,0:T(8,128)(2,1)S(1)}, u32[]{:S(2)}, u32[]{:S(2)}) %collective-permute-start.2) | collective-permute-done | bytes 36896 | tf_op jit(solution)/shard_map/ppermute | solution.py:385
  9.9 0.8 %project.1 = bf16[16,2048]{1,0:T(8,128)(2,1)S(1)} custom-call(bf16[1024,2048]{1,0:T(8,128)(2,1)S(1)} %copy-done.3, bf16[144,128]{1,0:T(8,128)(2,1)S(1)} %collective-permute-done.rest_0_, bf16[144,128]{1,0:T(8,128)(2,1)S(1)} %collective-permute-done.1.rest_1_, bf16[144,128]{1,0:T(8,128)(2,1)S(1)} %collective-permute-done.2.rest_2_, ...), custom_call_target="tpu_custom_call" | custom-call | flops 10000000000 | bytes 1048576 | tf_op jit(solution)/shard_map/project/pallas_call | solution.py:362
  10.7 1.3 %collective-permute-start.7 = (bf16[16,2048]{1,0:T(8,128)(2,1)S(1)}, bf16[16,2048]{1,0:T(8,128)(2,1)S(1)}, u32[]{:S(2)}, u32[]{:S(2)}) collective-permute-start(bf16[16,2048]{1,0:T(8,128)(2,1)S(1)} %project.1), channel_id=1, source_target_pairs={{0,25},{1,24},{2,27},{3,26},{4,29},{5,28},{6,31},{7,30},{8,17},{9,... | collective-permute-start | bytes 196616 | tf_op jit(solution)/shard_map/ppermute | solution.py:385
  12.0 0.4 collective-permute-start.6
  12.4 1.3 %collective-permute-start.5 = (bf16[16,2048]{1,0:T(8,128)(2,1)S(1)}, bf16[16,2048]{1,0:T(8,128)(2,1)S(1)}, u32[]{:S(2)}, u32[]{:S(2)}) collective-permute-start(bf16[16,2048]{1,0:T(8,128)(2,1)S(1)} %project.1), channel_id=1, source_target_pairs={{0,9},{1,8},{2,11},{3,10},{4,13},{5,12},{6,15},{7,14},{8,1},{9,0},... | collective-permute-start | bytes 196616 | tf_op jit(solution)/shard_map/ppermute | solution.py:385
  14.3 1.5 %collective-permute-done.7.rest_3_ = bf16[16,2048]{1,0:T(8,128)(2,1)S(1)} collective-permute-done((bf16[16,2048]{1,0:T(8,128)(2,1)S(1)}, bf16[16,2048]{1,0:T(8,128)(2,1)S(1)}, u32[]{:S(2)}, u32[]{:S(2)}) %collective-permute-start.7) | collective-permute-done | bytes 65568 | tf_op jit(solution)/shard_map/ppermute | solution.py:385
  15.8 1.6 %collective-permute-done.6.rest_2_ = bf16[16,2048]{1,0:T(8,128)(2,1)S(1)} collective-permute-done((bf16[16,2048]{1,0:T(8,128)(2,1)S(1)}, bf16[16,2048]{1,0:T(8,128)(2,1)S(1)}, u32[]{:S(2)}, u32[]{:S(2)}) %collective-permute-start.6) | collective-permute-done | bytes 65568 | tf_op jit(solution)/shard_map/ppermute | solution.py:385
  17.4 0.4 dispatch.1
  17.9 3.4 %collective-permute-start.8 = (bf16[8,2048]{1,0:T(8,128)(2,1)S(1)}, bf16[8,2048]{1,0:T(8,128)(2,1)S(1)}, u32[]{:S(2)}, u32[]{:S(2)}) collective-permute-start(bf16[8,2048]{1,0:T(8,128)(2,1)S(1)} %get-tuple-element.35), channel_id=1, source_target_pairs={{0,7},{1,6},{2,5},{3,4},{4,3},{5,2},{6,1},{7,0},{8,15},{9,14},{10,... | collective-permute-start | bytes 98312 | tf_op jit(solution)/shard_map/ppermute | solution.py:385
  21.3 0.6 %collective-permute-start.10 = (bf16[8,2048]{1,0:T(8,128)(2,1)S(1)}, bf16[8,2048]{1,0:T(8,128)(2,1)S(1)}, u32[]{:S(2)}, u32[]{:S(2)}) collective-permute-start(bf16[8,2048]{1,0:T(8,128)(2,1)S(1)} %get-tuple-element.37), channel_id=1, source_target_pairs={{0,5},{1,4},{2,7},{3,6},{4,1},{5,0},{6,3},{7,2},{8,13},{9,12},{10,... | collective-permute-start | bytes 98312 | tf_op jit(solution)/shard_map/ppermute | solution.py:385
  21.9 1.2 %collective-permute-done.8.refs_0_ = bf16[8,2048]{1,0:T(8,128)(2,1)S(1)} collective-permute-done((bf16[8,2048]{1,0:T(8,128)(2,1)S(1)}, bf16[8,2048]{1,0:T(8,128)(2,1)S(1)}, u32[]{:S(2)}, u32[]{:S(2)}) %collective-permute-start.8) | collective-permute-done | bytes 32800 | tf_op jit(solution)/shard_map/ppermute | solution.py:385
  23.1 1.5 %collective-permute-done.9.refs_1_ = bf16[8,2048]{1,0:T(8,128)(2,1)S(1)} collective-permute-done((bf16[8,2048]{1,0:T(8,128)(2,1)S(1)}, bf16[8,2048]{1,0:T(8,128)(2,1)S(1)}, u32[]{:S(2)}, u32[]{:S(2)}) %collective-permute-start.9) | collective-permute-done | bytes 32800 | tf_op jit(solution)/shard_map/ppermute | solution.py:385
  24.6 1.0 %collective-permute-done.10.refs_2_ = bf16[8,2048]{1,0:T(8,128)(2,1)S(1)} collective-permute-done((bf16[8,2048]{1,0:T(8,128)(2,1)S(1)}, bf16[8,2048]{1,0:T(8,128)(2,1)S(1)}, u32[]{:S(2)}, u32[]{:S(2)}) %collective-permute-start.10) | collective-permute-done | bytes 32800 | tf_op jit(solution)/shard_map/ppermute | solution.py:385
  25.6 0.4 collective-permute-start.11
  26.1 0.9 %collective-permute-done.11.got_ref = bf16[16,2048]{1,0:T(8,128)(2,1)S(1)} collective-permute-done((bf16[16,2048]{1,0:T(8,128)(2,1)S(1)}, bf16[16,2048]{1,0:T(8,128)(2,1)S(1)}, u32[]{:S(2)}, u32[]{:S(2)}) %collective-permute-start.11) | collective-permute-done | bytes 65568 | tf_op jit(solution)/shard_map/ppermute | solution.py:385
  27.0 1.9 %experts.1 = (bf16[16,2048]{1,0:T(8,128)(2,1)S(1)}, bf16[16,2048]{1,0:T(8,128)(2,1)S(1)}) custom-call(bf16[16,2048]{1,0:T(8,128)(2,1)S(1)} %get-tuple-element.39.kept_ref, bf16[16,2048]{1,0:T(8,128)(2,1)S(1)} %collective-permute-done.11.got_ref, bf16[1,2048,1024]{2,1,0:T(8,128)(2,1)S(1)} %copy-done.4, bf16[1,2048,1024]{2,1,0:T(8,128)(2,1)S(1)} %copy-done.5, ...), custom_call_target="tpu_custom_call" | custom-call | flops 10000000000 | bytes 1048576 | tf_op jit(solution)/shard_map/experts/pallas_call | solution.py:362
  29.3 0.9 %collective-permute-done.12.got_ref = bf16[16,2048]{1,0:T(8,128)(2,1)S(1)} collective-permute-done((bf16[16,2048]{1,0:T(8,128)(2,1)S(1)}, bf16[16,2048]{1,0:T(8,128)(2,1)S(1)}, u32[]{:S(2)}, u32[]{:S(2)}) %collective-permute-start.12) | collective-permute-done | bytes 65568 | tf_op jit(solution)/shard_map/ppermute | solution.py:385
  30.2 1.9 %collective-permute-start.13 = (bf16[8,2048]{1,0:T(8,128)(2,1)S(1)}, bf16[8,2048]{1,0:T(8,128)(2,1)S(1)}, u32[]{:S(2)}, u32[]{:S(2)}) collective-permute-start(bf16[8,2048]{1,0:T(8,128)(2,1)S(1)} %get-tuple-element.43), channel_id=1, source_target_pairs={{0,7},{1,6},{2,5},{3,4},{4,3},{5,2},{6,1},{7,0},{8,15},{9,14},{10,... | collective-permute-start | bytes 98312 | tf_op jit(solution)/shard_map/ppermute | solution.py:385
  32.2 2.1 %collective-permute-start.15 = (bf16[8,2048]{1,0:T(8,128)(2,1)S(1)}, bf16[8,2048]{1,0:T(8,128)(2,1)S(1)}, u32[]{:S(2)}, u32[]{:S(2)}) collective-permute-start(bf16[8,2048]{1,0:T(8,128)(2,1)S(1)} %get-tuple-element.45), channel_id=1, source_target_pairs={{0,5},{1,4},{2,7},{3,6},{4,1},{5,0},{6,3},{7,2},{8,13},{9,12},{10,... | collective-permute-start | bytes 98312 | tf_op jit(solution)/shard_map/ppermute | solution.py:385
  34.3 1.3 %collective-permute-done.13.refs_0_ = bf16[8,2048]{1,0:T(8,128)(2,1)S(1)} collective-permute-done((bf16[8,2048]{1,0:T(8,128)(2,1)S(1)}, bf16[8,2048]{1,0:T(8,128)(2,1)S(1)}, u32[]{:S(2)}, u32[]{:S(2)}) %collective-permute-start.13) | collective-permute-done | bytes 32800 | tf_op jit(solution)/shard_map/ppermute | solution.py:385
  35.6 1.5 %collective-permute-done.14.refs_1_ = bf16[8,2048]{1,0:T(8,128)(2,1)S(1)} collective-permute-done((bf16[8,2048]{1,0:T(8,128)(2,1)S(1)}, bf16[8,2048]{1,0:T(8,128)(2,1)S(1)}, u32[]{:S(2)}, u32[]{:S(2)}) %collective-permute-start.14) | collective-permute-done | bytes 32800 | tf_op jit(solution)/shard_map/ppermute | solution.py:385
  37.3 1.8 %collective-permute-start.18 = (bf16[16,2048]{1,0:T(8,128)(2,1)S(1)}, bf16[16,2048]{1,0:T(8,128)(2,1)S(1)}, u32[]{:S(2)}, u32[]{:S(2)}) collective-permute-start(bf16[16,2048]{1,0:T(8,128)(2,1)S(1)} %combine.1.refs_0_), channel_id=1, source_target_pairs={{0,24},{1,25},{2,26},{3,27},{4,28},{5,29},{6,30},{7,31},{8,16},{9,... | collective-permute-start | bytes 196616 | tf_op jit(solution)/shard_map/ppermute | solution.py:385
  39.1 0.4 collective-permute-start.17
  39.6 1.3 %collective-permute-start.16 = (bf16[16,2048]{1,0:T(8,128)(2,1)S(1)}, bf16[16,2048]{1,0:T(8,128)(2,1)S(1)}, u32[]{:S(2)}, u32[]{:S(2)}) collective-permute-start(bf16[16,2048]{1,0:T(8,128)(2,1)S(1)} %combine.1.refs_0_), channel_id=1, source_target_pairs={{0,8},{1,9},{2,10},{3,11},{4,12},{5,13},{6,14},{7,15},{8,0},{9,1},... | collective-permute-start | bytes 196616 | tf_op jit(solution)/shard_map/ppermute | solution.py:385
  40.9 1.7 %collective-permute-done.18.refs_3_ = bf16[16,2048]{1,0:T(8,128)(2,1)S(1)} collective-permute-done((bf16[16,2048]{1,0:T(8,128)(2,1)S(1)}, bf16[16,2048]{1,0:T(8,128)(2,1)S(1)}, u32[]{:S(2)}, u32[]{:S(2)}) %collective-permute-start.18) | collective-permute-done | bytes 65568 | tf_op jit(solution)/shard_map/ppermute | solution.py:385
  42.6 1.2 %collective-permute-done.17.refs_2_ = bf16[16,2048]{1,0:T(8,128)(2,1)S(1)} collective-permute-done((bf16[16,2048]{1,0:T(8,128)(2,1)S(1)}, bf16[16,2048]{1,0:T(8,128)(2,1)S(1)}, u32[]{:S(2)}, u32[]{:S(2)}) %collective-permute-start.17) | collective-permute-done | bytes 65568 | tf_op jit(solution)/shard_map/ppermute | solution.py:385
  43.8 0.8 %finish.1 = bf16[8,2,2048]{2,1,0:T(2,128)(2,1)} custom-call(f32[16,2048]{1,0:T(8,128)S(1)} %get-tuple-element.32.state_ref, bf16[16,2048]{1,0:T(8,128)(2,1)S(1)} %combine.1.refs_0_, bf16[16,2048]{1,0:T(8,128)(2,1)S(1)} %collective-permute-done.16.refs_1_, bf16[16,2048]{1,0:T(8,128)(2,1)S(1)} %collective-permute-done.17.refs_2_, ...), custom_call_target="tpu_custom_call" | custom-call | tf_op jit(solution)/shard_map/finish/pallas_call | solution.py:362
  (31 shorter events, 1.7 us)
Async XLA Ops:
  0.0 9.9 %copy-start.3 = (bf16[1024,2048]{1,0:T(8,128)(2,1)S(1)}, bf16[1024,2048]{1,0:T(8,128)(2,1)}, u32[]{:S(2)}) copy-start(bf16[1024,2048]{1,0:T(8,128)(2,1)} %w_ref.1) | copy-start | bytes 12582916
  2.0 5.3 %collective-permute-start = (bf16[144,128]{1,0:T(8,128)(2,1)S(1)}, bf16[144,128]{1,0:T(8,128)(2,1)S(1)}, u32[]{:S(2)}, u32[]{:S(2)}) collective-permute-start(bf16[144,128]{1,0:T(8,128)(2,1)S(1)} %get-tuple-element.28), channel_id=1, source_target_pairs={{0,25},{1,24},{2,27},{3,26},{4,29},{5,28},{6,31},{7,30},{8,17},{9,... | collective-permute-start | bytes 110600 | tf_op jit(solution)/shard_map/ppermute | solution.py:385
  5.4 3.4 %collective-permute-start.1 = (bf16[144,128]{1,0:T(8,128)(2,1)S(1)}, bf16[144,128]{1,0:T(8,128)(2,1)S(1)}, u32[]{:S(2)}, u32[]{:S(2)}) collective-permute-start(bf16[144,128]{1,0:T(8,128)(2,1)S(1)} %get-tuple-element.29), channel_id=1, source_target_pairs={{0,17},{1,16},{2,19},{3,18},{4,21},{5,20},{6,23},{7,22},{8,25},{9,... | collective-permute-start | bytes 110600 | tf_op jit(solution)/shard_map/ppermute | solution.py:385
  6.2 3.7 %collective-permute-start.2 = (bf16[144,128]{1,0:T(8,128)(2,1)S(1)}, bf16[144,128]{1,0:T(8,128)(2,1)S(1)}, u32[]{:S(2)}, u32[]{:S(2)}) collective-permute-start(bf16[144,128]{1,0:T(8,128)(2,1)S(1)} %get-tuple-element.30), channel_id=1, source_target_pairs={{0,9},{1,8},{2,11},{3,10},{4,13},{5,12},{6,15},{7,14},{8,1},{9,0},... | collective-permute-start | bytes 110600 | tf_op jit(solution)/shard_map/ppermute | solution.py:385
  6.3 7.8 %copy-start = (bf16[8,2,2048]{2,1,0:T(2,128)(2,1)S(1)}, bf16[8,2,2048]{2,1,0:T(2,128)(2,1)}, u32[]{:S(2)}) copy-start(bf16[8,2,2048]{2,1,0:T(2,128)(2,1)} %residual_ref.1) | copy-start | bytes 196612
  6.3 7.8 %copy-start.1 = (s32[8,2,8]{2,1,0:T(2,128)S(1)}, s32[8,2,8]{2,1,0:T(2,128)}, u32[]{:S(2)}) copy-start(s32[8,2,8]{2,1,0:T(2,128)} %param.23) | copy-start | bytes 1540
  6.3 7.8 %copy-start.2 = (f32[8,2,8]{2,1,0:T(2,128)S(1)}, f32[8,2,8]{2,1,0:T(2,128)}, u32[]{:S(2)}) copy-start(f32[8,2,8]{2,1,0:T(2,128)} %param.24) | copy-start | bytes 1540
  6.3 11.1 %copy-start.7 = (bf16[2048]{0:T(1024)(128)(2,1)S(1)}, bf16[2048]{0:T(1024)(128)(2,1)}, u32[]{:S(2)}) copy-start(bf16[2048]{0:T(1024)(128)(2,1)} %param.22) | copy-start | bytes 12292
  6.3 3.6 %collective-permute-start.3 = (bf16[144,128]{1,0:T(8,128)(2,1)S(1)}, bf16[144,128]{1,0:T(8,128)(2,1)S(1)}, u32[]{:S(2)}, u32[]{:S(2)}) collective-permute-start(bf16[144,128]{1,0:T(8,128)(2,1)S(1)} %get-tuple-element.31), channel_id=1, source_target_pairs={{0,1},{1,0},{2,3},{3,2},{4,5},{5,4},{6,7},{7,6},{8,9},{9,8},{10,11... | collective-permute-start | bytes 110600 | tf_op jit(solution)/shard_map/ppermute | solution.py:385
  10.7 5.1 %collective-permute-start.7 = (bf16[16,2048]{1,0:T(8,128)(2,1)S(1)}, bf16[16,2048]{1,0:T(8,128)(2,1)S(1)}, u32[]{:S(2)}, u32[]{:S(2)}) collective-permute-start(bf16[16,2048]{1,0:T(8,128)(2,1)S(1)} %project.1), channel_id=1, source_target_pairs={{0,25},{1,24},{2,27},{3,26},{4,29},{5,28},{6,31},{7,30},{8,17},{9,... | collective-permute-start | bytes 196616 | tf_op jit(solution)/shard_map/ppermute | solution.py:385
  12.0 5.4 %collective-permute-start.6 = (bf16[16,2048]{1,0:T(8,128)(2,1)S(1)}, bf16[16,2048]{1,0:T(8,128)(2,1)S(1)}, u32[]{:S(2)}, u32[]{:S(2)}) collective-permute-start(bf16[16,2048]{1,0:T(8,128)(2,1)S(1)} %project.1), channel_id=1, source_target_pairs={{0,17},{1,16},{2,19},{3,18},{4,21},{5,20},{6,23},{7,22},{8,25},{9,... | collective-permute-start | bytes 196616 | tf_op jit(solution)/shard_map/ppermute | solution.py:385
  12.4 5.0 %collective-permute-start.5 = (bf16[16,2048]{1,0:T(8,128)(2,1)S(1)}, bf16[16,2048]{1,0:T(8,128)(2,1)S(1)}, u32[]{:S(2)}, u32[]{:S(2)}) collective-permute-start(bf16[16,2048]{1,0:T(8,128)(2,1)S(1)} %project.1), channel_id=1, source_target_pairs={{0,9},{1,8},{2,11},{3,10},{4,13},{5,12},{6,15},{7,14},{8,1},{9,0},... | collective-permute-start | bytes 196616 | tf_op jit(solution)/shard_map/ppermute | solution.py:385
  13.7 3.7 %collective-permute-start.4 = (bf16[16,2048]{1,0:T(8,128)(2,1)S(1)}, bf16[16,2048]{1,0:T(8,128)(2,1)S(1)}, u32[]{:S(2)}, u32[]{:S(2)}) collective-permute-start(bf16[16,2048]{1,0:T(8,128)(2,1)S(1)} %project.1), channel_id=1, source_target_pairs={{0,1},{1,0},{2,3},{3,2},{4,5},{5,4},{6,7},{7,6},{8,9},{9,8},{10,11... | collective-permute-start | bytes 196616 | tf_op jit(solution)/shard_map/ppermute | solution.py:385
  17.4 9.6 %copy-start.4 = (bf16[1,2048,1024]{2,1,0:T(8,128)(2,1)S(1)}, bf16[1,2048,1024]{2,1,0:T(8,128)(2,1)}, u32[]{:S(2)}) copy-start(bf16[1,2048,1024]{2,1,0:T(8,128)(2,1)} %gate_ref.1) | copy-start | bytes 12582916
  17.4 9.6 %copy-start.5 = (bf16[1,2048,1024]{2,1,0:T(8,128)(2,1)S(1)}, bf16[1,2048,1024]{2,1,0:T(8,128)(2,1)}, u32[]{:S(2)}) copy-start(bf16[1,2048,1024]{2,1,0:T(8,128)(2,1)} %up_ref.1) | copy-start | bytes 12582916
  17.4 9.5 %copy-start.6 = (bf16[1,1024,2048]{2,1,0:T(8,128)(2,1)S(1)}, bf16[1,1024,2048]{2,1,0:T(8,128)(2,1)}, u32[]{:S(2)}) copy-start(bf16[1,1024,2048]{2,1,0:T(8,128)(2,1)} %down_ref.1) | copy-start | bytes 12582916
  17.9 5.2 %collective-permute-start.8 = (bf16[8,2048]{1,0:T(8,128)(2,1)S(1)}, bf16[8,2048]{1,0:T(8,128)(2,1)S(1)}, u32[]{:S(2)}, u32[]{:S(2)}) collective-permute-start(bf16[8,2048]{1,0:T(8,128)(2,1)S(1)} %get-tuple-element.35), channel_id=1, source_target_pairs={{0,7},{1,6},{2,5},{3,4},{4,3},{5,2},{6,1},{7,0},{8,15},{9,14},{10,... | collective-permute-start | bytes 98312 | tf_op jit(solution)/shard_map/ppermute | solution.py:385
  21.3 3.3 %collective-permute-start.9 = (bf16[8,2048]{1,0:T(8,128)(2,1)S(1)}, bf16[8,2048]{1,0:T(8,128)(2,1)S(1)}, u32[]{:S(2)}, u32[]{:S(2)}) collective-permute-start(bf16[8,2048]{1,0:T(8,128)(2,1)S(1)} %get-tuple-element.36), channel_id=1, source_target_pairs={{0,3},{1,2},{2,1},{3,0},{4,7},{5,6},{6,5},{7,4},{8,11},{9,10},{10,... | collective-permute-start | bytes 98312 | tf_op jit(solution)/shard_map/ppermute | solution.py:385
  21.3 4.3 %collective-permute-start.10 = (bf16[8,2048]{1,0:T(8,128)(2,1)S(1)}, bf16[8,2048]{1,0:T(8,128)(2,1)S(1)}, u32[]{:S(2)}, u32[]{:S(2)}) collective-permute-start(bf16[8,2048]{1,0:T(8,128)(2,1)S(1)} %get-tuple-element.37), channel_id=1, source_target_pairs={{0,5},{1,4},{2,7},{3,6},{4,1},{5,0},{6,3},{7,2},{8,13},{9,12},{10,... | collective-permute-start | bytes 98312 | tf_op jit(solution)/shard_map/ppermute | solution.py:385
  25.6 1.3 %collective-permute-start.11 = (bf16[16,2048]{1,0:T(8,128)(2,1)S(1)}, bf16[16,2048]{1,0:T(8,128)(2,1)S(1)}, u32[]{:S(2)}, u32[]{:S(2)}) collective-permute-start(bf16[16,2048]{1,0:T(8,128)(2,1)S(1)} %get-tuple-element.40), channel_id=1, source_target_pairs={{0,1},{1,0},{2,3},{3,2},{4,5},{5,4},{6,7},{7,6},{8,9},{9,8},{10,11... | collective-permute-start | bytes 196616 | tf_op jit(solution)/shard_map/ppermute | solution.py:385
  28.8 1.3 %collective-permute-start.12 = (bf16[16,2048]{1,0:T(8,128)(2,1)S(1)}, bf16[16,2048]{1,0:T(8,128)(2,1)S(1)}, u32[]{:S(2)}, u32[]{:S(2)}) collective-permute-start(bf16[16,2048]{1,0:T(8,128)(2,1)S(1)} %get-tuple-element.42), channel_id=1, source_target_pairs={{0,1},{1,0},{2,3},{3,2},{4,5},{5,4},{6,7},{7,6},{8,9},{9,8},{10,11... | collective-permute-start | bytes 196616 | tf_op jit(solution)/shard_map/ppermute | solution.py:385
  30.2 5.4 %collective-permute-start.13 = (bf16[8,2048]{1,0:T(8,128)(2,1)S(1)}, bf16[8,2048]{1,0:T(8,128)(2,1)S(1)}, u32[]{:S(2)}, u32[]{:S(2)}) collective-permute-start(bf16[8,2048]{1,0:T(8,128)(2,1)S(1)} %get-tuple-element.43), channel_id=1, source_target_pairs={{0,7},{1,6},{2,5},{3,4},{4,3},{5,2},{6,1},{7,0},{8,15},{9,14},{10,... | collective-permute-start | bytes 98312 | tf_op jit(solution)/shard_map/ppermute | solution.py:385
  32.1 4.9 %collective-permute-start.14 = (bf16[8,2048]{1,0:T(8,128)(2,1)S(1)}, bf16[8,2048]{1,0:T(8,128)(2,1)S(1)}, u32[]{:S(2)}, u32[]{:S(2)}) collective-permute-start(bf16[8,2048]{1,0:T(8,128)(2,1)S(1)} %get-tuple-element.44), channel_id=1, source_target_pairs={{0,3},{1,2},{2,1},{3,0},{4,7},{5,6},{6,5},{7,4},{8,11},{9,10},{10,... | collective-permute-start | bytes 98312 | tf_op jit(solution)/shard_map/ppermute | solution.py:385
  32.2 4.9 %collective-permute-start.15 = (bf16[8,2048]{1,0:T(8,128)(2,1)S(1)}, bf16[8,2048]{1,0:T(8,128)(2,1)S(1)}, u32[]{:S(2)}, u32[]{:S(2)}) collective-permute-start(bf16[8,2048]{1,0:T(8,128)(2,1)S(1)} %get-tuple-element.45), channel_id=1, source_target_pairs={{0,5},{1,4},{2,7},{3,6},{4,1},{5,0},{6,3},{7,2},{8,13},{9,12},{10,... | collective-permute-start | bytes 98312 | tf_op jit(solution)/shard_map/ppermute | solution.py:385
  37.3 5.3 %collective-permute-start.18 = (bf16[16,2048]{1,0:T(8,128)(2,1)S(1)}, bf16[16,2048]{1,0:T(8,128)(2,1)S(1)}, u32[]{:S(2)}, u32[]{:S(2)}) collective-permute-start(bf16[16,2048]{1,0:T(8,128)(2,1)S(1)} %combine.1.refs_0_), channel_id=1, source_target_pairs={{0,24},{1,25},{2,26},{3,27},{4,28},{5,29},{6,30},{7,31},{8,16},{9,... | collective-permute-start | bytes 196616 | tf_op jit(solution)/shard_map/ppermute | solution.py:385
  39.1 4.7 %collective-permute-start.17 = (bf16[16,2048]{1,0:T(8,128)(2,1)S(1)}, bf16[16,2048]{1,0:T(8,128)(2,1)S(1)}, u32[]{:S(2)}, u32[]{:S(2)}) collective-permute-start(bf16[16,2048]{1,0:T(8,128)(2,1)S(1)} %combine.1.refs_0_), channel_id=1, source_target_pairs={{0,16},{1,17},{2,18},{3,19},{4,20},{5,21},{6,22},{7,23},{8,24},{9,... | collective-permute-start | bytes 196616 | tf_op jit(solution)/shard_map/ppermute | solution.py:385
  39.6 4.3 %collective-permute-start.16 = (bf16[16,2048]{1,0:T(8,128)(2,1)S(1)}, bf16[16,2048]{1,0:T(8,128)(2,1)S(1)}, u32[]{:S(2)}, u32[]{:S(2)}) collective-permute-start(bf16[16,2048]{1,0:T(8,128)(2,1)S(1)} %combine.1.refs_0_), channel_id=1, source_target_pairs={{0,8},{1,9},{2,10},{3,11},{4,12},{5,13},{6,14},{7,15},{8,0},{9,1},... | collective-permute-start | bytes 196616 | tf_op jit(solution)/shard_map/ppermute | solution.py:385

commit v9 on v8

--- a/solution.py
+++ b/solution.py
@@ -229,8 +229,8 @@
 
 
 def route_kernel(
-    ctx_count, exp_count, capacity, me_ref, home_ref, ids_ref, weights_ref, residual_ref,
-    selector_ref, high_ref, low_ref, rows_ref
+    ctx_count, exp_count, capacity, me_ref, home_ref, ids_ref, weights_ref, gain_ref, residual_ref,
+    selector_ref, high_ref, low_ref, rows_ref, gains_ref
 ):
     rows, steps, _ = residual_ref.shape
     row_steps = rows * steps
@@ -261,6 +261,11 @@
     weight_high = weight.astype(jnp.bfloat16)
     high_ref[...] = weight_high
     low_ref[...] = (weight - weight_high.astype(jnp.float32)).astype(jnp.bfloat16)
+    gain = gain_ref[...].astype(jnp.float32)
+    for i in range(D // LANES):
+        gains_ref[:, i * LANES : (i + 1) * LANES] = jnp.broadcast_to(
+            gain[i : i + 1], (row_steps, LANES)
+        )
     rows_ref[...] = jnp.concatenate(
         [residual_ref[r].astype(jnp.float32) for r in range(rows)], 0
     )
@@ -278,12 +283,10 @@
     terms = tree_sum([decode(part[...]) for part in parts])
     state = residual_ref[...] + terms * (1.0 / TERM_SCALE)
     state_ref[...] = state
-    gains = gain_ref[...].astype(jnp.float32)
-    gain = jnp.concatenate([gains[i : i + 1] for i in range(D // LANES)], 1)
     normed = (
         state
         * lax.rsqrt(jnp.mean(state * state, -1, keepdims=True) + NORM_EPSILON)
-        * gain
+        * gain_ref[...]
     ).astype(jnp.bfloat16)
     picked = lax.dot_general(
         selector_ref[...],
@@ -320,11 +323,12 @@
     send_ref[...] = encode_square(result[half : 2 * half])
 
 
-def scatter_kernel(kept_ref, got_ref, *outs):
+def scatter_kernel(hops, back, kept_ref, got_ref, *outs):
     half = outs[0].shape[0] // 2
     kept, got = kept_ref[...].astype(jnp.float32), got_ref[...].astype(jnp.float32)
-    for j, out in enumerate(outs):
-        span = slice(j * half, (j + 1) * half)
+    for j, out in zip(back, outs):
+        first = hops.index(j) * half
+        span = slice(first, first + half)
         out[...] = jnp.concatenate([kept[span], got[span]], 0).astype(jnp.bfloat16)
 
 
@@ -410,7 +414,8 @@
     experts_all = exp_count * EXP_DEV
     capacity = max(2, (row_steps * TOPK + experts_all - 1) // experts_all)
     chips = exp_count // 2
-    hops = (chips - 1, *range(1, chips - 1), 0)
+    hops = tuple(reversed(range(chips)))
+    back = (chips - 1, *range(1, chips - 1), 0)
     span = HEADS // n * row_steps
     bf16, f32 = jnp.bfloat16, jnp.float32
     hidden = (row_steps, D)
@@ -432,16 +437,17 @@
         cost=cost(10),
     )
     got = [move(x, j, 1) for j, x in zip(reversed(range(n)), sent)]
-    selector, weight_high, weight_low, residual_rows = call(
+    selector, weight_high, weight_low, residual_rows, gain_rows = call(
         functools.partial(route_kernel, n, exp_count, capacity),
         "route",
-        [SMEM] * 2 + [VMEM] * 3,
-        [((row_steps, exp_count * capacity), bf16)] * 3 + [(hidden, f32)],
+        [SMEM] * 2 + [VMEM] * 4,
+        [((row_steps, exp_count * capacity), bf16)] * 3 + [(hidden, f32)] * 2,
         (
             me,
             home,
             expert_ids.reshape(row_steps, TOPK),
             expert_weights.reshape(row_steps, TOPK),
+            norm_gain.reshape(D // LANES, LANES),
             residual,
         ),
     )
@@ -460,11 +466,11 @@
         "dispatch",
         [VMEM] * (n + 3),
         [(hidden, f32)] + [(block, bf16)] * chips,
-        (residual_rows, norm_gain.reshape(D // LANES, LANES), selector, *got),
+        (residual_rows, gain_rows, selector, *got),
         cost=cost(10),
     )
 
-    def spread(blocks):
+    def spread(hops, blocks):
         return [x if j == 0 else move(x, 0, 2 * j + 1) for j, x in zip(hops, blocks)]
 
     kept, sent = call(
@@ -472,7 +478,7 @@
         "gather",
         [VMEM] * chips,
         [(half, bf16)] * 2,
-        spread(outgoing),
+        spread(hops, outgoing),
     )
     kept, sent = call(
         expert_kernel,
@@ -490,18 +496,18 @@
         cost=cost(10),
     )
     results = call(
-        scatter_kernel,
+        functools.partial(scatter_kernel, hops, back),
         "scatter",
         [VMEM] * 2,
         [(block, bf16)] * chips,
         (kept, move(sent, 0, 1)),
     )
     (mixture,) = call(
-        functools.partial(combine_kernel, hops),
+        functools.partial(combine_kernel, back),
         "combine",
         [VMEM] * (chips + 2),
         [(hidden, bf16)],
-        (weight_high, weight_low, *spread(results)),
+        (weight_high, weight_low, *spread(back, results)),
     )
     got = [move(mixture, j, 0) if j else mixture for j in range(n)]
     (layer_rows,) = call(

time: 44.7 us -> 44.5 us (level)
  no operation moved by 1% of the time
where the time goes in v9:
time: 44.5 us; the launch traced here: 44.4 us
  starting transfers between devices  20.4 us (46%)
  waiting for transfers between devices  17.5 us (39%)
  Pallas kernels  6.37 us (14%)
    ppermute x19, starting transfers between devices, move(): return lax.ppermute(block, ('ctx', 'exp'), pairs)  20.4 us
    ppermute x19, waiting for transfers between devices, move(): return lax.ppermute(block, ('ctx', 'exp'), pairs)  17.5 us
    pallas_call x9, Pallas kernels, call(): pl.pallas_call(kernel, name=name, in_specs=in_specs, out_specs=[out_spec...  6.37 us
  transfers between devices with their start and end apart: 19, of which 14 were waited for; matrix products, arithmetic and copies ran while one was open for 0% of the time, Pallas kernels for 0%

profile of v9, /device:TPU:0, one launch (start us, length us, event | category | flops | bytes accessed | tf_op | source)
XLA Modules:
  0.0 44.4 jit_solution(10400990294747614440)
XLA Ops:
  0.0 2.0 %attend.1 = (bf16[144,128]{1,0:T(8,128)(2,1)S(1)}, bf16[144,128]{1,0:T(8,128)(2,1)S(1)}, bf16[144,128]{1,0:T(8,128)(2,1)S(1)}, bf16[144,128]{1,0:T(8,128)(2,1)S(1)}) custom-call(s32[1]{0:T(128)} %bitcast.me_ref, s32[8]{0:T(128)} %len_hbm.1, bf16[8,2,4096]{2,1,0:T(2,128)(2,1)} %q_hbm.1, bf16[8,64,256]{2,1,0:T(8,128)(2,1)} %k_hbm.1, ...), custom_call_target="tpu_custom_call" | custom-call | flops 10000000000 | bytes 1048576 | tf_op jit(solution)/shard_map/attend/pallas_call | solution.py:366
  2.0 3.4 %collective-permute-start = (bf16[144,128]{1,0:T(8,128)(2,1)S(1)}, bf16[144,128]{1,0:T(8,128)(2,1)S(1)}, u32[]{:S(2)}, u32[]{:S(2)}) collective-permute-start(bf16[144,128]{1,0:T(8,128)(2,1)S(1)} %get-tuple-element.30), channel_id=1, source_target_pairs={{0,25},{1,24},{2,27},{3,26},{4,29},{5,28},{6,31},{7,30},{8,17},{9,... | collective-permute-start | bytes 110600 | tf_op jit(solution)/shard_map/ppermute | solution.py:389
  5.4 0.8 %collective-permute-start.1 = (bf16[144,128]{1,0:T(8,128)(2,1)S(1)}, bf16[144,128]{1,0:T(8,128)(2,1)S(1)}, u32[]{:S(2)}, u32[]{:S(2)}) collective-permute-start(bf16[144,128]{1,0:T(8,128)(2,1)S(1)} %get-tuple-element.31), channel_id=1, source_target_pairs={{0,17},{1,16},{2,19},{3,18},{4,21},{5,20},{6,23},{7,22},{8,25},{9,... | collective-permute-start | bytes 110600 | tf_op jit(solution)/shard_map/ppermute | solution.py:389
  6.4 0.9 %collective-permute-done.rest_0_ = bf16[144,128]{1,0:T(8,128)(2,1)S(1)} collective-permute-done((bf16[144,128]{1,0:T(8,128)(2,1)S(1)}, bf16[144,128]{1,0:T(8,128)(2,1)S(1)}, u32[]{:S(2)}, u32[]{:S(2)}) %collective-permute-start) | collective-permute-done | bytes 36896 | tf_op jit(solution)/shard_map/ppermute | solution.py:389
  7.3 1.5 %collective-permute-done.1.rest_1_ = bf16[144,128]{1,0:T(8,128)(2,1)S(1)} collective-permute-done((bf16[144,128]{1,0:T(8,128)(2,1)S(1)}, bf16[144,128]{1,0:T(8,128)(2,1)S(1)}, u32[]{:S(2)}, u32[]{:S(2)}) %collective-permute-start.1) | collective-permute-done | bytes 36896 | tf_op jit(solution)/shard_map/ppermute | solution.py:389
  8.8 1.1 %collective-permute-done.2.rest_2_ = bf16[144,128]{1,0:T(8,128)(2,1)S(1)} collective-permute-done((bf16[144,128]{1,0:T(8,128)(2,1)S(1)}, bf16[144,128]{1,0:T(8,128)(2,1)S(1)}, u32[]{:S(2)}, u32[]{:S(2)}) %collective-permute-start.2) | collective-permute-done | bytes 36896 | tf_op jit(solution)/shard_map/ppermute | solution.py:389
  9.9 0.8 %project.1 = bf16[16,2048]{1,0:T(8,128)(2,1)S(1)} custom-call(bf16[1024,2048]{1,0:T(8,128)(2,1)S(1)} %copy-done.4, bf16[144,128]{1,0:T(8,128)(2,1)S(1)} %collective-permute-done.rest_0_, bf16[144,128]{1,0:T(8,128)(2,1)S(1)} %collective-permute-done.1.rest_1_, bf16[144,128]{1,0:T(8,128)(2,1)S(1)} %collective-permute-done.2.rest_2_, ...), custom_call_target="tpu_custom_call" | custom-call | flops 10000000000 | bytes 1048576 | tf_op jit(solution)/shard_map/project/pallas_call | solution.py:366
  10.7 1.3 %collective-permute-start.7 = (bf16[16,2048]{1,0:T(8,128)(2,1)S(1)}, bf16[16,2048]{1,0:T(8,128)(2,1)S(1)}, u32[]{:S(2)}, u32[]{:S(2)}) collective-permute-start(bf16[16,2048]{1,0:T(8,128)(2,1)S(1)} %project.1), channel_id=1, source_target_pairs={{0,25},{1,24},{2,27},{3,26},{4,29},{5,28},{6,31},{7,30},{8,17},{9,... | collective-permute-start | bytes 196616 | tf_op jit(solution)/shard_map/ppermute | solution.py:389
  12.0 0.4 collective-permute-start.6
  12.4 1.3 %collective-permute-start.5 = (bf16[16,2048]{1,0:T(8,128)(2,1)S(1)}, bf16[16,2048]{1,0:T(8,128)(2,1)S(1)}, u32[]{:S(2)}, u32[]{:S(2)}) collective-permute-start(bf16[16,2048]{1,0:T(8,128)(2,1)S(1)} %project.1), channel_id=1, source_target_pairs={{0,9},{1,8},{2,11},{3,10},{4,13},{5,12},{6,15},{7,14},{8,1},{9,0},... | collective-permute-start | bytes 196616 | tf_op jit(solution)/shard_map/ppermute | solution.py:389
  14.4 1.5 %collective-permute-done.7.rest_3_ = bf16[16,2048]{1,0:T(8,128)(2,1)S(1)} collective-permute-done((bf16[16,2048]{1,0:T(8,128)(2,1)S(1)}, bf16[16,2048]{1,0:T(8,128)(2,1)S(1)}, u32[]{:S(2)}, u32[]{:S(2)}) %collective-permute-start.7) | collective-permute-done | bytes 65568 | tf_op jit(solution)/shard_map/ppermute | solution.py:389
  15.8 1.6 %collective-permute-done.6.rest_2_ = bf16[16,2048]{1,0:T(8,128)(2,1)S(1)} collective-permute-done((bf16[16,2048]{1,0:T(8,128)(2,1)S(1)}, bf16[16,2048]{1,0:T(8,128)(2,1)S(1)}, u32[]{:S(2)}, u32[]{:S(2)}) %collective-permute-start.6) | collective-permute-done | bytes 65568 | tf_op jit(solution)/shard_map/ppermute | solution.py:389
  17.4 0.4 %dispatch.1 = (f32[16,2048]{1,0:T(8,128)S(1)}, bf16[8,2048]{1,0:T(8,128)(2,1)S(1)}, bf16[8,2048]{1,0:T(8,128)(2,1)S(1)}, bf16[8,2048]{1,0:T(8,128)(2,1)S(1)}, bf16[8,2048]{1,0:T(8,128)(2,1)S(1)}) custom-call(f32[16,2048]{1,0:T(8,128)S(1)} %get-tuple-element.27.residual_ref, f32[16,2048]{1,0:T(8,128)S(1)} %get-tuple-element.28.gain_ref, ...), custom_call_target="tpu_custom_call" | custom-call | flops 10000000000 | bytes 1048576 | tf_op jit(solution)/shard_map/dispatch/pallas_call | solution.py:366
  17.9 3.4 %collective-permute-start.8 = (bf16[8,2048]{1,0:T(8,128)(2,1)S(1)}, bf16[8,2048]{1,0:T(8,128)(2,1)S(1)}, u32[]{:S(2)}, u32[]{:S(2)}) collective-permute-start(bf16[8,2048]{1,0:T(8,128)(2,1)S(1)} %get-tuple-element.37), channel_id=1, source_target_pairs={{0,7},{1,6},{2,5},{3,4},{4,3},{5,2},{6,1},{7,0},{8,15},{9,14},{10,... | collective-permute-start | bytes 98312 | tf_op jit(solution)/shard_map/ppermute | solution.py:389
  21.3 0.6 %collective-permute-start.10 = (bf16[8,2048]{1,0:T(8,128)(2,1)S(1)}, bf16[8,2048]{1,0:T(8,128)(2,1)S(1)}, u32[]{:S(2)}, u32[]{:S(2)}) collective-permute-start(bf16[8,2048]{1,0:T(8,128)(2,1)S(1)} %get-tuple-element.39), channel_id=1, source_target_pairs={{0,3},{1,2},{2,1},{3,0},{4,7},{5,6},{6,5},{7,4},{8,11},{9,10},{10,... | collective-permute-start | bytes 98312 | tf_op jit(solution)/shard_map/ppermute | solution.py:389
  21.9 1.2 %collective-permute-done.8.refs_0_ = bf16[8,2048]{1,0:T(8,128)(2,1)S(1)} collective-permute-done((bf16[8,2048]{1,0:T(8,128)(2,1)S(1)}, bf16[8,2048]{1,0:T(8,128)(2,1)S(1)}, u32[]{:S(2)}, u32[]{:S(2)}) %collective-permute-start.8) | collective-permute-done | bytes 32800 | tf_op jit(solution)/shard_map/ppermute | solution.py:389
  23.1 2.5 %collective-permute-done.9.refs_1_ = bf16[8,2048]{1,0:T(8,128)(2,1)S(1)} collective-permute-done((bf16[8,2048]{1,0:T(8,128)(2,1)S(1)}, bf16[8,2048]{1,0:T(8,128)(2,1)S(1)}, u32[]{:S(2)}, u32[]{:S(2)}) %collective-permute-start.9) | collective-permute-done | bytes 32800 | tf_op jit(solution)/shard_map/ppermute | solution.py:389
  25.6 0.4 collective-permute-start.11
  26.1 0.9 %collective-permute-done.11.got_ref = bf16[16,2048]{1,0:T(8,128)(2,1)S(1)} collective-permute-done((bf16[16,2048]{1,0:T(8,128)(2,1)S(1)}, bf16[16,2048]{1,0:T(8,128)(2,1)S(1)}, u32[]{:S(2)}, u32[]{:S(2)}) %collective-permute-start.11) | collective-permute-done | bytes 65568 | tf_op jit(solution)/shard_map/ppermute | solution.py:389
  27.0 1.9 %experts.1 = (bf16[16,2048]{1,0:T(8,128)(2,1)S(1)}, bf16[16,2048]{1,0:T(8,128)(2,1)S(1)}) custom-call(bf16[16,2048]{1,0:T(8,128)(2,1)S(1)} %get-tuple-element.41.kept_ref, bf16[16,2048]{1,0:T(8,128)(2,1)S(1)} %collective-permute-done.11.got_ref, bf16[1,2048,1024]{2,1,0:T(8,128)(2,1)S(1)} %copy-done.5, bf16[1,2048,1024]{2,1,0:T(8,128)(2,1)S(1)} %copy-done.6, ...), custom_call_target="tpu_custom_call" | custom-call | flops 10000000000 | bytes 1048576 | tf_op jit(solution)/shard_map/experts/pallas_call | solution.py:366
  29.3 0.9 %collective-permute-done.12.got_ref = bf16[16,2048]{1,0:T(8,128)(2,1)S(1)} collective-permute-done((bf16[16,2048]{1,0:T(8,128)(2,1)S(1)}, bf16[16,2048]{1,0:T(8,128)(2,1)S(1)}, u32[]{:S(2)}, u32[]{:S(2)}) %collective-permute-start.12) | collective-permute-done | bytes 65568 | tf_op jit(solution)/shard_map/ppermute | solution.py:389
  30.2 1.7 %collective-permute-start.13 = (bf16[8,2048]{1,0:T(8,128)(2,1)S(1)}, bf16[8,2048]{1,0:T(8,128)(2,1)S(1)}, u32[]{:S(2)}, u32[]{:S(2)}) collective-permute-start(bf16[8,2048]{1,0:T(8,128)(2,1)S(1)} %get-tuple-element.45), channel_id=1, source_target_pairs={{0,7},{1,6},{2,5},{3,4},{4,3},{5,2},{6,1},{7,0},{8,15},{9,14},{10,... | collective-permute-start | bytes 98312 | tf_op jit(solution)/shard_map/ppermute | solution.py:389
  31.9 0.7 %collective-permute-start.14 = (bf16[8,2048]{1,0:T(8,128)(2,1)S(1)}, bf16[8,2048]{1,0:T(8,128)(2,1)S(1)}, u32[]{:S(2)}, u32[]{:S(2)}) collective-permute-start(bf16[8,2048]{1,0:T(8,128)(2,1)S(1)} %get-tuple-element.46), channel_id=1, source_target_pairs={{0,3},{1,2},{2,1},{3,0},{4,7},{5,6},{6,5},{7,4},{8,11},{9,10},{10,... | collective-permute-start | bytes 98312 | tf_op jit(solution)/shard_map/ppermute | solution.py:389
  32.6 1.7 %collective-permute-start.15 = (bf16[8,2048]{1,0:T(8,128)(2,1)S(1)}, bf16[8,2048]{1,0:T(8,128)(2,1)S(1)}, u32[]{:S(2)}, u32[]{:S(2)}) collective-permute-start(bf16[8,2048]{1,0:T(8,128)(2,1)S(1)} %get-tuple-element.47), channel_id=1, source_target_pairs={{0,5},{1,4},{2,7},{3,6},{4,1},{5,0},{6,3},{7,2},{8,13},{9,12},{10,... | collective-permute-start | bytes 98312 | tf_op jit(solution)/shard_map/ppermute | solution.py:389
  34.3 1.2 %collective-permute-done.13.refs_0_ = bf16[8,2048]{1,0:T(8,128)(2,1)S(1)} collective-permute-done((bf16[8,2048]{1,0:T(8,128)(2,1)S(1)}, bf16[8,2048]{1,0:T(8,128)(2,1)S(1)}, u32[]{:S(2)}, u32[]{:S(2)}) %collective-permute-start.13) | collective-permute-done | bytes 32800 | tf_op jit(solution)/shard_map/ppermute | solution.py:389
  35.5 0.5 %collective-permute-done.14.refs_1_ = bf16[8,2048]{1,0:T(8,128)(2,1)S(1)} collective-permute-done((bf16[8,2048]{1,0:T(8,128)(2,1)S(1)}, bf16[8,2048]{1,0:T(8,128)(2,1)S(1)}, u32[]{:S(2)}, u32[]{:S(2)}) %collective-permute-start.14) | collective-permute-done | bytes 32800 | tf_op jit(solution)/shard_map/ppermute | solution.py:389
  36.0 0.9 %collective-permute-done.15.refs_2_ = bf16[8,2048]{1,0:T(8,128)(2,1)S(1)} collective-permute-done((bf16[8,2048]{1,0:T(8,128)(2,1)S(1)}, bf16[8,2048]{1,0:T(8,128)(2,1)S(1)}, u32[]{:S(2)}, u32[]{:S(2)}) %collective-permute-start.15) | collective-permute-done | bytes 32800 | tf_op jit(solution)/shard_map/ppermute | solution.py:389
  37.1 1.8 %collective-permute-start.18 = (bf16[16,2048]{1,0:T(8,128)(2,1)S(1)}, bf16[16,2048]{1,0:T(8,128)(2,1)S(1)}, u32[]{:S(2)}, u32[]{:S(2)}) collective-permute-start(bf16[16,2048]{1,0:T(8,128)(2,1)S(1)} %combine.1.refs_0_), channel_id=1, source_target_pairs={{0,24},{1,25},{2,26},{3,27},{4,28},{5,29},{6,30},{7,31},{8,16},{9,... | collective-permute-start | bytes 196616 | tf_op jit(solution)/shard_map/ppermute | solution.py:389
  39.3 1.4 %collective-permute-start.16 = (bf16[16,2048]{1,0:T(8,128)(2,1)S(1)}, bf16[16,2048]{1,0:T(8,128)(2,1)S(1)}, u32[]{:S(2)}, u32[]{:S(2)}) collective-permute-start(bf16[16,2048]{1,0:T(8,128)(2,1)S(1)} %combine.1.refs_0_), channel_id=1, source_target_pairs={{0,8},{1,9},{2,10},{3,11},{4,12},{5,13},{6,14},{7,15},{8,0},{9,1},... | collective-permute-start | bytes 196616 | tf_op jit(solution)/shard_map/ppermute | solution.py:389
  40.7 1.7 %collective-permute-done.18.refs_3_ = bf16[16,2048]{1,0:T(8,128)(2,1)S(1)} collective-permute-done((bf16[16,2048]{1,0:T(8,128)(2,1)S(1)}, bf16[16,2048]{1,0:T(8,128)(2,1)S(1)}, u32[]{:S(2)}, u32[]{:S(2)}) %collective-permute-start.18) | collective-permute-done | bytes 65568 | tf_op jit(solution)/shard_map/ppermute | solution.py:389
  42.4 1.2 %collective-permute-done.17.refs_2_ = bf16[16,2048]{1,0:T(8,128)(2,1)S(1)} collective-permute-done((bf16[16,2048]{1,0:T(8,128)(2,1)S(1)}, bf16[16,2048]{1,0:T(8,128)(2,1)S(1)}, u32[]{:S(2)}, u32[]{:S(2)}) %collective-permute-start.17) | collective-permute-done | bytes 65568 | tf_op jit(solution)/shard_map/ppermute | solution.py:389
  43.6 0.8 %finish.1 = bf16[8,2,2048]{2,1,0:T(2,128)(2,1)} custom-call(f32[16,2048]{1,0:T(8,128)S(1)} %get-tuple-element.34.state_ref, bf16[16,2048]{1,0:T(8,128)(2,1)S(1)} %combine.1.refs_0_, bf16[16,2048]{1,0:T(8,128)(2,1)S(1)} %collective-permute-done.16.refs_1_, bf16[16,2048]{1,0:T(8,128)(2,1)S(1)} %collective-permute-done.17.refs_2_, ...), custom_call_target="tpu_custom_call" | custom-call | tf_op jit(solution)/shard_map/finish/pallas_call | solution.py:366
  (31 shorter events, 2.0 us)
Async XLA Ops:
  0.0 9.9 %copy-start.4 = (bf16[1024,2048]{1,0:T(8,128)(2,1)S(1)}, bf16[1024,2048]{1,0:T(8,128)(2,1)}, u32[]{:S(2)}) copy-start(bf16[1024,2048]{1,0:T(8,128)(2,1)} %w_ref.1) | copy-start | bytes 12582916
  2.0 5.3 %collective-permute-start = (bf16[144,128]{1,0:T(8,128)(2,1)S(1)}, bf16[144,128]{1,0:T(8,128)(2,1)S(1)}, u32[]{:S(2)}, u32[]{:S(2)}) collective-permute-start(bf16[144,128]{1,0:T(8,128)(2,1)S(1)} %get-tuple-element.30), channel_id=1, source_target_pairs={{0,25},{1,24},{2,27},{3,26},{4,29},{5,28},{6,31},{7,30},{8,17},{9,... | collective-permute-start | bytes 110600 | tf_op jit(solution)/shard_map/ppermute | solution.py:389
  5.4 3.4 %collective-permute-start.1 = (bf16[144,128]{1,0:T(8,128)(2,1)S(1)}, bf16[144,128]{1,0:T(8,128)(2,1)S(1)}, u32[]{:S(2)}, u32[]{:S(2)}) collective-permute-start(bf16[144,128]{1,0:T(8,128)(2,1)S(1)} %get-tuple-element.31), channel_id=1, source_target_pairs={{0,17},{1,16},{2,19},{3,18},{4,21},{5,20},{6,23},{7,22},{8,25},{9,... | collective-permute-start | bytes 110600 | tf_op jit(solution)/shard_map/ppermute | solution.py:389
  6.2 3.7 %collective-permute-start.2 = (bf16[144,128]{1,0:T(8,128)(2,1)S(1)}, bf16[144,128]{1,0:T(8,128)(2,1)S(1)}, u32[]{:S(2)}, u32[]{:S(2)}) collective-permute-start(bf16[144,128]{1,0:T(8,128)(2,1)S(1)} %get-tuple-element.32), channel_id=1, source_target_pairs={{0,9},{1,8},{2,11},{3,10},{4,13},{5,12},{6,15},{7,14},{8,1},{9,0},... | collective-permute-start | bytes 110600 | tf_op jit(solution)/shard_map/ppermute | solution.py:389
  6.3 7.8 %copy-start = (bf16[8,2,2048]{2,1,0:T(2,128)(2,1)S(1)}, bf16[8,2,2048]{2,1,0:T(2,128)(2,1)}, u32[]{:S(2)}) copy-start(bf16[8,2,2048]{2,1,0:T(2,128)(2,1)} %residual_ref.1) | copy-start | bytes 196612
  6.3 7.8 %copy-start.1 = (s32[8,2,8]{2,1,0:T(2,128)S(1)}, s32[8,2,8]{2,1,0:T(2,128)}, u32[]{:S(2)}) copy-start(s32[8,2,8]{2,1,0:T(2,128)} %param.23) | copy-start | bytes 1540
  6.3 7.8 %copy-start.2 = (f32[8,2,8]{2,1,0:T(2,128)S(1)}, f32[8,2,8]{2,1,0:T(2,128)}, u32[]{:S(2)}) copy-start(f32[8,2,8]{2,1,0:T(2,128)} %param.24) | copy-start | bytes 1540
  6.3 7.8 %copy-start.3 = (bf16[2048]{0:T(1024)(128)(2,1)S(1)}, bf16[2048]{0:T(1024)(128)(2,1)}, u32[]{:S(2)}) copy-start(bf16[2048]{0:T(1024)(128)(2,1)} %param.22) | copy-start | bytes 12292
  6.3 3.6 %collective-permute-start.3 = (bf16[144,128]{1,0:T(8,128)(2,1)S(1)}, bf16[144,128]{1,0:T(8,128)(2,1)S(1)}, u32[]{:S(2)}, u32[]{:S(2)}) collective-permute-start(bf16[144,128]{1,0:T(8,128)(2,1)S(1)} %get-tuple-element.33), channel_id=1, source_target_pairs={{0,1},{1,0},{2,3},{3,2},{4,5},{5,4},{6,7},{7,6},{8,9},{9,8},{10,11... | collective-permute-start | bytes 110600 | tf_op jit(solution)/shard_map/ppermute | solution.py:389
  10.7 5.1 %collective-permute-start.7 = (bf16[16,2048]{1,0:T(8,128)(2,1)S(1)}, bf16[16,2048]{1,0:T(8,128)(2,1)S(1)}, u32[]{:S(2)}, u32[]{:S(2)}) collective-permute-start(bf16[16,2048]{1,0:T(8,128)(2,1)S(1)} %project.1), channel_id=1, source_target_pairs={{0,25},{1,24},{2,27},{3,26},{4,29},{5,28},{6,31},{7,30},{8,17},{9,... | collective-permute-start | bytes 196616 | tf_op jit(solution)/shard_map/ppermute | solution.py:389
  12.0 5.4 %collective-permute-start.6 = (bf16[16,2048]{1,0:T(8,128)(2,1)S(1)}, bf16[16,2048]{1,0:T(8,128)(2,1)S(1)}, u32[]{:S(2)}, u32[]{:S(2)}) collective-permute-start(bf16[16,2048]{1,0:T(8,128)(2,1)S(1)} %project.1), channel_id=1, source_target_pairs={{0,17},{1,16},{2,19},{3,18},{4,21},{5,20},{6,23},{7,22},{8,25},{9,... | collective-permute-start | bytes 196616 | tf_op jit(solution)/shard_map/ppermute | solution.py:389
  12.4 5.0 %collective-permute-start.5 = (bf16[16,2048]{1,0:T(8,128)(2,1)S(1)}, bf16[16,2048]{1,0:T(8,128)(2,1)S(1)}, u32[]{:S(2)}, u32[]{:S(2)}) collective-permute-start(bf16[16,2048]{1,0:T(8,128)(2,1)S(1)} %project.1), channel_id=1, source_target_pairs={{0,9},{1,8},{2,11},{3,10},{4,13},{5,12},{6,15},{7,14},{8,1},{9,0},... | collective-permute-start | bytes 196616 | tf_op jit(solution)/shard_map/ppermute | solution.py:389
  13.7 3.7 %collective-permute-start.4 = (bf16[16,2048]{1,0:T(8,128)(2,1)S(1)}, bf16[16,2048]{1,0:T(8,128)(2,1)S(1)}, u32[]{:S(2)}, u32[]{:S(2)}) collective-permute-start(bf16[16,2048]{1,0:T(8,128)(2,1)S(1)} %project.1), channel_id=1, source_target_pairs={{0,1},{1,0},{2,3},{3,2},{4,5},{5,4},{6,7},{7,6},{8,9},{9,8},{10,11... | collective-permute-start | bytes 196616 | tf_op jit(solution)/shard_map/ppermute | solution.py:389
  17.4 9.6 %copy-start.5 = (bf16[1,2048,1024]{2,1,0:T(8,128)(2,1)S(1)}, bf16[1,2048,1024]{2,1,0:T(8,128)(2,1)}, u32[]{:S(2)}) copy-start(bf16[1,2048,1024]{2,1,0:T(8,128)(2,1)} %gate_ref.1) | copy-start | bytes 12582916
  17.4 9.6 %copy-start.6 = (bf16[1,2048,1024]{2,1,0:T(8,128)(2,1)S(1)}, bf16[1,2048,1024]{2,1,0:T(8,128)(2,1)}, u32[]{:S(2)}) copy-start(bf16[1,2048,1024]{2,1,0:T(8,128)(2,1)} %up_ref.1) | copy-start | bytes 12582916
  17.4 9.5 %copy-start.7 = (bf16[1,1024,2048]{2,1,0:T(8,128)(2,1)S(1)}, bf16[1,1024,2048]{2,1,0:T(8,128)(2,1)}, u32[]{:S(2)}) copy-start(bf16[1,1024,2048]{2,1,0:T(8,128)(2,1)} %down_ref.1) | copy-start | bytes 12582916
  17.9 5.2 %collective-permute-start.8 = (bf16[8,2048]{1,0:T(8,128)(2,1)S(1)}, bf16[8,2048]{1,0:T(8,128)(2,1)S(1)}, u32[]{:S(2)}, u32[]{:S(2)}) collective-permute-start(bf16[8,2048]{1,0:T(8,128)(2,1)S(1)} %get-tuple-element.37), channel_id=1, source_target_pairs={{0,7},{1,6},{2,5},{3,4},{4,3},{5,2},{6,1},{7,0},{8,15},{9,14},{10,... | collective-permute-start | bytes 98312 | tf_op jit(solution)/shard_map/ppermute | solution.py:389
  21.3 4.3 %collective-permute-start.9 = (bf16[8,2048]{1,0:T(8,128)(2,1)S(1)}, bf16[8,2048]{1,0:T(8,128)(2,1)S(1)}, u32[]{:S(2)}, u32[]{:S(2)}) collective-permute-start(bf16[8,2048]{1,0:T(8,128)(2,1)S(1)} %get-tuple-element.38), channel_id=1, source_target_pairs={{0,5},{1,4},{2,7},{3,6},{4,1},{5,0},{6,3},{7,2},{8,13},{9,12},{10,... | collective-permute-start | bytes 98312 | tf_op jit(solution)/shard_map/ppermute | solution.py:389
  21.3 4.3 %collective-permute-start.10 = (bf16[8,2048]{1,0:T(8,128)(2,1)S(1)}, bf16[8,2048]{1,0:T(8,128)(2,1)S(1)}, u32[]{:S(2)}, u32[]{:S(2)}) collective-permute-start(bf16[8,2048]{1,0:T(8,128)(2,1)S(1)} %get-tuple-element.39), channel_id=1, source_target_pairs={{0,3},{1,2},{2,1},{3,0},{4,7},{5,6},{6,5},{7,4},{8,11},{9,10},{10,... | collective-permute-start | bytes 98312 | tf_op jit(solution)/shard_map/ppermute | solution.py:389
  25.6 1.3 %collective-permute-start.11 = (bf16[16,2048]{1,0:T(8,128)(2,1)S(1)}, bf16[16,2048]{1,0:T(8,128)(2,1)S(1)}, u32[]{:S(2)}, u32[]{:S(2)}) collective-permute-start(bf16[16,2048]{1,0:T(8,128)(2,1)S(1)} %get-tuple-element.42), channel_id=1, source_target_pairs={{0,1},{1,0},{2,3},{3,2},{4,5},{5,4},{6,7},{7,6},{8,9},{9,8},{10,11... | collective-permute-start | bytes 196616 | tf_op jit(solution)/shard_map/ppermute | solution.py:389
  28.8 1.3 %collective-permute-start.12 = (bf16[16,2048]{1,0:T(8,128)(2,1)S(1)}, bf16[16,2048]{1,0:T(8,128)(2,1)S(1)}, u32[]{:S(2)}, u32[]{:S(2)}) collective-permute-start(bf16[16,2048]{1,0:T(8,128)(2,1)S(1)} %get-tuple-element.44), channel_id=1, source_target_pairs={{0,1},{1,0},{2,3},{3,2},{4,5},{5,4},{6,7},{7,6},{8,9},{9,8},{10,11... | collective-permute-start | bytes 196616 | tf_op jit(solution)/shard_map/ppermute | solution.py:389
  30.2 5.3 %collective-permute-start.13 = (bf16[8,2048]{1,0:T(8,128)(2,1)S(1)}, bf16[8,2048]{1,0:T(8,128)(2,1)S(1)}, u32[]{:S(2)}, u32[]{:S(2)}) collective-permute-start(bf16[8,2048]{1,0:T(8,128)(2,1)S(1)} %get-tuple-element.45), channel_id=1, source_target_pairs={{0,7},{1,6},{2,5},{3,4},{4,3},{5,2},{6,1},{7,0},{8,15},{9,14},{10,... | collective-permute-start | bytes 98312 | tf_op jit(solution)/shard_map/ppermute | solution.py:389
  31.9 4.0 %collective-permute-start.14 = (bf16[8,2048]{1,0:T(8,128)(2,1)S(1)}, bf16[8,2048]{1,0:T(8,128)(2,1)S(1)}, u32[]{:S(2)}, u32[]{:S(2)}) collective-permute-start(bf16[8,2048]{1,0:T(8,128)(2,1)S(1)} %get-tuple-element.46), channel_id=1, source_target_pairs={{0,3},{1,2},{2,1},{3,0},{4,7},{5,6},{6,5},{7,4},{8,11},{9,10},{10,... | collective-permute-start | bytes 98312 | tf_op jit(solution)/shard_map/ppermute | solution.py:389
  32.6 4.2 %collective-permute-start.15 = (bf16[8,2048]{1,0:T(8,128)(2,1)S(1)}, bf16[8,2048]{1,0:T(8,128)(2,1)S(1)}, u32[]{:S(2)}, u32[]{:S(2)}) collective-permute-start(bf16[8,2048]{1,0:T(8,128)(2,1)S(1)} %get-tuple-element.47), channel_id=1, source_target_pairs={{0,5},{1,4},{2,7},{3,6},{4,1},{5,0},{6,3},{7,2},{8,13},{9,12},{10,... | collective-permute-start | bytes 98312 | tf_op jit(solution)/shard_map/ppermute | solution.py:389
  37.1 5.3 %collective-permute-start.18 = (bf16[16,2048]{1,0:T(8,128)(2,1)S(1)}, bf16[16,2048]{1,0:T(8,128)(2,1)S(1)}, u32[]{:S(2)}, u32[]{:S(2)}) collective-permute-start(bf16[16,2048]{1,0:T(8,128)(2,1)S(1)} %combine.1.refs_0_), channel_id=1, source_target_pairs={{0,24},{1,25},{2,26},{3,27},{4,28},{5,29},{6,30},{7,31},{8,16},{9,... | collective-permute-start | bytes 196616 | tf_op jit(solution)/shard_map/ppermute | solution.py:389
  38.9 4.7 %collective-permute-start.17 = (bf16[16,2048]{1,0:T(8,128)(2,1)S(1)}, bf16[16,2048]{1,0:T(8,128)(2,1)S(1)}, u32[]{:S(2)}, u32[]{:S(2)}) collective-permute-start(bf16[16,2048]{1,0:T(8,128)(2,1)S(1)} %combine.1.refs_0_), channel_id=1, source_target_pairs={{0,16},{1,17},{2,18},{3,19},{4,20},{5,21},{6,22},{7,23},{8,24},{9,... | collective-permute-start | bytes 196616 | tf_op jit(solution)/shard_map/ppermute | solution.py:389
  39.3 4.4 %collective-permute-start.16 = (bf16[16,2048]{1,0:T(8,128)(2,1)S(1)}, bf16[16,2048]{1,0:T(8,128)(2,1)S(1)}, u32[]{:S(2)}, u32[]{:S(2)}) collective-permute-start(bf16[16,2048]{1,0:T(8,128)(2,1)S(1)} %combine.1.refs_0_), channel_id=1, source_target_pairs={{0,8},{1,9},{2,10},{3,11},{4,12},{5,13},{6,14},{7,15},{8,0},{9,1},... | collective-permute-start | bytes 196616 | tf_op jit(solution)/shard_map/ppermute | solution.py:389

commit v10 on v9

--- a/solution.py
+++ b/solution.py
@@ -201,7 +201,7 @@
                 if sub > 0:
                     piece = jnp.concatenate([stats[:, sub * span :], stats[:, : sub * span]], 1)
                 blocks[dest, span:, :] = piece
-    for k, out in zip(reversed(range(ctx_count)), outs):
+    for k, out in zip((*reversed(range(2, ctx_count)), 0, 1), outs):
         out[...] = blocks[me ^ k]
 
 
@@ -436,7 +436,7 @@
         + [pltpu.SemaphoreType.DMA((len(inputs),))],
         cost=cost(10),
     )
-    got = [move(x, j, 1) for j, x in zip(reversed(range(n)), sent)]
+    got = [move(x, j, 1) for j, x in zip((*reversed(range(2, n)), 0, 1), sent)]
     selector, weight_high, weight_low, residual_rows, gain_rows = call(
         functools.partial(route_kernel, n, exp_count, capacity),
         "route",

time: 44.5 us -> 44.3 us (level)
  no operation moved by 1% of the time
where the time goes in v10:
time: 44.3 us; the launch traced here: 44.1 us
  starting transfers between devices  20.3 us (46%)
  waiting for transfers between devices  17.3 us (39%)
  Pallas kernels  6.36 us (14%)
    ppermute x19, starting transfers between devices, move(): return lax.ppermute(block, ('ctx', 'exp'), pairs)  20.3 us
    ppermute x19, waiting for transfers between devices, move(): return lax.ppermute(block, ('ctx', 'exp'), pairs)  17.3 us
    pallas_call x9, Pallas kernels, call(): pl.pallas_call(kernel, name=name, in_specs=in_specs, out_specs=[out_spec...  6.36 us
  transfers between devices with their start and end apart: 19, of which 14 were waited for; matrix products, arithmetic and copies ran while one was open for 0% of the time, Pallas kernels for 0%

profile of v10, /device:TPU:0, one launch (start us, length us, event | category | flops | bytes accessed | tf_op | source)
XLA Modules:
  0.0 44.1 jit_solution(6177435287837828503)
XLA Ops:
  0.0 2.0 %attend.1 = (bf16[144,128]{1,0:T(8,128)(2,1)S(1)}, bf16[144,128]{1,0:T(8,128)(2,1)S(1)}, bf16[144,128]{1,0:T(8,128)(2,1)S(1)}, bf16[144,128]{1,0:T(8,128)(2,1)S(1)}) custom-call(s32[1]{0:T(128)} %bitcast.me_ref, s32[8]{0:T(128)} %len_hbm.1, bf16[8,2,4096]{2,1,0:T(2,128)(2,1)} %q_hbm.1, bf16[8,64,256]{2,1,0:T(8,128)(2,1)} %k_hbm.1, ...), custom_call_target="tpu_custom_call" | custom-call | flops 10000000000 | bytes 1048576 | tf_op jit(solution)/shard_map/attend/pallas_call | solution.py:366
  2.0 3.4 %collective-permute-start = (bf16[144,128]{1,0:T(8,128)(2,1)S(1)}, bf16[144,128]{1,0:T(8,128)(2,1)S(1)}, u32[]{:S(2)}, u32[]{:S(2)}) collective-permute-start(bf16[144,128]{1,0:T(8,128)(2,1)S(1)} %get-tuple-element.30), channel_id=1, source_target_pairs={{0,25},{1,24},{2,27},{3,26},{4,29},{5,28},{6,31},{7,30},{8,17},{9,... | collective-permute-start | bytes 110600 | tf_op jit(solution)/shard_map/ppermute | solution.py:389
  5.4 0.8 %collective-permute-start.1 = (bf16[144,128]{1,0:T(8,128)(2,1)S(1)}, bf16[144,128]{1,0:T(8,128)(2,1)S(1)}, u32[]{:S(2)}, u32[]{:S(2)}) collective-permute-start(bf16[144,128]{1,0:T(8,128)(2,1)S(1)} %get-tuple-element.31), channel_id=1, source_target_pairs={{0,17},{1,16},{2,19},{3,18},{4,21},{5,20},{6,23},{7,22},{8,25},{9,... | collective-permute-start | bytes 110600 | tf_op jit(solution)/shard_map/ppermute | solution.py:389
  6.4 0.9 %collective-permute-done.rest_0_ = bf16[144,128]{1,0:T(8,128)(2,1)S(1)} collective-permute-done((bf16[144,128]{1,0:T(8,128)(2,1)S(1)}, bf16[144,128]{1,0:T(8,128)(2,1)S(1)}, u32[]{:S(2)}, u32[]{:S(2)}) %collective-permute-start) | collective-permute-done | bytes 36896 | tf_op jit(solution)/shard_map/ppermute | solution.py:389
  7.3 1.5 %collective-permute-done.1.rest_1_ = bf16[144,128]{1,0:T(8,128)(2,1)S(1)} collective-permute-done((bf16[144,128]{1,0:T(8,128)(2,1)S(1)}, bf16[144,128]{1,0:T(8,128)(2,1)S(1)}, u32[]{:S(2)}, u32[]{:S(2)}) %collective-permute-start.1) | collective-permute-done | bytes 36896 | tf_op jit(solution)/shard_map/ppermute | solution.py:389
  8.8 0.9 %collective-permute-done.3.rest_3_ = bf16[144,128]{1,0:T(8,128)(2,1)S(1)} collective-permute-done((bf16[144,128]{1,0:T(8,128)(2,1)S(1)}, bf16[144,128]{1,0:T(8,128)(2,1)S(1)}, u32[]{:S(2)}, u32[]{:S(2)}) %collective-permute-start.3) | collective-permute-done | bytes 36896 | tf_op jit(solution)/shard_map/ppermute | solution.py:389
  9.7 0.8 %project.1 = bf16[16,2048]{1,0:T(8,128)(2,1)S(1)} custom-call(bf16[1024,2048]{1,0:T(8,128)(2,1)S(1)} %copy-done.4, bf16[144,128]{1,0:T(8,128)(2,1)S(1)} %collective-permute-done.rest_0_, bf16[144,128]{1,0:T(8,128)(2,1)S(1)} %collective-permute-done.1.rest_1_, bf16[144,128]{1,0:T(8,128)(2,1)S(1)} %collective-permute-done.2.rest_2_, ...), custom_call_target="tpu_custom_call" | custom-call | flops 10000000000 | bytes 1048576 | tf_op jit(solution)/shard_map/project/pallas_call | solution.py:366
  10.5 1.7 %collective-permute-start.7 = (bf16[16,2048]{1,0:T(8,128)(2,1)S(1)}, bf16[16,2048]{1,0:T(8,128)(2,1)S(1)}, u32[]{:S(2)}, u32[]{:S(2)}) collective-permute-start(bf16[16,2048]{1,0:T(8,128)(2,1)S(1)} %project.1), channel_id=1, source_target_pairs={{0,25},{1,24},{2,27},{3,26},{4,29},{5,28},{6,31},{7,30},{8,17},{9,... | collective-permute-start | bytes 196616 | tf_op jit(solution)/shard_map/ppermute | solution.py:389
  12.4 1.4 %collective-permute-start.5 = (bf16[16,2048]{1,0:T(8,128)(2,1)S(1)}, bf16[16,2048]{1,0:T(8,128)(2,1)S(1)}, u32[]{:S(2)}, u32[]{:S(2)}) collective-permute-start(bf16[16,2048]{1,0:T(8,128)(2,1)S(1)} %project.1), channel_id=1, source_target_pairs={{0,9},{1,8},{2,11},{3,10},{4,13},{5,12},{6,15},{7,14},{8,1},{9,0},... | collective-permute-start | bytes 196616 | tf_op jit(solution)/shard_map/ppermute | solution.py:389
  14.1 1.1 %collective-permute-done.7.rest_3_ = bf16[16,2048]{1,0:T(8,128)(2,1)S(1)} collective-permute-done((bf16[16,2048]{1,0:T(8,128)(2,1)S(1)}, bf16[16,2048]{1,0:T(8,128)(2,1)S(1)}, u32[]{:S(2)}, u32[]{:S(2)}) %collective-permute-start.7) | collective-permute-done | bytes 65568 | tf_op jit(solution)/shard_map/ppermute | solution.py:389
  15.2 2.0 %collective-permute-done.6.rest_2_ = bf16[16,2048]{1,0:T(8,128)(2,1)S(1)} collective-permute-done((bf16[16,2048]{1,0:T(8,128)(2,1)S(1)}, bf16[16,2048]{1,0:T(8,128)(2,1)S(1)}, u32[]{:S(2)}, u32[]{:S(2)}) %collective-permute-start.6) | collective-permute-done | bytes 65568 | tf_op jit(solution)/shard_map/ppermute | solution.py:389
  17.2 0.4 %dispatch.1 = (f32[16,2048]{1,0:T(8,128)S(1)}, bf16[8,2048]{1,0:T(8,128)(2,1)S(1)}, bf16[8,2048]{1,0:T(8,128)(2,1)S(1)}, bf16[8,2048]{1,0:T(8,128)(2,1)S(1)}, bf16[8,2048]{1,0:T(8,128)(2,1)S(1)}) custom-call(f32[16,2048]{1,0:T(8,128)S(1)} %get-tuple-element.27.residual_ref, f32[16,2048]{1,0:T(8,128)S(1)} %get-tuple-element.28.gain_ref, ...), custom_call_target="tpu_custom_call" | custom-call | flops 10000000000 | bytes 1048576 | tf_op jit(solution)/shard_map/dispatch/pallas_call | solution.py:366
  17.7 3.4 %collective-permute-start.8 = (bf16[8,2048]{1,0:T(8,128)(2,1)S(1)}, bf16[8,2048]{1,0:T(8,128)(2,1)S(1)}, u32[]{:S(2)}, u32[]{:S(2)}) collective-permute-start(bf16[8,2048]{1,0:T(8,128)(2,1)S(1)} %get-tuple-element.37), channel_id=1, source_target_pairs={{0,7},{1,6},{2,5},{3,4},{4,3},{5,2},{6,1},{7,0},{8,15},{9,14},{10,... | collective-permute-start | bytes 98312 | tf_op jit(solution)/shard_map/ppermute | solution.py:389
  21.1 0.6 %collective-permute-start.10 = (bf16[8,2048]{1,0:T(8,128)(2,1)S(1)}, bf16[8,2048]{1,0:T(8,128)(2,1)S(1)}, u32[]{:S(2)}, u32[]{:S(2)}) collective-permute-start(bf16[8,2048]{1,0:T(8,128)(2,1)S(1)} %get-tuple-element.39), channel_id=1, source_target_pairs={{0,3},{1,2},{2,1},{3,0},{4,7},{5,6},{6,5},{7,4},{8,11},{9,10},{10,... | collective-permute-start | bytes 98312 | tf_op jit(solution)/shard_map/ppermute | solution.py:389
  21.7 1.2 %collective-permute-done.8.refs_0_ = bf16[8,2048]{1,0:T(8,128)(2,1)S(1)} collective-permute-done((bf16[8,2048]{1,0:T(8,128)(2,1)S(1)}, bf16[8,2048]{1,0:T(8,128)(2,1)S(1)}, u32[]{:S(2)}, u32[]{:S(2)}) %collective-permute-start.8) | collective-permute-done | bytes 32800 | tf_op jit(solution)/shard_map/ppermute | solution.py:389
  22.9 2.5 %collective-permute-done.9.refs_1_ = bf16[8,2048]{1,0:T(8,128)(2,1)S(1)} collective-permute-done((bf16[8,2048]{1,0:T(8,128)(2,1)S(1)}, bf16[8,2048]{1,0:T(8,128)(2,1)S(1)}, u32[]{:S(2)}, u32[]{:S(2)}) %collective-permute-start.9) | collective-permute-done | bytes 32800 | tf_op jit(solution)/shard_map/ppermute | solution.py:389
  25.4 0.4 collective-permute-start.11
  25.8 0.9 %collective-permute-done.11.got_ref = bf16[16,2048]{1,0:T(8,128)(2,1)S(1)} collective-permute-done((bf16[16,2048]{1,0:T(8,128)(2,1)S(1)}, bf16[16,2048]{1,0:T(8,128)(2,1)S(1)}, u32[]{:S(2)}, u32[]{:S(2)}) %collective-permute-start.11) | collective-permute-done | bytes 65568 | tf_op jit(solution)/shard_map/ppermute | solution.py:389
  26.7 1.9 %experts.1 = (bf16[16,2048]{1,0:T(8,128)(2,1)S(1)}, bf16[16,2048]{1,0:T(8,128)(2,1)S(1)}) custom-call(bf16[16,2048]{1,0:T(8,128)(2,1)S(1)} %get-tuple-element.41.kept_ref, bf16[16,2048]{1,0:T(8,128)(2,1)S(1)} %collective-permute-done.11.got_ref, bf16[1,2048,1024]{2,1,0:T(8,128)(2,1)S(1)} %copy-done.5, bf16[1,2048,1024]{2,1,0:T(8,128)(2,1)S(1)} %copy-done.6, ...), custom_call_target="tpu_custom_call" | custom-call | flops 10000000000 | bytes 1048576 | tf_op jit(solution)/shard_map/experts/pallas_call | solution.py:366
  29.0 0.9 %collective-permute-done.12.got_ref = bf16[16,2048]{1,0:T(8,128)(2,1)S(1)} collective-permute-done((bf16[16,2048]{1,0:T(8,128)(2,1)S(1)}, bf16[16,2048]{1,0:T(8,128)(2,1)S(1)}, u32[]{:S(2)}, u32[]{:S(2)}) %collective-permute-start.12) | collective-permute-done | bytes 65568 | tf_op jit(solution)/shard_map/ppermute | solution.py:389
  30.0 1.8 %collective-permute-start.13 = (bf16[8,2048]{1,0:T(8,128)(2,1)S(1)}, bf16[8,2048]{1,0:T(8,128)(2,1)S(1)}, u32[]{:S(2)}, u32[]{:S(2)}) collective-permute-start(bf16[8,2048]{1,0:T(8,128)(2,1)S(1)} %get-tuple-element.45), channel_id=1, source_target_pairs={{0,7},{1,6},{2,5},{3,4},{4,3},{5,2},{6,1},{7,0},{8,15},{9,14},{10,... | collective-permute-start | bytes 98312 | tf_op jit(solution)/shard_map/ppermute | solution.py:389
  31.8 0.6 %collective-permute-start.14 = (bf16[8,2048]{1,0:T(8,128)(2,1)S(1)}, bf16[8,2048]{1,0:T(8,128)(2,1)S(1)}, u32[]{:S(2)}, u32[]{:S(2)}) collective-permute-start(bf16[8,2048]{1,0:T(8,128)(2,1)S(1)} %get-tuple-element.46), channel_id=1, source_target_pairs={{0,3},{1,2},{2,1},{3,0},{4,7},{5,6},{6,5},{7,4},{8,11},{9,10},{10,... | collective-permute-start | bytes 98312 | tf_op jit(solution)/shard_map/ppermute | solution.py:389
  32.3 1.8 %collective-permute-start.15 = (bf16[8,2048]{1,0:T(8,128)(2,1)S(1)}, bf16[8,2048]{1,0:T(8,128)(2,1)S(1)}, u32[]{:S(2)}, u32[]{:S(2)}) collective-permute-start(bf16[8,2048]{1,0:T(8,128)(2,1)S(1)} %get-tuple-element.47), channel_id=1, source_target_pairs={{0,5},{1,4},{2,7},{3,6},{4,1},{5,0},{6,3},{7,2},{8,13},{9,12},{10,... | collective-permute-start | bytes 98312 | tf_op jit(solution)/shard_map/ppermute | solution.py:389
  34.1 1.2 %collective-permute-done.13.refs_0_ = bf16[8,2048]{1,0:T(8,128)(2,1)S(1)} collective-permute-done((bf16[8,2048]{1,0:T(8,128)(2,1)S(1)}, bf16[8,2048]{1,0:T(8,128)(2,1)S(1)}, u32[]{:S(2)}, u32[]{:S(2)}) %collective-permute-start.13) | collective-permute-done | bytes 32800 | tf_op jit(solution)/shard_map/ppermute | solution.py:389
  35.3 0.7 %collective-permute-done.14.refs_1_ = bf16[8,2048]{1,0:T(8,128)(2,1)S(1)} collective-permute-done((bf16[8,2048]{1,0:T(8,128)(2,1)S(1)}, bf16[8,2048]{1,0:T(8,128)(2,1)S(1)}, u32[]{:S(2)}, u32[]{:S(2)}) %collective-permute-start.14) | collective-permute-done | bytes 32800 | tf_op jit(solution)/shard_map/ppermute | solution.py:389
  36.0 0.6 %collective-permute-done.15.refs_2_ = bf16[8,2048]{1,0:T(8,128)(2,1)S(1)} collective-permute-done((bf16[8,2048]{1,0:T(8,128)(2,1)S(1)}, bf16[8,2048]{1,0:T(8,128)(2,1)S(1)}, u32[]{:S(2)}, u32[]{:S(2)}) %collective-permute-start.15) | collective-permute-done | bytes 32800 | tf_op jit(solution)/shard_map/ppermute | solution.py:389
  36.8 1.5 %collective-permute-start.18 = (bf16[16,2048]{1,0:T(8,128)(2,1)S(1)}, bf16[16,2048]{1,0:T(8,128)(2,1)S(1)}, u32[]{:S(2)}, u32[]{:S(2)}) collective-permute-start(bf16[16,2048]{1,0:T(8,128)(2,1)S(1)} %combine.1.refs_0_), channel_id=1, source_target_pairs={{0,24},{1,25},{2,26},{3,27},{4,28},{5,29},{6,30},{7,31},{8,16},{9,... | collective-permute-start | bytes 196616 | tf_op jit(solution)/shard_map/ppermute | solution.py:389
  38.3 0.6 %collective-permute-start.17 = (bf16[16,2048]{1,0:T(8,128)(2,1)S(1)}, bf16[16,2048]{1,0:T(8,128)(2,1)S(1)}, u32[]{:S(2)}, u32[]{:S(2)}) collective-permute-start(bf16[16,2048]{1,0:T(8,128)(2,1)S(1)} %combine.1.refs_0_), channel_id=1, source_target_pairs={{0,16},{1,17},{2,18},{3,19},{4,20},{5,21},{6,22},{7,23},{8,24},{9,... | collective-permute-start | bytes 196616 | tf_op jit(solution)/shard_map/ppermute | solution.py:389
  38.9 1.4 %collective-permute-start.16 = (bf16[16,2048]{1,0:T(8,128)(2,1)S(1)}, bf16[16,2048]{1,0:T(8,128)(2,1)S(1)}, u32[]{:S(2)}, u32[]{:S(2)}) collective-permute-start(bf16[16,2048]{1,0:T(8,128)(2,1)S(1)} %combine.1.refs_0_), channel_id=1, source_target_pairs={{0,8},{1,9},{2,10},{3,11},{4,12},{5,13},{6,14},{7,15},{8,0},{9,1},... | collective-permute-start | bytes 196616 | tf_op jit(solution)/shard_map/ppermute | solution.py:389
  40.4 1.7 %collective-permute-done.18.refs_3_ = bf16[16,2048]{1,0:T(8,128)(2,1)S(1)} collective-permute-done((bf16[16,2048]{1,0:T(8,128)(2,1)S(1)}, bf16[16,2048]{1,0:T(8,128)(2,1)S(1)}, u32[]{:S(2)}, u32[]{:S(2)}) %collective-permute-start.18) | collective-permute-done | bytes 65568 | tf_op jit(solution)/shard_map/ppermute | solution.py:389
  42.1 1.2 %collective-permute-done.17.refs_2_ = bf16[16,2048]{1,0:T(8,128)(2,1)S(1)} collective-permute-done((bf16[16,2048]{1,0:T(8,128)(2,1)S(1)}, bf16[16,2048]{1,0:T(8,128)(2,1)S(1)}, u32[]{:S(2)}, u32[]{:S(2)}) %collective-permute-start.17) | collective-permute-done | bytes 65568 | tf_op jit(solution)/shard_map/ppermute | solution.py:389
  43.4 0.8 %finish.1 = bf16[8,2,2048]{2,1,0:T(2,128)(2,1)} custom-call(f32[16,2048]{1,0:T(8,128)S(1)} %get-tuple-element.34.state_ref, bf16[16,2048]{1,0:T(8,128)(2,1)S(1)} %combine.1.refs_0_, bf16[16,2048]{1,0:T(8,128)(2,1)S(1)} %collective-permute-done.16.refs_1_, bf16[16,2048]{1,0:T(8,128)(2,1)S(1)} %collective-permute-done.17.refs_2_, ...), custom_call_target="tpu_custom_call" | custom-call | tf_op jit(solution)/shard_map/finish/pallas_call | solution.py:366
  (31 shorter events, 1.5 us)
Async XLA Ops:
  0.0 9.7 %copy-start.4 = (bf16[1024,2048]{1,0:T(8,128)(2,1)S(1)}, bf16[1024,2048]{1,0:T(8,128)(2,1)}, u32[]{:S(2)}) copy-start(bf16[1024,2048]{1,0:T(8,128)(2,1)} %w_ref.1) | copy-start | bytes 12582916
  2.0 5.3 %collective-permute-start = (bf16[144,128]{1,0:T(8,128)(2,1)S(1)}, bf16[144,128]{1,0:T(8,128)(2,1)S(1)}, u32[]{:S(2)}, u32[]{:S(2)}) collective-permute-start(bf16[144,128]{1,0:T(8,128)(2,1)S(1)} %get-tuple-element.30), channel_id=1, source_target_pairs={{0,25},{1,24},{2,27},{3,26},{4,29},{5,28},{6,31},{7,30},{8,17},{9,... | collective-permute-start | bytes 110600 | tf_op jit(solution)/shard_map/ppermute | solution.py:389
  5.4 3.4 %collective-permute-start.1 = (bf16[144,128]{1,0:T(8,128)(2,1)S(1)}, bf16[144,128]{1,0:T(8,128)(2,1)S(1)}, u32[]{:S(2)}, u32[]{:S(2)}) collective-permute-start(bf16[144,128]{1,0:T(8,128)(2,1)S(1)} %get-tuple-element.31), channel_id=1, source_target_pairs={{0,17},{1,16},{2,19},{3,18},{4,21},{5,20},{6,23},{7,22},{8,25},{9,... | collective-permute-start | bytes 110600 | tf_op jit(solution)/shard_map/ppermute | solution.py:389
  6.2 2.6 %collective-permute-start.2 = (bf16[144,128]{1,0:T(8,128)(2,1)S(1)}, bf16[144,128]{1,0:T(8,128)(2,1)S(1)}, u32[]{:S(2)}, u32[]{:S(2)}) collective-permute-start(bf16[144,128]{1,0:T(8,128)(2,1)S(1)} %get-tuple-element.32), channel_id=1, source_target_pairs={{0,1},{1,0},{2,3},{3,2},{4,5},{5,4},{6,7},{7,6},{8,9},{9,8},{10,11... | collective-permute-start | bytes 110600 | tf_op jit(solution)/shard_map/ppermute | solution.py:389
  6.2 7.7 %copy-start = (bf16[8,2,2048]{2,1,0:T(2,128)(2,1)S(1)}, bf16[8,2,2048]{2,1,0:T(2,128)(2,1)}, u32[]{:S(2)}) copy-start(bf16[8,2,2048]{2,1,0:T(2,128)(2,1)} %residual_ref.1) | copy-start | bytes 196612
  6.2 7.7 %copy-start.1 = (s32[8,2,8]{2,1,0:T(2,128)S(1)}, s32[8,2,8]{2,1,0:T(2,128)}, u32[]{:S(2)}) copy-start(s32[8,2,8]{2,1,0:T(2,128)} %param.23) | copy-start | bytes 1540
  6.2 7.7 %copy-start.2 = (f32[8,2,8]{2,1,0:T(2,128)S(1)}, f32[8,2,8]{2,1,0:T(2,128)}, u32[]{:S(2)}) copy-start(f32[8,2,8]{2,1,0:T(2,128)} %param.24) | copy-start | bytes 1540
  6.2 7.7 %copy-start.3 = (bf16[2048]{0:T(1024)(128)(2,1)S(1)}, bf16[2048]{0:T(1024)(128)(2,1)}, u32[]{:S(2)}) copy-start(bf16[2048]{0:T(1024)(128)(2,1)} %param.22) | copy-start | bytes 12292
  6.2 3.4 %collective-permute-start.3 = (bf16[144,128]{1,0:T(8,128)(2,1)S(1)}, bf16[144,128]{1,0:T(8,128)(2,1)S(1)}, u32[]{:S(2)}, u32[]{:S(2)}) collective-permute-start(bf16[144,128]{1,0:T(8,128)(2,1)S(1)} %get-tuple-element.33), channel_id=1, source_target_pairs={{0,9},{1,8},{2,11},{3,10},{4,13},{5,12},{6,15},{7,14},{8,1},{9,0},... | collective-permute-start | bytes 110600 | tf_op jit(solution)/shard_map/ppermute | solution.py:389
  10.5 4.7 %collective-permute-start.7 = (bf16[16,2048]{1,0:T(8,128)(2,1)S(1)}, bf16[16,2048]{1,0:T(8,128)(2,1)S(1)}, u32[]{:S(2)}, u32[]{:S(2)}) collective-permute-start(bf16[16,2048]{1,0:T(8,128)(2,1)S(1)} %project.1), channel_id=1, source_target_pairs={{0,25},{1,24},{2,27},{3,26},{4,29},{5,28},{6,31},{7,30},{8,17},{9,... | collective-permute-start | bytes 196616 | tf_op jit(solution)/shard_map/ppermute | solution.py:389
  12.1 5.1 %collective-permute-start.6 = (bf16[16,2048]{1,0:T(8,128)(2,1)S(1)}, bf16[16,2048]{1,0:T(8,128)(2,1)S(1)}, u32[]{:S(2)}, u32[]{:S(2)}) collective-permute-start(bf16[16,2048]{1,0:T(8,128)(2,1)S(1)} %project.1), channel_id=1, source_target_pairs={{0,17},{1,16},{2,19},{3,18},{4,21},{5,20},{6,23},{7,22},{8,25},{9,... | collective-permute-start | bytes 196616 | tf_op jit(solution)/shard_map/ppermute | solution.py:389
  12.4 4.8 %collective-permute-start.5 = (bf16[16,2048]{1,0:T(8,128)(2,1)S(1)}, bf16[16,2048]{1,0:T(8,128)(2,1)S(1)}, u32[]{:S(2)}, u32[]{:S(2)}) collective-permute-start(bf16[16,2048]{1,0:T(8,128)(2,1)S(1)} %project.1), channel_id=1, source_target_pairs={{0,9},{1,8},{2,11},{3,10},{4,13},{5,12},{6,15},{7,14},{8,1},{9,0},... | collective-permute-start | bytes 196616 | tf_op jit(solution)/shard_map/ppermute | solution.py:389
  13.8 3.4 %collective-permute-start.4 = (bf16[16,2048]{1,0:T(8,128)(2,1)S(1)}, bf16[16,2048]{1,0:T(8,128)(2,1)S(1)}, u32[]{:S(2)}, u32[]{:S(2)}) collective-permute-start(bf16[16,2048]{1,0:T(8,128)(2,1)S(1)} %project.1), channel_id=1, source_target_pairs={{0,1},{1,0},{2,3},{3,2},{4,5},{5,4},{6,7},{7,6},{8,9},{9,8},{10,11... | collective-permute-start | bytes 196616 | tf_op jit(solution)/shard_map/ppermute | solution.py:389
  17.2 9.5 %copy-start.5 = (bf16[1,2048,1024]{2,1,0:T(8,128)(2,1)S(1)}, bf16[1,2048,1024]{2,1,0:T(8,128)(2,1)}, u32[]{:S(2)}) copy-start(bf16[1,2048,1024]{2,1,0:T(8,128)(2,1)} %gate_ref.1) | copy-start | bytes 12582916
  17.2 9.5 %copy-start.6 = (bf16[1,2048,1024]{2,1,0:T(8,128)(2,1)S(1)}, bf16[1,2048,1024]{2,1,0:T(8,128)(2,1)}, u32[]{:S(2)}) copy-start(bf16[1,2048,1024]{2,1,0:T(8,128)(2,1)} %up_ref.1) | copy-start | bytes 12582916
  17.2 9.5 %copy-start.7 = (bf16[1,1024,2048]{2,1,0:T(8,128)(2,1)S(1)}, bf16[1,1024,2048]{2,1,0:T(8,128)(2,1)}, u32[]{:S(2)}) copy-start(bf16[1,1024,2048]{2,1,0:T(8,128)(2,1)} %down_ref.1) | copy-start | bytes 12582916
  17.7 5.2 %collective-permute-start.8 = (bf16[8,2048]{1,0:T(8,128)(2,1)S(1)}, bf16[8,2048]{1,0:T(8,128)(2,1)S(1)}, u32[]{:S(2)}, u32[]{:S(2)}) collective-permute-start(bf16[8,2048]{1,0:T(8,128)(2,1)S(1)} %get-tuple-element.37), channel_id=1, source_target_pairs={{0,7},{1,6},{2,5},{3,4},{4,3},{5,2},{6,1},{7,0},{8,15},{9,14},{10,... | collective-permute-start | bytes 98312 | tf_op jit(solution)/shard_map/ppermute | solution.py:389
  21.1 4.3 %collective-permute-start.9 = (bf16[8,2048]{1,0:T(8,128)(2,1)S(1)}, bf16[8,2048]{1,0:T(8,128)(2,1)S(1)}, u32[]{:S(2)}, u32[]{:S(2)}) collective-permute-start(bf16[8,2048]{1,0:T(8,128)(2,1)S(1)} %get-tuple-element.38), channel_id=1, source_target_pairs={{0,5},{1,4},{2,7},{3,6},{4,1},{5,0},{6,3},{7,2},{8,13},{9,12},{10,... | collective-permute-start | bytes 98312 | tf_op jit(solution)/shard_map/ppermute | solution.py:389
  21.1 4.3 %collective-permute-start.10 = (bf16[8,2048]{1,0:T(8,128)(2,1)S(1)}, bf16[8,2048]{1,0:T(8,128)(2,1)S(1)}, u32[]{:S(2)}, u32[]{:S(2)}) collective-permute-start(bf16[8,2048]{1,0:T(8,128)(2,1)S(1)} %get-tuple-element.39), channel_id=1, source_target_pairs={{0,3},{1,2},{2,1},{3,0},{4,7},{5,6},{6,5},{7,4},{8,11},{9,10},{10,... | collective-permute-start | bytes 98312 | tf_op jit(solution)/shard_map/ppermute | solution.py:389
  25.4 1.3 %collective-permute-start.11 = (bf16[16,2048]{1,0:T(8,128)(2,1)S(1)}, bf16[16,2048]{1,0:T(8,128)(2,1)S(1)}, u32[]{:S(2)}, u32[]{:S(2)}) collective-permute-start(bf16[16,2048]{1,0:T(8,128)(2,1)S(1)} %get-tuple-element.42), channel_id=1, source_target_pairs={{0,1},{1,0},{2,3},{3,2},{4,5},{5,4},{6,7},{7,6},{8,9},{9,8},{10,11... | collective-permute-start | bytes 196616 | tf_op jit(solution)/shard_map/ppermute | solution.py:389
  28.6 1.3 %collective-permute-start.12 = (bf16[16,2048]{1,0:T(8,128)(2,1)S(1)}, bf16[16,2048]{1,0:T(8,128)(2,1)S(1)}, u32[]{:S(2)}, u32[]{:S(2)}) collective-permute-start(bf16[16,2048]{1,0:T(8,128)(2,1)S(1)} %get-tuple-element.44), channel_id=1, source_target_pairs={{0,1},{1,0},{2,3},{3,2},{4,5},{5,4},{6,7},{7,6},{8,9},{9,8},{10,11... | collective-permute-start | bytes 196616 | tf_op jit(solution)/shard_map/ppermute | solution.py:389
  30.0 5.3 %collective-permute-start.13 = (bf16[8,2048]{1,0:T(8,128)(2,1)S(1)}, bf16[8,2048]{1,0:T(8,128)(2,1)S(1)}, u32[]{:S(2)}, u32[]{:S(2)}) collective-permute-start(bf16[8,2048]{1,0:T(8,128)(2,1)S(1)} %get-tuple-element.45), channel_id=1, source_target_pairs={{0,7},{1,6},{2,5},{3,4},{4,3},{5,2},{6,1},{7,0},{8,15},{9,14},{10,... | collective-permute-start | bytes 98312 | tf_op jit(solution)/shard_map/ppermute | solution.py:389
  31.8 4.2 %collective-permute-start.14 = (bf16[8,2048]{1,0:T(8,128)(2,1)S(1)}, bf16[8,2048]{1,0:T(8,128)(2,1)S(1)}, u32[]{:S(2)}, u32[]{:S(2)}) collective-permute-start(bf16[8,2048]{1,0:T(8,128)(2,1)S(1)} %get-tuple-element.46), channel_id=1, source_target_pairs={{0,3},{1,2},{2,1},{3,0},{4,7},{5,6},{6,5},{7,4},{8,11},{9,10},{10,... | collective-permute-start | bytes 98312 | tf_op jit(solution)/shard_map/ppermute | solution.py:389
  32.3 4.2 %collective-permute-start.15 = (bf16[8,2048]{1,0:T(8,128)(2,1)S(1)}, bf16[8,2048]{1,0:T(8,128)(2,1)S(1)}, u32[]{:S(2)}, u32[]{:S(2)}) collective-permute-start(bf16[8,2048]{1,0:T(8,128)(2,1)S(1)} %get-tuple-element.47), channel_id=1, source_target_pairs={{0,5},{1,4},{2,7},{3,6},{4,1},{5,0},{6,3},{7,2},{8,13},{9,12},{10,... | collective-permute-start | bytes 98312 | tf_op jit(solution)/shard_map/ppermute | solution.py:389
  36.8 5.3 %collective-permute-start.18 = (bf16[16,2048]{1,0:T(8,128)(2,1)S(1)}, bf16[16,2048]{1,0:T(8,128)(2,1)S(1)}, u32[]{:S(2)}, u32[]{:S(2)}) collective-permute-start(bf16[16,2048]{1,0:T(8,128)(2,1)S(1)} %combine.1.refs_0_), channel_id=1, source_target_pairs={{0,24},{1,25},{2,26},{3,27},{4,28},{5,29},{6,30},{7,31},{8,16},{9,... | collective-permute-start | bytes 196616 | tf_op jit(solution)/shard_map/ppermute | solution.py:389
  38.3 5.0 %collective-permute-start.17 = (bf16[16,2048]{1,0:T(8,128)(2,1)S(1)}, bf16[16,2048]{1,0:T(8,128)(2,1)S(1)}, u32[]{:S(2)}, u32[]{:S(2)}) collective-permute-start(bf16[16,2048]{1,0:T(8,128)(2,1)S(1)} %combine.1.refs_0_), channel_id=1, source_target_pairs={{0,16},{1,17},{2,18},{3,19},{4,20},{5,21},{6,22},{7,23},{8,24},{9,... | collective-permute-start | bytes 196616 | tf_op jit(solution)/shard_map/ppermute | solution.py:389
  38.9 4.4 %collective-permute-start.16 = (bf16[16,2048]{1,0:T(8,128)(2,1)S(1)}, bf16[16,2048]{1,0:T(8,128)(2,1)S(1)}, u32[]{:S(2)}, u32[]{:S(2)}) collective-permute-start(bf16[16,2048]{1,0:T(8,128)(2,1)S(1)} %combine.1.refs_0_), channel_id=1, source_target_pairs={{0,8},{1,9},{2,10},{3,11},{4,12},{5,13},{6,14},{7,15},{8,0},{9,1},... | collective-permute-start | bytes 196616 | tf_op jit(solution)/shard_map/ppermute | solution.py:389
